TPU v7x, 32 devices: a whole 2x2x4 slice. The times are simulated.
32 devices in a mesh: grp: 2 (over x), lon: 16 (over z, y, core).
Axes of the slice: x: 2, y: 2, z: 4, core: 2. Of those that a mesh axis runs over, the one named last changes fastest.
Arguments:
- tracer_pert: float32 [4, 50, 32, 1024], P('grp', None, 'lon'), parts along dimension 0, may hold values from -60 to 60
- surface_pert: float32 [4, 32, 1024], P('grp', 'lon'), parts along dimension 0, may hold values from -60 to 60
- zonal_flow: float32 [50, 32, 1024], P(None, 'lon'), may hold values from -3.2 to 3.2
- merid_flow: float32 [50, 32, 1024], P(None, 'lon'), may hold values from -3.2 to 3.2
- bottom_level: int32 [32, 1024], P('lon'), may hold values from 0 to 50
Outputs:
- tracer_vec: float32 [4, 50, 32, 1024], P('grp', None, 'lon'), parts along dimension 0
- surface_vec: float32 [4, 32, 1024], P('grp', 'lon'), parts along dimension 0
- growth: float32 [6], P('grp'), parts along dimension 0
There are 2 independent parts, one for each index of `grp`. A program takes and returns all parts, laid end to end along the dimension named above; an argument that names none is the same for every part. Nothing has to cross between parts.
Inputs may be any that keep to these rules, and one draw needn't show every extreme that they name: `bottom_level`: 0 marks a land column, 50 a column wet to the bottom level.
All inputs are finite; a program needn't handle non-finite values.
Results may differ from a plain program's by a relative error of at most 0.0001.
Values sent between devices are 32-bit elements; how exact they have to be, the bound alone decides.
No kernel may reach another device: no remote copies, remote signals or barrier semaphores. Data moves between devices by JAX's collectives and lax.ppermute only.
A program may use at most 64 MiB of HBM per device.

v0:
```python
import jax
import jax.numpy as jnp
from jax import lax
from jax.sharding import PartitionSpec as P

ITERS = 3


DIFFUSIVITY = 0.5
TIME_STEP = 0.2
SURFACE_COUPLING = 0.5
STERIC_GAIN = 2.0
EPSILON = 1e-06


def extended_2(block, sides, width):
    for axis, dim in sides:
        count = lax.axis_size(axis)
        forward = [(i, i + 1) for i in range(count - 1)]
        forward.append((count - 1, 0))
        backward = [(target, source) for source, target in forward]
        low = lax.ppermute(
            lax.slice_in_dim(block, block.shape[dim] - width, None, axis=dim), axis, forward
        )
        high = lax.ppermute(lax.slice_in_dim(block, 0, width, axis=dim), axis, backward)
        block = jnp.concatenate([low, block, high], axis=dim)
    return block


def tracer_update(tracer, zonal_flow, merid_flow, wet_cells):
    face_x = wet_cells[:, :-1] * wet_cells[:, 1:]
    flow_x = 0.5 * (zonal_flow[:, :-1] + zonal_flow[:, 1:])
    west_vals = tracer[:, :, :-1]
    east_vals = tracer[:, :, 1:]
    flux_x = face_x * (
        0.5 * flow_x * (west_vals + east_vals) - DIFFUSIVITY * (east_vals - west_vals)
    )
    div_x = flux_x[:, :, 1:] - flux_x[:, :, :-1]
    interior = tracer[:, :, 1:-1]
    wet_mid = wet_cells[:, 1:-1]
    merid_mid = merid_flow[:, 1:-1]
    face_y = wet_mid[..., :-1] * wet_mid[..., 1:]
    flow_y = 0.5 * (merid_mid[..., :-1] + merid_mid[..., 1:])
    flux_y = face_y * (
        0.5 * flow_y * (interior[..., :-1] + interior[..., 1:])
        - DIFFUSIVITY * (interior[..., 1:] - interior[..., :-1])
    )
    padded = jnp.pad(flux_y, ((0, 0), (0, 0), (0, 0), (1, 1)))
    div_y = padded[..., 1:] - padded[..., :-1]
    return interior - TIME_STEP * (div_x + div_y)


def surface_operator(extended, face_x, face_y):
    grad_x = face_x * (extended[:, 1:] - extended[:, :-1])
    lap_x = grad_x[:, 1:] - grad_x[:, :-1]
    center = extended[:, 1:-1]
    grad_y = face_y * (center[..., 1:] - center[..., :-1])
    padded = jnp.pad(grad_y, ((0, 0), (0, 0), (1, 1)))
    lap_y = padded[..., 1:] - padded[..., :-1]
    return center - SURFACE_COUPLING * (lap_x + lap_y)


def apply_operator(surface, face_x, face_y):
    extended = extended_2(surface, (("lon", 1),), 1)
    return surface_operator(extended, face_x, face_y)


def local_products(lhs_field, rhs_field):
    return jnp.sum(lhs_field * rhs_field, axis=(1, 2))


def residual_squares(residual):
    return lax.psum(local_products(residual, residual), "lon")


def on_device(tracer_pert, surface_pert, zonal_flow, merid_flow, bottom_level):
    vectors, levels_count, columns, lat_rows = tracer_pert.shape
    levels = jnp.arange(levels_count, dtype=jnp.float32)[:, None, None]
    depths = bottom_level.astype(jnp.float32)
    wet_cells = (levels < depths[None]).astype(jnp.float32)
    tracer = wet_cells[None] * tracer_pert
    lead_rows = vectors * levels_count
    stacked = jnp.concatenate(
        [
            tracer.reshape(lead_rows, columns, lat_rows),
            surface_pert,
            zonal_flow,
            merid_flow,
            depths[None],
        ],
        axis=0,
    )
    extended = extended_2(stacked, (("lon", 1),), 1)
    tracer_ext = extended[:lead_rows].reshape(vectors, levels_count, columns + 2, lat_rows)
    zonal_ext = extended[lead_rows + vectors : lead_rows + vectors + levels_count]
    merid_ext = extended[
        lead_rows + vectors + levels_count : lead_rows + vectors + 2 * levels_count
    ]
    depth_ext = extended[-1]
    wet_ext = (levels < depth_ext[None]).astype(jnp.float32)
    tracer = tracer_update(tracer_ext, zonal_ext, merid_ext, wet_ext)
    refreshed = extended_2(tracer, (("lon", 2),), 1)
    tracer = tracer_update(refreshed, zonal_ext, merid_ext, wet_ext)
    surface_rim = extended[lead_rows : lead_rows + vectors]
    depth_rim = extended[-1]
    land_free = (depth_rim > 0).astype(jnp.float32)
    height_ext = surface_rim * land_free[None]
    face_x = jnp.minimum(depth_rim[:-1], depth_rim[1:])
    depth_mid = depth_rim[1:-1]
    face_y = jnp.minimum(depth_mid[:, :-1], depth_mid[:, 1:])
    height = height_ext[:, 1:-1]
    forcing = height + STERIC_GAIN * jnp.sum(tracer, axis=1) / levels_count
    residual = forcing - surface_operator(height_ext, face_x, face_y)
    solution = height
    direction = residual
    norm_now = residual_squares(residual)
    for iteration in range(ITERS):
        image_vec = apply_operator(direction, face_x, face_y)
        step_size = norm_now / lax.psum(local_products(direction, image_vec), "lon")
        solution = solution + step_size[:, None, None] * direction
        residual = residual - step_size[:, None, None] * image_vec
        if iteration + 1 < ITERS:
            norm_next = residual_squares(residual)
            direction = residual + (norm_next / norm_now)[:, None, None] * direction
            norm_now = norm_next
    cell_count = (levels_count + 1) * columns * lat_rows * lax.axis_size("lon")

    def local_inner(tracer_a, surface_a, tracer_b, surface_b):
        return (jnp.sum(tracer_a * tracer_b) + jnp.sum(surface_a * surface_b)) / cell_count

    first_tracer, second_tracer = (tracer[0], tracer[1])
    first_surface, second_surface = (solution[0], solution[1])
    gram_one, gram_mix, gram_two = lax.psum(
        (
            local_inner(first_tracer, first_surface, first_tracer, first_surface),
            local_inner(second_tracer, second_surface, first_tracer, first_surface),
            local_inner(second_tracer, second_surface, second_tracer, second_surface),
        ),
        "lon",
    )
    scale_one = jnp.sqrt(gram_one + EPSILON)
    cross = gram_mix / scale_one
    unit_tracer = first_tracer / scale_one
    unit_surface = first_surface / scale_one
    rest_tracer = second_tracer - cross * unit_tracer
    rest_surface = second_surface - cross * unit_surface
    rest_norm = gram_two - 2.0 * cross * cross + cross * cross * gram_one / (gram_one + EPSILON)
    scale_two = jnp.sqrt(rest_norm + EPSILON)
    tracer_vec = jnp.stack([unit_tracer, rest_tracer / scale_two])
    surface_vec = jnp.stack([unit_surface, rest_surface / scale_two])
    growth = jnp.stack([scale_one, cross, scale_two])
    return (tracer_vec, surface_vec, growth)


def solution(mesh):
    placed = (
        P("grp", None, "lon", None),
        P("grp", "lon", None),
        P(None, "lon", None),
        P(None, "lon", None),
        P("lon", None),
    )
    return jax.shard_map(
        on_device,
        mesh=mesh,
        in_specs=placed,
        out_specs=(P("grp", None, "lon", None), P("grp", "lon", None), P("grp")),
        check_vma=False,
    )
```

profile of v0, /device:TPU:0, one launch (start us, length us, event | category | flops | bytes accessed | tf_op | source)
XLA Modules:
  0.0 270.8 jit_solution(4647945465952432828)
XLA Ops:
  0.6 0.7 convert_element_type.23
  1.5 1.6 broadcast_multiply_fusion
  3.3 0.8 copy-done
  4.2 1.3 fusion.35
  5.6 5.5 %collective-permute-start.1 = (f32[203,1,1024]{2,0,1:T(8,128)S(1)}, f32[203,1,1024]{2,0,1:T(8,128)S(1)}, u32[]{:S(2)}, u32[]{:S(2)}) collective-permute-start(f32[203,1,1024]{2,0,1:T(8,128)S(1)} %copy.20), channel_id=1, source_target_pairs={{1,0},{2,1},{3,2},{4,3},{5,4},{6,5},{7,6},{8,7},{9,8},{10,9},{11,1... | collective-permute-start | bytes 2494472 | tf_op jit(solution)/shard_map/ppermute | solution.py:25
  11.3 0.2 collective-permute-start
  11.6 0.5 add_multiply_fusion
  12.1 9.2 %collective-permute-done.1 = f32[203,1,1024]{2,0,1:T(8,128)S(1)} collective-permute-done((f32[203,1,1024]{2,0,1:T(8,128)S(1)}, f32[203,1,1024]{2,0,1:T(8,128)S(1)}, u32[]{:S(2)}, u32[]{:S(2)}) %collective-permute-start.1) | collective-permute-done | bytes 831520 | tf_op jit(solution)/shard_map/ppermute | solution.py:25
  21.3 0.9 copy.22
  22.2 4.2 %collective-permute-done = f32[203,1,1024]{2,0,1:T(8,128)S(1)} collective-permute-done((f32[203,1,1024]{2,0,1:T(8,128)S(1)}, f32[203,1,1024]{2,0,1:T(8,128)S(1)}, u32[]{:S(2)}, u32[]{:S(2)}) %collective-permute-start) | collective-permute-done | bytes 831520 | tf_op jit(solution)/shard_map/ppermute | solution.py:22
  26.4 0.9 copy.21
  27.3 0.2 fusion.7
  27.5 0.5 slice_multiply_fusion.1
  28.0 0.9 fusion.6
  28.9 2.6 pad_maximum_fusion
  31.7 1.5 subtract_multiply_fusion.3
  33.2 0.9 subtract_multiply_fusion.1
  34.1 1.5 fusion.5
  35.6 0.6 fusion.36
  36.2 2.8 %collective-permute-start.2 = (f32[2,50,1,1024]{3,2,1,0:T(1,128)S(1)}, f32[2,50,1,1024]{3,2,1,0:T(1,128)S(1)}, u32[]{:S(2)}, u32[]{:S(2)}) collective-permute-start(f32[2,50,1,1024]{3,2,1,0:T(1,128)S(1)} %get-tuple-element.36), channel_id=1, source_target_pairs={{0,1},{1,2},{2,3},{3,4},{4,5},{5,6},{6,7},{7,8},{8,9},{9,10},{10,1... | collective-permute-start | bytes 1228808 | tf_op jit(solution)/shard_map/ppermute | solution.py:22
  39.0 1.7 collective-permute-start.3
  40.8 1.1 subtract_multiply_fusion.2
  41.9 4.5 %collective-permute-done.2 = f32[2,50,1,1024]{3,2,1,0:T(1,128)S(1)} collective-permute-done((f32[2,50,1,1024]{3,2,1,0:T(1,128)S(1)}, f32[2,50,1,1024]{3,2,1,0:T(1,128)S(1)}, u32[]{:S(2)}, u32[]{:S(2)}) %collective-permute-start.2) | collective-permute-done | bytes 409632 | tf_op jit(solution)/shard_map/ppermute | solution.py:22
  46.5 1.7 subtract_multiply_fusion
  48.2 1.5 fusion.33
  49.9 4.2 %collective-permute-start.5 = (f32[2,1,1024]{2,1,0:T(1,128)S(1)}, f32[2,1,1024]{2,1,0:T(1,128)S(1)}, u32[]{:S(2)}, u32[]{:S(2)}) collective-permute-start(f32[2,1,1024]{2,1,0:T(1,128)S(1)} %get-tuple-element.42), channel_id=1, source_target_pairs={{0,1},{1,2},{2,3},{3,4},{4,5},{5,6},{6,7},{7,8},{8,9},{9,10},{10,1... | collective-permute-start | bytes 24584 | tf_op jit(solution)/shard_map/ppermute | solution.py:22
  54.1 0.4 collective-permute-start.4
  54.5 1.2 collective-permute-done.5
  55.7 0.5 collective-permute-done.4
  56.2 0.2 multiply_reduce_fusion.6
  56.4 33.5 %all-reduce.7 = (f32[2]{0:T(128)S(1)}, f32[2]{0:T(128)S(1)}) all-reduce(f32[2]{0:T(128)S(1)} %get-tuple-element.13, f32[2]{0:T(128)S(1)} %get-tuple-element.12), channel_id=1, replica_groups=mesh['grp'=2,'lon'=16] {'lon'}, use_global_device_ids=true, to_apply=%region_3.4 | all-reduce | flops 4 | bytes 32 | tf_op jit(solution)/shard_map/psum | solution.py:73
  89.9 0.2 multiply_reduce_fusion.5
  90.1 29.5 %psum.65 = f32[2]{0:T(128)S(1)} all-reduce(f32[2]{0:T(128)S(1)} %get-tuple-element.27), channel_id=1, replica_groups=mesh['grp'=2,'lon'=16] {'lon'}, use_global_device_ids=true, to_apply=%region_7.8 | all-reduce | flops 2 | bytes 16 | tf_op jit(solution)/shard_map/psum | solution.py:73
  119.8 4.4 %collective-permute-start.6 = (f32[2,1,1024]{2,1,0:T(1,128)S(1)}, f32[2,1,1024]{2,1,0:T(1,128)S(1)}, u32[]{:S(2)}, u32[]{:S(2)}) collective-permute-start(f32[2,1,1024]{2,1,0:T(1,128)S(1)} %get-tuple-element.41), channel_id=1, source_target_pairs={{1,0},{2,1},{3,2},{4,3},{5,4},{6,5},{7,6},{8,7},{9,8},{10,9},{11,1... | collective-permute-start | bytes 24584 | tf_op jit(solution)/shard_map/ppermute | solution.py:25
  124.3 1.2 collective-permute-done.7
  125.6 0.2 multiply_reduce_fusion.4
  125.8 33.9 %psum.66 = f32[2]{0:T(128)S(1)} all-reduce(f32[2]{0:T(128)S(1)} %get-tuple-element.25), channel_id=1, replica_groups=mesh['grp'=2,'lon'=16] {'lon'}, use_global_device_ids=true, to_apply=%region_9.10 | all-reduce | flops 2 | bytes 16 | tf_op jit(solution)/shard_map/psum | solution.py:119
  159.8 29.5 %psum.67 = f32[2]{0:T(128)S(1)} all-reduce(f32[2]{0:T(128)S(1)} %get-tuple-element.23), channel_id=1, replica_groups=mesh['grp'=2,'lon'=16] {'lon'}, use_global_device_ids=true, to_apply=%region_11.12 | all-reduce | flops 2 | bytes 16 | tf_op jit(solution)/shard_map/psum | solution.py:73
  189.5 4.4 %collective-permute-start.8 = (f32[2,1,1024]{2,1,0:T(1,128)S(1)}, f32[2,1,1024]{2,1,0:T(1,128)S(1)}, u32[]{:S(2)}, u32[]{:S(2)}) collective-permute-start(f32[2,1,1024]{2,1,0:T(1,128)S(1)} %get-tuple-element.39), channel_id=1, source_target_pairs={{1,0},{2,1},{3,2},{4,3},{5,4},{6,5},{7,6},{8,7},{9,8},{10,9},{11,1... | collective-permute-start | bytes 24584 | tf_op jit(solution)/shard_map/ppermute | solution.py:25
  194.0 1.2 collective-permute-done.9
  195.5 1.2 multiply_reduce_fusion.1
  196.7 33.9 %psum.68 = f32[2]{0:T(128)S(1)} all-reduce(f32[2]{0:T(128)S(1)} %fusion.12), channel_id=1, replica_groups=mesh['grp'=2,'lon'=16] {'lon'}, use_global_device_ids=true, to_apply=%region_13.14 | all-reduce | flops 2 | bytes 16 | tf_op jit(solution)/shard_map/psum | solution.py:119
  230.7 0.7 multiply_reduce_fusion.9
  235.2 30.0 %all-reduce.6 = (f32[]{:T(128)}, f32[]{:T(128)}, f32[]{:T(128)}) all-reduce(f32[]{:T(128)S(6)} %div.73, f32[]{:T(128)S(6)} %div.78, f32[]{:T(128)S(6)} %div.76), channel_id=1, replica_groups=mesh['grp'=2,'lon'=16] {'lon'}, use_global_device_ids=true, to_apply=%region_15.16 | all-reduce | flops 3 | bytes 24 | tf_op jit(solution)/shard_map/psum | solution.py:133
  268.0 0.3 subtract_divide_fusion
  268.3 0.6 pad_maximum_fusion.7
  268.9 1.3 pad_maximum_fusion.3
  270.2 0.6 pad_maximum_fusion.8
  (48 shorter events, 2.4 us)
Async XLA Ops:
  1.5 1.7 copy-start.3
  1.5 1.7 copy-start.1
  3.1 1.0 copy-start
  3.1 1.1 copy-start.2
  5.6 15.7 %collective-permute-start.1 = (f32[203,1,1024]{2,0,1:T(8,128)S(1)}, f32[203,1,1024]{2,0,1:T(8,128)S(1)}, u32[]{:S(2)}, u32[]{:S(2)}) collective-permute-start(f32[203,1,1024]{2,0,1:T(8,128)S(1)} %copy.20), channel_id=1, source_target_pairs={{1,0},{2,1},{3,2},{4,3},{5,4},{6,5},{7,6},{8,7},{9,8},{10,9},{11,1... | collective-permute-start | bytes 2494472 | tf_op jit(solution)/shard_map/ppermute | solution.py:25
  11.3 15.2 %collective-permute-start = (f32[203,1,1024]{2,0,1:T(8,128)S(1)}, f32[203,1,1024]{2,0,1:T(8,128)S(1)}, u32[]{:S(2)}, u32[]{:S(2)}) collective-permute-start(f32[203,1,1024]{2,0,1:T(8,128)S(1)} %copy.19), channel_id=1, source_target_pairs={{0,1},{1,2},{2,3},{3,4},{4,5},{5,6},{6,7},{7,8},{8,9},{9,10},{10,1... | collective-permute-start | bytes 2494472 | tf_op jit(solution)/shard_map/ppermute | solution.py:22
  36.2 10.2 %collective-permute-start.2 = (f32[2,50,1,1024]{3,2,1,0:T(1,128)S(1)}, f32[2,50,1,1024]{3,2,1,0:T(1,128)S(1)}, u32[]{:S(2)}, u32[]{:S(2)}) collective-permute-start(f32[2,50,1,1024]{3,2,1,0:T(1,128)S(1)} %get-tuple-element.36), channel_id=1, source_target_pairs={{0,1},{1,2},{2,3},{3,4},{4,5},{5,6},{6,7},{7,8},{8,9},{9,10},{10,1... | collective-permute-start | bytes 1228808 | tf_op jit(solution)/shard_map/ppermute | solution.py:22
  39.0 7.5 %collective-permute-start.3 = (f32[2,50,1,1024]{3,2,1,0:T(1,128)S(1)}, f32[2,50,1,1024]{3,2,1,0:T(1,128)S(1)}, u32[]{:S(2)}, u32[]{:S(2)}) collective-permute-start(f32[2,50,1,1024]{3,2,1,0:T(1,128)S(1)} %get-tuple-element.37), channel_id=1, source_target_pairs={{1,0},{2,1},{3,2},{4,3},{5,4},{6,5},{7,6},{8,7},{9,8},{10,9},{11,1... | collective-permute-start | bytes 1228808 | tf_op jit(solution)/shard_map/ppermute | solution.py:25
  49.9 5.8 %collective-permute-start.5 = (f32[2,1,1024]{2,1,0:T(1,128)S(1)}, f32[2,1,1024]{2,1,0:T(1,128)S(1)}, u32[]{:S(2)}, u32[]{:S(2)}) collective-permute-start(f32[2,1,1024]{2,1,0:T(1,128)S(1)} %get-tuple-element.42), channel_id=1, source_target_pairs={{0,1},{1,2},{2,3},{3,4},{4,5},{5,6},{6,7},{7,8},{8,9},{9,10},{10,1... | collective-permute-start | bytes 24584 | tf_op jit(solution)/shard_map/ppermute | solution.py:22
  54.1 2.1 collective-permute-start.4
  119.7 5.8 %collective-permute-start.7 = (f32[2,1,1024]{2,1,0:T(1,128)S(1)}, f32[2,1,1024]{2,1,0:T(1,128)S(1)}, u32[]{:S(2)}, u32[]{:S(2)}) collective-permute-start(f32[2,1,1024]{2,1,0:T(1,128)S(1)} %get-tuple-element.40), channel_id=1, source_target_pairs={{0,1},{1,2},{2,3},{3,4},{4,5},{5,6},{6,7},{7,8},{8,9},{9,10},{10,1... | collective-permute-start | bytes 24584 | tf_op jit(solution)/shard_map/ppermute | solution.py:22
  119.8 5.8 %collective-permute-start.6 = (f32[2,1,1024]{2,1,0:T(1,128)S(1)}, f32[2,1,1024]{2,1,0:T(1,128)S(1)}, u32[]{:S(2)}, u32[]{:S(2)}) collective-permute-start(f32[2,1,1024]{2,1,0:T(1,128)S(1)} %get-tuple-element.41), channel_id=1, source_target_pairs={{1,0},{2,1},{3,2},{4,3},{5,4},{6,5},{7,6},{8,7},{9,8},{10,9},{11,1... | collective-permute-start | bytes 24584 | tf_op jit(solution)/shard_map/ppermute | solution.py:25
  189.4 5.8 %collective-permute-start.9 = (f32[2,1,1024]{2,1,0:T(1,128)S(1)}, f32[2,1,1024]{2,1,0:T(1,128)S(1)}, u32[]{:S(2)}, u32[]{:S(2)}) collective-permute-start(f32[2,1,1024]{2,1,0:T(1,128)S(1)} %get-tuple-element.38), channel_id=1, source_target_pairs={{0,1},{1,2},{2,3},{3,4},{4,5},{5,6},{6,7},{7,8},{8,9},{9,10},{10,1... | collective-permute-start | bytes 24584 | tf_op jit(solution)/shard_map/ppermute | solution.py:22
  189.5 5.8 %collective-permute-start.8 = (f32[2,1,1024]{2,1,0:T(1,128)S(1)}, f32[2,1,1024]{2,1,0:T(1,128)S(1)}, u32[]{:S(2)}, u32[]{:S(2)}) collective-permute-start(f32[2,1,1024]{2,1,0:T(1,128)S(1)} %get-tuple-element.39), channel_id=1, source_target_pairs={{1,0},{2,1},{3,2},{4,3},{5,4},{6,5},{7,6},{8,7},{9,8},{10,9},{11,1... | collective-permute-start | bytes 24584 | tf_op jit(solution)/shard_map/ppermute | solution.py:25
where the time goes:
time: 271 us
  blocking collectives  190 us (70%)
  starting transfers between devices  23.8 us (9%)
  waiting for transfers between devices  22.2 us (8%)
  other arithmetic  21.9 us (8%)
  between operations  7.55 us (3%)
  local copies, waits for them, and re-layouts  5.13 us (2%)
    psum x3, blocking collectives, residual_squares(): return lax.psum(local_products(residual, residual), 'lon')  92.5 us
    psum x2, blocking collectives, on_device(): step_size = norm_now / lax.psum(local_products(direction, image_vec), 'lon')  67.8 us
    psum x1, blocking collectives, on_device(): lax.psum((local_inner(first_tracer, first_surface, first_tracer, first_su...  30 us
    ppermute x5, starting transfers between devices, extended_2(): lax.ppermute(lax.slice_in_dim(block, 0, width, axis=dim), axis, backward)  16.5 us
    ppermute x5, waiting for transfers between devices, extended_2(): lax.ppermute(lax.slice_in_dim(block, block.shape[dim] - width, None, axis...  12.4 us
    ppermute x5, waiting for transfers between devices, extended_2(): lax.ppermute(lax.slice_in_dim(block, 0, width, axis=dim), axis, backward)  9.76 us
    ppermute x5, starting transfers between devices, extended_2(): lax.ppermute(lax.slice_in_dim(block, block.shape[dim] - width, None, axis...  7.27 us
  transfers between devices with their start and end apart: 10, of which 7 were waited for; matrix products, arithmetic and copies ran while one was open for 1% of the time, Pallas kernels for 0%

commit v1 on v0

v1 whole, which is shorter than its diff:
```python
import functools

import jax
import jax.numpy as jnp
from jax import lax
from jax.experimental import pallas as pl
from jax.experimental.pallas import tpu as pltpu
from jax.sharding import PartitionSpec as P

ITERS = 3


DIFFUSIVITY = 0.5
TIME_STEP = 0.2
SURFACE_COUPLING = 0.5
STERIC_GAIN = 2.0
EPSILON = 1e-06

LANES = 128
VECTORS = 2
SLOPE = 0.25 * TIME_STEP
SPREAD = TIME_STEP * DIFFUSIVITY


def next_row(tile):
    turned = pltpu.roll(tile, LANES - 1, 1)
    carried = pltpu.roll(turned, tile.shape[0] - 1, 0)
    lane = lax.broadcasted_iota(jnp.int32, tile.shape, 1)
    return jnp.where(lane == LANES - 1, carried, turned)


def prior_row(tile):
    turned = pltpu.roll(tile, 1, 1)
    carried = pltpu.roll(turned, 1, 0)
    lane = lax.broadcasted_iota(jnp.int32, tile.shape, 1)
    return jnp.where(lane == 0, carried, turned)


def wall_depth(depth):
    subs, lane = (lax.broadcasted_iota(jnp.int32, depth.shape, axis) for axis in (0, 1))
    last = (subs == depth.shape[0] - 1) & (lane == LANES - 1)
    return jnp.where(last, jnp.zeros_like(depth), jnp.minimum(depth, next_row(depth)))


def face_pair(level, face_depth, flow_sum):
    slope = SLOPE * flow_sum
    open_face = level < face_depth
    return (
        jnp.where(open_face, slope + SPREAD, 0.0),
        jnp.where(open_face, slope - SPREAD, 0.0),
    )


def outflow(pair, near, far):
    return pair[0] * near + pair[1] * far


def divergence_y(pair, tile):
    flux = outflow(pair, tile, next_row(tile))
    return flux - prior_row(flux)


def orientation():
    outer = lax.rem(lax.axis_index("lon"), 2)
    return outer, 1 - outer, (2 * outer - 1).astype(jnp.float32)


def first_kernel(levels, sub, tracer, zonal, merid, bottom, cross, mate):
    outer, inner, sign = orientation()

    def column(ref, where, *lead):
        return ref[(*lead, pl.ds(where, sub, stride=2), slice(None))]

    depth = [column(bottom, where).astype(jnp.float32) for where in (outer, inner)]
    between = jnp.minimum(*depth)
    along = [wall_depth(d) for d in depth]
    for buffer, d in zip((cross, mate), depth):
        buffer[(VECTORS * 2 + 1) * levels] = d

    def body(k, carry):
        level = k.astype(jnp.float32)
        flow = [column(zonal, where, k) for where in (outer, inner)]
        turn = [column(merid, where, k) for where in (outer, inner)]
        middle = face_pair(level, between, -sign * (flow[0] + flow[1]))
        sides = [face_pair(level, along[c], turn[c] + next_row(turn[c])) for c in range(2)]
        for v in range(VECTORS):
            cells = [column(tracer, where, v, k) for where in (outer, inner)]
            flux = outflow(middle, *cells)
            for c, buffer in enumerate((cross, mate)):
                kept = jnp.where(level < depth[c], cells[c], 0.0)
                gone = flux if c == 0 else -flux
                buffer[v * levels + k] = cells[c]
                buffer[(VECTORS + 1 + v) * levels + k] = (
                    kept - gone - divergence_y(sides[c], cells[c])
                )
        for c, buffer in enumerate((cross, mate)):
            buffer[VECTORS * levels + k] = flow[c]
        return carry

    lax.fori_loop(0, levels, body, 0, unroll=2)


def second_kernel(levels, sub, cross, mate, cross_far, mate_far, merid, tracer, message):
    outer, inner, sign = orientation()
    depth_row = (VECTORS * 2 + 1) * levels
    near, far = (cross, mate), (cross_far, mate_far)
    depth = [ref[depth_row] for ref in near]
    beside = [jnp.minimum(d, ref[depth_row]) for d, ref in zip(depth, far)]
    between = jnp.minimum(*depth)
    along = [wall_depth(d) for d in depth]
    zero = jnp.zeros_like(between)

    def body(k, carry):
        level = k.astype(jnp.float32)
        flow = [ref[VECTORS * levels + k] for ref in near]
        flow_far = [ref[VECTORS * levels + k] for ref in far]
        turn = [merid[k, pl.ds(where, sub, stride=2), :] for where in (outer, inner)]
        middle = face_pair(level, between, -sign * (flow[0] + flow[1]))
        edges = [
            face_pair(level, beside[c], (sign, -sign)[c] * (flow[c] + flow_far[c]))
            for c in range(2)
        ]
        sides = [face_pair(level, along[c], turn[c] + next_row(turn[c])) for c in range(2)]
        totals, grams = list(carry[:4]), list(carry[4:])
        done = []
        for v in range(VECTORS):
            first, last = v * levels + k, (VECTORS + 1 + v) * levels + k
            own, other = [], []
            for c in range(2):
                flux = outflow(edges[c], near[c][first], far[c][first])
                own.append(near[c][last] - flux)
                other.append(far[c][last] + flux)
            crossing = outflow(middle, *own)
            fresh = []
            for c, where in enumerate((outer, inner)):
                gone = crossing if c == 0 else -crossing
                value = (
                    own[c]
                    - outflow(edges[c], own[c], other[c])
                    - gone
                    - divergence_y(sides[c], own[c])
                )
                tracer[v, k, pl.ds(where, sub, stride=2), :] = value
                totals[v * 2 + c] = totals[v * 2 + c] + value
                fresh.append(value)
            done.append(fresh)
        for c in range(2):
            a, b = done[0][c], done[1][c]
            grams = [grams[0] + a * a, grams[1] + a * b, grams[2] + b * b]
        return (*totals, *grams)

    sums = lax.fori_loop(0, levels, body, (zero,) * 7, unroll=2)
    gain = STERIC_GAIN / levels
    subs = lax.broadcasted_iota(jnp.int32, zero.shape, 0)
    packed = zero
    for i, gram in enumerate(sums[4:]):
        packed = jnp.where(subs == i, jnp.sum(gram, axis=0, keepdims=True), packed)

    def copy(d, carry):
        for v in range(VECTORS):
            for c, where in enumerate((outer, inner)):
                message[d, v * 2 + where] = gain * sums[v * 2 + c]
        message[d, VECTORS * 2] = packed
        return carry

    lax.fori_loop(0, message.shape[0], copy, 0)


def total(tile):
    return jnp.sum(jnp.sum(tile, axis=0, keepdims=True), axis=1, keepdims=True)


def third_kernel(
    levels, sub, gathered, rim, tracer, tracer_out, surface_out, growth, pole, residual, answer, image, face_x, face_y
):
    count = gathered.shape[0]
    width = 2 * count
    me = lax.axis_index("lon")
    zero = jnp.zeros((sub, LANES), jnp.float32)
    group = 2

    def over(body, init, step=1):
        return lax.fori_loop(0, count, body, init, unroll=min(count, 4))

    def depth_of(d, c):
        return rim[d, VECTORS, pl.ds(c, sub, stride=2), :]

    def prepare(d, carry):
        here = [depth_of(d, c) for c in range(group)]
        after = depth_of(lax.rem(d + 1, count), 0)
        spans = [jnp.minimum(here[0], here[1]), jnp.minimum(here[1], after)]
        for c in range(group):
            face_x[2 * d + c + 1] = SURFACE_COUPLING * spans[c]
            face_y[2 * d + c] = SURFACE_COUPLING * wall_depth(here[c])
            for v in range(VECTORS):
                height = jnp.where(here[c] > 0, rim[d, v, pl.ds(c, sub, stride=2), :], 0.0)
                answer[v, 2 * d + c] = height
                pole[v, 2 * d + c + 1] = height
        return carry

    def close(v):
        pole[v, 0] = pole[v, width]
        pole[v, width + 1] = pole[v, 1]

    def spread(d, v):
        x = 2 * d
        cells = [pole[v, x + j] for j in range(group + 2)]
        flux = [face_x[x + j] * (cells[j + 1] - cells[j]) for j in range(group + 1)]
        found = []
        for j in range(group):
            centre = cells[j + 1]
            rise = face_y[x + j] * (next_row(centre) - centre)
            found.append((centre, (flux[j + 1] - flux[j]) + (rise - prior_row(rise))))
        return found

    over(prepare, 0)
    face_x[0] = face_x[width]
    for v in range(VECTORS):
        close(v)

    def start(d, carry):
        sums = list(carry)
        for v in range(VECTORS):
            for c, (_, lap) in enumerate(spread(d, v)):
                value = gathered[d, v * 2 + c] + lap
                residual[v, 2 * d + c] = value
                sums[v] = sums[v] + value * value
        return tuple(sums)

    norm = [total(t) for t in over(start, (zero,) * VECTORS)]

    def restart(d, carry):
        for v in range(VECTORS):
            for c in range(group):
                pole[v, 2 * d + c + 1] = residual[v, 2 * d + c]
        return carry

    over(restart, 0)
    for v in range(VECTORS):
        close(v)

    def apply(d, carry):
        sums = list(carry)
        for v in range(VECTORS):
            for c, (centre, lap) in enumerate(spread(d, v)):
                value = centre - lap
                image[v, 2 * d + c] = value
                sums[v] = sums[v] + centre * value
        return tuple(sums)

    for iteration in range(ITERS):
        energy = [total(t) for t in over(apply, (zero,) * VECTORS)]
        size = [n / e for n, e in zip(norm, energy)]
        if iteration + 1 < ITERS:

            def advance(d, carry, size=size):
                sums = list(carry)
                for v in range(VECTORS):
                    for c in range(group):
                        x = 2 * d + c
                        answer[v, x] = answer[v, x] + size[v] * pole[v, x + 1]
                        value = residual[v, x] - size[v] * image[v, x]
                        residual[v, x] = value
                        sums[v] = sums[v] + value * value
                return tuple(sums)

            fresh = [total(t) for t in over(advance, (zero,) * VECTORS)]
            ratio = [f / n for f, n in zip(fresh, norm)]

            def turn(d, carry, ratio=ratio):
                for v in range(VECTORS):
                    for c in range(group):
                        x = 2 * d + c
                        pole[v, x + 1] = residual[v, x] + ratio[v] * pole[v, x + 1]
                return carry

            over(turn, 0)
            for v in range(VECTORS):
                close(v)
            norm = fresh

    def finish(d, carry):
        grams = list(carry)
        for c in range(group):
            x = 2 * d + c
            a, b = (answer[v, x] + size[v] * pole[v, x + 1] for v in range(VECTORS))
            answer[0, x], answer[1, x] = a, b
            grams = [grams[0] + a * a, grams[1] + a * b, grams[2] + b * b]
        return (*grams, carry[3] + gathered[d, VECTORS * 2])

    *grams, packed = over(finish, (zero,) * 4)
    cells = (levels + 1) * width * sub * LANES
    one, mix, two = (
        (total(g) + jnp.sum(packed[i : i + 1], axis=1, keepdims=True)) / cells
        for i, g in enumerate(grams)
    )
    scale_one = jnp.sqrt(one + EPSILON)
    cross = mix / scale_one
    rest = two - 2.0 * cross * cross + cross * cross * one / (one + EPSILON)
    scale_two = jnp.sqrt(rest + EPSILON)
    over_one, over_two = 1.0 / scale_one, 1.0 / scale_two
    for i, value in enumerate((scale_one, cross, scale_two)):
        growth[i] = value[0, 0]

    for c in range(group):
        x = 2 * me + c
        unit = answer[0, x] * over_one
        surface_out[0, pl.ds(c, sub, stride=2), :] = unit
        surface_out[1, pl.ds(c, sub, stride=2), :] = (answer[1, x] - cross * unit) * over_two

    def scale(k, carry):
        unit = tracer[0, k] * over_one
        tracer_out[0, k] = unit
        tracer_out[1, k] = (tracer[1, k] - cross * unit) * over_two
        return carry

    lax.fori_loop(0, levels, scale, 0, unroll=5)


def tiled(array):
    *lead, columns, rows = array.shape
    split = array.reshape(*lead, columns, rows // LANES, LANES)
    return jnp.swapaxes(split, -3, -2).reshape(*lead, rows // LANES * columns, LANES)


def untiled(array, columns):
    *lead, high, lanes = array.shape
    split = array.reshape(*lead, high // columns, columns, lanes)
    return jnp.swapaxes(split, -3, -2).reshape(*lead, columns, high // columns * lanes)


def on_device(tracer_pert, surface_pert, zonal_flow, merid_flow, bottom_level):
    vectors, levels, columns, rows = tracer_pert.shape
    count = lax.axis_size("lon")
    sub = rows // LANES
    assert vectors == VECTORS and columns == 2 and count % 2 == 0 and rows % LANES == 0
    f32 = jnp.float32
    vmem = pl.BlockSpec(memory_space=pltpu.VMEM)
    params = pltpu.CompilerParams(vmem_limit_bytes=24 * 2**20)

    rim = lax.all_gather(
        jnp.concatenate([surface_pert, bottom_level[None].astype(f32)]), "lon"
    )
    merid = tiled(merid_flow)
    planes = (VECTORS * 2 + 1) * levels + 1
    edge = jax.ShapeDtypeStruct((planes, sub, LANES), f32)
    cross, mate = pl.pallas_call(
        functools.partial(first_kernel, levels, sub),
        out_shape=(edge, edge),
        in_specs=[vmem] * 4,
        out_specs=(vmem, vmem),
        compiler_params=params,
        name="partial_step",
    )(tiled(tracer_pert), tiled(zonal_flow), merid, tiled(bottom_level))
    cross_far = lax.ppermute(
        cross, "lon", [(i, (i + 1) % count if i % 2 else (i - 1) % count) for i in range(count)]
    )
    mate_far = lax.ppermute(mate, "lon", [(i, i + 1 - 2 * (i % 2)) for i in range(count)])
    blocks = VECTORS * 2 + 1
    tracer, message = pl.pallas_call(
        functools.partial(second_kernel, levels, sub),
        out_shape=(
            jax.ShapeDtypeStruct((vectors, levels, sub * 2, LANES), f32),
            jax.ShapeDtypeStruct((count, blocks, sub, LANES), f32),
        ),
        in_specs=[vmem] * 5,
        out_specs=(vmem, vmem),
        compiler_params=params,
        name="both_steps",
    )(cross, mate, cross_far, mate_far, merid)
    gathered = lax.all_to_all(message, "lon", 0, 0)
    width = 2 * count
    field = lambda extra: pltpu.VMEM((vectors, width + extra, sub, LANES), f32)
    tracer_vec, surface_vec, growth = pl.pallas_call(
        functools.partial(third_kernel, levels, sub),
        out_shape=(
            jax.ShapeDtypeStruct((vectors, levels, sub * 2, LANES), f32),
            jax.ShapeDtypeStruct((vectors, sub * 2, LANES), f32),
            jax.ShapeDtypeStruct((3,), f32),
        ),
        in_specs=[vmem] * 3,
        out_specs=(vmem, vmem, pl.BlockSpec(memory_space=pltpu.SMEM)),
        scratch_shapes=[
            field(2),
            field(0),
            field(0),
            field(0),
            pltpu.VMEM((width + 1, sub, LANES), f32),
            pltpu.VMEM((width, sub, LANES), f32),
        ],
        compiler_params=pltpu.CompilerParams(vmem_limit_bytes=32 * 2**20),
        name="surface_and_scale",
    )(gathered, tiled(rim), tracer)
    return (untiled(tracer_vec, 2), untiled(surface_vec, 2), growth)


def solution(mesh):
    placed = (
        P("grp", None, "lon", None),
        P("grp", "lon", None),
        P(None, "lon", None),
        P(None, "lon", None),
        P("lon", None),
    )
    return jax.shard_map(
        on_device,
        mesh=mesh,
        in_specs=placed,
        out_specs=(P("grp", None, "lon", None), P("grp", "lon", None), P("grp")),
        check_vma=False,
    )
```

time: 271 us -> 75.2 us (0.28)
  blocking collectives: 190 us -> 22.8 us
  other arithmetic: 21.9 us -> 0.02 us
  Pallas kernels: 0 us -> 14.1 us
  waiting for transfers between devices: 22.2 us -> 12.4 us
  between operations: 7.55 us -> 0.69 us
  starting transfers between devices: 23.8 us -> 20.2 us
    psum x6 -> x0, blocking collectives: 190 us -> none  [the longest x3 92.5 us: residual_squares(): return lax.psum(local_products(residual, residual), 'lon')]
    all_gather x0 -> x1, blocking collectives: none -> 22.8 us  [on_device(): lax.all_gather(jnp.concatenate([surface_pert, bottom_level[None].astype(f...]
    ppermute x10 -> x2, starting transfers between devices: 23.8 us -> 5.51 us  [the longest x1 5.51 us: on_device(): lax.ppermute(cross, 'lon', [(i, (i + 1) % count if i % 2 else (i - 1) % c...]
    all_to_all x0 -> x1, starting transfers between devices: none -> 14.7 us  [on_device(): gathered = lax.all_to_all(message, 'lon', 0, 0)]
    pallas_call x0 -> x3, Pallas kernels: none -> 14.1 us  [the longest x1 5.09 us: on_device(): pl.pallas_call(functools.partial(second_kernel, levels, sub), out_shape=(...]
    ppermute x10 -> x2, waiting for transfers between devices: 22.2 us -> 12.4 us  [the longest x1 12.4 us: on_device(): lax.ppermute(cross, 'lon', [(i, (i + 1) % count if i % 2 else (i - 1) % c...]
    mul x19 -> x0, other arithmetic: 9.15 us -> none  [the longest x2 2.62 us: tracer_update(): face_x * (0.5 * flow_x * (west_vals + east_vals) - DIFFUSIVITY * (east_va...]
    reduce_sum x8 -> x0, other arithmetic: 4.36 us -> none  [the longest x1 1.54 us: on_device(): forcing = height + STERIC_GAIN * jnp.sum(tracer, axis=1) / levels_count]
  transfers between devices with their start and end apart: 10 -> 3, of which waited for: 7 -> 1; matrix products, arithmetic and copies ran while one was open for 1% -> 0% of each run, Pallas kernels for 0% -> 0%
where the time goes in v1:
time: 75.2 us; the launch traced here: 74.7 us
  blocking collectives  22.8 us (30%)
  starting transfers between devices  20.2 us (27%)
  Pallas kernels  14.1 us (19%)
  waiting for transfers between devices  12.4 us (16%)
  local copies, waits for them, and re-layouts  4.54 us (6%)
    all_gather x1, blocking collectives, on_device(): lax.all_gather(jnp.concatenate([surface_pert, bottom_level[None].astype(f...  22.8 us
    all_to_all x1, starting transfers between devices, on_device(): gathered = lax.all_to_all(message, 'lon', 0, 0)  14.7 us
    ppermute x1, waiting for transfers between devices, on_device(): lax.ppermute(cross, 'lon', [(i, (i + 1) % count if i % 2 else (i - 1) % c...  12.4 us
    ppermute x1, starting transfers between devices, on_device(): lax.ppermute(cross, 'lon', [(i, (i + 1) % count if i % 2 else (i - 1) % c...  5.51 us
    pallas_call x1, Pallas kernels, on_device(): pl.pallas_call(functools.partial(second_kernel, levels, sub), out_shape=(...  5.09 us
    pallas_call x1, Pallas kernels, on_device(): pl.pallas_call(functools.partial(third_kernel, levels, sub), out_shape=(j...  4.98 us
    unnamed x14, local copies, waits for them, and re-layouts  4.54 us
    pallas_call x1, Pallas kernels, on_device(): pl.pallas_call(functools.partial(first_kernel, levels, sub), out_shape=(e...  3.98 us
  transfers between devices with their start and end apart: 3, of which 1 were waited for; matrix products, arithmetic and copies ran while one was open for 0% of the time, Pallas kernels for 0%

profile of v1, /device:TPU:0, one launch (start us, length us, event | category | flops | bytes accessed | tf_op | source)
XLA Modules:
  0.0 74.7 jit_solution(598330176402087039)
XLA Ops:
  0.6 0.0 copy-start
  0.6 1.0 %copy-done = f32[50,2,1024]{2,1,0:T(2,128)S(1)} copy-done((f32[50,2,1024]{2,1,0:T(2,128)S(1)}, f32[50,2,1024]{2,1,0:T(2,128)}, u32[]{:S(2)}) %copy-start) | copy-done | bytes 409624
  1.6 0.0 copy-start.2
  1.6 1.1 %copy-done.2 = f32[2,50,2,1024]{3,2,1,0:T(2,128)S(1)} copy-done((f32[2,50,2,1024]{3,2,1,0:T(2,128)S(1)}, f32[2,50,2,1024]{3,2,1,0:T(2,128)}, u32[]{:S(2)}) %copy-start.2) | copy-done | bytes 819224
  2.8 0.0 copy-start.3
  2.8 1.0 %copy-done.3 = f32[50,2,1024]{2,1,0:T(2,128)S(1)} copy-done((f32[50,2,1024]{2,1,0:T(2,128)S(1)}, f32[50,2,1024]{2,1,0:T(2,128)}, u32[]{:S(2)}) %copy-start.3) | copy-done | bytes 409624
  3.8 0.0 copy-start.4
  3.8 0.7 copy-done.4
  4.5 0.0 copy-start.1
  4.5 4.0 %partial_step.1 = (f32[251,8,128]{2,1,0:T(8,128)S(1)}, f32[251,8,128]{2,1,0:T(8,128)S(1)}) custom-call(f32[2,50,16,128]{3,2,1,0:T(8,128)S(1)} %bitcast.40, f32[50,16,128]{2,1,0:T(8,128)S(1)} %bitcast.41, f32[50,16,128]{2,1,0:T(8,128)S(1)} %bitcast.37, s32[16,128]{1,0:T(8,128)S(1)} %bitcast.42), custom_call_target="tpu_custom_call" | custom-call | tf_op jit(solution)/shard_map/partial_step/pallas_call | solution.py:347
  8.5 5.5 %collective-permute-start = (f32[251,8,128]{2,1,0:T(8,128)S(1)}, f32[251,8,128]{2,1,0:T(8,128)S(1)}, u32[]{:S(2)}, u32[]{:S(2)}) collective-permute-start(f32[251,8,128]{2,1,0:T(8,128)S(1)} %get-tuple-element.10.cross), channel_id=1, source_target_pairs={{0,15},{1,2},{2,1},{3,4},{4,3},{5,6},{6,5},{7,8},{8,7},{9,10},{10,... | collective-permute-start | bytes 3084296 | tf_op jit(solution)/shard_map/ppermute | solution.py:355
  14.0 0.0 collective-permute-start.1
  14.0 12.4 %collective-permute-done.cross_far = f32[251,8,128]{2,1,0:T(8,128)S(1)} collective-permute-done((f32[251,8,128]{2,1,0:T(8,128)S(1)}, f32[251,8,128]{2,1,0:T(8,128)S(1)}, u32[]{:S(2)}, u32[]{:S(2)}) %collective-permute-start) | collective-permute-done | bytes 1028128 | tf_op jit(solution)/shard_map/ppermute | solution.py:355
  26.3 0.0 collective-permute-done.1.mate_far
  26.4 0.0 copy-done.1
  26.4 5.1 %both_steps.1 = (f32[2,50,16,128]{3,2,1,0:T(8,128)S(1)}, f32[16,5,8,128]{3,2,1,0:T(8,128)}) custom-call(f32[251,8,128]{2,1,0:T(8,128)S(1)} %get-tuple-element.10.cross, f32[251,8,128]{2,1,0:T(8,128)S(1)} %get-tuple-element.11.mate, f32[251,8,128]{2,1,0:T(8,128)S(1)} %collective-permute-done.cross_far, f32[251,8,128]{2,1,0:T(8,128)S(1)} %collective-permute-done.1.mate_far, ...), custom_call_target="tpu_custom_call" | custom-call | tf_op jit(solution)/shard_map/both_steps/pallas_call | solution.py:360
  31.4 0.0 copy-start.5
  31.4 14.7 %all-to-all-start = ((f32[16,5,8,128]{3,2,1,0:T(8,128)}), f32[16,5,8,128]{3,2,1,0:T(8,128)S(1)}, u32[]{:S(2)}, u32[]{:S(2)}) async-start(f32[16,5,8,128]{3,2,1,0:T(8,128)} %get-tuple-element.12), calls=%async_computation | async-start | bytes 655360 | tf_op jit(solution)/shard_map/all_to_all | solution.py:371
  46.2 0.0 copy-done.5
  46.2 0.0 copy-start.6
  46.2 0.7 copy-done.6
  46.9 22.8 %all-gather = f32[48,2,1024]{2,1,0:T(2,128)S(1)} all-gather(f32[3,2,1024]{2,1,0:T(2,128)S(1)} %pad_maximum_fusion), channel_id=2, replica_groups=mesh['grp'=2,'lon'=16] {'lon'}, dimensions={0}, use_global_device_ids=true | all-gather | bytes 417792 | tf_op jit(solution)/shard_map/all_gather | solution.py:341
  69.8 0.0 all-to-all-done.gathered
  69.8 5.0 %surface_and_scale.1 = (f32[2,50,16,128]{3,2,1,0:T(8,128)}, f32[2,16,128]{2,1,0:T(8,128)}, f32[3]{0:T(128)}) custom-call(f32[16,5,8,128]{3,2,1,0:T(8,128)S(1)} %all-to-all-done.gathered, f32[16,3,16,128]{3,2,1,0:T(8,128)S(1)} %bitcast.39, f32[2,50,16,128]{3,2,1,0:T(8,128)S(1)} %get-tuple-element.13.tracer), custom_call_target="tpu_custom_call" | custom-call | tf_op jit(solution)/shard_map/surface_and_scale/pallas_call | solution.py:374
  (2 shorter events, 0.0 us)
Async XLA Ops:
  0.6 1.0 %copy-start = (f32[50,2,1024]{2,1,0:T(2,128)S(1)}, f32[50,2,1024]{2,1,0:T(2,128)}, u32[]{:S(2)}) copy-start(f32[50,2,1024]{2,1,0:T(2,128)} %param.8) | copy-start | bytes 1228804
  1.6 1.1 %copy-start.2 = (f32[2,50,2,1024]{3,2,1,0:T(2,128)S(1)}, f32[2,50,2,1024]{3,2,1,0:T(2,128)}, u32[]{:S(2)}) copy-start(f32[2,50,2,1024]{3,2,1,0:T(2,128)} %param.5) | copy-start | bytes 2457604
  2.8 1.0 %copy-start.3 = (f32[50,2,1024]{2,1,0:T(2,128)S(1)}, f32[50,2,1024]{2,1,0:T(2,128)}, u32[]{:S(2)}) copy-start(f32[50,2,1024]{2,1,0:T(2,128)} %param.7) | copy-start | bytes 1228804
  3.8 0.7 copy-start.4
  4.5 21.9 %copy-start.1 = (f32[50,2,1024]{2,1,0:T(2,128)S(1)}, f32[50,2,1024]{2,1,0:T(2,128)}, u32[]{:S(2)}) copy-start(f32[50,2,1024]{2,1,0:T(2,128)} %param.8) | copy-start | bytes 1228804
  8.5 17.9 %collective-permute-start = (f32[251,8,128]{2,1,0:T(8,128)S(1)}, f32[251,8,128]{2,1,0:T(8,128)S(1)}, u32[]{:S(2)}, u32[]{:S(2)}) collective-permute-start(f32[251,8,128]{2,1,0:T(8,128)S(1)} %get-tuple-element.10.cross), channel_id=1, source_target_pairs={{0,15},{1,2},{2,1},{3,4},{4,3},{5,6},{6,5},{7,8},{8,7},{9,10},{10,... | collective-permute-start | bytes 3084296 | tf_op jit(solution)/shard_map/ppermute | solution.py:355
  14.0 12.4 %collective-permute-start.1 = (f32[251,8,128]{2,1,0:T(8,128)S(1)}, f32[251,8,128]{2,1,0:T(8,128)S(1)}, u32[]{:S(2)}, u32[]{:S(2)}) collective-permute-start(f32[251,8,128]{2,1,0:T(8,128)S(1)} %get-tuple-element.11.mate), channel_id=1, source_target_pairs={{0,1},{1,0},{2,3},{3,2},{4,5},{5,4},{6,7},{7,6},{8,9},{9,8},{10,11... | collective-permute-start | bytes 3084296 | tf_op jit(solution)/shard_map/ppermute | solution.py:358
  31.4 14.7 %copy-start.5 = (s32[2,1024]{1,0:T(2,128)S(1)}, s32[2,1024]{1,0:T(2,128)}, u32[]{:S(2)}) copy-start(s32[2,1024]{1,0:T(2,128)} %param.9) | copy-start | bytes 24580
  31.4 38.3 %all-to-all-start = ((f32[16,5,8,128]{3,2,1,0:T(8,128)}), f32[16,5,8,128]{3,2,1,0:T(8,128)S(1)}, u32[]{:S(2)}, u32[]{:S(2)}) async-start(f32[16,5,8,128]{3,2,1,0:T(8,128)} %get-tuple-element.12), calls=%async_computation | async-start | bytes 655360 | tf_op jit(solution)/shard_map/all_to_all | solution.py:371
  46.2 0.7 copy-start.6

commit v2 on v1

--- a/solution.py
+++ b/solution.py
@@ -20,6 +20,10 @@
 VECTORS = 2
 SLOPE = 0.25 * TIME_STEP
 SPREAD = TIME_STEP * DIFFUSIVITY
+HEIGHTS = VECTORS * 2
+DEPTHS = HEIGHTS + VECTORS * 2
+GRAMS = DEPTHS + 2
+BLOCKS = GRAMS + 1
 
 
 def next_row(tile):
@@ -55,9 +59,20 @@
     return pair[0] * near + pair[1] * far
 
 
-def divergence_y(pair, tile):
-    flux = outflow(pair, tile, next_row(tile))
-    return flux - prior_row(flux)
+def side_pairs(level, depths, flow):
+    return (
+        face_pair(level, depths[0], flow + next_row(flow)),
+        face_pair(level, depths[1], -(flow + prior_row(flow))),
+    )
+
+
+def divergence_y(pairs, tile):
+    return outflow(pairs[0], tile, next_row(tile)) + outflow(pairs[1], tile, prior_row(tile))
+
+
+def side_depths(depth):
+    north = wall_depth(depth)
+    return north, prior_row(north)
 
 
 def orientation():
@@ -73,7 +88,7 @@
 
     depth = [column(bottom, where).astype(jnp.float32) for where in (outer, inner)]
     between = jnp.minimum(*depth)
-    along = [wall_depth(d) for d in depth]
+    along = [side_depths(d) for d in depth]
     for buffer, d in zip((cross, mate), depth):
         buffer[(VECTORS * 2 + 1) * levels] = d
 
@@ -82,7 +97,7 @@
         flow = [column(zonal, where, k) for where in (outer, inner)]
         turn = [column(merid, where, k) for where in (outer, inner)]
         middle = face_pair(level, between, -sign * (flow[0] + flow[1]))
-        sides = [face_pair(level, along[c], turn[c] + next_row(turn[c])) for c in range(2)]
+        sides = [side_pairs(level, along[c], turn[c]) for c in range(2)]
         for v in range(VECTORS):
             cells = [column(tracer, where, v, k) for where in (outer, inner)]
             flux = outflow(middle, *cells)
@@ -97,17 +112,19 @@
             buffer[VECTORS * levels + k] = flow[c]
         return carry
 
-    lax.fori_loop(0, levels, body, 0, unroll=2)
-
-
-def second_kernel(levels, sub, cross, mate, cross_far, mate_far, merid, tracer, message):
+    lax.fori_loop(0, levels, body, 0, unroll=10)
+
+
+def second_kernel(
+    levels, sub, cross, mate, cross_far, mate_far, merid, surface, bottom, tracer, message
+):
     outer, inner, sign = orientation()
     depth_row = (VECTORS * 2 + 1) * levels
     near, far = (cross, mate), (cross_far, mate_far)
     depth = [ref[depth_row] for ref in near]
     beside = [jnp.minimum(d, ref[depth_row]) for d, ref in zip(depth, far)]
     between = jnp.minimum(*depth)
-    along = [wall_depth(d) for d in depth]
+    along = [side_depths(d) for d in depth]
     zero = jnp.zeros_like(between)
 
     def body(k, carry):
@@ -120,7 +137,7 @@
             face_pair(level, beside[c], (sign, -sign)[c] * (flow[c] + flow_far[c]))
             for c in range(2)
         ]
-        sides = [face_pair(level, along[c], turn[c] + next_row(turn[c])) for c in range(2)]
+        sides = [side_pairs(level, along[c], turn[c]) for c in range(2)]
         totals, grams = list(carry[:4]), list(carry[4:])
         done = []
         for v in range(VECTORS):
@@ -149,7 +166,7 @@
             grams = [grams[0] + a * a, grams[1] + a * b, grams[2] + b * b]
         return (*totals, *grams)
 
-    sums = lax.fori_loop(0, levels, body, (zero,) * 7, unroll=2)
+    sums = lax.fori_loop(0, levels, body, (zero,) * 7, unroll=10)
     gain = STERIC_GAIN / levels
     subs = lax.broadcasted_iota(jnp.int32, zero.shape, 0)
     packed = zero
@@ -160,7 +177,11 @@
         for v in range(VECTORS):
             for c, where in enumerate((outer, inner)):
                 message[d, v * 2 + where] = gain * sums[v * 2 + c]
-        message[d, VECTORS * 2] = packed
+            for c in range(2):
+                message[d, HEIGHTS + v * 2 + c] = surface[v, pl.ds(c, sub, stride=2), :]
+        for c in range(2):
+            message[d, DEPTHS + c] = bottom[pl.ds(c, sub, stride=2), :].astype(jnp.float32)
+        message[d, GRAMS] = packed
         return carry
 
     lax.fori_loop(0, message.shape[0], copy, 0)
@@ -171,7 +192,7 @@
 
 
 def third_kernel(
-    levels, sub, gathered, rim, tracer, tracer_out, surface_out, growth, pole, residual, answer, image, face_x, face_y
+    levels, sub, gathered, tracer, tracer_out, surface_out, growth, pole, residual, answer, image, face_x, face_y
 ):
     count = gathered.shape[0]
     width = 2 * count
@@ -183,7 +204,7 @@
         return lax.fori_loop(0, count, body, init, unroll=min(count, 4))
 
     def depth_of(d, c):
-        return rim[d, VECTORS, pl.ds(c, sub, stride=2), :]
+        return gathered[d, DEPTHS + c]
 
     def prepare(d, carry):
         here = [depth_of(d, c) for c in range(group)]
@@ -193,7 +214,7 @@
             face_x[2 * d + c + 1] = SURFACE_COUPLING * spans[c]
             face_y[2 * d + c] = SURFACE_COUPLING * wall_depth(here[c])
             for v in range(VECTORS):
-                height = jnp.where(here[c] > 0, rim[d, v, pl.ds(c, sub, stride=2), :], 0.0)
+                height = jnp.where(here[c] > 0, gathered[d, HEIGHTS + v * 2 + c], 0.0)
                 answer[v, 2 * d + c] = height
                 pole[v, 2 * d + c + 1] = height
         return carry
@@ -286,7 +307,7 @@
             a, b = (answer[v, x] + size[v] * pole[v, x + 1] for v in range(VECTORS))
             answer[0, x], answer[1, x] = a, b
             grams = [grams[0] + a * a, grams[1] + a * b, grams[2] + b * b]
-        return (*grams, carry[3] + gathered[d, VECTORS * 2])
+        return (*grams, carry[3] + gathered[d, GRAMS])
 
     *grams, packed = over(finish, (zero,) * 4)
     cells = (levels + 1) * width * sub * LANES
@@ -338,9 +359,6 @@
     vmem = pl.BlockSpec(memory_space=pltpu.VMEM)
     params = pltpu.CompilerParams(vmem_limit_bytes=24 * 2**20)
 
-    rim = lax.all_gather(
-        jnp.concatenate([surface_pert, bottom_level[None].astype(f32)]), "lon"
-    )
     merid = tiled(merid_flow)
     planes = (VECTORS * 2 + 1) * levels + 1
     edge = jax.ShapeDtypeStruct((planes, sub, LANES), f32)
@@ -356,18 +374,17 @@
         cross, "lon", [(i, (i + 1) % count if i % 2 else (i - 1) % count) for i in range(count)]
     )
     mate_far = lax.ppermute(mate, "lon", [(i, i + 1 - 2 * (i % 2)) for i in range(count)])
-    blocks = VECTORS * 2 + 1
     tracer, message = pl.pallas_call(
         functools.partial(second_kernel, levels, sub),
         out_shape=(
             jax.ShapeDtypeStruct((vectors, levels, sub * 2, LANES), f32),
-            jax.ShapeDtypeStruct((count, blocks, sub, LANES), f32),
+            jax.ShapeDtypeStruct((count, BLOCKS, sub, LANES), f32),
         ),
-        in_specs=[vmem] * 5,
+        in_specs=[vmem] * 7,
         out_specs=(vmem, vmem),
         compiler_params=params,
         name="both_steps",
-    )(cross, mate, cross_far, mate_far, merid)
+    )(cross, mate, cross_far, mate_far, merid, tiled(surface_pert), tiled(bottom_level))
     gathered = lax.all_to_all(message, "lon", 0, 0)
     width = 2 * count
     field = lambda extra: pltpu.VMEM((vectors, width + extra, sub, LANES), f32)
@@ -378,7 +395,7 @@
             jax.ShapeDtypeStruct((vectors, sub * 2, LANES), f32),
             jax.ShapeDtypeStruct((3,), f32),
         ),
-        in_specs=[vmem] * 3,
+        in_specs=[vmem] * 2,
         out_specs=(vmem, vmem, pl.BlockSpec(memory_space=pltpu.SMEM)),
         scratch_shapes=[
             field(2),
@@ -390,7 +407,7 @@
         ],
         compiler_params=pltpu.CompilerParams(vmem_limit_bytes=32 * 2**20),
         name="surface_and_scale",
-    )(gathered, tiled(rim), tracer)
+    )(gathered, tracer)
     return (untiled(tracer_vec, 2), untiled(surface_vec, 2), growth)
 
 

time: 75.2 us -> 64.2 us (0.85)
  starting transfers between devices: 20.2 us -> 5.51 us
  blocking collectives: 22.8 us -> 33.5 us
  Pallas kernels: 14.1 us -> 7.72 us
    all_to_all x0 -> x1, blocking collectives: none -> 33.5 us  [on_device(): gathered = lax.all_to_all(message, 'lon', 0, 0)]
    all_gather x1 -> x0, blocking collectives: 22.8 us -> none  [on_device(): lax.all_gather(jnp.concatenate([surface_pert, bottom_level[None].astype(f...]
    all_to_all x1 -> x0, starting transfers between devices: 14.7 us -> none  [on_device(): gathered = lax.all_to_all(message, 'lon', 0, 0)]
    pallas_call x1, Pallas kernels: 5.09 us -> 1.56 us  [on_device(): pl.pallas_call(functools.partial(second_kernel, levels, sub), out_shape=(...]
    pallas_call x1, Pallas kernels: 3.98 us -> 1.19 us  [on_device(): pl.pallas_call(functools.partial(first_kernel, levels, sub), out_shape=(e...]
  transfers between devices with their start and end apart: 3 -> 2, of which waited for: 1 -> 1; matrix products, arithmetic and copies ran while one was open for 0% -> 0% of each run, Pallas kernels for 0% -> 0%
where the time goes in v2:
time: 64.2 us; the launch traced here: 63.6 us
  blocking collectives  33.5 us (52%)
  waiting for transfers between devices  12.4 us (19%)
  Pallas kernels  7.72 us (12%)
  starting transfers between devices  5.51 us (9%)
  local copies, waits for them, and re-layouts  3.85 us (6%)
  between operations  0.67 us (1%)
    all_to_all x1, blocking collectives, on_device(): gathered = lax.all_to_all(message, 'lon', 0, 0)  33.5 us
    ppermute x1, waiting for transfers between devices, on_device(): lax.ppermute(cross, 'lon', [(i, (i + 1) % count if i % 2 else (i - 1) % c...  12.4 us
    ppermute x1, starting transfers between devices, on_device(): lax.ppermute(cross, 'lon', [(i, (i + 1) % count if i % 2 else (i - 1) % c...  5.51 us
    pallas_call x1, Pallas kernels, on_device(): pl.pallas_call(functools.partial(third_kernel, levels, sub), out_shape=(j...  4.97 us
    unnamed x14, local copies, waits for them, and re-layouts  3.85 us
    pallas_call x1, Pallas kernels, on_device(): pl.pallas_call(functools.partial(second_kernel, levels, sub), out_shape=(...  1.56 us
  transfers between devices with their start and end apart: 2, of which 1 were waited for; matrix products, arithmetic and copies ran while one was open for 0% of the time, Pallas kernels for 0%

profile of v2, /device:TPU:0, one launch (start us, length us, event | category | flops | bytes accessed | tf_op | source)
XLA Modules:
  0.0 63.6 jit_solution(506475294153318748)
XLA Ops:
  0.6 0.0 copy-start
  0.6 1.0 %copy-done = f32[50,2,1024]{2,1,0:T(2,128)S(1)} copy-done((f32[50,2,1024]{2,1,0:T(2,128)S(1)}, f32[50,2,1024]{2,1,0:T(2,128)}, u32[]{:S(2)}) %copy-start) | copy-done | bytes 409624
  1.6 0.0 copy-start.2
  1.6 1.1 %copy-done.2 = f32[2,50,2,1024]{3,2,1,0:T(2,128)S(1)} copy-done((f32[2,50,2,1024]{3,2,1,0:T(2,128)S(1)}, f32[2,50,2,1024]{3,2,1,0:T(2,128)}, u32[]{:S(2)}) %copy-start.2) | copy-done | bytes 819224
  2.8 0.0 copy-start.3
  2.8 1.0 %copy-done.3 = f32[50,2,1024]{2,1,0:T(2,128)S(1)} copy-done((f32[50,2,1024]{2,1,0:T(2,128)S(1)}, f32[50,2,1024]{2,1,0:T(2,128)}, u32[]{:S(2)}) %copy-start.3) | copy-done | bytes 409624
  3.8 0.0 copy-start.4
  3.8 0.7 %copy-done.4 = s32[2,1024]{1,0:T(2,128)S(1)} copy-done((s32[2,1024]{1,0:T(2,128)S(1)}, s32[2,1024]{1,0:T(2,128)}, u32[]{:S(2)}) %copy-start.4) | copy-done | bytes 8216
  4.5 0.0 copy-start.1
  4.5 0.0 copy-start.5
  4.5 0.0 copy-start.6
  4.5 1.2 %partial_step.1 = (f32[251,8,128]{2,1,0:T(8,128)S(1)}, f32[251,8,128]{2,1,0:T(8,128)S(1)}) custom-call(f32[2,50,16,128]{3,2,1,0:T(8,128)S(1)} %bitcast.37, f32[50,16,128]{2,1,0:T(8,128)S(1)} %bitcast.38, f32[50,16,128]{2,1,0:T(8,128)S(1)} %bitcast.35, s32[16,128]{1,0:T(8,128)S(1)} %bitcast.39), custom_call_target="tpu_custom_call" | custom-call | tf_op jit(solution)/shard_map/partial_step/pallas_call | solution.py:365
  5.7 5.5 %collective-permute-start = (f32[251,8,128]{2,1,0:T(8,128)S(1)}, f32[251,8,128]{2,1,0:T(8,128)S(1)}, u32[]{:S(2)}, u32[]{:S(2)}) collective-permute-start(f32[251,8,128]{2,1,0:T(8,128)S(1)} %get-tuple-element.10.cross), channel_id=1, source_target_pairs={{0,15},{1,2},{2,1},{3,4},{4,3},{5,6},{6,5},{7,8},{8,7},{9,10},{10,... | collective-permute-start | bytes 3084296 | tf_op jit(solution)/shard_map/ppermute | solution.py:373
  11.2 0.0 collective-permute-start.1
  11.2 12.4 %collective-permute-done.cross_far = f32[251,8,128]{2,1,0:T(8,128)S(1)} collective-permute-done((f32[251,8,128]{2,1,0:T(8,128)S(1)}, f32[251,8,128]{2,1,0:T(8,128)S(1)}, u32[]{:S(2)}, u32[]{:S(2)}) %collective-permute-start) | collective-permute-done | bytes 1028128 | tf_op jit(solution)/shard_map/ppermute | solution.py:373
  23.6 0.0 collective-permute-done.1.mate_far
  23.6 0.0 copy-done.1
  23.6 0.0 copy-done.5
  23.6 0.0 copy-done.6
  23.6 1.6 %both_steps.1 = (f32[2,50,16,128]{3,2,1,0:T(8,128)S(1)}, f32[16,11,8,128]{3,2,1,0:T(8,128)S(1)}) custom-call(f32[251,8,128]{2,1,0:T(8,128)S(1)} %get-tuple-element.10.cross, f32[251,8,128]{2,1,0:T(8,128)S(1)} %get-tuple-element.11.mate, f32[251,8,128]{2,1,0:T(8,128)S(1)} %collective-permute-done.cross_far, ...), custom_call_target="tpu_custom_call" | custom-call | tf_op jit(solution)/shard_map/both_steps/pallas_call | solution.py:377
  25.1 33.5 %all_to_all.5.gathered = f32[16,11,8,128]{3,2,1,0:T(8,128)S(1)} all-to-all(f32[16,11,8,128]{3,2,1,0:T(8,128)S(1)} %get-tuple-element.12), channel_id=1, replica_groups=mesh['grp'=2,'lon'=16] {'lon'}, dimensions={0} | all-to-all | bytes 1441792 | tf_op jit(solution)/shard_map/all_to_all | solution.py:388
  58.7 5.0 %surface_and_scale.1 = (f32[2,50,16,128]{3,2,1,0:T(8,128)}, f32[2,16,128]{2,1,0:T(8,128)}, f32[3]{0:T(128)}) custom-call(f32[16,11,8,128]{3,2,1,0:T(8,128)S(1)} %all_to_all.5.gathered, f32[2,50,16,128]{3,2,1,0:T(8,128)S(1)} %get-tuple-element.13.tracer), custom_call_target="tpu_custom_call" | custom-call | tf_op jit(solution)/shard_map/surface_and_scale/pallas_call | solution.py:391
Async XLA Ops:
  0.6 1.0 %copy-start = (f32[50,2,1024]{2,1,0:T(2,128)S(1)}, f32[50,2,1024]{2,1,0:T(2,128)}, u32[]{:S(2)}) copy-start(f32[50,2,1024]{2,1,0:T(2,128)} %param.8) | copy-start | bytes 1228804
  1.6 1.1 %copy-start.2 = (f32[2,50,2,1024]{3,2,1,0:T(2,128)S(1)}, f32[2,50,2,1024]{3,2,1,0:T(2,128)}, u32[]{:S(2)}) copy-start(f32[2,50,2,1024]{3,2,1,0:T(2,128)} %param.5) | copy-start | bytes 2457604
  2.8 1.0 %copy-start.3 = (f32[50,2,1024]{2,1,0:T(2,128)S(1)}, f32[50,2,1024]{2,1,0:T(2,128)}, u32[]{:S(2)}) copy-start(f32[50,2,1024]{2,1,0:T(2,128)} %param.7) | copy-start | bytes 1228804
  3.8 0.7 %copy-start.4 = (s32[2,1024]{1,0:T(2,128)S(1)}, s32[2,1024]{1,0:T(2,128)}, u32[]{:S(2)}) copy-start(s32[2,1024]{1,0:T(2,128)} %param.9) | copy-start | bytes 24580
  4.5 19.1 %copy-start.1 = (f32[50,2,1024]{2,1,0:T(2,128)S(1)}, f32[50,2,1024]{2,1,0:T(2,128)}, u32[]{:S(2)}) copy-start(f32[50,2,1024]{2,1,0:T(2,128)} %param.8) | copy-start | bytes 1228804
  4.5 19.1 %copy-start.5 = (s32[2,1024]{1,0:T(2,128)S(1)}, s32[2,1024]{1,0:T(2,128)}, u32[]{:S(2)}) copy-start(s32[2,1024]{1,0:T(2,128)} %param.9) | copy-start | bytes 24580
  4.5 19.1 %copy-start.6 = (f32[2,2,1024]{2,1,0:T(2,128)S(1)}, f32[2,2,1024]{2,1,0:T(2,128)}, u32[]{:S(2)}) copy-start(f32[2,2,1024]{2,1,0:T(2,128)} %param.6) | copy-start | bytes 49156
  5.7 17.9 %collective-permute-start = (f32[251,8,128]{2,1,0:T(8,128)S(1)}, f32[251,8,128]{2,1,0:T(8,128)S(1)}, u32[]{:S(2)}, u32[]{:S(2)}) collective-permute-start(f32[251,8,128]{2,1,0:T(8,128)S(1)} %get-tuple-element.10.cross), channel_id=1, source_target_pairs={{0,15},{1,2},{2,1},{3,4},{4,3},{5,6},{6,5},{7,8},{8,7},{9,10},{10,... | collective-permute-start | bytes 3084296 | tf_op jit(solution)/shard_map/ppermute | solution.py:373
  11.2 12.4 %collective-permute-start.1 = (f32[251,8,128]{2,1,0:T(8,128)S(1)}, f32[251,8,128]{2,1,0:T(8,128)S(1)}, u32[]{:S(2)}, u32[]{:S(2)}) collective-permute-start(f32[251,8,128]{2,1,0:T(8,128)S(1)} %get-tuple-element.11.mate), channel_id=1, source_target_pairs={{0,1},{1,0},{2,3},{3,2},{4,5},{5,4},{6,7},{7,6},{8,9},{9,8},{10,11... | collective-permute-start | bytes 3084296 | tf_op jit(solution)/shard_map/ppermute | solution.py:376

commit v3 on v2

v3 whole, which is shorter than its diff:
```python
import functools

import jax
import jax.numpy as jnp
from jax import lax
from jax.experimental import pallas as pl
from jax.experimental.pallas import tpu as pltpu
from jax.sharding import PartitionSpec as P

ITERS = 3


DIFFUSIVITY = 0.5
TIME_STEP = 0.2
SURFACE_COUPLING = 0.5
STERIC_GAIN = 2.0
EPSILON = 1e-06

LANES = 128
VECTORS = 2
SLOPE = 0.25 * TIME_STEP
SPREAD = TIME_STEP * DIFFUSIVITY
GRAMS = VECTORS * 2
BLOCKS = GRAMS + 1
DEPTHS = VECTORS * 2
RIM = DEPTHS + 2


def next_row(tile):
    turned = pltpu.roll(tile, LANES - 1, 1)
    carried = pltpu.roll(turned, tile.shape[0] - 1, 0)
    lane = lax.broadcasted_iota(jnp.int32, tile.shape, 1)
    return jnp.where(lane == LANES - 1, carried, turned)


def prior_row(tile):
    turned = pltpu.roll(tile, 1, 1)
    carried = pltpu.roll(turned, 1, 0)
    lane = lax.broadcasted_iota(jnp.int32, tile.shape, 1)
    return jnp.where(lane == 0, carried, turned)


def wall_depth(depth):
    subs, lane = (lax.broadcasted_iota(jnp.int32, depth.shape, axis) for axis in (0, 1))
    last = (subs == depth.shape[0] - 1) & (lane == LANES - 1)
    return jnp.where(last, jnp.zeros_like(depth), jnp.minimum(depth, next_row(depth)))


def face_pair(level, face_depth, flow_sum):
    slope = SLOPE * flow_sum
    open_face = level < face_depth
    return (
        jnp.where(open_face, slope + SPREAD, 0.0),
        jnp.where(open_face, slope - SPREAD, 0.0),
    )


def outflow(pair, near, far):
    return pair[0] * near + pair[1] * far


def side_pairs(level, depths, flow):
    return (
        face_pair(level, depths[0], flow + next_row(flow)),
        face_pair(level, depths[1], -(flow + prior_row(flow))),
    )


def divergence_y(pairs, tile):
    return outflow(pairs[0], tile, next_row(tile)) + outflow(pairs[1], tile, prior_row(tile))


def side_depths(depth):
    north = wall_depth(depth)
    return north, prior_row(north)


def orientation():
    outer = lax.rem(lax.axis_index("lon"), 2)
    return outer, 1 - outer, (2 * outer - 1).astype(jnp.float32)


def steps(count, most):
    return max(u for u in range(1, most + 1) if count % u == 0)


def share(levels):
    size = lax.axis_size("grp")
    assert size == 2
    part = (levels + 1) // 2
    return lax.axis_index("grp") * (levels - part), part


def first_kernel(
    levels, sub, tracer_hbm, zonal_hbm, merid_hbm, surface_hbm, bottom_hbm,
    cross_hbm, flow_hbm, mate_hbm, rim_hbm,
    tracer, zonal, merid, surface, bottom, cross, flow_part, mate, rim, sems_in, sems_out,
):
    outer, inner, sign = orientation()
    part_start, part = share(levels)
    chunk = steps(levels, 10)
    parts = levels // chunk

    def moves(pairs, sems):
        copies = [
            pltpu.make_async_copy(source, target, sems.at[i])
            for i, (source, target) in enumerate(pairs)
        ]
        for copy in copies:
            copy.start()
        return copies

    def rows(n):
        return pl.ds(n * chunk, chunk)

    small = moves([(bottom_hbm, bottom), (surface_hbm, surface)], sems_in.at[parts])
    arrivals = [
        moves(
            [
                (tracer_hbm.at[:, rows(n)], tracer.at[:, rows(n)]),
                (zonal_hbm.at[rows(n)], zonal.at[rows(n)]),
                (merid_hbm.at[rows(n)], merid.at[rows(n)]),
            ],
            sems_in.at[n],
        )
        for n in range(parts)
    ]

    def column(ref, where, *lead):
        return ref[(*lead, pl.ds(where, sub, stride=2), slice(None))]

    for copy in small:
        copy.wait()
    for c in range(2):
        for v in range(VECTORS):
            rim[v * 2 + c] = column(surface, c, v)
        rim[DEPTHS + c] = column(bottom, c).astype(jnp.float32)
    depth = [column(bottom, where).astype(jnp.float32) for where in (outer, inner)]
    between = jnp.minimum(*depth)
    along = [side_depths(d) for d in depth]
    departures = moves([(rim, rim_hbm)], sems_out.at[parts])

    def body(k, carry):
        level = k.astype(jnp.float32)
        flow = [column(zonal, where, k) for where in (outer, inner)]
        turn = [column(merid, where, k) for where in (outer, inner)]
        middle = face_pair(level, between, -sign * (flow[0] + flow[1]))
        sides = [side_pairs(level, along[c], turn[c]) for c in range(2)]
        for v in range(VECTORS):
            cells = [column(tracer, where, v, k) for where in (outer, inner)]
            flux = outflow(middle, *cells)
            kept = [
                jnp.where(level < depth[c], cells[c], 0.0) - divergence_y(sides[c], cells[c])
                for c in range(2)
            ]
            cross[v, k] = cells[0]
            cross[VECTORS + v, k] = kept[0] - flux
            mate[v, k] = cells[1]
            mate[VECTORS + v, k] = kept[1] + flux
        mate[VECTORS * 2, k] = flow[1]
        return carry

    for n in range(parts):
        for copy in arrivals[n]:
            copy.wait()
        lax.fori_loop(n * chunk, (n + 1) * chunk, body, 0, unroll=chunk)
        departures += moves(
            [
                (cross.at[:, rows(n)], cross_hbm.at[:, rows(n)]),
                (mate.at[:, rows(n)], mate_hbm.at[:, rows(n)]),
            ],
            sems_out.at[n],
        )

    def pack(i, carry):
        flow_part[i] = column(zonal, outer, part_start + i)
        return carry

    lax.fori_loop(0, part, pack, 0, unroll=steps(part, 10))
    departures += moves([(flow_part, flow_hbm)], sems_out.at[parts + 1])
    for copy in departures:
        copy.wait()


def surface_kernel(
    count, quad, far, far_mate, depth, face_x, face_y, face_z, height, lap, pole
):
    me = lax.axis_index("lon")
    core = lax.rem(me, 2)
    width = 2 * count

    def place(owner, block):
        for c in range(2):
            depth[2 * owner + c] = block(DEPTHS + c)
            for v in range(VECTORS):
                wet = block(DEPTHS + c) > 0
                height[v, 2 * owner + c] = jnp.where(wet, block(v * 2 + c), 0.0)

    for slot in range(quad.shape[0]):
        place(me ^ slot, lambda row, slot=slot: quad[slot, row])
    groups = count // quad.shape[0]
    for ref, flip in ((far, 0), (far_mate, 1)):
        for j in range(far.shape[0]):
            mask = 2 * j + 1 + (core ^ flip)
            for slot in range(quad.shape[0]):

                @pl.when(mask < groups)
                def _(ref=ref, flip=flip, j=j, mask=mask, slot=slot):
                    owner = me ^ flip ^ (mask * quad.shape[0]) ^ slot
                    place(owner, lambda row: ref[j, slot, row])

    def prepare(x, carry):
        here, after = depth[x], depth[lax.rem(x + 1, width)]
        face_x[x + 1] = SURFACE_COUPLING * jnp.minimum(here, after)
        north, south = side_depths(here)
        face_y[x] = SURFACE_COUPLING * north
        face_z[x] = SURFACE_COUPLING * south
        for v in range(VECTORS):
            pole[v, x + 1] = height[v, x]
        return carry

    lax.fori_loop(0, width, prepare, 0, unroll=steps(width, 8))
    face_x[0] = face_x[width]
    wrap(pole, width)

    def bend(x, carry):
        for v in range(VECTORS):
            lap[v, x] = spread(pole, face_x, face_y, face_z, v, x)
        return carry

    lax.fori_loop(0, width, bend, 0, unroll=steps(width, 8))


def wrap(pole, width):
    for v in range(VECTORS):
        pole[v, 0] = pole[v, width]
        pole[v, width + 1] = pole[v, 1]


def spread(pole, face_x, face_y, face_z, v, x):
    west, centre, east = (pole[v, x + j] for j in range(3))
    return (face_x[x + 1] * (east - centre) - face_x[x] * (centre - west)) + (
        face_y[x] * (next_row(centre) - centre) - face_z[x] * (centre - prior_row(centre))
    )


def second_kernel(
    levels, sub, cross, mate, cross_far, mate_far, flow_half, flow_other, zonal, merid, depths,
    tracer, message, flow_far,
):
    outer, inner, sign = orientation()
    part_start, part = share(levels)
    me, width = lax.axis_index("lon"), depths.shape[0]

    def unpack(i, carry):
        flow_far[part_start + i] = flow_half[i]
        flow_far[levels - part - part_start + i] = flow_other[i]
        return carry

    lax.fori_loop(0, part, unpack, 0, unroll=steps(part, 10))
    depth = [depths[2 * me + where] for where in (outer, inner)]
    beside = [
        jnp.minimum(depth[0], depths[lax.rem(2 * me + 3 * outer - 1 + width, width)]),
        jnp.minimum(depth[1], depths[2 * me + 3 * inner - 1]),
    ]
    between = jnp.minimum(*depth)
    along = [side_depths(d) for d in depth]
    zero = jnp.zeros_like(between)
    near, far = (cross, mate), (cross_far, mate_far)

    def body(k, carry):
        level = k.astype(jnp.float32)
        flow = [zonal[k, pl.ds(outer, sub, stride=2), :], mate[VECTORS * 2, k]]
        beyond = [flow_far[k], mate_far[VECTORS * 2, k]]
        turn = [merid[k, pl.ds(where, sub, stride=2), :] for where in (outer, inner)]
        middle = face_pair(level, between, -sign * (flow[0] + flow[1]))
        edges = [
            face_pair(level, beside[c], (sign, -sign)[c] * (flow[c] + beyond[c])) for c in range(2)
        ]
        sides = [side_pairs(level, along[c], turn[c]) for c in range(2)]
        totals, grams = list(carry[:4]), list(carry[4:])
        done = []
        for v in range(VECTORS):
            own, other = [], []
            for c in range(2):
                flux = outflow(edges[c], near[c][v, k], far[c][v, k])
                own.append(near[c][VECTORS + v, k] - flux)
                other.append(far[c][VECTORS + v, k] + flux)
            crossing = outflow(middle, *own)
            fresh = []
            for c, where in enumerate((outer, inner)):
                gone = crossing if c == 0 else -crossing
                value = (
                    own[c]
                    - outflow(edges[c], own[c], other[c])
                    - gone
                    - divergence_y(sides[c], own[c])
                )
                tracer[v, k, pl.ds(where, sub, stride=2), :] = value
                totals[v * 2 + c] = totals[v * 2 + c] + value
                fresh.append(value)
            done.append(fresh)
        for c in range(2):
            a, b = done[0][c], done[1][c]
            grams = [grams[0] + a * a, grams[1] + a * b, grams[2] + b * b]
        return (*totals, *grams)

    sums = lax.fori_loop(0, levels, body, (zero,) * 7, unroll=steps(levels, 10))
    gain = STERIC_GAIN / levels
    subs = lax.broadcasted_iota(jnp.int32, zero.shape, 0)
    packed = zero
    for i, gram in enumerate(sums[4:]):
        packed = jnp.where(subs == i, jnp.sum(gram, axis=0, keepdims=True), packed)

    def copy(d, carry):
        for v in range(VECTORS):
            for c, where in enumerate((outer, inner)):
                message[d, v * 2 + where] = gain * sums[v * 2 + c]
        message[d, GRAMS] = packed
        return carry

    count = message.shape[0]
    lax.fori_loop(0, count, copy, 0, unroll=steps(count, 16))


def total(tile):
    return jnp.sum(jnp.sum(tile, axis=0, keepdims=True), axis=1, keepdims=True)


def third_kernel(
    levels, sub, gathered, face_x, face_y, face_z, height, lap, tracer,
    tracer_out, surface_out, growth, pole, residual, answer, image,
):
    count = gathered.shape[0]
    width = 2 * count
    me = lax.axis_index("lon")
    zero = jnp.zeros((sub, LANES), jnp.float32)
    none = (zero,) * VECTORS

    def over(body, init):
        return lax.fori_loop(0, count, body, init, unroll=steps(count, 16))

    def each(d):
        return [(v, c, 2 * d + c) for v in range(VECTORS) for c in range(2)]

    def start(d, carry):
        sums = list(carry)
        for v, c, x in each(d):
            value = gathered[d, v * 2 + c] + lap[v, x]
            residual[v, x] = value
            pole[v, x + 1] = value
            sums[v] = sums[v] + value * value
        return tuple(sums)

    norm = [total(t) for t in over(start, none)]
    wrap(pole, width)

    def apply(d, carry):
        sums = list(carry)
        for v, _, x in each(d):
            centre = pole[v, x + 1]
            value = centre - spread(pole, face_x, face_y, face_z, v, x)
            image[v, x] = value
            sums[v] = sums[v] + centre * value
        return tuple(sums)

    for iteration in range(ITERS):
        energy = [total(t) for t in over(apply, none)]
        size = [n / e for n, e in zip(norm, energy)]
        held = height if iteration == 0 else answer
        if iteration + 1 < ITERS:

            def advance(d, carry, size=size, held=held):
                sums = list(carry)
                for v, _, x in each(d):
                    answer[v, x] = held[v, x] + size[v] * pole[v, x + 1]
                    value = residual[v, x] - size[v] * image[v, x]
                    residual[v, x] = value
                    sums[v] = sums[v] + value * value
                return tuple(sums)

            fresh = [total(t) for t in over(advance, none)]
            ratio = [f / n for f, n in zip(fresh, norm)]

            def turn(d, carry, ratio=ratio):
                for v, _, x in each(d):
                    pole[v, x + 1] = residual[v, x] + ratio[v] * pole[v, x + 1]
                return carry

            over(turn, 0)
            wrap(pole, width)
            norm = fresh

    def finish(d, carry):
        grams = list(carry)
        for x in (2 * d, 2 * d + 1):
            a, b = (held[v, x] + size[v] * pole[v, x + 1] for v in range(VECTORS))
            answer[0, x], answer[1, x] = a, b
            grams = [grams[0] + a * a, grams[1] + a * b, grams[2] + b * b]
        return (*grams, carry[3] + gathered[d, GRAMS])

    *grams, packed = over(finish, (zero,) * 4)
    cells = (levels + 1) * width * sub * LANES
    one, mix, two = (
        (total(g) + jnp.sum(packed[i : i + 1], axis=1, keepdims=True)) / cells
        for i, g in enumerate(grams)
    )
    scale_one = jnp.sqrt(one + EPSILON)
    cross = mix / scale_one
    rest = two - 2.0 * cross * cross + cross * cross * one / (one + EPSILON)
    scale_two = jnp.sqrt(rest + EPSILON)
    over_one, over_two = 1.0 / scale_one, 1.0 / scale_two

    def scale(k, carry):
        unit = tracer[0, k] * over_one
        tracer_out[0, k] = unit
        tracer_out[1, k] = (tracer[1, k] - cross * unit) * over_two
        return carry

    lax.fori_loop(0, levels, scale, 0, unroll=steps(levels, 10))
    for c in range(2):
        x = 2 * me + c
        unit = answer[0, x] * over_one
        surface_out[0, pl.ds(c, sub, stride=2), :] = unit
        surface_out[1, pl.ds(c, sub, stride=2), :] = (answer[1, x] - cross * unit) * over_two
    for i, value in enumerate((scale_one, cross, scale_two)):
        growth[i] = value[0, 0]


def tiled(array):
    *lead, columns, rows = array.shape
    split = array.reshape(*lead, columns, rows // LANES, LANES)
    return jnp.swapaxes(split, -3, -2).reshape(*lead, rows // LANES * columns, LANES)


def untiled(array, columns):
    *lead, high, lanes = array.shape
    split = array.reshape(*lead, high // columns, columns, lanes)
    return jnp.swapaxes(split, -3, -2).reshape(*lead, columns, high // columns * lanes)


def swap(array, mask):
    count = lax.axis_size("lon")
    return lax.ppermute(array, "lon", [(i, i ^ mask) for i in range(count)])


def early_gather(rim):
    count = lax.axis_size("lon")
    pair = jnp.stack([rim, swap(rim, 1)])
    quad = jnp.concatenate([pair, swap(pair, 2)])
    size = quad.shape[0]
    groups = count // size
    far = []
    for j in range(groups // 2):
        masks = (2 * j + 1, 2 * j + 2)
        moves = [
            (i, i ^ (masks[i % 2] * size)) for i in range(count) if masks[i % 2] < groups
        ]
        far.append(lax.ppermute(quad, "lon", moves))
    far = jnp.stack(far)
    return quad, far, swap(far, 1)


def on_device(tracer_pert, surface_pert, zonal_flow, merid_flow, bottom_level):
    vectors, levels, columns, rows = tracer_pert.shape
    count = lax.axis_size("lon")
    sub = rows // LANES
    assert vectors == VECTORS and columns == 2 and rows % LANES == 0
    assert count >= 8 and count & (count - 1) == 0
    width = 2 * count
    f32 = jnp.float32
    vmem = pl.BlockSpec(memory_space=pltpu.VMEM)
    hbm = pl.BlockSpec(memory_space=pltpu.HBM)
    params = pltpu.CompilerParams(vmem_limit_bytes=24 * 2**20)

    def shaped(*shape):
        return jax.ShapeDtypeStruct((*shape, sub, LANES), f32)

    def held(*shape):
        return pltpu.VMEM((*shape, sub, LANES), f32)

    both = pltpu.VMEM((vectors, levels, sub * 2, LANES), f32)
    single = pltpu.VMEM((levels, sub * 2, LANES), f32)
    tracer_pert, zonal_flow, merid_flow = map(tiled, (tracer_pert, zonal_flow, merid_flow))
    outward = [(i, (i + 1) % count if i % 2 else (i - 1) % count) for i in range(count)]
    part = (levels + 1) // 2
    chunks = levels // steps(levels, 10)

    packed = (
        (vectors * 2, levels),
        (part,),
        (vectors * 2 + 1, levels),
        (RIM,),
    )
    cross, flow_half, mate, rim = pl.pallas_call(
        functools.partial(first_kernel, levels, sub),
        out_shape=tuple(shaped(*shape) for shape in packed),
        in_specs=[hbm] * 5,
        out_specs=(hbm,) * 4,
        scratch_shapes=[
            both,
            single,
            single,
            pltpu.VMEM((vectors, sub * 2, LANES), f32),
            pltpu.VMEM((sub * 2, LANES), jnp.int32),
            *(held(*shape) for shape in packed),
            pltpu.SemaphoreType.DMA((chunks + 1, 3)),
            pltpu.SemaphoreType.DMA((chunks + 2, 2)),
        ],
        compiler_params=pltpu.CompilerParams(vmem_limit_bytes=60 * 2**20),
        name="partial_step",
    )(tracer_pert, zonal_flow, merid_flow, tiled(surface_pert), tiled(bottom_level))
    flow_half = lax.ppermute(flow_half, "lon", outward)
    flow_other = lax.ppermute(flow_half, "grp", [(0, 1), (1, 0)])
    cross_far = lax.ppermute(cross, "lon", outward)
    mate_far = swap(mate, 1)
    fields = pl.pallas_call(
        functools.partial(surface_kernel, count),
        out_shape=(
            shaped(width),
            shaped(width + 1),
            shaped(width),
            shaped(width),
            shaped(vectors, width),
            shaped(vectors, width),
        ),
        in_specs=[vmem] * 3,
        out_specs=(vmem,) * 6,
        scratch_shapes=[held(vectors, width + 2)],
        compiler_params=params,
        name="surface_faces",
    )(*early_gather(rim))
    tracer, message = pl.pallas_call(
        functools.partial(second_kernel, levels, sub),
        out_shape=(
            jax.ShapeDtypeStruct((vectors, levels, sub * 2, LANES), f32),
            shaped(count, BLOCKS),
        ),
        in_specs=[vmem] * 9,
        out_specs=(vmem, vmem),
        scratch_shapes=[held(levels)],
        compiler_params=params,
        name="both_steps",
    )(cross, mate, cross_far, mate_far, flow_half, flow_other, zonal_flow, merid_flow, fields[0])
    gathered = lax.all_to_all(message, "lon", 0, 0)
    tracer_vec, surface_vec, growth = pl.pallas_call(
        functools.partial(third_kernel, levels, sub),
        out_shape=(
            jax.ShapeDtypeStruct((vectors, levels, sub * 2, LANES), f32),
            jax.ShapeDtypeStruct((vectors, sub * 2, LANES), f32),
            jax.ShapeDtypeStruct((3,), f32),
        ),
        in_specs=[vmem] * 7,
        out_specs=(vmem, vmem, pl.BlockSpec(memory_space=pltpu.SMEM)),
        scratch_shapes=[held(vectors, width + 2)] + [held(vectors, width)] * 3,
        compiler_params=pltpu.CompilerParams(vmem_limit_bytes=40 * 2**20),
        name="surface_and_scale",
    )(gathered, *fields[1:], tracer)
    return (untiled(tracer_vec, 2), untiled(surface_vec, 2), growth)


def solution(mesh):
    placed = (
        P("grp", None, "lon", None),
        P("grp", "lon", None),
        P(None, "lon", None),
        P(None, "lon", None),
        P("lon", None),
    )
    return jax.shard_map(
        on_device,
        mesh=mesh,
        in_specs=placed,
        out_specs=(P("grp", None, "lon", None), P("grp", "lon", None), P("grp")),
        check_vma=False,
    )
```

time: 64.2 us -> 65.3 us (1.017)
  blocking collectives: 33.5 us -> 13.7 us
  waiting for transfers between devices: 12.4 us -> 25.2 us
  starting transfers between devices: 5.51 us -> 13.9 us
  local copies, waits for them, and re-layouts: 3.85 us -> 2.37 us
  other arithmetic: 0 us -> 0.84 us
    all_to_all x1, blocking collectives: 33.5 us -> 13.7 us  [on_device(): gathered = lax.all_to_all(message, 'lon', 0, 0)]
    ppermute x2 -> x9, waiting for transfers between devices: 12.4 us -> 25.2 us  [the longest x4 16.5 us: swap(): return lax.ppermute(array, 'lon', [(i, i ^ mask) for i in range(count)])]
    ppermute x2 -> x9, starting transfers between devices: 5.51 us -> 13.9 us  [the longest x2 6.12 us: early_gather(): far.append(lax.ppermute(quad, 'lon', moves))]
    pallas_call x1 -> x2, Pallas kernels: 1.19 us -> 4.2 us  [the longest x1 3.11 us: on_device(): pl.pallas_call(functools.partial(first_kernel, levels, sub), out_shape=tu...]
    pallas_call x1, Pallas kernels: 4.97 us -> 2.42 us  [on_device(): pl.pallas_call(functools.partial(third_kernel, levels, sub), out_shape=(j...]
    unnamed x14 -> x12, local copies, waits for them, and re-layouts: 3.85 us -> 2.37 us
    another operation x0 -> x2, other arithmetic: none -> 0.83 us  [the longest x1 0.81 us: early_gather(): pair = jnp.stack([rim, swap(rim, 1)])]
  transfers between devices with their start and end apart: 2 -> 9, of which waited for: 1 -> 6; matrix products, arithmetic and copies ran while one was open for 0% -> 1% of each run, Pallas kernels for 0% -> 2%
where the time goes in v3:
time: 65.3 us; the launch traced here: 64.9 us
  waiting for transfers between devices  25.2 us (39%)
  starting transfers between devices  13.9 us (21%)
  blocking collectives  13.7 us (21%)
  Pallas kernels  8.15 us (12%)
  local copies, waits for them, and re-layouts  2.37 us (4%)
  other arithmetic  0.84 us (1%)
  between operations  0.73 us (1%)
    ppermute x4, waiting for transfers between devices, swap(): return lax.ppermute(array, 'lon', [(i, i ^ mask) for i in range(count)])  16.5 us
    all_to_all x1, blocking collectives, on_device(): gathered = lax.all_to_all(message, 'lon', 0, 0)  13.7 us
    ppermute x2, starting transfers between devices, early_gather(): far.append(lax.ppermute(quad, 'lon', moves))  6.12 us
    ppermute x1, starting transfers between devices, on_device(): cross_far = lax.ppermute(cross, 'lon', outward)  5.67 us
    ppermute x2, waiting for transfers between devices, early_gather(): far.append(lax.ppermute(quad, 'lon', moves))  4.51 us
    pallas_call x1, Pallas kernels, on_device(): pl.pallas_call(functools.partial(first_kernel, levels, sub), out_shape=tu...  3.11 us
    pallas_call x1, Pallas kernels, on_device(): pl.pallas_call(functools.partial(third_kernel, levels, sub), out_shape=(j...  2.42 us
    unnamed x12, local copies, waits for them, and re-layouts  2.37 us
  transfers between devices with their start and end apart: 9, of which 6 were waited for; matrix products, arithmetic and copies ran while one was open for 1% of the time, Pallas kernels for 2%

profile of v3, /device:TPU:0, one launch (start us, length us, event | category | flops | bytes accessed | tf_op | source)
XLA Modules:
  0.0 64.9 jit_solution(16064073668419419808)
XLA Ops:
  0.6 3.1 %partial_step.1 = (f32[4,50,8,128]{3,2,1,0:T(8,128)}, f32[25,8,128]{2,1,0:T(8,128)}, f32[5,50,8,128]{3,2,1,0:T(8,128)}, f32[6,8,128]{2,1,0:T(8,128)}) custom-call(f32[2,50,16,128]{3,2,1,0:T(8,128)} %bitcast.43, f32[50,16,128]{2,1,0:T(8,128)} %bitcast.39, f32[50,16,128]{2,1,0:T(8,128)} %bitcast.41, f32[2,16,128]{2,1,0:T(8,128)} %bitcast.50, s32[16,128]{1,0:T(8,128)} %bitcast.51), custom_call_target="tpu_custom_call" | custom-call | tf_op jit(solution)/shard_map/partial_step/pallas_call | solution.py:495
  3.7 0.5 collective-permute-start.1
  4.3 5.7 %collective-permute-start = (f32[4,50,8,128]{3,2,1,0:T(8,128)}, f32[4,50,8,128]{3,2,1,0:T(8,128)S(1)}, u32[]{:S(2)}, u32[]{:S(2)}) collective-permute-start(f32[4,50,8,128]{3,2,1,0:T(8,128)} %get-tuple-element.18.cross), channel_id=1, source_target_pairs={{0,15},{1,2},{2,1},{3,4},{4,3},{5,6},{6,5},{7,8},{8,7},{9,10},{10,... | collective-permute-start | bytes 2457608 | tf_op jit(solution)/shard_map/ppermute | solution.py:515
  9.9 0.0 collective-permute-start.4
  9.9 1.4 %collective-permute-done.4 = f32[6,8,128]{2,1,0:T(8,128)S(1)} collective-permute-done((f32[6,8,128]{2,1,0:T(8,128)}, f32[6,8,128]{2,1,0:T(8,128)S(1)}, u32[]{:S(2)}, u32[]{:S(2)}) %collective-permute-start.4) | collective-permute-done | bytes 24608 | tf_op jit(solution)/shard_map/ppermute | solution.py:444
  11.3 0.0 copy-start.4
  11.3 0.8 %pad_maximum_fusion.2 = f32[2,6,8,128]{3,2,1,0:T(8,128)S(1)} fusion(f32[1,6,8,128]{3,2,1,0:T(8,128)S(1)} %bitcast.46, f32[1,6,8,128]{3,2,1,0:T(8,128)} %bitcast.44), kind=kLoop, calls=%fused_computation.2 | loop fusion | flops 12288 | bytes 98304 | tf_op jit(solution)/shard_map/stack | solution.py:449
  12.2 0.0 copy-start.5
  12.2 0.0 collective-permute-start.5
  12.2 15.1 %collective-permute-done.5 = f32[2,6,8,128]{3,2,1,0:T(8,128)S(1)} collective-permute-done((f32[2,6,8,128]{3,2,1,0:T(8,128)S(1)}, f32[2,6,8,128]{3,2,1,0:T(8,128)S(1)}, u32[]{:S(2)}, u32[]{:S(2)}) %collective-permute-start.5) | collective-permute-done | bytes 49184 | tf_op jit(solution)/shard_map/ppermute | solution.py:444
  27.2 0.0 copy-done.4
  27.2 6.0 %collective-permute-start.7 = (f32[4,6,8,128]{3,2,1,0:T(8,128)S(1)}, f32[4,6,8,128]{3,2,1,0:T(8,128)S(1)}, u32[]{:S(2)}, u32[]{:S(2)}) collective-permute-start(f32[4,6,8,128]{3,2,1,0:T(8,128)S(1)} %pad_maximum_fusion.1.quad), channel_id=1, source_target_pairs={{0,12},{2,14},{4,8},{6,10},{8,4},{10,6},{12,0},{14,2},{16,28},{18,... | collective-permute-start | bytes 294920 | tf_op jit(solution)/shard_map/ppermute | solution.py:459
  33.3 0.1 collective-permute-start.6
  33.4 0.0 copy-done.5
  33.4 0.1 collective-permute-start.2
  33.5 2.5 %collective-permute-done.7 = f32[4,6,8,128]{3,2,1,0:T(8,128)S(1)} collective-permute-done((f32[4,6,8,128]{3,2,1,0:T(8,128)S(1)}, f32[4,6,8,128]{3,2,1,0:T(8,128)S(1)}, u32[]{:S(2)}, u32[]{:S(2)}) %collective-permute-start.7) | collective-permute-done | bytes 98336 | tf_op jit(solution)/shard_map/ppermute | solution.py:459
  36.0 2.0 %collective-permute-done.6 = f32[4,6,8,128]{3,2,1,0:T(8,128)S(1)} collective-permute-done((f32[4,6,8,128]{3,2,1,0:T(8,128)S(1)}, f32[4,6,8,128]{3,2,1,0:T(8,128)S(1)}, u32[]{:S(2)}, u32[]{:S(2)}) %collective-permute-start.6) | collective-permute-done | bytes 98336 | tf_op jit(solution)/shard_map/ppermute | solution.py:459
  38.0 0.0 copy-start
  38.0 0.0 copy-start.1
  38.0 0.1 collective-permute-start.8
  38.1 2.2 %collective-permute-done.2.flow_half = f32[25,8,128]{2,1,0:T(8,128)S(1)} collective-permute-done((f32[25,8,128]{2,1,0:T(8,128)S(1)}, f32[25,8,128]{2,1,0:T(8,128)S(1)}, u32[]{:S(2)}, u32[]{:S(2)}) %collective-permute-start.2) | collective-permute-done | bytes 102432 | tf_op jit(solution)/shard_map/ppermute | solution.py:513
  40.2 1.5 %collective-permute-start.3 = (f32[25,8,128]{2,1,0:T(8,128)S(1)}, f32[25,8,128]{2,1,0:T(8,128)S(1)}, u32[]{:S(2)}, u32[]{:S(2)}) collective-permute-start(f32[25,8,128]{2,1,0:T(8,128)S(1)} %collective-permute-done.2.flow_half), channel_id=1, source_target_pairs={{0,16},{16,0},{1,17},{17,1},{2,18},{18,2},{3,19},{19,3},{4,20},{20... | collective-permute-start | bytes 307208 | tf_op jit(solution)/shard_map/ppermute | solution.py:514
  41.7 0.0 collective-permute-done.8.far_mate
  41.7 1.1 %surface_faces.1 = (f32[32,8,128]{2,1,0:T(8,128)S(1)}, f32[33,8,128]{2,1,0:T(8,128)S(1)}, f32[32,8,128]{2,1,0:T(8,128)S(1)}, f32[32,8,128]{2,1,0:T(8,128)S(1)}, ...) custom-call(f32[4,6,8,128]{3,2,1,0:T(8,128)S(1)} %pad_maximum_fusion.1.quad, ...), custom_call_target="tpu_custom_call" | custom-call | tf_op jit(solution)/shard_map/surface_faces/pallas_call | solution.py:517
  42.8 2.1 %collective-permute-done.3.flow_other = f32[25,8,128]{2,1,0:T(8,128)S(1)} collective-permute-done((f32[25,8,128]{2,1,0:T(8,128)S(1)}, f32[25,8,128]{2,1,0:T(8,128)S(1)}, u32[]{:S(2)}, u32[]{:S(2)}) %collective-permute-start.3) | collective-permute-done | bytes 102432 | tf_op jit(solution)/shard_map/ppermute | solution.py:514
  44.9 0.0 collective-permute-done.cross_far
  44.9 0.0 collective-permute-done.1.mate_far
  44.9 0.0 copy-done
  44.9 0.0 copy-done.1
  44.9 0.0 copy-start.2
  44.9 1.2 %copy-done.2 = f32[5,50,8,128]{3,2,1,0:T(8,128)S(1)} copy-done((f32[5,50,8,128]{3,2,1,0:T(8,128)S(1)}, f32[5,50,8,128]{3,2,1,0:T(8,128)}, u32[]{:S(2)}) %copy-start.2) | copy-done | bytes 1024024
  46.1 0.0 copy-start.3
  46.1 1.1 %copy-done.3 = f32[4,50,8,128]{3,2,1,0:T(8,128)S(1)} copy-done((f32[4,50,8,128]{3,2,1,0:T(8,128)S(1)}, f32[4,50,8,128]{3,2,1,0:T(8,128)}, u32[]{:S(2)}) %copy-start.3) | copy-done | bytes 819224
  47.3 1.5 %both_steps.1 = (f32[2,50,16,128]{3,2,1,0:T(8,128)S(1)}, f32[16,5,8,128]{3,2,1,0:T(8,128)S(1)}) custom-call(f32[4,50,8,128]{3,2,1,0:T(8,128)S(1)} %copy-done.3, f32[5,50,8,128]{3,2,1,0:T(8,128)S(1)} %copy-done.2, f32[4,50,8,128]{3,2,1,0:T(8,128)S(1)} %collective-permute-done.cross_far, f32[5,50,8,128]{3,2,1,0:T(8,128)S(1)} %collective-permute-done.1.mate_far, ...), custom_call_target="tpu_custom_call" | custom-call | tf_op jit(solution)/shard_map/both_steps/pallas_call | solution.py:533
  48.8 13.7 %all_to_all.5.gathered = f32[16,5,8,128]{3,2,1,0:T(8,128)S(1)} all-to-all(f32[16,5,8,128]{3,2,1,0:T(8,128)S(1)} %get-tuple-element.23), channel_id=1, replica_groups=mesh['grp'=2,'lon'=16] {'lon'}, dimensions={0} | all-to-all | bytes 655360 | tf_op jit(solution)/shard_map/all_to_all | solution.py:545
  62.5 2.4 %surface_and_scale.1 = (f32[2,50,16,128]{3,2,1,0:T(8,128)}, f32[2,16,128]{2,1,0:T(8,128)}, f32[3]{0:T(128)}) custom-call(f32[16,5,8,128]{3,2,1,0:T(8,128)S(1)} %all_to_all.5.gathered, f32[33,8,128]{2,1,0:T(8,128)S(1)} %get-tuple-element.24.face_x, f32[32,8,128]{2,1,0:T(8,128)S(1)} %get-tuple-element.25.face_y, f32[32,8,128]{2,1,0:T(8,128)S(1)} %get-tuple-element.26.face_z, ...), custom_call_target="tpu_custom_call" | custom-call | tf_op jit(solution)/shard_map/surface_and_scale/pallas_call | solution.py:546
  (2 shorter events, 0.0 us)
Async XLA Ops:
  3.7 41.1 %collective-permute-start.1 = (f32[5,50,8,128]{3,2,1,0:T(8,128)}, f32[5,50,8,128]{3,2,1,0:T(8,128)S(1)}, u32[]{:S(2)}, u32[]{:S(2)}) collective-permute-start(f32[5,50,8,128]{3,2,1,0:T(8,128)} %get-tuple-element.19.mate), channel_id=1, source_target_pairs={{0,1},{1,0},{2,3},{3,2},{4,5},{5,4},{6,7},{7,6},{8,9},{9,8},{10,11... | collective-permute-start | bytes 3072008 | tf_op jit(solution)/shard_map/ppermute | solution.py:444
  4.3 40.6 %collective-permute-start = (f32[4,50,8,128]{3,2,1,0:T(8,128)}, f32[4,50,8,128]{3,2,1,0:T(8,128)S(1)}, u32[]{:S(2)}, u32[]{:S(2)}) collective-permute-start(f32[4,50,8,128]{3,2,1,0:T(8,128)} %get-tuple-element.18.cross), channel_id=1, source_target_pairs={{0,15},{1,2},{2,1},{3,4},{4,3},{5,6},{6,5},{7,8},{8,7},{9,10},{10,... | collective-permute-start | bytes 2457608 | tf_op jit(solution)/shard_map/ppermute | solution.py:515
  9.9 1.4 %collective-permute-start.4 = (f32[6,8,128]{2,1,0:T(8,128)}, f32[6,8,128]{2,1,0:T(8,128)S(1)}, u32[]{:S(2)}, u32[]{:S(2)}) collective-permute-start(f32[6,8,128]{2,1,0:T(8,128)} %get-tuple-element.21), channel_id=1, source_target_pairs={{0,1},{1,0},{2,3},{3,2},{4,5},{5,4},{6,7},{7,6},{8,9},{9,8},{10,11... | collective-permute-start | bytes 73736 | tf_op jit(solution)/shard_map/ppermute | solution.py:444
  11.3 15.9 %copy-start.4 = (f32[6,8,128]{2,1,0:T(8,128)S(1)}, f32[6,8,128]{2,1,0:T(8,128)}, u32[]{:S(2)}) copy-start(f32[6,8,128]{2,1,0:T(8,128)} %get-tuple-element.21) | copy-start | bytes 73732
  12.2 21.2 %copy-start.5 = (f32[25,8,128]{2,1,0:T(8,128)S(1)}, f32[25,8,128]{2,1,0:T(8,128)}, u32[]{:S(2)}) copy-start(f32[25,8,128]{2,1,0:T(8,128)} %get-tuple-element.20) | copy-start | bytes 307204
  12.2 15.1 %collective-permute-start.5 = (f32[2,6,8,128]{3,2,1,0:T(8,128)S(1)}, f32[2,6,8,128]{3,2,1,0:T(8,128)S(1)}, u32[]{:S(2)}, u32[]{:S(2)}) collective-permute-start(f32[2,6,8,128]{3,2,1,0:T(8,128)S(1)} %pad_maximum_fusion.2), channel_id=1, source_target_pairs={{0,2},{1,3},{2,0},{3,1},{4,6},{5,7},{6,4},{7,5},{8,10},{9,11},{10,... | collective-permute-start | bytes 147464 | tf_op jit(solution)/shard_map/ppermute | solution.py:444
  27.2 8.7 %collective-permute-start.7 = (f32[4,6,8,128]{3,2,1,0:T(8,128)S(1)}, f32[4,6,8,128]{3,2,1,0:T(8,128)S(1)}, u32[]{:S(2)}, u32[]{:S(2)}) collective-permute-start(f32[4,6,8,128]{3,2,1,0:T(8,128)S(1)} %pad_maximum_fusion.1.quad), channel_id=1, source_target_pairs={{0,12},{2,14},{4,8},{6,10},{8,4},{10,6},{12,0},{14,2},{16,28},{18,... | collective-permute-start | bytes 294920 | tf_op jit(solution)/shard_map/ppermute | solution.py:459
  33.3 4.7 %collective-permute-start.6 = (f32[4,6,8,128]{3,2,1,0:T(8,128)S(1)}, f32[4,6,8,128]{3,2,1,0:T(8,128)S(1)}, u32[]{:S(2)}, u32[]{:S(2)}) collective-permute-start(f32[4,6,8,128]{3,2,1,0:T(8,128)S(1)} %pad_maximum_fusion.1.quad), channel_id=1, source_target_pairs={{0,4},{1,9},{2,6},{3,11},{4,0},{5,13},{6,2},{7,15},{8,12},{9,1},{1... | collective-permute-start | bytes 294920 | tf_op jit(solution)/shard_map/ppermute | solution.py:459
  33.4 6.8 %collective-permute-start.2 = (f32[25,8,128]{2,1,0:T(8,128)S(1)}, f32[25,8,128]{2,1,0:T(8,128)S(1)}, u32[]{:S(2)}, u32[]{:S(2)}) collective-permute-start(f32[25,8,128]{2,1,0:T(8,128)S(1)} %copy-done.5), channel_id=1, source_target_pairs={{0,15},{1,2},{2,1},{3,4},{4,3},{5,6},{6,5},{7,8},{8,7},{9,10},{10,... | collective-permute-start | bytes 307208 | tf_op jit(solution)/shard_map/ppermute | solution.py:513
  38.0 6.9 %copy-start = (f32[50,2,1024]{2,1,0:T(2,128)S(1)}, f32[50,2,1024]{2,1,0:T(2,128)}, u32[]{:S(2)}) copy-start(f32[50,2,1024]{2,1,0:T(2,128)} %param.7) | copy-start | bytes 1228804
  38.0 6.9 %copy-start.1 = (f32[50,2,1024]{2,1,0:T(2,128)S(1)}, f32[50,2,1024]{2,1,0:T(2,128)}, u32[]{:S(2)}) copy-start(f32[50,2,1024]{2,1,0:T(2,128)} %param.8) | copy-start | bytes 1228804
  38.0 3.7 %collective-permute-start.8 = (f32[2,4,6,8,128]{4,3,2,1,0:T(8,128)S(1)}, f32[2,4,6,8,128]{4,3,2,1,0:T(8,128)S(1)}, u32[]{:S(2)}, u32[]{:S(2)}) collective-permute-start(f32[2,4,6,8,128]{4,3,2,1,0:T(8,128)S(1)} %pad_maximum_fusion.far), channel_id=1, source_target_pairs={{0,1},{1,0},{2,3},{3,2},{4,5},{5,4},{6,7},{7,6},{8,9},{9,8},{10,11... | collective-permute-start | bytes 589832 | tf_op jit(solution)/shard_map/ppermute | solution.py:444
  40.2 4.7 %collective-permute-start.3 = (f32[25,8,128]{2,1,0:T(8,128)S(1)}, f32[25,8,128]{2,1,0:T(8,128)S(1)}, u32[]{:S(2)}, u32[]{:S(2)}) collective-permute-start(f32[25,8,128]{2,1,0:T(8,128)S(1)} %collective-permute-done.2.flow_half), channel_id=1, source_target_pairs={{0,16},{16,0},{1,17},{17,1},{2,18},{18,2},{3,19},{19,3},{4,20},{20... | collective-permute-start | bytes 307208 | tf_op jit(solution)/shard_map/ppermute | solution.py:514
  44.9 1.2 %copy-start.2 = (f32[5,50,8,128]{3,2,1,0:T(8,128)S(1)}, f32[5,50,8,128]{3,2,1,0:T(8,128)}, u32[]{:S(2)}) copy-start(f32[5,50,8,128]{3,2,1,0:T(8,128)} %get-tuple-element.19.mate) | copy-start | bytes 3072004
  46.1 1.1 %copy-start.3 = (f32[4,50,8,128]{3,2,1,0:T(8,128)S(1)}, f32[4,50,8,128]{3,2,1,0:T(8,128)}, u32[]{:S(2)}) copy-start(f32[4,50,8,128]{3,2,1,0:T(8,128)} %get-tuple-element.18.cross) | copy-start | bytes 2457604

commit v4 on v3

v4 whole, which is shorter than its diff:
```python
import functools

import jax
import jax.numpy as jnp
from jax import lax
from jax.experimental import pallas as pl
from jax.experimental.pallas import tpu as pltpu
from jax.sharding import PartitionSpec as P

ITERS = 3


DIFFUSIVITY = 0.5
TIME_STEP = 0.2
SURFACE_COUPLING = 0.5
STERIC_GAIN = 2.0
EPSILON = 1e-06

LANES = 128
VECTORS = 2
SLOPE = 0.25 * TIME_STEP
SPREAD = TIME_STEP * DIFFUSIVITY
HEIGHTS = VECTORS * 2
DEPTHS = HEIGHTS + VECTORS * 2
GRAMS = DEPTHS + 2
BLOCKS = GRAMS + 1


def next_row(tile):
    turned = pltpu.roll(tile, LANES - 1, 1)
    carried = pltpu.roll(turned, tile.shape[0] - 1, 0)
    lane = lax.broadcasted_iota(jnp.int32, tile.shape, 1)
    return jnp.where(lane == LANES - 1, carried, turned)


def prior_row(tile):
    turned = pltpu.roll(tile, 1, 1)
    carried = pltpu.roll(turned, 1, 0)
    lane = lax.broadcasted_iota(jnp.int32, tile.shape, 1)
    return jnp.where(lane == 0, carried, turned)


def wall_depth(depth):
    subs, lane = (lax.broadcasted_iota(jnp.int32, depth.shape, axis) for axis in (0, 1))
    last = (subs == depth.shape[0] - 1) & (lane == LANES - 1)
    return jnp.where(last, jnp.zeros_like(depth), jnp.minimum(depth, next_row(depth)))


def face_pair(level, face_depth, flow_sum):
    slope = SLOPE * flow_sum
    open_face = level < face_depth
    return (
        jnp.where(open_face, slope + SPREAD, 0.0),
        jnp.where(open_face, slope - SPREAD, 0.0),
    )


def outflow(pair, near, far):
    return pair[0] * near + pair[1] * far


def side_pairs(level, depths, flow):
    return (
        face_pair(level, depths[0], flow + next_row(flow)),
        face_pair(level, depths[1], -(flow + prior_row(flow))),
    )


def divergence_y(pairs, tile):
    return outflow(pairs[0], tile, next_row(tile)) + outflow(pairs[1], tile, prior_row(tile))


def side_depths(depth):
    north = wall_depth(depth)
    return north, prior_row(north)


def orientation():
    outer = lax.rem(lax.axis_index("lon"), 2)
    return outer, 1 - outer, (2 * outer - 1).astype(jnp.float32)


def steps(count, most):
    return max(u for u in range(1, most + 1) if count % u == 0)


def share(levels):
    size = lax.axis_size("grp")
    assert size == 2
    part = (levels + 1) // 2
    return lax.axis_index("grp") * (levels - part), part


def edge_kernel(
    levels, sub, tracer_hbm, zonal_hbm, edge_hbm, tracer, zonal, edge, sems_in, sems_out
):
    outer, _, _ = orientation()
    start, part = share(levels)

    def move(source, target, sem):
        copy = pltpu.make_async_copy(source, target, sem)
        copy.start()
        return copy

    arrivals = [
        move(tracer_hbm.at[v], tracer.at[v], sems_in.at[v]) for v in range(VECTORS)
    ] + [move(zonal_hbm.at[pl.ds(start, part)], zonal, sems_in.at[VECTORS])]
    departures = []
    for v, arrival in enumerate(arrivals):
        number = part if v == VECTORS else levels
        arrival.wait()

        def body(k, carry, v=v):
            source = zonal if v == VECTORS else tracer.at[v]
            edge[v * levels + k] = source[k, pl.ds(outer, sub, stride=2), :]
            return carry

        lax.fori_loop(0, number, body, 0, unroll=steps(number, 10))
        rows = pl.ds(v * levels, number)
        departures.append(move(edge.at[rows], edge_hbm.at[rows], sems_out.at[v]))
    for departure in departures:
        departure.wait()


def first_kernel(
    levels, sub, edge, tracer, zonal, merid, bottom, cross, mate, raw, mate_raw, flow_in, mate_flow
):
    del edge
    outer, inner, sign = orientation()

    def column(ref, where, *lead):
        return ref[(*lead, pl.ds(where, sub, stride=2), slice(None))]

    depth = [column(bottom, where).astype(jnp.float32) for where in (outer, inner)]
    between = jnp.minimum(*depth)
    along = [side_depths(d) for d in depth]
    cross[VECTORS * levels] = depth[0]
    mate[VECTORS * levels] = depth[1]

    def body(k, carry):
        level = k.astype(jnp.float32)
        flow = [column(zonal, where, k) for where in (outer, inner)]
        turn = [column(merid, where, k) for where in (outer, inner)]
        middle = face_pair(level, between, -sign * (flow[0] + flow[1]))
        sides = [side_pairs(level, along[c], turn[c]) for c in range(2)]
        for v in range(VECTORS):
            cells = [column(tracer, where, v, k) for where in (outer, inner)]
            flux = outflow(middle, *cells)
            kept = [
                jnp.where(level < depth[c], cells[c], 0.0) - divergence_y(sides[c], cells[c])
                for c in range(2)
            ]
            cross[v * levels + k] = kept[0] - flux
            raw[v * levels + k] = cells[0]
            mate[v * levels + k] = kept[1] + flux
            mate_raw[v * levels + k] = cells[1]
        flow_in[k] = flow[0]
        mate_flow[k] = flow[1]
        return carry

    lax.fori_loop(0, levels, body, 0, unroll=steps(levels, 10))


def wrap(pole, width):
    for v in range(VECTORS):
        pole[v, 0] = pole[v, width]
        pole[v, width + 1] = pole[v, 1]


def spread(pole, face_x, face_y, face_z, v, x):
    west, centre, east = (pole[v, x + j] for j in range(3))
    return (face_x[x + 1] * (east - centre) - face_x[x] * (centre - west)) + (
        face_y[x] * (next_row(centre) - centre) - face_z[x] * (centre - prior_row(centre))
    )


def second_kernel(
    levels, sub, raw, cross, mate, mate_raw, flow_in, mate_flow,
    raw_far, cross_far, mate_far, mate_raw_far, mate_flow_far, flow_other,
    merid, surface, bottom, tracer, message, flow_far,
):
    outer, inner, sign = orientation()
    start, part = share(levels)
    last = VECTORS * levels

    def unpack(i, carry):
        flow_far[start + i] = raw_far[VECTORS * levels + i]
        flow_far[levels - part - start + i] = flow_other[i]
        return carry

    lax.fori_loop(0, part, unpack, 0, unroll=steps(part, 10))
    near = [(raw, cross), (mate_raw, mate)]
    far = [(raw_far, cross_far), (mate_raw_far, mate_far)]
    depth = [cross[last], mate[last]]
    beside = [jnp.minimum(depth[0], cross_far[last]), jnp.minimum(depth[1], mate_far[last])]
    between = jnp.minimum(*depth)
    along = [side_depths(d) for d in depth]
    zero = jnp.zeros_like(between)

    def body(k, carry):
        level = k.astype(jnp.float32)
        flow = [flow_in[k], mate_flow[k]]
        beyond = [flow_far[k], mate_flow_far[k]]
        turn = [merid[k, pl.ds(where, sub, stride=2), :] for where in (outer, inner)]
        middle = face_pair(level, between, -sign * (flow[0] + flow[1]))
        edges = [
            face_pair(level, beside[c], (sign, -sign)[c] * (flow[c] + beyond[c])) for c in range(2)
        ]
        sides = [side_pairs(level, along[c], turn[c]) for c in range(2)]
        totals, grams = list(carry[:4]), list(carry[4:])
        done = []
        for v in range(VECTORS):
            own, other = [], []
            for c in range(2):
                (first, kept), (first_far, kept_far) = near[c], far[c]
                row = v * levels + k
                flux = outflow(edges[c], first[row], first_far[row])
                own.append(kept[row] - flux)
                other.append(kept_far[row] + flux)
            crossing = outflow(middle, *own)
            fresh = []
            for c, where in enumerate((outer, inner)):
                gone = crossing if c == 0 else -crossing
                value = (
                    own[c]
                    - outflow(edges[c], own[c], other[c])
                    - gone
                    - divergence_y(sides[c], own[c])
                )
                tracer[v, k, pl.ds(where, sub, stride=2), :] = value
                totals[v * 2 + c] = totals[v * 2 + c] + value
                fresh.append(value)
            done.append(fresh)
        for c in range(2):
            a, b = done[0][c], done[1][c]
            grams = [grams[0] + a * a, grams[1] + a * b, grams[2] + b * b]
        return (*totals, *grams)

    sums = lax.fori_loop(0, levels, body, (zero,) * 7, unroll=steps(levels, 10))
    gain = STERIC_GAIN / levels
    subs = lax.broadcasted_iota(jnp.int32, zero.shape, 0)
    packed = zero
    for i, gram in enumerate(sums[4:]):
        packed = jnp.where(subs == i, jnp.sum(gram, axis=0, keepdims=True), packed)
    message[GRAMS] = packed
    for v in range(VECTORS):
        for c, where in enumerate((outer, inner)):
            message[v * 2 + where] = gain * sums[v * 2 + c]
            message[HEIGHTS + v * 2 + c] = surface[v, pl.ds(c, sub, stride=2), :]
    for c in range(2):
        message[DEPTHS + c] = bottom[pl.ds(c, sub, stride=2), :].astype(jnp.float32)


def total(tile):
    return jnp.sum(jnp.sum(tile, axis=0, keepdims=True), axis=1, keepdims=True)


def third_kernel(
    levels, sub, count, pair, fetched, fetched_mate, tracer, tracer_out, surface_out, growth,
    pole, residual, answer, image, height, depth, face_x, face_y, face_z, packed,
):
    width = 2 * count
    me = lax.axis_index("lon")
    core = lax.rem(me, 2)
    zero = jnp.zeros((sub, LANES), jnp.float32)
    none = (zero,) * VECTORS

    def place(owner, block):
        packed[owner] = block(GRAMS)
        for c in range(2):
            x = 2 * owner + c
            floor = block(DEPTHS + c)
            depth[x] = floor
            for v in range(VECTORS):
                tall = jnp.where(floor > 0, block(HEIGHTS + v * 2 + c), 0.0)
                height[v, x] = tall
                pole[v, x + 1] = tall
                residual[v, x] = block(v * 2 + c)

    for slot in range(2):
        place(me ^ slot, lambda row, slot=slot: pair[slot, row])
    for ref, flip in ((fetched, 0), (fetched_mate, 1)):
        for j, masks in enumerate(chip_masks(count)):
            mask = jnp.where((core ^ flip) == 0, *masks)
            for slot in range(2):
                owner = me ^ flip ^ slot ^ (2 * mask)

                def put(owner=owner, ref=ref, j=j, slot=slot):
                    place(owner, lambda row: ref[j, slot, row])

                if all(masks):
                    put()
                else:
                    pl.when(mask > 0)(put)

    def over(body, init):
        return lax.fori_loop(0, count, body, init, unroll=steps(count, 16))

    def each(d):
        return [(v, c, 2 * d + c) for v in range(VECTORS) for c in range(2)]

    def prepare(d, carry):
        for x in (2 * d, 2 * d + 1):
            here, after = depth[x], depth[lax.rem(x + 1, width)]
            face_x[x + 1] = SURFACE_COUPLING * jnp.minimum(here, after)
            north, south = side_depths(here)
            face_y[x] = SURFACE_COUPLING * north
            face_z[x] = SURFACE_COUPLING * south
        return carry

    over(prepare, 0)
    face_x[0] = face_x[width]
    wrap(pole, width)

    def start(d, carry):
        sums = list(carry)
        for v, _, x in each(d):
            value = residual[v, x] + spread(pole, face_x, face_y, face_z, v, x)
            residual[v, x] = value
            sums[v] = sums[v] + value * value
        return tuple(sums)

    norm = [total(t) for t in over(start, none)]

    def aim(d, carry):
        for v, _, x in each(d):
            pole[v, x + 1] = residual[v, x]
        return carry

    over(aim, 0)
    wrap(pole, width)

    def apply(d, carry):
        sums = list(carry)
        for v, _, x in each(d):
            centre = pole[v, x + 1]
            value = centre - spread(pole, face_x, face_y, face_z, v, x)
            image[v, x] = value
            sums[v] = sums[v] + centre * value
        return tuple(sums)

    for iteration in range(ITERS):
        energy = [total(t) for t in over(apply, none)]
        size = [n / e for n, e in zip(norm, energy)]
        held = height if iteration == 0 else answer
        if iteration + 1 < ITERS:

            def advance(d, carry, size=size, held=held):
                sums = list(carry)
                for v, _, x in each(d):
                    answer[v, x] = held[v, x] + size[v] * pole[v, x + 1]
                    value = residual[v, x] - size[v] * image[v, x]
                    residual[v, x] = value
                    sums[v] = sums[v] + value * value
                return tuple(sums)

            fresh = [total(t) for t in over(advance, none)]
            ratio = [f / n for f, n in zip(fresh, norm)]

            def turn(d, carry, ratio=ratio):
                for v, _, x in each(d):
                    pole[v, x + 1] = residual[v, x] + ratio[v] * pole[v, x + 1]
                return carry

            over(turn, 0)
            wrap(pole, width)
            norm = fresh

    def finish(d, carry):
        grams = list(carry)
        for x in (2 * d, 2 * d + 1):
            a, b = (held[v, x] + size[v] * pole[v, x + 1] for v in range(VECTORS))
            answer[0, x], answer[1, x] = a, b
            grams = [grams[0] + a * a, grams[1] + a * b, grams[2] + b * b]
        return (*grams, carry[3] + packed[d])

    *grams, share_of = over(finish, (zero,) * 4)
    cells = (levels + 1) * width * sub * LANES
    one, mix, two = (
        (total(g) + jnp.sum(share_of[i : i + 1], axis=1, keepdims=True)) / cells
        for i, g in enumerate(grams)
    )
    scale_one = jnp.sqrt(one + EPSILON)
    cross = mix / scale_one
    rest = two - 2.0 * cross * cross + cross * cross * one / (one + EPSILON)
    scale_two = jnp.sqrt(rest + EPSILON)
    over_one, over_two = 1.0 / scale_one, 1.0 / scale_two

    def scale(k, carry):
        unit = tracer[0, k] * over_one
        tracer_out[0, k] = unit
        tracer_out[1, k] = (tracer[1, k] - cross * unit) * over_two
        return carry

    lax.fori_loop(0, levels, scale, 0, unroll=steps(levels, 10))
    for c in range(2):
        x = 2 * me + c
        unit = answer[0, x] * over_one
        surface_out[0, pl.ds(c, sub, stride=2), :] = unit
        surface_out[1, pl.ds(c, sub, stride=2), :] = (answer[1, x] - cross * unit) * over_two
    for i, value in enumerate((scale_one, cross, scale_two)):
        growth[i] = value[0, 0]


def tiled(array):
    *lead, columns, rows = array.shape
    split = array.reshape(*lead, columns, rows // LANES, LANES)
    return jnp.swapaxes(split, -3, -2).reshape(*lead, rows // LANES * columns, LANES)


def untiled(array, columns):
    *lead, high, lanes = array.shape
    split = array.reshape(*lead, high // columns, columns, lanes)
    return jnp.swapaxes(split, -3, -2).reshape(*lead, columns, high // columns * lanes)


def swap(array, mask):
    count = lax.axis_size("lon")
    return lax.ppermute(array, "lon", [(i, i ^ mask) for i in range(count)])


def chip_masks(count):
    lists, loads = ([], []), [0, 0]
    for mask in range(count // 2 - 1, 0, -1):
        core = int(loads[1] < loads[0])
        lists[core].append(mask)
        loads[core] += mask % 2 + mask // 2
    longest = max(map(len, lists))
    return list(zip(*(one + [0] * (longest - len(one)) for one in lists)))


def gather(block):
    count = lax.axis_size("lon")
    pair = jnp.stack([block, swap(block, 1)])
    fetched = []
    for masks in chip_masks(count):
        moves = [(i, i ^ (2 * masks[i % 2])) for i in range(count) if masks[i % 2]]
        fetched.append(lax.ppermute(pair, "lon", moves))
    fetched = jnp.stack(fetched)
    return pair, fetched, swap(fetched, 1)


def on_device(tracer_pert, surface_pert, zonal_flow, merid_flow, bottom_level):
    vectors, levels, columns, rows = tracer_pert.shape
    count = lax.axis_size("lon")
    sub = rows // LANES
    assert vectors == VECTORS and columns == 2 and rows % LANES == 0
    assert count >= 8 and count & (count - 1) == 0
    width = 2 * count
    f32 = jnp.float32
    vmem = pl.BlockSpec(memory_space=pltpu.VMEM)
    hbm = pl.BlockSpec(memory_space=pltpu.HBM)
    params = pltpu.CompilerParams(vmem_limit_bytes=24 * 2**20)

    def shaped(*shape):
        return jax.ShapeDtypeStruct((*shape, sub, LANES), f32)

    def held(*shape):
        return pltpu.VMEM((*shape, sub, LANES), f32)

    both = pltpu.VMEM((vectors, levels, sub * 2, LANES), f32)
    tracer_pert, zonal_flow, merid_flow = map(tiled, (tracer_pert, zonal_flow, merid_flow))
    outward = [(i, (i + 1) % count if i % 2 else (i - 1) % count) for i in range(count)]
    part = (levels + 1) // 2
    bottom = tiled(bottom_level)
    edge_rows = VECTORS * levels + part

    edge = pl.pallas_call(
        functools.partial(edge_kernel, levels, sub),
        out_shape=shaped(edge_rows),
        in_specs=[hbm] * 2,
        out_specs=hbm,
        scratch_shapes=[
            both,
            pltpu.VMEM((part, sub * 2, LANES), f32),
            held(edge_rows),
            pltpu.SemaphoreType.DMA((VECTORS + 1,)),
            pltpu.SemaphoreType.DMA((VECTORS + 1,)),
        ],
        compiler_params=pltpu.CompilerParams(vmem_limit_bytes=60 * 2**20),
        name="edge_columns",
    )(tracer_pert, zonal_flow)
    edge_far = lax.ppermute(edge, "lon", outward)
    flow_other = lax.ppermute(edge_far[VECTORS * levels :], "grp", [(0, 1), (1, 0)])
    cross, mate, raw, mate_raw, flow_in, mate_flow = pl.pallas_call(
        functools.partial(first_kernel, levels, sub),
        out_shape=(
            shaped(VECTORS * levels + 1),
            shaped(VECTORS * levels + 1),
            shaped(VECTORS * levels),
            shaped(VECTORS * levels),
            shaped(levels),
            shaped(levels),
        ),
        in_specs=[pl.BlockSpec(memory_space=pl.ANY)] + [vmem] * 4,
        out_specs=(vmem,) * 6,
        compiler_params=params,
        name="partial_step",
    )(edge, tracer_pert, zonal_flow, merid_flow, bottom)
    cross_far = lax.ppermute(cross, "lon", outward)
    mate_far, mate_raw_far, mate_flow_far = (swap(x, 1) for x in (mate, mate_raw, mate_flow))
    tracer, message = pl.pallas_call(
        functools.partial(second_kernel, levels, sub),
        out_shape=(
            jax.ShapeDtypeStruct((vectors, levels, sub * 2, LANES), f32),
            shaped(BLOCKS),
        ),
        in_specs=[vmem] * 15,
        out_specs=(vmem, vmem),
        scratch_shapes=[held(levels)],
        compiler_params=params,
        name="both_steps",
    )(
        raw, cross, mate, mate_raw, flow_in, mate_flow,
        edge_far, cross_far, mate_far, mate_raw_far, mate_flow_far, flow_other,
        merid_flow, tiled(surface_pert), bottom,
    )
    tracer_vec, surface_vec, growth = pl.pallas_call(
        functools.partial(third_kernel, levels, sub, count),
        out_shape=(
            jax.ShapeDtypeStruct((vectors, levels, sub * 2, LANES), f32),
            jax.ShapeDtypeStruct((vectors, sub * 2, LANES), f32),
            jax.ShapeDtypeStruct((3,), f32),
        ),
        in_specs=[vmem] * 4,
        out_specs=(vmem, vmem, pl.BlockSpec(memory_space=pltpu.SMEM)),
        scratch_shapes=[
            held(vectors, width + 2),
            *[held(vectors, width)] * 4,
            held(width),
            held(width + 1),
            held(width),
            held(width),
            held(count),
        ],
        compiler_params=pltpu.CompilerParams(vmem_limit_bytes=32 * 2**20),
        name="surface_and_scale",
    )(*gather(message), tracer)
    return (untiled(tracer_vec, 2), untiled(surface_vec, 2), growth)


def solution(mesh):
    placed = (
        P("grp", None, "lon", None),
        P("grp", "lon", None),
        P(None, "lon", None),
        P(None, "lon", None),
        P("lon", None),
    )
    return jax.shard_map(
        on_device,
        mesh=mesh,
        in_specs=placed,
        out_specs=(P("grp", None, "lon", None), P("grp", "lon", None), P("grp")),
        check_vma=False,
    )
```

time: 65.3 us -> 49.2 us (0.75)
  blocking collectives: 13.7 us -> 0 us
  starting transfers between devices: 13.9 us -> 21.3 us
  waiting for transfers between devices: 25.2 us -> 18.2 us
  local copies, waits for them, and re-layouts: 2.37 us -> 1.08 us
  other arithmetic: 0.84 us -> 0.04 us
    ppermute x4 -> x5, waiting for transfers between devices: 16.5 us -> 2.55 us  [swap(): return lax.ppermute(array, 'lon', [(i, i ^ mask) for i in range(count)])]
    all_to_all x1 -> x0, blocking collectives: 13.7 us -> none  [on_device(): gathered = lax.all_to_all(message, 'lon', 0, 0)]
    ppermute x4 -> x5, starting transfers between devices: 0.59 us -> 7.12 us  [swap(): return lax.ppermute(array, 'lon', [(i, i ^ mask) for i in range(count)])]
    ppermute x4 -> x6, starting transfers between devices: 7.68 us -> 14.1 us  [the longest x4 6.58 us: gather(): fetched.append(lax.ppermute(pair, 'lon', moves))]
    ppermute x1, starting transfers between devices: 5.67 us -> 0.11 us  [on_device(): cross_far = lax.ppermute(cross, 'lon', outward)]
    ppermute x1, waiting for transfers between devices: 0.01 us -> 3.49 us  [on_device(): cross_far = lax.ppermute(cross, 'lon', outward)]
    ppermute x4 -> x6, waiting for transfers between devices: 8.74 us -> 12.2 us  [the longest x4 8.13 us: gather(): fetched.append(lax.ppermute(pair, 'lon', moves))]
    unnamed x12, local copies, waits for them, and re-layouts: 2.37 us -> 1.07 us
  transfers between devices with their start and end apart: 9 -> 12, of which waited for: 6 -> 6; matrix products, arithmetic and copies ran while one was open for 1% -> 0% of each run, Pallas kernels for 2% -> 2%
where the time goes in v4:
time: 49.2 us; the launch traced here: 49 us
  starting transfers between devices  21.3 us (43%)
  waiting for transfers between devices  18.2 us (37%)
  Pallas kernels  7.58 us (15%)
  local copies, waits for them, and re-layouts  1.08 us (2%)
  between operations  0.74 us (2%)
    ppermute x4, waiting for transfers between devices, gather(): fetched.append(lax.ppermute(pair, 'lon', moves))  8.13 us
    ppermute x5, starting transfers between devices, swap(): return lax.ppermute(array, 'lon', [(i, i ^ mask) for i in range(count)])  7.12 us
    ppermute x4, starting transfers between devices, gather(): fetched.append(lax.ppermute(pair, 'lon', moves))  6.58 us
    ppermute x1, starting transfers between devices, on_device(): edge_far = lax.ppermute(edge, 'lon', outward)  5.51 us
    ppermute x1, waiting for transfers between devices, on_device(): edge_far = lax.ppermute(edge, 'lon', outward)  4.04 us
    ppermute x1, waiting for transfers between devices, on_device(): cross_far = lax.ppermute(cross, 'lon', outward)  3.49 us
    pallas_call x1, Pallas kernels, on_device(): pl.pallas_call(functools.partial(third_kernel, levels, sub, count), out_s...  2.87 us
    ppermute x5, waiting for transfers between devices, swap(): return lax.ppermute(array, 'lon', [(i, i ^ mask) for i in range(count)])  2.55 us
  transfers between devices with their start and end apart: 12, of which 6 were waited for; matrix products, arithmetic and copies ran while one was open for 0% of the time, Pallas kernels for 2%

profile of v4, /device:TPU:0, one launch (start us, length us, event | category | flops | bytes accessed | tf_op | source)
XLA Modules:
  0.0 49.0 jit_solution(12673953191138414883)
XLA Ops:
  0.6 0.0 copy-start
  0.6 0.0 copy-start.2
  0.7 0.0 copy-start.3
  0.7 0.0 copy-start.4
  0.7 2.0 %edge_columns.1.edge = f32[125,8,128]{2,1,0:T(8,128)} custom-call(f32[2,50,16,128]{3,2,1,0:T(8,128)} %bitcast.41, f32[50,16,128]{2,1,0:T(8,128)} %bitcast.45), custom_call_target="tpu_custom_call" | custom-call | tf_op jit(solution)/shard_map/edge_columns/pallas_call | solution.py:468
  2.7 5.5 %collective-permute-start = (f32[125,8,128]{2,1,0:T(8,128)}, f32[125,8,128]{2,1,0:T(8,128)S(1)}, u32[]{:S(2)}, u32[]{:S(2)}) collective-permute-start(f32[125,8,128]{2,1,0:T(8,128)} %edge_columns.1.edge), channel_id=1, source_target_pairs={{0,15},{1,2},{2,1},{3,4},{4,3},{5,6},{6,5},{7,8},{8,7},{9,10},{10,... | collective-permute-start | bytes 1536008 | tf_op jit(solution)/shard_map/ppermute | solution.py:483
  8.2 0.0 copy-done
  8.2 0.0 copy-done.2
  8.2 0.0 copy-done.3
  8.2 0.0 copy-done.4
  8.2 0.0 copy-start.1
  8.2 1.0 %copy-done.1 = f32[125,8,128]{2,1,0:T(8,128)S(1)} copy-done((f32[125,8,128]{2,1,0:T(8,128)S(1)}, f32[125,8,128]{2,1,0:T(8,128)}, u32[]{:S(2)}) %copy-start.1) | copy-done | bytes 512024
  9.3 1.2 %partial_step.1 = (f32[101,8,128]{2,1,0:T(8,128)S(1)}, f32[101,8,128]{2,1,0:T(8,128)S(1)}, f32[100,8,128]{2,1,0:T(8,128)S(1)}, f32[100,8,128]{2,1,0:T(8,128)S(1)...) custom-call(f32[125,8,128]{2,1,0:T(8,128)S(1)} %copy-done.1, f32[2,50,16,128]{3,2,1,0:T(8,128)S(1)} %bitcast.42, ...), custom_call_target="tpu_custom_call" | custom-call | tf_op jit(solution)/shard_map/partial_step/pallas_call | solution.py:485
  10.5 0.1 collective-permute-start.1
  10.6 0.0 collective-permute-start.2
  10.6 0.5 %collective-permute-start.3 = (f32[100,8,128]{2,1,0:T(8,128)S(1)}, f32[100,8,128]{2,1,0:T(8,128)S(1)}, u32[]{:S(2)}, u32[]{:S(2)}) collective-permute-start(f32[100,8,128]{2,1,0:T(8,128)S(1)} %get-tuple-element.17.mate_raw), channel_id=1, source_target_pairs={{0,1},{1,0},{2,3},{3,2},{4,5},{5,4},{6,7},{7,6},{8,9},{9,8},{10,11... | collective-permute-start | bytes 1228808 | tf_op jit(solution)/shard_map/ppermute | solution.py:419
  11.1 0.1 collective-permute-start.4
  11.2 4.0 %collective-permute-done.raw_far = f32[125,8,128]{2,1,0:T(8,128)S(1)} collective-permute-done((f32[125,8,128]{2,1,0:T(8,128)}, f32[125,8,128]{2,1,0:T(8,128)S(1)}, u32[]{:S(2)}, u32[]{:S(2)}) %collective-permute-start) | collective-permute-done | bytes 512032 | tf_op jit(solution)/shard_map/ppermute | solution.py:483
  15.3 0.0 copy-start.5
  15.3 2.0 %collective-permute-start.5 = (f32[25,8,128]{2,1,0:T(8,128)S(1)}, f32[25,8,128]{2,1,0:T(8,128)S(1)}, u32[]{:S(2)}, u32[]{:S(2)}) collective-permute-start(f32[25,8,128]{2,1,0:T(8,128)S(1)} %slice.4), channel_id=1, source_target_pairs={{0,16},{16,0},{1,17},{17,1},{2,18},{18,2},{3,19},{19,3},{4,20},{20... | collective-permute-start | bytes 307208 | tf_op jit(solution)/shard_map/ppermute | solution.py:484
  17.3 0.0 collective-permute-done.4.mate_flow_far
  17.3 0.0 collective-permute-done.3.mate_raw_far
  17.3 3.5 %collective-permute-done.1.cross_far = f32[101,8,128]{2,1,0:T(8,128)S(1)} collective-permute-done((f32[101,8,128]{2,1,0:T(8,128)S(1)}, f32[101,8,128]{2,1,0:T(8,128)S(1)}, u32[]{:S(2)}, u32[]{:S(2)}) %collective-permute-start.1) | collective-permute-done | bytes 413728 | tf_op jit(solution)/shard_map/ppermute | solution.py:500
  20.8 0.0 collective-permute-done.2.mate_far
  20.8 0.0 collective-permute-done.5.flow_other
  20.8 0.0 copy-done.5
  20.8 1.5 %both_steps.1 = (f32[2,50,16,128]{3,2,1,0:T(8,128)S(1)}, f32[11,8,128]{2,1,0:T(8,128)S(1)}) custom-call(f32[100,8,128]{2,1,0:T(8,128)S(1)} %get-tuple-element.14.raw, f32[101,8,128]{2,1,0:T(8,128)S(1)} %get-tuple-element.15.cross, f32[101,8,128]{2,1,0:T(8,128)S(1)} %get-tuple-element.16.mate, f32[100,8,128]{2,1,0:T(8,128)S(1)} %get-tuple-element.17.mate_raw, ...), custom_call_target="tpu_custom_call" | custom-call | tf_op jit(solution)/shard_map/both_steps/pallas_call | solution.py:502
  22.3 6.4 %collective-permute-start.6 = (f32[11,8,128]{2,1,0:T(8,128)S(1)}, f32[11,8,128]{2,1,0:T(8,128)S(1)}, u32[]{:S(2)}, u32[]{:S(2)}) collective-permute-start(f32[11,8,128]{2,1,0:T(8,128)S(1)} %get-tuple-element.20), channel_id=1, source_target_pairs={{0,1},{1,0},{2,3},{3,2},{4,5},{5,4},{6,7},{7,6},{8,9},{9,8},{10,11... | collective-permute-start | bytes 135176 | tf_op jit(solution)/shard_map/ppermute | solution.py:419
  28.7 0.9 %collective-permute-done.6 = f32[11,8,128]{2,1,0:T(8,128)S(1)} collective-permute-done((f32[11,8,128]{2,1,0:T(8,128)S(1)}, f32[11,8,128]{2,1,0:T(8,128)S(1)}, u32[]{:S(2)}, u32[]{:S(2)}) %collective-permute-start.6) | collective-permute-done | bytes 45088 | tf_op jit(solution)/shard_map/ppermute | solution.py:419
  29.6 0.7 %collective-permute-start.10 = (f32[2,11,8,128]{3,2,1,0:T(8,128)S(1)}, f32[2,11,8,128]{3,2,1,0:T(8,128)S(1)}, u32[]{:S(2)}, u32[]{:S(2)}) collective-permute-start(f32[2,11,8,128]{3,2,1,0:T(8,128)S(1)} %pad_maximum_fusion.1.pair), channel_id=1, source_target_pairs={{1,3},{3,1},{5,7},{7,5},{9,11},{11,9},{13,15},{15,13},{17,19},{19,... | collective-permute-start | bytes 270344 | tf_op jit(solution)/shard_map/ppermute | solution.py:438
  30.3 3.3 %collective-permute-start.9 = (f32[2,11,8,128]{3,2,1,0:T(8,128)S(1)}, f32[2,11,8,128]{3,2,1,0:T(8,128)S(1)}, u32[]{:S(2)}, u32[]{:S(2)}) collective-permute-start(f32[2,11,8,128]{3,2,1,0:T(8,128)S(1)} %pad_maximum_fusion.1.pair), channel_id=1, source_target_pairs={{0,6},{1,5},{2,4},{3,7},{4,2},{5,1},{6,0},{7,3},{8,14},{9,13},{10,... | collective-permute-start | bytes 270344 | tf_op jit(solution)/shard_map/ppermute | solution.py:438
  33.6 2.6 %collective-permute-start.8 = (f32[2,11,8,128]{3,2,1,0:T(8,128)S(1)}, f32[2,11,8,128]{3,2,1,0:T(8,128)S(1)}, u32[]{:S(2)}, u32[]{:S(2)}) collective-permute-start(f32[2,11,8,128]{3,2,1,0:T(8,128)S(1)} %pad_maximum_fusion.1.pair), channel_id=1, source_target_pairs={{0,8},{1,11},{2,10},{3,9},{4,12},{5,15},{6,14},{7,13},{8,0},{9,3},... | collective-permute-start | bytes 270344 | tf_op jit(solution)/shard_map/ppermute | solution.py:438
  36.2 0.0 collective-permute-start.7
  36.2 0.0 collective-permute-done.10
  36.2 0.0 collective-permute-done.9
  36.2 7.3 %collective-permute-done.8 = f32[2,11,8,128]{3,2,1,0:T(8,128)S(1)} collective-permute-done((f32[2,11,8,128]{3,2,1,0:T(8,128)S(1)}, f32[2,11,8,128]{3,2,1,0:T(8,128)S(1)}, u32[]{:S(2)}, u32[]{:S(2)}) %collective-permute-start.8) | collective-permute-done | bytes 90144 | tf_op jit(solution)/shard_map/ppermute | solution.py:438
  43.6 0.8 %collective-permute-done.7 = f32[2,11,8,128]{3,2,1,0:T(8,128)S(1)} collective-permute-done((f32[2,11,8,128]{3,2,1,0:T(8,128)S(1)}, f32[2,11,8,128]{3,2,1,0:T(8,128)S(1)}, u32[]{:S(2)}, u32[]{:S(2)}) %collective-permute-start.7) | collective-permute-done | bytes 90144 | tf_op jit(solution)/shard_map/ppermute | solution.py:438
  44.4 0.1 collective-permute-start.11
  44.4 1.7 %collective-permute-done.11.fetched_mate = f32[4,2,11,8,128]{4,3,2,1,0:T(8,128)S(1)} collective-permute-done((f32[4,2,11,8,128]{4,3,2,1,0:T(8,128)S(1)}, f32[4,2,11,8,128]{4,3,2,1,0:T(8,128)S(1)}, u32[]{:S(2)}, u32[]{:S(2)}) %collective-permute-start.11) | collective-permute-done | bytes 360480 | tf_op jit(solution)/shard_map/ppermute | solution.py:419
  46.1 2.9 %surface_and_scale.1 = (f32[2,50,16,128]{3,2,1,0:T(8,128)}, f32[2,16,128]{2,1,0:T(8,128)}, f32[3]{0:T(128)}) custom-call(f32[2,11,8,128]{3,2,1,0:T(8,128)S(1)} %pad_maximum_fusion.1.pair, f32[4,2,11,8,128]{4,3,2,1,0:T(8,128)S(1)} %pad_maximum_fusion.fetched, f32[4,2,11,8,128]{4,3,2,1,0:T(8,128)S(1)} %collective-permute-done.11.fetched_mate, ...), custom_call_target="tpu_custom_call" | custom-call | tf_op jit(solution)/shard_map/surface_and_scale/pallas_call | solution.py:518
  (3 shorter events, 0.0 us)
Async XLA Ops:
  0.6 7.6 %copy-start = (f32[2,50,2,1024]{3,2,1,0:T(2,128)S(1)}, f32[2,50,2,1024]{3,2,1,0:T(2,128)}, u32[]{:S(2)}) copy-start(f32[2,50,2,1024]{3,2,1,0:T(2,128)} %param.5) | copy-start | bytes 2457604
  0.6 7.6 %copy-start.2 = (f32[50,2,1024]{2,1,0:T(2,128)S(1)}, f32[50,2,1024]{2,1,0:T(2,128)}, u32[]{:S(2)}) copy-start(f32[50,2,1024]{2,1,0:T(2,128)} %param.8) | copy-start | bytes 1228804
  0.7 7.6 %copy-start.3 = (f32[50,2,1024]{2,1,0:T(2,128)S(1)}, f32[50,2,1024]{2,1,0:T(2,128)}, u32[]{:S(2)}) copy-start(f32[50,2,1024]{2,1,0:T(2,128)} %param.7) | copy-start | bytes 1228804
  0.7 7.6 %copy-start.4 = (s32[2,1024]{1,0:T(2,128)S(1)}, s32[2,1024]{1,0:T(2,128)}, u32[]{:S(2)}) copy-start(s32[2,1024]{1,0:T(2,128)} %param.9) | copy-start | bytes 24580
  2.7 12.6 %collective-permute-start = (f32[125,8,128]{2,1,0:T(8,128)}, f32[125,8,128]{2,1,0:T(8,128)S(1)}, u32[]{:S(2)}, u32[]{:S(2)}) collective-permute-start(f32[125,8,128]{2,1,0:T(8,128)} %edge_columns.1.edge), channel_id=1, source_target_pairs={{0,15},{1,2},{2,1},{3,4},{4,3},{5,6},{6,5},{7,8},{8,7},{9,10},{10,... | collective-permute-start | bytes 1536008 | tf_op jit(solution)/shard_map/ppermute | solution.py:483
  8.2 1.1 %copy-start.1 = (f32[125,8,128]{2,1,0:T(8,128)S(1)}, f32[125,8,128]{2,1,0:T(8,128)}, u32[]{:S(2)}) copy-start(f32[125,8,128]{2,1,0:T(8,128)} %edge_columns.1.edge) | copy-start | bytes 1536004
  10.5 10.3 %collective-permute-start.1 = (f32[101,8,128]{2,1,0:T(8,128)S(1)}, f32[101,8,128]{2,1,0:T(8,128)S(1)}, u32[]{:S(2)}, u32[]{:S(2)}) collective-permute-start(f32[101,8,128]{2,1,0:T(8,128)S(1)} %get-tuple-element.15.cross), channel_id=1, source_target_pairs={{0,15},{1,2},{2,1},{3,4},{4,3},{5,6},{6,5},{7,8},{8,7},{9,10},{10,... | collective-permute-start | bytes 1241096 | tf_op jit(solution)/shard_map/ppermute | solution.py:500
  10.6 10.2 %collective-permute-start.2 = (f32[101,8,128]{2,1,0:T(8,128)S(1)}, f32[101,8,128]{2,1,0:T(8,128)S(1)}, u32[]{:S(2)}, u32[]{:S(2)}) collective-permute-start(f32[101,8,128]{2,1,0:T(8,128)S(1)} %get-tuple-element.16.mate), channel_id=1, source_target_pairs={{0,1},{1,0},{2,3},{3,2},{4,5},{5,4},{6,7},{7,6},{8,9},{9,8},{10,11... | collective-permute-start | bytes 1241096 | tf_op jit(solution)/shard_map/ppermute | solution.py:419
  10.6 6.6 %collective-permute-start.3 = (f32[100,8,128]{2,1,0:T(8,128)S(1)}, f32[100,8,128]{2,1,0:T(8,128)S(1)}, u32[]{:S(2)}, u32[]{:S(2)}) collective-permute-start(f32[100,8,128]{2,1,0:T(8,128)S(1)} %get-tuple-element.17.mate_raw), channel_id=1, source_target_pairs={{0,1},{1,0},{2,3},{3,2},{4,5},{5,4},{6,7},{7,6},{8,9},{9,8},{10,11... | collective-permute-start | bytes 1228808 | tf_op jit(solution)/shard_map/ppermute | solution.py:419
  11.1 6.1 %collective-permute-start.4 = (f32[50,8,128]{2,1,0:T(8,128)S(1)}, f32[50,8,128]{2,1,0:T(8,128)S(1)}, u32[]{:S(2)}, u32[]{:S(2)}) collective-permute-start(f32[50,8,128]{2,1,0:T(8,128)S(1)} %get-tuple-element.19.mate_flow), channel_id=1, source_target_pairs={{0,1},{1,0},{2,3},{3,2},{4,5},{5,4},{6,7},{7,6},{8,9},{9,8},{10,11... | collective-permute-start | bytes 614408 | tf_op jit(solution)/shard_map/ppermute | solution.py:419
  15.3 5.5 %copy-start.5 = (f32[2,2,1024]{2,1,0:T(2,128)S(1)}, f32[2,2,1024]{2,1,0:T(2,128)}, u32[]{:S(2)}) copy-start(f32[2,2,1024]{2,1,0:T(2,128)} %param.6) | copy-start | bytes 49156
  15.3 5.5 %collective-permute-start.5 = (f32[25,8,128]{2,1,0:T(8,128)S(1)}, f32[25,8,128]{2,1,0:T(8,128)S(1)}, u32[]{:S(2)}, u32[]{:S(2)}) collective-permute-start(f32[25,8,128]{2,1,0:T(8,128)S(1)} %slice.4), channel_id=1, source_target_pairs={{0,16},{16,0},{1,17},{17,1},{2,18},{18,2},{3,19},{19,3},{4,20},{20... | collective-permute-start | bytes 307208 | tf_op jit(solution)/shard_map/ppermute | solution.py:484
  22.3 7.3 %collective-permute-start.6 = (f32[11,8,128]{2,1,0:T(8,128)S(1)}, f32[11,8,128]{2,1,0:T(8,128)S(1)}, u32[]{:S(2)}, u32[]{:S(2)}) collective-permute-start(f32[11,8,128]{2,1,0:T(8,128)S(1)} %get-tuple-element.20), channel_id=1, source_target_pairs={{0,1},{1,0},{2,3},{3,2},{4,5},{5,4},{6,7},{7,6},{8,9},{9,8},{10,11... | collective-permute-start | bytes 135176 | tf_op jit(solution)/shard_map/ppermute | solution.py:419
  29.6 6.6 %collective-permute-start.10 = (f32[2,11,8,128]{3,2,1,0:T(8,128)S(1)}, f32[2,11,8,128]{3,2,1,0:T(8,128)S(1)}, u32[]{:S(2)}, u32[]{:S(2)}) collective-permute-start(f32[2,11,8,128]{3,2,1,0:T(8,128)S(1)} %pad_maximum_fusion.1.pair), channel_id=1, source_target_pairs={{1,3},{3,1},{5,7},{7,5},{9,11},{11,9},{13,15},{15,13},{17,19},{19,... | collective-permute-start | bytes 270344 | tf_op jit(solution)/shard_map/ppermute | solution.py:438
  30.3 6.0 %collective-permute-start.9 = (f32[2,11,8,128]{3,2,1,0:T(8,128)S(1)}, f32[2,11,8,128]{3,2,1,0:T(8,128)S(1)}, u32[]{:S(2)}, u32[]{:S(2)}) collective-permute-start(f32[2,11,8,128]{3,2,1,0:T(8,128)S(1)} %pad_maximum_fusion.1.pair), channel_id=1, source_target_pairs={{0,6},{1,5},{2,4},{3,7},{4,2},{5,1},{6,0},{7,3},{8,14},{9,13},{10,... | collective-permute-start | bytes 270344 | tf_op jit(solution)/shard_map/ppermute | solution.py:438
  33.6 10.0 %collective-permute-start.8 = (f32[2,11,8,128]{3,2,1,0:T(8,128)S(1)}, f32[2,11,8,128]{3,2,1,0:T(8,128)S(1)}, u32[]{:S(2)}, u32[]{:S(2)}) collective-permute-start(f32[2,11,8,128]{3,2,1,0:T(8,128)S(1)} %pad_maximum_fusion.1.pair), channel_id=1, source_target_pairs={{0,8},{1,11},{2,10},{3,9},{4,12},{5,15},{6,14},{7,13},{8,0},{9,3},... | collective-permute-start | bytes 270344 | tf_op jit(solution)/shard_map/ppermute | solution.py:438
  36.2 8.1 %collective-permute-start.7 = (f32[2,11,8,128]{3,2,1,0:T(8,128)S(1)}, f32[2,11,8,128]{3,2,1,0:T(8,128)S(1)}, u32[]{:S(2)}, u32[]{:S(2)}) collective-permute-start(f32[2,11,8,128]{3,2,1,0:T(8,128)S(1)} %pad_maximum_fusion.1.pair), channel_id=1, source_target_pairs={{0,14},{1,13},{2,12},{3,15},{4,10},{5,9},{6,8},{7,11},{8,6},{9,5},... | collective-permute-start | bytes 270344 | tf_op jit(solution)/shard_map/ppermute | solution.py:438
  44.4 1.7 %collective-permute-start.11 = (f32[4,2,11,8,128]{4,3,2,1,0:T(8,128)S(1)}, f32[4,2,11,8,128]{4,3,2,1,0:T(8,128)S(1)}, u32[]{:S(2)}, u32[]{:S(2)}) collective-permute-start(f32[4,2,11,8,128]{4,3,2,1,0:T(8,128)S(1)} %pad_maximum_fusion.fetched), channel_id=1, source_target_pairs={{0,1},{1,0},{2,3},{3,2},{4,5},{5,4},{6,7},{7,6},{8,9},{9,8},{10,11... | collective-permute-start | bytes 1081352 | tf_op jit(solution)/shard_map/ppermute | solution.py:419

commit v5 on v4

--- a/solution.py
+++ b/solution.py
@@ -20,10 +20,10 @@
 VECTORS = 2
 SLOPE = 0.25 * TIME_STEP
 SPREAD = TIME_STEP * DIFFUSIVITY
-HEIGHTS = VECTORS * 2
-DEPTHS = HEIGHTS + VECTORS * 2
-GRAMS = DEPTHS + 2
-BLOCKS = GRAMS + 1
+GRAMS = VECTORS * 2
+SUMS = GRAMS + 1
+DEPTHS = VECTORS * 2
+RIM = DEPTHS + 2
 
 
 def next_row(tile):
@@ -123,7 +123,8 @@
 
 
 def first_kernel(
-    levels, sub, edge, tracer, zonal, merid, bottom, cross, mate, raw, mate_raw, flow_in, mate_flow
+    levels, sub, edge, tracer, zonal, merid, surface, bottom,
+    cross, mate, raw, mate_raw, flow_in, mate_flow,
 ):
     del edge
     outer, inner, sign = orientation()
@@ -136,6 +137,10 @@
     along = [side_depths(d) for d in depth]
     cross[VECTORS * levels] = depth[0]
     mate[VECTORS * levels] = depth[1]
+    for c in range(2):
+        for v in range(VECTORS):
+            mate_flow[levels + v * 2 + c] = column(surface, c, v)
+        mate_flow[levels + DEPTHS + c] = column(bottom, c).astype(jnp.float32)
 
     def body(k, carry):
         level = k.astype(jnp.float32)
@@ -177,7 +182,7 @@
 def second_kernel(
     levels, sub, raw, cross, mate, mate_raw, flow_in, mate_flow,
     raw_far, cross_far, mate_far, mate_raw_far, mate_flow_far, flow_other,
-    merid, surface, bottom, tracer, message, flow_far,
+    merid, tracer, late, early, flow_far,
 ):
     outer, inner, sign = orientation()
     start, part = share(levels)
@@ -242,56 +247,69 @@
     packed = zero
     for i, gram in enumerate(sums[4:]):
         packed = jnp.where(subs == i, jnp.sum(gram, axis=0, keepdims=True), packed)
-    message[GRAMS] = packed
+    late[GRAMS] = packed
+    early[GRAMS] = packed
     for v in range(VECTORS):
         for c, where in enumerate((outer, inner)):
-            message[v * 2 + where] = gain * sums[v * 2 + c]
-            message[HEIGHTS + v * 2 + c] = surface[v, pl.ds(c, sub, stride=2), :]
-    for c in range(2):
-        message[DEPTHS + c] = bottom[pl.ds(c, sub, stride=2), :].astype(jnp.float32)
+            late[v * 2 + where] = gain * sums[v * 2 + c]
+            early[v * 2 + where] = gain * sums[v * 2 + c]
+    for row in range(RIM):
+        early[SUMS + row] = mate_flow[levels + row]
+        early[SUMS + RIM + row] = mate_flow_far[levels + row]
 
 
 def total(tile):
     return jnp.sum(jnp.sum(tile, axis=0, keepdims=True), axis=1, keepdims=True)
 
 
-def third_kernel(
-    levels, sub, count, pair, fetched, fetched_mate, tracer, tracer_out, surface_out, growth,
-    pole, residual, answer, image, height, depth, face_x, face_y, face_z, packed,
-):
+def early_of(chip):
+    return 2 * chip + chip % 2
+
+
+def late_of(chip):
+    return 2 * chip + 1 - chip % 2
+
+
+def third_kernel(levels, sub, count, *refs):
+    chips = count // 2
+    lates, (early, beside), around = refs[:chips], refs[chips : chips + 2], refs[chips + 2 : chips + 1 + chips // 2]
+    (own, mates, pole, residual, answer, image, height, depth, face_x, face_y, face_z, packed) = refs[
+        chips + 1 + chips // 2 :
+    ]
     width = 2 * count
-    me = lax.axis_index("lon")
-    core = lax.rem(me, 2)
+    chip = lax.axis_index("lon") // 2
     zero = jnp.zeros((sub, LANES), jnp.float32)
     none = (zero,) * VECTORS
 
-    def place(owner, block):
-        packed[owner] = block(GRAMS)
+    def device(of, mask):
+        where = chip ^ mask
+        odd = lax.rem(where, 2)
+        return 2 * where + (odd if of is early_of else 1 - odd)
+
+    def place_sums(owner, block):
+        packed[owner] = block[GRAMS]
+        for c in range(2):
+            for v in range(VECTORS):
+                residual[v, 2 * owner + c] = block[v * 2 + c]
+
+    def place_rim(owner, block, base):
         for c in range(2):
             x = 2 * owner + c
-            floor = block(DEPTHS + c)
+            floor = block[base + DEPTHS + c]
             depth[x] = floor
             for v in range(VECTORS):
-                tall = jnp.where(floor > 0, block(HEIGHTS + v * 2 + c), 0.0)
+                tall = jnp.where(floor > 0, block[base + v * 2 + c], 0.0)
                 height[v, x] = tall
                 pole[v, x + 1] = tall
-                residual[v, x] = block(v * 2 + c)
-
-    for slot in range(2):
-        place(me ^ slot, lambda row, slot=slot: pair[slot, row])
-    for ref, flip in ((fetched, 0), (fetched_mate, 1)):
-        for j, masks in enumerate(chip_masks(count)):
-            mask = jnp.where((core ^ flip) == 0, *masks)
-            for slot in range(2):
-                owner = me ^ flip ^ slot ^ (2 * mask)
-
-                def put(owner=owner, ref=ref, j=j, slot=slot):
-                    place(owner, lambda row: ref[j, slot, row])
-
-                if all(masks):
-                    put()
-                else:
-                    pl.when(mask > 0)(put)
+
+    for mask, block in enumerate(lates):
+        place_sums(device(late_of, mask), block)
+    pairs = [(early, beside)] + [(ref.at[0], ref.at[1]) for ref in around]
+    for mask, pair in enumerate(pairs):
+        for slot, block in enumerate(pair):
+            place_sums(device(early_of, 2 * mask + slot), block)
+            place_rim(device(early_of, 2 * mask + slot), block, SUMS)
+            place_rim(device(late_of, 2 * mask + slot), block, SUMS + RIM)
 
     def over(body, init):
         return lax.fori_loop(0, count, body, init, unroll=steps(count, 16))
@@ -386,6 +404,34 @@
     scale_two = jnp.sqrt(rest + EPSILON)
     over_one, over_two = 1.0 / scale_one, 1.0 / scale_two
 
+    factors = (over_one, cross, over_two, scale_one, scale_two)
+    subs = lax.broadcasted_iota(jnp.int32, zero.shape, 0)
+    listed = zero
+    for i, factor in enumerate(factors):
+        listed = jnp.where(subs == i, factor, listed)
+    for of, result in ((early_of, own), (late_of, mates)):
+        for v in range(VECTORS):
+            for c in range(2):
+                result[v * 2 + c] = answer[v, 2 * device(of, 0) + c]
+        result[VECTORS * 2] = listed
+
+
+def fourth_kernel(levels, sub, solved, told, tracer, tracer_out, surface_out, growth):
+    me = lax.axis_index("lon")
+    solver = lax.rem((me + 1) // 2, 2) == 0
+
+    def known(row):
+        return jnp.where(solver, solved[row], told[row])
+
+    listed = known(VECTORS * 2)
+    over_one, cross, over_two = (listed[i : i + 1, :1] for i in range(3))
+    for i in range(3):
+        growth[i] = listed[(3, 1, 4)[i], 0]
+    for c in range(2):
+        unit = known(c) * over_one
+        surface_out[0, pl.ds(c, sub, stride=2), :] = unit
+        surface_out[1, pl.ds(c, sub, stride=2), :] = (known(2 + c) - cross * unit) * over_two
+
     def scale(k, carry):
         unit = tracer[0, k] * over_one
         tracer_out[0, k] = unit
@@ -393,13 +439,6 @@
         return carry
 
     lax.fori_loop(0, levels, scale, 0, unroll=steps(levels, 10))
-    for c in range(2):
-        x = 2 * me + c
-        unit = answer[0, x] * over_one
-        surface_out[0, pl.ds(c, sub, stride=2), :] = unit
-        surface_out[1, pl.ds(c, sub, stride=2), :] = (answer[1, x] - cross * unit) * over_two
-    for i, value in enumerate((scale_one, cross, scale_two)):
-        growth[i] = value[0, 0]
 
 
 def tiled(array):
@@ -419,25 +458,32 @@
     return lax.ppermute(array, "lon", [(i, i ^ mask) for i in range(count)])
 
 
-def chip_masks(count):
-    lists, loads = ([], []), [0, 0]
-    for mask in range(count // 2 - 1, 0, -1):
-        core = int(loads[1] < loads[0])
-        lists[core].append(mask)
-        loads[core] += mask % 2 + mask // 2
-    longest = max(map(len, lists))
-    return list(zip(*(one + [0] * (longest - len(one)) for one in lists)))
-
-
-def gather(block):
+def chip_moves(count, source, target, mask):
+    return [(source(chip), target(chip ^ mask)) for chip in range(count // 2)]
+
+
+def gather(late, early):
     count = lax.axis_size("lon")
-    pair = jnp.stack([block, swap(block, 1)])
-    fetched = []
-    for masks in chip_masks(count):
-        moves = [(i, i ^ (2 * masks[i % 2])) for i in range(count) if masks[i % 2]]
-        fetched.append(lax.ppermute(pair, "lon", moves))
-    fetched = jnp.stack(fetched)
-    return pair, fetched, swap(fetched, 1)
+    chips = count // 2
+    lates = [
+        lax.ppermute(late, "lon", chip_moves(count, late_of, early_of, mask)) for mask in range(chips)
+    ]
+
+    def exchange(block):
+        beside = lax.ppermute(block, "lon", chip_moves(count, early_of, early_of, 1))
+        pair = jnp.stack([block, beside])
+        around = [
+            lax.ppermute(pair, "lon", chip_moves(count, early_of, early_of, mask))
+            for mask in range(2, chips, 2)
+        ]
+        return (beside, *around)
+
+    def nothing(block):
+        return (block, *[jnp.stack([block, block])] * (chips // 2 - 1))
+
+    waits = ((lax.axis_index("lon") + 1) // 2) % 2 == 0
+    beside, *around = lax.cond(waits, exchange, nothing, early)
+    return [*lates, early, beside, *around]
 
 
 def on_device(tracer_pert, surface_pert, zonal_flow, merid_flow, bottom_level):
@@ -462,7 +508,6 @@
     tracer_pert, zonal_flow, merid_flow = map(tiled, (tracer_pert, zonal_flow, merid_flow))
     outward = [(i, (i + 1) % count if i % 2 else (i - 1) % count) for i in range(count)]
     part = (levels + 1) // 2
-    bottom = tiled(bottom_level)
     edge_rows = VECTORS * levels + part
 
     edge = pl.pallas_call(
@@ -490,40 +535,39 @@
             shaped(VECTORS * levels),
             shaped(VECTORS * levels),
             shaped(levels),
-            shaped(levels),
+            shaped(levels + RIM),
         ),
-        in_specs=[pl.BlockSpec(memory_space=pl.ANY)] + [vmem] * 4,
+        in_specs=[pl.BlockSpec(memory_space=pl.ANY)] + [vmem] * 5,
         out_specs=(vmem,) * 6,
         compiler_params=params,
         name="partial_step",
-    )(edge, tracer_pert, zonal_flow, merid_flow, bottom)
+    )(edge, tracer_pert, zonal_flow, merid_flow, tiled(surface_pert), tiled(bottom_level))
     cross_far = lax.ppermute(cross, "lon", outward)
     mate_far, mate_raw_far, mate_flow_far = (swap(x, 1) for x in (mate, mate_raw, mate_flow))
-    tracer, message = pl.pallas_call(
+    tracer, late, early = pl.pallas_call(
         functools.partial(second_kernel, levels, sub),
         out_shape=(
             jax.ShapeDtypeStruct((vectors, levels, sub * 2, LANES), f32),
-            shaped(BLOCKS),
+            shaped(SUMS),
+            shaped(SUMS + 2 * RIM),
         ),
-        in_specs=[vmem] * 15,
-        out_specs=(vmem, vmem),
+        in_specs=[vmem] * 13,
+        out_specs=(vmem,) * 3,
         scratch_shapes=[held(levels)],
         compiler_params=params,
         name="both_steps",
     )(
         raw, cross, mate, mate_raw, flow_in, mate_flow,
         edge_far, cross_far, mate_far, mate_raw_far, mate_flow_far, flow_other,
-        merid_flow, tiled(surface_pert), bottom,
+        merid_flow,
     )
-    tracer_vec, surface_vec, growth = pl.pallas_call(
+    blocks = gather(late, early)
+    result = shaped(SUMS)
+    solved, solved_mate = pl.pallas_call(
         functools.partial(third_kernel, levels, sub, count),
-        out_shape=(
-            jax.ShapeDtypeStruct((vectors, levels, sub * 2, LANES), f32),
-            jax.ShapeDtypeStruct((vectors, sub * 2, LANES), f32),
-            jax.ShapeDtypeStruct((3,), f32),
-        ),
-        in_specs=[vmem] * 4,
-        out_specs=(vmem, vmem, pl.BlockSpec(memory_space=pltpu.SMEM)),
+        out_shape=(result, result),
+        in_specs=[vmem] * len(blocks),
+        out_specs=(vmem, vmem),
         scratch_shapes=[
             held(vectors, width + 2),
             *[held(vectors, width)] * 4,
@@ -534,8 +578,21 @@
             held(count),
         ],
         compiler_params=pltpu.CompilerParams(vmem_limit_bytes=32 * 2**20),
-        name="surface_and_scale",
-    )(*gather(message), tracer)
+        name="surface_solve",
+    )(*blocks)
+    told = lax.ppermute(solved_mate, "lon", chip_moves(count, early_of, late_of, 0))
+    tracer_vec, surface_vec, growth = pl.pallas_call(
+        functools.partial(fourth_kernel, levels, sub),
+        out_shape=(
+            jax.ShapeDtypeStruct((vectors, levels, sub * 2, LANES), f32),
+            jax.ShapeDtypeStruct((vectors, sub * 2, LANES), f32),
+            jax.ShapeDtypeStruct((3,), f32),
+        ),
+        in_specs=[vmem] * 3,
+        out_specs=(vmem, vmem, pl.BlockSpec(memory_space=pltpu.SMEM)),
+        compiler_params=params,
+        name="scale",
+    )(solved, told, tracer)
     return (untiled(tracer_vec, 2), untiled(surface_vec, 2), growth)
 
 

time: 49.2 us -> 75 us (1.52)
  starting transfers between devices: 21.3 us -> 31.7 us
  local copies, waits for them, and re-layouts: 1.08 us -> 7.75 us
  waiting for transfers between devices: 18.2 us -> 22.7 us
  Pallas kernels: 7.58 us -> 10.4 us
  other arithmetic: 0.04 us -> 0.89 us
    ppermute x4 -> x13, starting transfers between devices: 6.58 us -> 23.7 us  [the longest x8 10.3 us: gather(): lax.ppermute(late, 'lon', chip_moves(count, late_of, early_of, mask))]
    ppermute x4 -> x13, waiting for transfers between devices: 8.13 us -> 15 us  [the longest x8 7.17 us: gather(): lax.ppermute(late, 'lon', chip_moves(count, late_of, early_of, mask))]
    unnamed x12 -> x28, local copies, waits for them, and re-layouts: 1.07 us -> 7.74 us
    ppermute x5 -> x3, starting transfers between devices: 7.12 us -> 0.51 us  [swap(): return lax.ppermute(array, 'lon', [(i, i ^ mask) for i in range(count)])]
    ppermute x5 -> x3, waiting for transfers between devices: 2.55 us -> 0.01 us  [swap(): return lax.ppermute(array, 'lon', [(i, i ^ mask) for i in range(count)])]
    ppermute x1, waiting for transfers between devices: 3.49 us -> 5.62 us  [on_device(): cross_far = lax.ppermute(cross, 'lon', outward)]
    ppermute x1, waiting for transfers between devices: 4.04 us -> 2.02 us  [on_device(): edge_far = lax.ppermute(edge, 'lon', outward)]
    pallas_call x1, Pallas kernels: 1.5 us -> 2.59 us  [on_device(): pl.pallas_call(functools.partial(second_kernel, levels, sub), out_shape=(...]
  transfers between devices with their start and end apart: 12 -> 19, of which waited for: 6 -> 8; matrix products, arithmetic and copies ran while one was open for 0% -> 1% of each run, Pallas kernels for 2% -> 3%
where the time goes in v5:
time: 75 us; the launch traced here: 74.4 us
  starting transfers between devices  31.7 us (42%)
  waiting for transfers between devices  22.7 us (30%)
  Pallas kernels  10.4 us (14%)
  local copies, waits for them, and re-layouts  7.75 us (10%)
  other arithmetic  0.89 us (1%)
  between operations  0.83 us (1%)
    ppermute x8, starting transfers between devices, gather(): lax.ppermute(late, 'lon', chip_moves(count, late_of, early_of, mask))  10.3 us
    ppermute x3, starting transfers between devices, exchange(): lax.ppermute(pair, 'lon', chip_moves(count, early_of, early_of, mask))  10.1 us
    unnamed x28, local copies, waits for them, and re-layouts  7.74 us
    ppermute x8, waiting for transfers between devices, gather(): lax.ppermute(late, 'lon', chip_moves(count, late_of, early_of, mask))  7.17 us
    ppermute x1, waiting for transfers between devices, on_device(): cross_far = lax.ppermute(cross, 'lon', outward)  5.62 us
    ppermute x1, starting transfers between devices, on_device(): edge_far = lax.ppermute(edge, 'lon', outward)  5.51 us
    ppermute x1, waiting for transfers between devices, exchange(): lax.ppermute(block, 'lon', chip_moves(count, early_of, early_of, 1))  3.81 us
    ppermute x3, waiting for transfers between devices, exchange(): lax.ppermute(pair, 'lon', chip_moves(count, early_of, early_of, mask))  3.22 us
  transfers between devices with their start and end apart: 19, of which 8 were waited for; matrix products, arithmetic and copies ran while one was open for 1% of the time, Pallas kernels for 3%

profile of v5, /device:TPU:0, one launch (start us, length us, event | category | flops | bytes accessed | tf_op | source)
XLA Modules:
  0.0 74.4 jit_solution(8968698097551051170)
XLA Ops:
  0.7 2.0 %edge_columns.1.edge = f32[125,8,128]{2,1,0:T(8,128)} custom-call(f32[2,50,16,128]{3,2,1,0:T(8,128)} %bitcast.38, f32[50,16,128]{2,1,0:T(8,128)} %bitcast.42), custom_call_target="tpu_custom_call" | custom-call | tf_op jit(solution)/shard_map/edge_columns/pallas_call | solution.py:513
  2.7 5.5 %collective-permute-start.4 = (f32[125,8,128]{2,1,0:T(8,128)}, f32[125,8,128]{2,1,0:T(8,128)S(1)}, u32[]{:S(2)}, u32[]{:S(2)}) collective-permute-start(f32[125,8,128]{2,1,0:T(8,128)} %edge_columns.1.edge), channel_id=1, source_target_pairs={{0,15},{1,2},{2,1},{3,4},{4,3},{5,6},{6,5},{7,8},{8,7},{9,10},{10,... | collective-permute-start | bytes 1536008 | tf_op jit(solution)/shard_map/ppermute | solution.py:528
  8.2 0.0 copy-start.1
  8.3 1.0 %copy-done.1 = f32[125,8,128]{2,1,0:T(8,128)S(1)} copy-done((f32[125,8,128]{2,1,0:T(8,128)S(1)}, f32[125,8,128]{2,1,0:T(8,128)}, u32[]{:S(2)}) %copy-start.1) | copy-done | bytes 512024
  9.3 1.9 %partial_step.1 = (f32[101,8,128]{2,1,0:T(8,128)S(1)}, f32[101,8,128]{2,1,0:T(8,128)S(1)}, f32[100,8,128]{2,1,0:T(8,128)S(1)}, f32[100,8,128]{2,1,0:T(8,128)}, f...) custom-call(f32[125,8,128]{2,1,0:T(8,128)S(1)} %copy-done.1, f32[2,50,16,128]{3,2,1,0:T(8,128)S(1)} %bitcast.39, ...), custom_call_target="tpu_custom_call" | custom-call | tf_op jit(solution)/shard_map/partial_step/pallas_call | solution.py:530
  11.2 0.8 %copy-done.6 = f32[100,8,128]{2,1,0:T(8,128)} copy-done((f32[100,8,128]{2,1,0:T(8,128)}, f32[100,8,128]{2,1,0:T(8,128)S(1)}, u32[]{:S(2)}) %copy-start.6) | copy-done | bytes 409624
  12.0 0.7 copy-done.8
  12.7 0.0 collective-permute-start.5
  12.7 0.0 collective-permute-start.6
  12.7 0.5 collective-permute-start.7
  13.2 2.0 %collective-permute-done.4.raw_far = f32[125,8,128]{2,1,0:T(8,128)S(1)} collective-permute-done((f32[125,8,128]{2,1,0:T(8,128)}, f32[125,8,128]{2,1,0:T(8,128)S(1)}, u32[]{:S(2)}, u32[]{:S(2)}) %collective-permute-start.4) | collective-permute-done | bytes 512032 | tf_op jit(solution)/shard_map/ppermute | solution.py:528
  15.3 2.0 %collective-permute-start.9 = (f32[25,8,128]{2,1,0:T(8,128)S(1)}, f32[25,8,128]{2,1,0:T(8,128)S(1)}, u32[]{:S(2)}, u32[]{:S(2)}) collective-permute-start(f32[25,8,128]{2,1,0:T(8,128)S(1)} %slice.4), channel_id=1, source_target_pairs={{0,16},{16,0},{1,17},{17,1},{2,18},{18,2},{3,19},{19,3},{4,20},{20... | collective-permute-start | bytes 307208 | tf_op jit(solution)/shard_map/ppermute | solution.py:529
  17.3 5.6 %collective-permute-done.5.cross_far = f32[101,8,128]{2,1,0:T(8,128)S(1)} collective-permute-done((f32[101,8,128]{2,1,0:T(8,128)S(1)}, f32[101,8,128]{2,1,0:T(8,128)S(1)}, u32[]{:S(2)}, u32[]{:S(2)}) %collective-permute-start.5) | collective-permute-done | bytes 413728 | tf_op jit(solution)/shard_map/ppermute | solution.py:545
  22.9 0.0 collective-permute-done.6.mate_far
  22.9 0.8 %copy-done.4 = f32[101,8,128]{2,1,0:T(8,128)} copy-done((f32[101,8,128]{2,1,0:T(8,128)}, f32[101,8,128]{2,1,0:T(8,128)S(1)}, u32[]{:S(2)}) %copy-start.4) | copy-done | bytes 413720
  23.7 0.7 copy-done.10
  24.3 1.0 %copy-done.5 = f32[101,8,128]{2,1,0:T(8,128)S(1)} copy-done((f32[101,8,128]{2,1,0:T(8,128)S(1)}, f32[101,8,128]{2,1,0:T(8,128)}, u32[]{:S(2)}) %copy-start.5) | copy-done | bytes 413720
  25.3 1.0 %copy-done.7 = f32[100,8,128]{2,1,0:T(8,128)S(1)} copy-done((f32[100,8,128]{2,1,0:T(8,128)S(1)}, f32[100,8,128]{2,1,0:T(8,128)}, u32[]{:S(2)}) %copy-start.7) | copy-done | bytes 409624
  26.3 0.9 %copy-done.9 = f32[50,8,128]{2,1,0:T(8,128)S(1)} copy-done((f32[50,8,128]{2,1,0:T(8,128)S(1)}, f32[50,8,128]{2,1,0:T(8,128)}, u32[]{:S(2)}) %copy-start.9) | copy-done | bytes 204824
  27.3 0.9 %copy-done.11 = f32[25,8,128]{2,1,0:T(8,128)S(1)} copy-done((f32[25,8,128]{2,1,0:T(8,128)S(1)}, f32[25,8,128]{2,1,0:T(8,128)}, u32[]{:S(2)}) %copy-start.11) | copy-done | bytes 102424
  28.2 2.6 %both_steps.1 = (f32[2,50,16,128]{3,2,1,0:T(8,128)S(1)}, f32[5,8,128]{2,1,0:T(8,128)S(1)}, f32[17,8,128]{2,1,0:T(8,128)S(1)}) custom-call(f32[100,8,128]{2,1,0:T(8,128)S(1)} %copy-done.7, f32[101,8,128]{2,1,0:T(8,128)S(1)} %get-tuple-element.24.cross, f32[101,8,128]{2,1,0:T(8,128)S(1)} %get-tuple-element.25.mate, f32[100,8,128]{2,1,0:T(8,128)} %get-tuple-element.26.mate_raw, ...), custom_call_target="tpu_custom_call" | custom-call | tf_op jit(solution)/shard_map/both_steps/pallas_call | solution.py:547
  30.8 1.3 %collective-permute-start.10 = (f32[5,8,128]{2,1,0:T(8,128)S(1)}, f32[5,8,128]{2,1,0:T(8,128)S(1)}, u32[]{:S(2)}, u32[]{:S(2)}) collective-permute-start(f32[5,8,128]{2,1,0:T(8,128)S(1)} %get-tuple-element.29), channel_id=1, source_target_pairs={{1,0},{2,3},{5,4},{6,7},{9,8},{10,11},{13,12},{14,15},{17,16},{18,... | collective-permute-start | bytes 61448 | tf_op jit(solution)/shard_map/ppermute | solution.py:469
  32.1 1.3 %collective-permute-start.11 = (f32[5,8,128]{2,1,0:T(8,128)S(1)}, f32[5,8,128]{2,1,0:T(8,128)S(1)}, u32[]{:S(2)}, u32[]{:S(2)}) collective-permute-start(f32[5,8,128]{2,1,0:T(8,128)S(1)} %get-tuple-element.29), channel_id=1, source_target_pairs={{1,3},{2,0},{5,7},{6,4},{9,11},{10,8},{13,15},{14,12},{17,19},{18,... | collective-permute-start | bytes 61448 | tf_op jit(solution)/shard_map/ppermute | solution.py:469
  33.4 20.0 %conditional.1 = (f32[17,8,128]{2,1,0:T(8,128)}, f32[2,17,8,128]{3,2,1,0:T(8,128)}, f32[2,17,8,128]{3,2,1,0:T(8,128)}, f32[2,17,8,128]{3,2,1,0:T(8,128)}) conditional(s32[]{:T(128)} %convert_element_type.3, f32[17,8,128]{2,1,0:T(8,128)S(1)} %get-tuple-element.30.refs_8_, f32[17,8,128]{2,1,0:T(8,128)S(1)} %get-tuple-element.30.refs_8_), branch_computations={%region_0.1_spmd, %region_1.2_spmd} | conditional | flops 34816 | bytes 2228416 | solution.py:485
  33.4 1.9 %collective-permute-start = (f32[17,8,128]{2,1,0:T(8,128)S(1)}, f32[17,8,128]{2,1,0:T(8,128)}, u32[]{:S(2)}, u32[]{:S(2)}) collective-permute-start(f32[17,8,128]{2,1,0:T(8,128)S(1)} %param.1), channel_id=1, source_target_pairs={{0,3},{3,0},{4,7},{7,4},{8,11},{11,8},{12,15},{15,12},{16,19},{19,... | collective-permute-start | bytes 208904 | tf_op jit(solution)/shard_map/cond/branch_1_fun/ppermute | solution.py:473
  35.3 3.8 %collective-permute-done = f32[17,8,128]{2,1,0:T(8,128)} collective-permute-done((f32[17,8,128]{2,1,0:T(8,128)S(1)}, f32[17,8,128]{2,1,0:T(8,128)}, u32[]{:S(2)}, u32[]{:S(2)}) %collective-permute-start) | collective-permute-done | bytes 69664 | tf_op jit(solution)/shard_map/cond/branch_1_fun/ppermute | solution.py:473
  39.1 0.9 %pad_maximum_fusion.1 = f32[2,17,8,128]{3,2,1,0:T(8,128)S(1)} fusion(f32[1,17,8,128]{3,2,1,0:T(8,128)} %bitcast.2, f32[1,17,8,128]{3,2,1,0:T(8,128)S(1)} %bitcast.47), kind=kLoop, calls=%fused_computation.1 | loop fusion | flops 34816 | bytes 278528 | tf_op jit(solution)/shard_map/cond/branch_1_fun/stack | solution.py:474
  40.0 1.9 %collective-permute-start.1 = (f32[2,17,8,128]{3,2,1,0:T(8,128)S(1)}, f32[2,17,8,128]{3,2,1,0:T(8,128)}, u32[]{:S(2)}, u32[]{:S(2)}) collective-permute-start(f32[2,17,8,128]{3,2,1,0:T(8,128)S(1)} %pad_maximum_fusion.1), channel_id=1, source_target_pairs={{0,4},{3,7},{4,0},{7,3},{8,12},{11,15},{12,8},{15,11},{16,20},{19,... | collective-permute-start | bytes 417800 | tf_op jit(solution)/shard_map/cond/branch_1_fun/ppermute | solution.py:476
  41.9 2.5 %collective-permute-start.2 = (f32[2,17,8,128]{3,2,1,0:T(8,128)S(1)}, f32[2,17,8,128]{3,2,1,0:T(8,128)}, u32[]{:S(2)}, u32[]{:S(2)}) collective-permute-start(f32[2,17,8,128]{3,2,1,0:T(8,128)S(1)} %pad_maximum_fusion.1), channel_id=1, source_target_pairs={{0,8},{3,11},{4,12},{7,15},{8,0},{11,3},{12,4},{15,7},{16,24},{19,... | collective-permute-start | bytes 417800 | tf_op jit(solution)/shard_map/cond/branch_1_fun/ppermute | solution.py:476
  44.5 5.7 %collective-permute-start.3 = (f32[2,17,8,128]{3,2,1,0:T(8,128)S(1)}, f32[2,17,8,128]{3,2,1,0:T(8,128)}, u32[]{:S(2)}, u32[]{:S(2)}) collective-permute-start(f32[2,17,8,128]{3,2,1,0:T(8,128)S(1)} %pad_maximum_fusion.1), channel_id=1, source_target_pairs={{0,12},{3,15},{4,8},{7,11},{8,4},{11,7},{12,0},{15,3},{16,28},{19,... | collective-permute-start | bytes 417800 | tf_op jit(solution)/shard_map/cond/branch_1_fun/ppermute | solution.py:476
  50.1 0.0 collective-permute-done.1
  50.2 0.0 collective-permute-done.2
  50.2 3.2 %collective-permute-done.3 = f32[2,17,8,128]{3,2,1,0:T(8,128)} collective-permute-done((f32[2,17,8,128]{3,2,1,0:T(8,128)S(1)}, f32[2,17,8,128]{3,2,1,0:T(8,128)}, u32[]{:S(2)}, u32[]{:S(2)}) %collective-permute-start.3) | collective-permute-done | bytes 139296 | tf_op jit(solution)/shard_map/cond/branch_1_fun/ppermute | solution.py:476
  53.4 1.3 %collective-permute-start.12 = (f32[5,8,128]{2,1,0:T(8,128)S(1)}, f32[5,8,128]{2,1,0:T(8,128)S(1)}, u32[]{:S(2)}, u32[]{:S(2)}) collective-permute-start(f32[5,8,128]{2,1,0:T(8,128)S(1)} %get-tuple-element.29), channel_id=1, source_target_pairs={{1,4},{2,7},{5,0},{6,3},{9,12},{10,15},{13,8},{14,11},{17,20},{18,... | collective-permute-start | bytes 61448 | tf_op jit(solution)/shard_map/ppermute | solution.py:469
  54.7 1.3 %collective-permute-start.13 = (f32[5,8,128]{2,1,0:T(8,128)S(1)}, f32[5,8,128]{2,1,0:T(8,128)S(1)}, u32[]{:S(2)}, u32[]{:S(2)}) collective-permute-start(f32[5,8,128]{2,1,0:T(8,128)S(1)} %get-tuple-element.29), channel_id=1, source_target_pairs={{1,7},{2,4},{5,3},{6,0},{9,15},{10,12},{13,11},{14,8},{17,23},{18,... | collective-permute-start | bytes 61448 | tf_op jit(solution)/shard_map/ppermute | solution.py:469
  56.0 1.3 %collective-permute-start.14 = (f32[5,8,128]{2,1,0:T(8,128)S(1)}, f32[5,8,128]{2,1,0:T(8,128)S(1)}, u32[]{:S(2)}, u32[]{:S(2)}) collective-permute-start(f32[5,8,128]{2,1,0:T(8,128)S(1)} %get-tuple-element.29), channel_id=1, source_target_pairs={{1,8},{2,11},{5,12},{6,15},{9,0},{10,3},{13,4},{14,7},{17,24},{18,... | collective-permute-start | bytes 61448 | tf_op jit(solution)/shard_map/ppermute | solution.py:469
  57.3 0.0 collective-permute-done.10.refs_0_
  57.3 1.3 %collective-permute-start.15 = (f32[5,8,128]{2,1,0:T(8,128)S(1)}, f32[5,8,128]{2,1,0:T(8,128)S(1)}, u32[]{:S(2)}, u32[]{:S(2)}) collective-permute-start(f32[5,8,128]{2,1,0:T(8,128)S(1)} %get-tuple-element.29), channel_id=1, source_target_pairs={{1,11},{2,8},{5,15},{6,12},{9,3},{10,0},{13,7},{14,4},{17,27},{18,... | collective-permute-start | bytes 61448 | tf_op jit(solution)/shard_map/ppermute | solution.py:469
  58.6 1.3 %collective-permute-start.16 = (f32[5,8,128]{2,1,0:T(8,128)S(1)}, f32[5,8,128]{2,1,0:T(8,128)S(1)}, u32[]{:S(2)}, u32[]{:S(2)}) collective-permute-start(f32[5,8,128]{2,1,0:T(8,128)S(1)} %get-tuple-element.29), channel_id=1, source_target_pairs={{1,12},{2,15},{5,8},{6,11},{9,4},{10,7},{13,0},{14,3},{17,28},{18,... | collective-permute-start | bytes 61448 | tf_op jit(solution)/shard_map/ppermute | solution.py:469
  59.9 1.3 %collective-permute-start.17 = (f32[5,8,128]{2,1,0:T(8,128)S(1)}, f32[5,8,128]{2,1,0:T(8,128)S(1)}, u32[]{:S(2)}, u32[]{:S(2)}) collective-permute-start(f32[5,8,128]{2,1,0:T(8,128)S(1)} %get-tuple-element.29), channel_id=1, source_target_pairs={{1,15},{2,12},{5,11},{6,8},{9,7},{10,4},{13,3},{14,0},{17,31},{18,... | collective-permute-start | bytes 61448 | tf_op jit(solution)/shard_map/ppermute | solution.py:469
  61.2 0.0 collective-permute-done.13.refs_3_
  61.2 2.1 %collective-permute-done.14.refs_4_ = f32[5,8,128]{2,1,0:T(8,128)S(1)} collective-permute-done((f32[5,8,128]{2,1,0:T(8,128)S(1)}, f32[5,8,128]{2,1,0:T(8,128)S(1)}, u32[]{:S(2)}, u32[]{:S(2)}) %collective-permute-start.14) | collective-permute-done | bytes 20512 | tf_op jit(solution)/shard_map/ppermute | solution.py:469
  63.3 2.8 %collective-permute-done.15.refs_5_ = f32[5,8,128]{2,1,0:T(8,128)S(1)} collective-permute-done((f32[5,8,128]{2,1,0:T(8,128)S(1)}, f32[5,8,128]{2,1,0:T(8,128)S(1)}, u32[]{:S(2)}, u32[]{:S(2)}) %collective-permute-start.15) | collective-permute-done | bytes 20512 | tf_op jit(solution)/shard_map/ppermute | solution.py:469
  66.1 2.3 %collective-permute-done.17.refs_7_ = f32[5,8,128]{2,1,0:T(8,128)S(1)} collective-permute-done((f32[5,8,128]{2,1,0:T(8,128)S(1)}, f32[5,8,128]{2,1,0:T(8,128)S(1)}, u32[]{:S(2)}, u32[]{:S(2)}) %collective-permute-start.17) | collective-permute-done | bytes 20512 | tf_op jit(solution)/shard_map/ppermute | solution.py:469
  68.4 2.8 %surface_solve.1 = (f32[5,8,128]{2,1,0:T(8,128)S(1)}, f32[5,8,128]{2,1,0:T(8,128)S(1)}) custom-call(f32[5,8,128]{2,1,0:T(8,128)S(1)} %collective-permute-done.10.refs_0_, f32[5,8,128]{2,1,0:T(8,128)S(1)} %collective-permute-done.11.refs_1_, f32[5,8,128]{2,1,0:T(8,128)S(1)} %collective-permute-done.12.refs_2_, ...), custom_call_target="tpu_custom_call" | custom-call | tf_op jit(solution)/shard_map/surface_solve/pallas_call | solution.py:566
  71.2 1.3 %collective-permute-start.18 = (f32[5,8,128]{2,1,0:T(8,128)S(1)}, f32[5,8,128]{2,1,0:T(8,128)S(1)}, u32[]{:S(2)}, u32[]{:S(2)}) collective-permute-start(f32[5,8,128]{2,1,0:T(8,128)S(1)} %get-tuple-element.36), channel_id=1, source_target_pairs={{0,1},{3,2},{4,5},{7,6},{8,9},{11,10},{12,13},{15,14},{16,17},{19,... | collective-permute-start | bytes 61448 | tf_op jit(solution)/shard_map/ppermute | solution.py:583
  72.5 0.8 %collective-permute-done.18.told = f32[5,8,128]{2,1,0:T(8,128)S(1)} collective-permute-done((f32[5,8,128]{2,1,0:T(8,128)S(1)}, f32[5,8,128]{2,1,0:T(8,128)S(1)}, u32[]{:S(2)}, u32[]{:S(2)}) %collective-permute-start.18) | collective-permute-done | bytes 20512 | tf_op jit(solution)/shard_map/ppermute | solution.py:583
  73.3 1.0 %scale.1 = (f32[2,50,16,128]{3,2,1,0:T(8,128)}, f32[2,16,128]{2,1,0:T(8,128)}, f32[3]{0:T(128)}) custom-call(f32[5,8,128]{2,1,0:T(8,128)S(1)} %get-tuple-element.35.solved, f32[5,8,128]{2,1,0:T(8,128)S(1)} %collective-permute-done.18.told, f32[2,50,16,128]{3,2,1,0:T(8,128)S(1)} %get-tuple-element.37.tracer), custom_call_target="tpu_custom_call" | custom-call | tf_op jit(solution)/shard_map/scale/pallas_call | solution.py:584
  (26 shorter events, 0.1 us)
Async XLA Ops:
  0.6 7.6 %copy-start = (f32[2,50,2,1024]{3,2,1,0:T(2,128)S(1)}, f32[2,50,2,1024]{3,2,1,0:T(2,128)}, u32[]{:S(2)}) copy-start(f32[2,50,2,1024]{3,2,1,0:T(2,128)} %param.7) | copy-start | bytes 2457604
  0.6 7.6 %copy-start.2 = (f32[50,2,1024]{2,1,0:T(2,128)S(1)}, f32[50,2,1024]{2,1,0:T(2,128)}, u32[]{:S(2)}) copy-start(f32[50,2,1024]{2,1,0:T(2,128)} %param.10) | copy-start | bytes 1228804
  0.7 7.6 %copy-start.3 = (f32[50,2,1024]{2,1,0:T(2,128)S(1)}, f32[50,2,1024]{2,1,0:T(2,128)}, u32[]{:S(2)}) copy-start(f32[50,2,1024]{2,1,0:T(2,128)} %param.9) | copy-start | bytes 1228804
  0.7 7.6 %copy-start.12 = (f32[2,2,1024]{2,1,0:T(2,128)S(1)}, f32[2,2,1024]{2,1,0:T(2,128)}, u32[]{:S(2)}) copy-start(f32[2,2,1024]{2,1,0:T(2,128)} %param.8) | copy-start | bytes 49156
  0.7 7.6 %copy-start.13 = (s32[2,1024]{1,0:T(2,128)S(1)}, s32[2,1024]{1,0:T(2,128)}, u32[]{:S(2)}) copy-start(s32[2,1024]{1,0:T(2,128)} %param.11) | copy-start | bytes 24580
  2.7 12.6 %collective-permute-start.4 = (f32[125,8,128]{2,1,0:T(8,128)}, f32[125,8,128]{2,1,0:T(8,128)S(1)}, u32[]{:S(2)}, u32[]{:S(2)}) collective-permute-start(f32[125,8,128]{2,1,0:T(8,128)} %edge_columns.1.edge), channel_id=1, source_target_pairs={{0,15},{1,2},{2,1},{3,4},{4,3},{5,6},{6,5},{7,8},{8,7},{9,10},{10,... | collective-permute-start | bytes 1536008 | tf_op jit(solution)/shard_map/ppermute | solution.py:528
  8.2 1.0 %copy-start.1 = (f32[125,8,128]{2,1,0:T(8,128)S(1)}, f32[125,8,128]{2,1,0:T(8,128)}, u32[]{:S(2)}) copy-start(f32[125,8,128]{2,1,0:T(8,128)} %edge_columns.1.edge) | copy-start | bytes 1536004
  11.2 0.8 %copy-start.6 = (f32[100,8,128]{2,1,0:T(8,128)}, f32[100,8,128]{2,1,0:T(8,128)S(1)}, u32[]{:S(2)}) copy-start(f32[100,8,128]{2,1,0:T(8,128)S(1)} %get-tuple-element.23.raw) | copy-start | bytes 1228804
  12.0 0.7 copy-start.8
  12.7 10.2 %collective-permute-start.5 = (f32[101,8,128]{2,1,0:T(8,128)S(1)}, f32[101,8,128]{2,1,0:T(8,128)S(1)}, u32[]{:S(2)}, u32[]{:S(2)}) collective-permute-start(f32[101,8,128]{2,1,0:T(8,128)S(1)} %get-tuple-element.24.cross), channel_id=1, source_target_pairs={{0,15},{1,2},{2,1},{3,4},{4,3},{5,6},{6,5},{7,8},{8,7},{9,10},{10,... | collective-permute-start | bytes 1241096 | tf_op jit(solution)/shard_map/ppermute | solution.py:545
  12.7 10.2 %collective-permute-start.6 = (f32[101,8,128]{2,1,0:T(8,128)S(1)}, f32[101,8,128]{2,1,0:T(8,128)S(1)}, u32[]{:S(2)}, u32[]{:S(2)}) collective-permute-start(f32[101,8,128]{2,1,0:T(8,128)S(1)} %get-tuple-element.25.mate), channel_id=1, source_target_pairs={{0,1},{1,0},{2,3},{3,2},{4,5},{5,4},{6,7},{7,6},{8,9},{9,8},{10,11... | collective-permute-start | bytes 1241096 | tf_op jit(solution)/shard_map/ppermute | solution.py:458
  12.7 4.6 %collective-permute-start.7 = (f32[100,8,128]{2,1,0:T(8,128)}, f32[100,8,128]{2,1,0:T(8,128)}, u32[]{:S(2)}, u32[]{:S(2)}) collective-permute-start(f32[100,8,128]{2,1,0:T(8,128)} %get-tuple-element.26.mate_raw), channel_id=1, source_target_pairs={{0,1},{1,0},{2,3},{3,2},{4,5},{5,4},{6,7},{7,6},{8,9},{9,8},{10,11... | collective-permute-start | bytes 1228808 | tf_op jit(solution)/shard_map/ppermute | solution.py:458
  13.2 4.0 %collective-permute-start.8 = (f32[56,8,128]{2,1,0:T(8,128)S(1)}, f32[56,8,128]{2,1,0:T(8,128)S(1)}, u32[]{:S(2)}, u32[]{:S(2)}) collective-permute-start(f32[56,8,128]{2,1,0:T(8,128)S(1)} %get-tuple-element.28.mate_flow), channel_id=1, source_target_pairs={{0,1},{1,0},{2,3},{3,2},{4,5},{5,4},{6,7},{7,6},{8,9},{9,8},{10,11... | collective-permute-start | bytes 688136 | tf_op jit(solution)/shard_map/ppermute | solution.py:458
  15.3 8.4 %collective-permute-start.9 = (f32[25,8,128]{2,1,0:T(8,128)S(1)}, f32[25,8,128]{2,1,0:T(8,128)S(1)}, u32[]{:S(2)}, u32[]{:S(2)}) collective-permute-start(f32[25,8,128]{2,1,0:T(8,128)S(1)} %slice.4), channel_id=1, source_target_pairs={{0,16},{16,0},{1,17},{17,1},{2,18},{18,2},{3,19},{19,3},{4,20},{20... | collective-permute-start | bytes 307208 | tf_op jit(solution)/shard_map/ppermute | solution.py:529
  22.9 0.8 %copy-start.4 = (f32[101,8,128]{2,1,0:T(8,128)}, f32[101,8,128]{2,1,0:T(8,128)S(1)}, u32[]{:S(2)}) copy-start(f32[101,8,128]{2,1,0:T(8,128)S(1)} %collective-permute-done.6.mate_far) | copy-start | bytes 1241092
  23.7 0.7 copy-start.10
  24.3 1.0 %copy-start.5 = (f32[101,8,128]{2,1,0:T(8,128)S(1)}, f32[101,8,128]{2,1,0:T(8,128)}, u32[]{:S(2)}) copy-start(f32[101,8,128]{2,1,0:T(8,128)} %copy-done.4) | copy-start | bytes 1241092
  25.3 1.0 %copy-start.7 = (f32[100,8,128]{2,1,0:T(8,128)S(1)}, f32[100,8,128]{2,1,0:T(8,128)}, u32[]{:S(2)}) copy-start(f32[100,8,128]{2,1,0:T(8,128)} %copy-done.6) | copy-start | bytes 1228804
  26.3 0.9 %copy-start.9 = (f32[50,8,128]{2,1,0:T(8,128)S(1)}, f32[50,8,128]{2,1,0:T(8,128)}, u32[]{:S(2)}) copy-start(f32[50,8,128]{2,1,0:T(8,128)} %copy-done.8) | copy-start | bytes 614404
  27.3 0.9 %copy-start.11 = (f32[25,8,128]{2,1,0:T(8,128)S(1)}, f32[25,8,128]{2,1,0:T(8,128)}, u32[]{:S(2)}) copy-start(f32[25,8,128]{2,1,0:T(8,128)} %copy-done.10) | copy-start | bytes 307204
  30.8 26.5 %collective-permute-start.10 = (f32[5,8,128]{2,1,0:T(8,128)S(1)}, f32[5,8,128]{2,1,0:T(8,128)S(1)}, u32[]{:S(2)}, u32[]{:S(2)}) collective-permute-start(f32[5,8,128]{2,1,0:T(8,128)S(1)} %get-tuple-element.29), channel_id=1, source_target_pairs={{1,0},{2,3},{5,4},{6,7},{9,8},{10,11},{13,12},{14,15},{17,16},{18,... | collective-permute-start | bytes 61448 | tf_op jit(solution)/shard_map/ppermute | solution.py:469
  32.1 26.5 %collective-permute-start.11 = (f32[5,8,128]{2,1,0:T(8,128)S(1)}, f32[5,8,128]{2,1,0:T(8,128)S(1)}, u32[]{:S(2)}, u32[]{:S(2)}) collective-permute-start(f32[5,8,128]{2,1,0:T(8,128)S(1)} %get-tuple-element.29), channel_id=1, source_target_pairs={{1,3},{2,0},{5,7},{6,4},{9,11},{10,8},{13,15},{14,12},{17,19},{18,... | collective-permute-start | bytes 61448 | tf_op jit(solution)/shard_map/ppermute | solution.py:469
  33.4 5.7 %collective-permute-start = (f32[17,8,128]{2,1,0:T(8,128)S(1)}, f32[17,8,128]{2,1,0:T(8,128)}, u32[]{:S(2)}, u32[]{:S(2)}) collective-permute-start(f32[17,8,128]{2,1,0:T(8,128)S(1)} %param.1), channel_id=1, source_target_pairs={{0,3},{3,0},{4,7},{7,4},{8,11},{11,8},{12,15},{15,12},{16,19},{19,... | collective-permute-start | bytes 208904 | tf_op jit(solution)/shard_map/cond/branch_1_fun/ppermute | solution.py:473
  40.0 10.1 %collective-permute-start.1 = (f32[2,17,8,128]{3,2,1,0:T(8,128)S(1)}, f32[2,17,8,128]{3,2,1,0:T(8,128)}, u32[]{:S(2)}, u32[]{:S(2)}) collective-permute-start(f32[2,17,8,128]{3,2,1,0:T(8,128)S(1)} %pad_maximum_fusion.1), channel_id=1, source_target_pairs={{0,4},{3,7},{4,0},{7,3},{8,12},{11,15},{12,8},{15,11},{16,20},{19,... | collective-permute-start | bytes 417800 | tf_op jit(solution)/shard_map/cond/branch_1_fun/ppermute | solution.py:476
  41.9 8.2 %collective-permute-start.2 = (f32[2,17,8,128]{3,2,1,0:T(8,128)S(1)}, f32[2,17,8,128]{3,2,1,0:T(8,128)}, u32[]{:S(2)}, u32[]{:S(2)}) collective-permute-start(f32[2,17,8,128]{3,2,1,0:T(8,128)S(1)} %pad_maximum_fusion.1), channel_id=1, source_target_pairs={{0,8},{3,11},{4,12},{7,15},{8,0},{11,3},{12,4},{15,7},{16,24},{19,... | collective-permute-start | bytes 417800 | tf_op jit(solution)/shard_map/cond/branch_1_fun/ppermute | solution.py:476
  44.5 8.9 %collective-permute-start.3 = (f32[2,17,8,128]{3,2,1,0:T(8,128)S(1)}, f32[2,17,8,128]{3,2,1,0:T(8,128)}, u32[]{:S(2)}, u32[]{:S(2)}) collective-permute-start(f32[2,17,8,128]{3,2,1,0:T(8,128)S(1)} %pad_maximum_fusion.1), channel_id=1, source_target_pairs={{0,12},{3,15},{4,8},{7,11},{8,4},{11,7},{12,0},{15,3},{16,28},{19,... | collective-permute-start | bytes 417800 | tf_op jit(solution)/shard_map/cond/branch_1_fun/ppermute | solution.py:476
  53.4 6.5 %collective-permute-start.12 = (f32[5,8,128]{2,1,0:T(8,128)S(1)}, f32[5,8,128]{2,1,0:T(8,128)S(1)}, u32[]{:S(2)}, u32[]{:S(2)}) collective-permute-start(f32[5,8,128]{2,1,0:T(8,128)S(1)} %get-tuple-element.29), channel_id=1, source_target_pairs={{1,4},{2,7},{5,0},{6,3},{9,12},{10,15},{13,8},{14,11},{17,20},{18,... | collective-permute-start | bytes 61448 | tf_op jit(solution)/shard_map/ppermute | solution.py:469
  54.7 6.6 %collective-permute-start.13 = (f32[5,8,128]{2,1,0:T(8,128)S(1)}, f32[5,8,128]{2,1,0:T(8,128)S(1)}, u32[]{:S(2)}, u32[]{:S(2)}) collective-permute-start(f32[5,8,128]{2,1,0:T(8,128)S(1)} %get-tuple-element.29), channel_id=1, source_target_pairs={{1,7},{2,4},{5,3},{6,0},{9,15},{10,12},{13,11},{14,8},{17,23},{18,... | collective-permute-start | bytes 61448 | tf_op jit(solution)/shard_map/ppermute | solution.py:469
  56.0 7.3 %collective-permute-start.14 = (f32[5,8,128]{2,1,0:T(8,128)S(1)}, f32[5,8,128]{2,1,0:T(8,128)S(1)}, u32[]{:S(2)}, u32[]{:S(2)}) collective-permute-start(f32[5,8,128]{2,1,0:T(8,128)S(1)} %get-tuple-element.29), channel_id=1, source_target_pairs={{1,8},{2,11},{5,12},{6,15},{9,0},{10,3},{13,4},{14,7},{17,24},{18,... | collective-permute-start | bytes 61448 | tf_op jit(solution)/shard_map/ppermute | solution.py:469
  57.3 8.8 %collective-permute-start.15 = (f32[5,8,128]{2,1,0:T(8,128)S(1)}, f32[5,8,128]{2,1,0:T(8,128)S(1)}, u32[]{:S(2)}, u32[]{:S(2)}) collective-permute-start(f32[5,8,128]{2,1,0:T(8,128)S(1)} %get-tuple-element.29), channel_id=1, source_target_pairs={{1,11},{2,8},{5,15},{6,12},{9,3},{10,0},{13,7},{14,4},{17,27},{18,... | collective-permute-start | bytes 61448 | tf_op jit(solution)/shard_map/ppermute | solution.py:469
  58.6 7.5 %collective-permute-start.16 = (f32[5,8,128]{2,1,0:T(8,128)S(1)}, f32[5,8,128]{2,1,0:T(8,128)S(1)}, u32[]{:S(2)}, u32[]{:S(2)}) collective-permute-start(f32[5,8,128]{2,1,0:T(8,128)S(1)} %get-tuple-element.29), channel_id=1, source_target_pairs={{1,12},{2,15},{5,8},{6,11},{9,4},{10,7},{13,0},{14,3},{17,28},{18,... | collective-permute-start | bytes 61448 | tf_op jit(solution)/shard_map/ppermute | solution.py:469
  59.9 8.5 %collective-permute-start.17 = (f32[5,8,128]{2,1,0:T(8,128)S(1)}, f32[5,8,128]{2,1,0:T(8,128)S(1)}, u32[]{:S(2)}, u32[]{:S(2)}) collective-permute-start(f32[5,8,128]{2,1,0:T(8,128)S(1)} %get-tuple-element.29), channel_id=1, source_target_pairs={{1,15},{2,12},{5,11},{6,8},{9,7},{10,4},{13,3},{14,0},{17,31},{18,... | collective-permute-start | bytes 61448 | tf_op jit(solution)/shard_map/ppermute | solution.py:469
  71.2 2.1 %collective-permute-start.18 = (f32[5,8,128]{2,1,0:T(8,128)S(1)}, f32[5,8,128]{2,1,0:T(8,128)S(1)}, u32[]{:S(2)}, u32[]{:S(2)}) collective-permute-start(f32[5,8,128]{2,1,0:T(8,128)S(1)} %get-tuple-element.36), channel_id=1, source_target_pairs={{0,1},{3,2},{4,5},{7,6},{8,9},{11,10},{12,13},{15,14},{16,17},{19,... | collective-permute-start | bytes 61448 | tf_op jit(solution)/shard_map/ppermute | solution.py:583

commit v6 on v4

--- a/solution.py
+++ b/solution.py
@@ -426,7 +426,7 @@
         lists[core].append(mask)
         loads[core] += mask % 2 + mask // 2
     longest = max(map(len, lists))
-    return list(zip(*(one + [0] * (longest - len(one)) for one in lists)))
+    return list(zip(*([0] * (longest - len(one)) + one[::-1] for one in lists)))
 
 
 def gather(block):

time: 49.2 us -> 46.7 us (0.949)
  waiting for transfers between devices: 18.2 us -> 15.2 us
  starting transfers between devices: 21.3 us -> 21.9 us
    ppermute x4, waiting for transfers between devices: 8.13 us -> 5.47 us  [gather(): fetched.append(lax.ppermute(pair, 'lon', moves))]
    ppermute x5, starting transfers between devices: 7.12 us -> 7.65 us  [swap(): return lax.ppermute(array, 'lon', [(i, i ^ mask) for i in range(count)])]
  transfers between devices with their start and end apart: 12 -> 12, of which waited for: 6 -> 6; matrix products, arithmetic and copies ran while one was open for 0% -> 0% of each run, Pallas kernels for 2% -> 3%
where the time goes in v6:
time: 46.7 us; the launch traced here: 46.5 us
  starting transfers between devices  21.9 us (47%)
  waiting for transfers between devices  15.2 us (33%)
  Pallas kernels  7.55 us (16%)
  local copies, waits for them, and re-layouts  1.08 us (2%)
  between operations  0.74 us (2%)
    ppermute x5, starting transfers between devices, swap(): return lax.ppermute(array, 'lon', [(i, i ^ mask) for i in range(count)])  7.65 us
    ppermute x4, starting transfers between devices, gather(): fetched.append(lax.ppermute(pair, 'lon', moves))  6.64 us
    ppermute x1, starting transfers between devices, on_device(): edge_far = lax.ppermute(edge, 'lon', outward)  5.51 us
    ppermute x4, waiting for transfers between devices, gather(): fetched.append(lax.ppermute(pair, 'lon', moves))  5.47 us
    ppermute x1, waiting for transfers between devices, on_device(): edge_far = lax.ppermute(edge, 'lon', outward)  4.04 us
    ppermute x1, waiting for transfers between devices, on_device(): cross_far = lax.ppermute(cross, 'lon', outward)  3.49 us
    pallas_call x1, Pallas kernels, on_device(): pl.pallas_call(functools.partial(third_kernel, levels, sub, count), out_s...  2.83 us
    ppermute x5, waiting for transfers between devices, swap(): return lax.ppermute(array, 'lon', [(i, i ^ mask) for i in range(count)])  2.19 us
  transfers between devices with their start and end apart: 12, of which 6 were waited for; matrix products, arithmetic and copies ran while one was open for 0% of the time, Pallas kernels for 3%

profile of v6, /device:TPU:0, one launch (start us, length us, event | category | flops | bytes accessed | tf_op | source)
XLA Modules:
  0.0 46.5 jit_solution(8208342636158545461)
XLA Ops:
  0.6 0.0 copy-start
  0.6 0.0 copy-start.2
  0.7 0.0 copy-start.3
  0.7 0.0 copy-start.4
  0.7 2.0 %edge_columns.1.edge = f32[125,8,128]{2,1,0:T(8,128)} custom-call(f32[2,50,16,128]{3,2,1,0:T(8,128)} %bitcast.41, f32[50,16,128]{2,1,0:T(8,128)} %bitcast.45), custom_call_target="tpu_custom_call" | custom-call | tf_op jit(solution)/shard_map/edge_columns/pallas_call | solution.py:468
  2.7 5.5 %collective-permute-start = (f32[125,8,128]{2,1,0:T(8,128)}, f32[125,8,128]{2,1,0:T(8,128)S(1)}, u32[]{:S(2)}, u32[]{:S(2)}) collective-permute-start(f32[125,8,128]{2,1,0:T(8,128)} %edge_columns.1.edge), channel_id=1, source_target_pairs={{0,15},{1,2},{2,1},{3,4},{4,3},{5,6},{6,5},{7,8},{8,7},{9,10},{10,... | collective-permute-start | bytes 1536008 | tf_op jit(solution)/shard_map/ppermute | solution.py:483
  8.2 0.0 copy-done
  8.2 0.0 copy-done.2
  8.2 0.0 copy-done.3
  8.2 0.0 copy-done.4
  8.2 0.0 copy-start.1
  8.2 1.0 %copy-done.1 = f32[125,8,128]{2,1,0:T(8,128)S(1)} copy-done((f32[125,8,128]{2,1,0:T(8,128)S(1)}, f32[125,8,128]{2,1,0:T(8,128)}, u32[]{:S(2)}) %copy-start.1) | copy-done | bytes 512024
  9.3 1.2 %partial_step.1 = (f32[101,8,128]{2,1,0:T(8,128)S(1)}, f32[101,8,128]{2,1,0:T(8,128)S(1)}, f32[100,8,128]{2,1,0:T(8,128)S(1)}, f32[100,8,128]{2,1,0:T(8,128)S(1)...) custom-call(f32[125,8,128]{2,1,0:T(8,128)S(1)} %copy-done.1, f32[2,50,16,128]{3,2,1,0:T(8,128)S(1)} %bitcast.42, ...), custom_call_target="tpu_custom_call" | custom-call | tf_op jit(solution)/shard_map/partial_step/pallas_call | solution.py:485
  10.5 0.1 collective-permute-start.1
  10.6 0.0 collective-permute-start.2
  10.6 0.5 %collective-permute-start.3 = (f32[100,8,128]{2,1,0:T(8,128)S(1)}, f32[100,8,128]{2,1,0:T(8,128)S(1)}, u32[]{:S(2)}, u32[]{:S(2)}) collective-permute-start(f32[100,8,128]{2,1,0:T(8,128)S(1)} %get-tuple-element.17.mate_raw), channel_id=1, source_target_pairs={{0,1},{1,0},{2,3},{3,2},{4,5},{5,4},{6,7},{7,6},{8,9},{9,8},{10,11... | collective-permute-start | bytes 1228808 | tf_op jit(solution)/shard_map/ppermute | solution.py:419
  11.1 0.1 collective-permute-start.4
  11.2 4.0 %collective-permute-done.raw_far = f32[125,8,128]{2,1,0:T(8,128)S(1)} collective-permute-done((f32[125,8,128]{2,1,0:T(8,128)}, f32[125,8,128]{2,1,0:T(8,128)S(1)}, u32[]{:S(2)}, u32[]{:S(2)}) %collective-permute-start) | collective-permute-done | bytes 512032 | tf_op jit(solution)/shard_map/ppermute | solution.py:483
  15.3 0.0 copy-start.5
  15.3 2.0 %collective-permute-start.5 = (f32[25,8,128]{2,1,0:T(8,128)S(1)}, f32[25,8,128]{2,1,0:T(8,128)S(1)}, u32[]{:S(2)}, u32[]{:S(2)}) collective-permute-start(f32[25,8,128]{2,1,0:T(8,128)S(1)} %slice.4), channel_id=1, source_target_pairs={{0,16},{16,0},{1,17},{17,1},{2,18},{18,2},{3,19},{19,3},{4,20},{20... | collective-permute-start | bytes 307208 | tf_op jit(solution)/shard_map/ppermute | solution.py:484
  17.3 0.0 collective-permute-done.4.mate_flow_far
  17.3 0.0 collective-permute-done.3.mate_raw_far
  17.3 3.5 %collective-permute-done.1.cross_far = f32[101,8,128]{2,1,0:T(8,128)S(1)} collective-permute-done((f32[101,8,128]{2,1,0:T(8,128)S(1)}, f32[101,8,128]{2,1,0:T(8,128)S(1)}, u32[]{:S(2)}, u32[]{:S(2)}) %collective-permute-start.1) | collective-permute-done | bytes 413728 | tf_op jit(solution)/shard_map/ppermute | solution.py:500
  20.8 0.0 collective-permute-done.2.mate_far
  20.8 0.0 collective-permute-done.5.flow_other
  20.8 0.0 copy-done.5
  20.8 1.5 %both_steps.1 = (f32[2,50,16,128]{3,2,1,0:T(8,128)S(1)}, f32[11,8,128]{2,1,0:T(8,128)S(1)}) custom-call(f32[100,8,128]{2,1,0:T(8,128)S(1)} %get-tuple-element.14.raw, f32[101,8,128]{2,1,0:T(8,128)S(1)} %get-tuple-element.15.cross, f32[101,8,128]{2,1,0:T(8,128)S(1)} %get-tuple-element.16.mate, f32[100,8,128]{2,1,0:T(8,128)S(1)} %get-tuple-element.17.mate_raw, ...), custom_call_target="tpu_custom_call" | custom-call | tf_op jit(solution)/shard_map/both_steps/pallas_call | solution.py:502
  22.3 6.4 %collective-permute-start.6 = (f32[11,8,128]{2,1,0:T(8,128)S(1)}, f32[11,8,128]{2,1,0:T(8,128)S(1)}, u32[]{:S(2)}, u32[]{:S(2)}) collective-permute-start(f32[11,8,128]{2,1,0:T(8,128)S(1)} %get-tuple-element.20), channel_id=1, source_target_pairs={{0,1},{1,0},{2,3},{3,2},{4,5},{5,4},{6,7},{7,6},{8,9},{9,8},{10,11... | collective-permute-start | bytes 135176 | tf_op jit(solution)/shard_map/ppermute | solution.py:419
  28.7 0.9 %collective-permute-done.6 = f32[11,8,128]{2,1,0:T(8,128)S(1)} collective-permute-done((f32[11,8,128]{2,1,0:T(8,128)S(1)}, f32[11,8,128]{2,1,0:T(8,128)S(1)}, u32[]{:S(2)}, u32[]{:S(2)}) %collective-permute-start.6) | collective-permute-done | bytes 45088 | tf_op jit(solution)/shard_map/ppermute | solution.py:419
  29.6 5.3 %collective-permute-start.10 = (f32[2,11,8,128]{3,2,1,0:T(8,128)S(1)}, f32[2,11,8,128]{3,2,1,0:T(8,128)S(1)}, u32[]{:S(2)}, u32[]{:S(2)}) collective-permute-start(f32[2,11,8,128]{3,2,1,0:T(8,128)S(1)} %pad_maximum_fusion.1.pair), channel_id=1, source_target_pairs={{0,14},{1,13},{2,12},{3,15},{4,10},{5,9},{6,8},{7,11},{8,6},{9,5},... | collective-permute-start | bytes 270344 | tf_op jit(solution)/shard_map/ppermute | solution.py:438
  35.0 0.0 collective-permute-start.9
  35.0 0.6 %collective-permute-start.8 = (f32[2,11,8,128]{3,2,1,0:T(8,128)S(1)}, f32[2,11,8,128]{3,2,1,0:T(8,128)S(1)}, u32[]{:S(2)}, u32[]{:S(2)}) collective-permute-start(f32[2,11,8,128]{3,2,1,0:T(8,128)S(1)} %pad_maximum_fusion.1.pair), channel_id=1, source_target_pairs={{0,6},{1,5},{2,4},{3,7},{4,2},{5,1},{6,0},{7,3},{8,14},{9,13},{10,... | collective-permute-start | bytes 270344 | tf_op jit(solution)/shard_map/ppermute | solution.py:438
  35.6 0.7 %collective-permute-start.7 = (f32[2,11,8,128]{3,2,1,0:T(8,128)S(1)}, f32[2,11,8,128]{3,2,1,0:T(8,128)S(1)}, u32[]{:S(2)}, u32[]{:S(2)}) collective-permute-start(f32[2,11,8,128]{3,2,1,0:T(8,128)S(1)} %pad_maximum_fusion.1.pair), channel_id=1, source_target_pairs={{1,3},{3,1},{5,7},{7,5},{9,11},{11,9},{13,15},{15,13},{17,19},{19,... | collective-permute-start | bytes 270344 | tf_op jit(solution)/shard_map/ppermute | solution.py:438
  36.3 2.2 %collective-permute-done.10 = f32[2,11,8,128]{3,2,1,0:T(8,128)S(1)} collective-permute-done((f32[2,11,8,128]{3,2,1,0:T(8,128)S(1)}, f32[2,11,8,128]{3,2,1,0:T(8,128)S(1)}, u32[]{:S(2)}, u32[]{:S(2)}) %collective-permute-start.10) | collective-permute-done | bytes 90144 | tf_op jit(solution)/shard_map/ppermute | solution.py:438
  38.5 3.3 %collective-permute-done.9 = f32[2,11,8,128]{3,2,1,0:T(8,128)S(1)} collective-permute-done((f32[2,11,8,128]{3,2,1,0:T(8,128)S(1)}, f32[2,11,8,128]{3,2,1,0:T(8,128)S(1)}, u32[]{:S(2)}, u32[]{:S(2)}) %collective-permute-start.9) | collective-permute-done | bytes 90144 | tf_op jit(solution)/shard_map/ppermute | solution.py:438
  41.7 0.0 collective-permute-done.8
  41.7 0.0 collective-permute-done.7
  41.8 0.6 %collective-permute-start.11 = (f32[4,2,11,8,128]{4,3,2,1,0:T(8,128)S(1)}, f32[4,2,11,8,128]{4,3,2,1,0:T(8,128)S(1)}, u32[]{:S(2)}, u32[]{:S(2)}) collective-permute-start(f32[4,2,11,8,128]{4,3,2,1,0:T(8,128)S(1)} %pad_maximum_fusion.fetched), channel_id=1, source_target_pairs={{0,1},{1,0},{2,3},{3,2},{4,5},{5,4},{6,7},{7,6},{8,9},{9,8},{10,11... | collective-permute-start | bytes 1081352 | tf_op jit(solution)/shard_map/ppermute | solution.py:419
  42.4 1.3 %collective-permute-done.11.fetched_mate = f32[4,2,11,8,128]{4,3,2,1,0:T(8,128)S(1)} collective-permute-done((f32[4,2,11,8,128]{4,3,2,1,0:T(8,128)S(1)}, f32[4,2,11,8,128]{4,3,2,1,0:T(8,128)S(1)}, u32[]{:S(2)}, u32[]{:S(2)}) %collective-permute-start.11) | collective-permute-done | bytes 360480 | tf_op jit(solution)/shard_map/ppermute | solution.py:419
  43.7 2.8 %surface_and_scale.1 = (f32[2,50,16,128]{3,2,1,0:T(8,128)}, f32[2,16,128]{2,1,0:T(8,128)}, f32[3]{0:T(128)}) custom-call(f32[2,11,8,128]{3,2,1,0:T(8,128)S(1)} %pad_maximum_fusion.1.pair, f32[4,2,11,8,128]{4,3,2,1,0:T(8,128)S(1)} %pad_maximum_fusion.fetched, f32[4,2,11,8,128]{4,3,2,1,0:T(8,128)S(1)} %collective-permute-done.11.fetched_mate, ...), custom_call_target="tpu_custom_call" | custom-call | tf_op jit(solution)/shard_map/surface_and_scale/pallas_call | solution.py:518
  (3 shorter events, 0.0 us)
Async XLA Ops:
  0.6 7.6 %copy-start = (f32[2,50,2,1024]{3,2,1,0:T(2,128)S(1)}, f32[2,50,2,1024]{3,2,1,0:T(2,128)}, u32[]{:S(2)}) copy-start(f32[2,50,2,1024]{3,2,1,0:T(2,128)} %param.5) | copy-start | bytes 2457604
  0.6 7.6 %copy-start.2 = (f32[50,2,1024]{2,1,0:T(2,128)S(1)}, f32[50,2,1024]{2,1,0:T(2,128)}, u32[]{:S(2)}) copy-start(f32[50,2,1024]{2,1,0:T(2,128)} %param.8) | copy-start | bytes 1228804
  0.7 7.6 %copy-start.3 = (f32[50,2,1024]{2,1,0:T(2,128)S(1)}, f32[50,2,1024]{2,1,0:T(2,128)}, u32[]{:S(2)}) copy-start(f32[50,2,1024]{2,1,0:T(2,128)} %param.7) | copy-start | bytes 1228804
  0.7 7.6 %copy-start.4 = (s32[2,1024]{1,0:T(2,128)S(1)}, s32[2,1024]{1,0:T(2,128)}, u32[]{:S(2)}) copy-start(s32[2,1024]{1,0:T(2,128)} %param.9) | copy-start | bytes 24580
  2.7 12.6 %collective-permute-start = (f32[125,8,128]{2,1,0:T(8,128)}, f32[125,8,128]{2,1,0:T(8,128)S(1)}, u32[]{:S(2)}, u32[]{:S(2)}) collective-permute-start(f32[125,8,128]{2,1,0:T(8,128)} %edge_columns.1.edge), channel_id=1, source_target_pairs={{0,15},{1,2},{2,1},{3,4},{4,3},{5,6},{6,5},{7,8},{8,7},{9,10},{10,... | collective-permute-start | bytes 1536008 | tf_op jit(solution)/shard_map/ppermute | solution.py:483
  8.2 1.1 %copy-start.1 = (f32[125,8,128]{2,1,0:T(8,128)S(1)}, f32[125,8,128]{2,1,0:T(8,128)}, u32[]{:S(2)}) copy-start(f32[125,8,128]{2,1,0:T(8,128)} %edge_columns.1.edge) | copy-start | bytes 1536004
  10.5 10.3 %collective-permute-start.1 = (f32[101,8,128]{2,1,0:T(8,128)S(1)}, f32[101,8,128]{2,1,0:T(8,128)S(1)}, u32[]{:S(2)}, u32[]{:S(2)}) collective-permute-start(f32[101,8,128]{2,1,0:T(8,128)S(1)} %get-tuple-element.15.cross), channel_id=1, source_target_pairs={{0,15},{1,2},{2,1},{3,4},{4,3},{5,6},{6,5},{7,8},{8,7},{9,10},{10,... | collective-permute-start | bytes 1241096 | tf_op jit(solution)/shard_map/ppermute | solution.py:500
  10.6 10.2 %collective-permute-start.2 = (f32[101,8,128]{2,1,0:T(8,128)S(1)}, f32[101,8,128]{2,1,0:T(8,128)S(1)}, u32[]{:S(2)}, u32[]{:S(2)}) collective-permute-start(f32[101,8,128]{2,1,0:T(8,128)S(1)} %get-tuple-element.16.mate), channel_id=1, source_target_pairs={{0,1},{1,0},{2,3},{3,2},{4,5},{5,4},{6,7},{7,6},{8,9},{9,8},{10,11... | collective-permute-start | bytes 1241096 | tf_op jit(solution)/shard_map/ppermute | solution.py:419
  10.6 6.6 %collective-permute-start.3 = (f32[100,8,128]{2,1,0:T(8,128)S(1)}, f32[100,8,128]{2,1,0:T(8,128)S(1)}, u32[]{:S(2)}, u32[]{:S(2)}) collective-permute-start(f32[100,8,128]{2,1,0:T(8,128)S(1)} %get-tuple-element.17.mate_raw), channel_id=1, source_target_pairs={{0,1},{1,0},{2,3},{3,2},{4,5},{5,4},{6,7},{7,6},{8,9},{9,8},{10,11... | collective-permute-start | bytes 1228808 | tf_op jit(solution)/shard_map/ppermute | solution.py:419
  11.1 6.1 %collective-permute-start.4 = (f32[50,8,128]{2,1,0:T(8,128)S(1)}, f32[50,8,128]{2,1,0:T(8,128)S(1)}, u32[]{:S(2)}, u32[]{:S(2)}) collective-permute-start(f32[50,8,128]{2,1,0:T(8,128)S(1)} %get-tuple-element.19.mate_flow), channel_id=1, source_target_pairs={{0,1},{1,0},{2,3},{3,2},{4,5},{5,4},{6,7},{7,6},{8,9},{9,8},{10,11... | collective-permute-start | bytes 614408 | tf_op jit(solution)/shard_map/ppermute | solution.py:419
  15.3 5.5 %copy-start.5 = (f32[2,2,1024]{2,1,0:T(2,128)S(1)}, f32[2,2,1024]{2,1,0:T(2,128)}, u32[]{:S(2)}) copy-start(f32[2,2,1024]{2,1,0:T(2,128)} %param.6) | copy-start | bytes 49156
  15.3 5.5 %collective-permute-start.5 = (f32[25,8,128]{2,1,0:T(8,128)S(1)}, f32[25,8,128]{2,1,0:T(8,128)S(1)}, u32[]{:S(2)}, u32[]{:S(2)}) collective-permute-start(f32[25,8,128]{2,1,0:T(8,128)S(1)} %slice.4), channel_id=1, source_target_pairs={{0,16},{16,0},{1,17},{17,1},{2,18},{18,2},{3,19},{19,3},{4,20},{20... | collective-permute-start | bytes 307208 | tf_op jit(solution)/shard_map/ppermute | solution.py:484
  22.3 7.3 %collective-permute-start.6 = (f32[11,8,128]{2,1,0:T(8,128)S(1)}, f32[11,8,128]{2,1,0:T(8,128)S(1)}, u32[]{:S(2)}, u32[]{:S(2)}) collective-permute-start(f32[11,8,128]{2,1,0:T(8,128)S(1)} %get-tuple-element.20), channel_id=1, source_target_pairs={{0,1},{1,0},{2,3},{3,2},{4,5},{5,4},{6,7},{7,6},{8,9},{9,8},{10,11... | collective-permute-start | bytes 135176 | tf_op jit(solution)/shard_map/ppermute | solution.py:419
  29.6 8.9 %collective-permute-start.10 = (f32[2,11,8,128]{3,2,1,0:T(8,128)S(1)}, f32[2,11,8,128]{3,2,1,0:T(8,128)S(1)}, u32[]{:S(2)}, u32[]{:S(2)}) collective-permute-start(f32[2,11,8,128]{3,2,1,0:T(8,128)S(1)} %pad_maximum_fusion.1.pair), channel_id=1, source_target_pairs={{0,14},{1,13},{2,12},{3,15},{4,10},{5,9},{6,8},{7,11},{8,6},{9,5},... | collective-permute-start | bytes 270344 | tf_op jit(solution)/shard_map/ppermute | solution.py:438
  35.0 6.8 %collective-permute-start.9 = (f32[2,11,8,128]{3,2,1,0:T(8,128)S(1)}, f32[2,11,8,128]{3,2,1,0:T(8,128)S(1)}, u32[]{:S(2)}, u32[]{:S(2)}) collective-permute-start(f32[2,11,8,128]{3,2,1,0:T(8,128)S(1)} %pad_maximum_fusion.1.pair), channel_id=1, source_target_pairs={{0,8},{1,11},{2,10},{3,9},{4,12},{5,15},{6,14},{7,13},{8,0},{9,3},... | collective-permute-start | bytes 270344 | tf_op jit(solution)/shard_map/ppermute | solution.py:438
  35.0 6.8 %collective-permute-start.8 = (f32[2,11,8,128]{3,2,1,0:T(8,128)S(1)}, f32[2,11,8,128]{3,2,1,0:T(8,128)S(1)}, u32[]{:S(2)}, u32[]{:S(2)}) collective-permute-start(f32[2,11,8,128]{3,2,1,0:T(8,128)S(1)} %pad_maximum_fusion.1.pair), channel_id=1, source_target_pairs={{0,6},{1,5},{2,4},{3,7},{4,2},{5,1},{6,0},{7,3},{8,14},{9,13},{10,... | collective-permute-start | bytes 270344 | tf_op jit(solution)/shard_map/ppermute | solution.py:438
  35.6 6.1 %collective-permute-start.7 = (f32[2,11,8,128]{3,2,1,0:T(8,128)S(1)}, f32[2,11,8,128]{3,2,1,0:T(8,128)S(1)}, u32[]{:S(2)}, u32[]{:S(2)}) collective-permute-start(f32[2,11,8,128]{3,2,1,0:T(8,128)S(1)} %pad_maximum_fusion.1.pair), channel_id=1, source_target_pairs={{1,3},{3,1},{5,7},{7,5},{9,11},{11,9},{13,15},{15,13},{17,19},{19,... | collective-permute-start | bytes 270344 | tf_op jit(solution)/shard_map/ppermute | solution.py:438
  41.8 1.9 %collective-permute-start.11 = (f32[4,2,11,8,128]{4,3,2,1,0:T(8,128)S(1)}, f32[4,2,11,8,128]{4,3,2,1,0:T(8,128)S(1)}, u32[]{:S(2)}, u32[]{:S(2)}) collective-permute-start(f32[4,2,11,8,128]{4,3,2,1,0:T(8,128)S(1)} %pad_maximum_fusion.fetched), channel_id=1, source_target_pairs={{0,1},{1,0},{2,3},{3,2},{4,5},{5,4},{6,7},{7,6},{8,9},{9,8},{10,11... | collective-permute-start | bytes 1081352 | tf_op jit(solution)/shard_map/ppermute | solution.py:419

commit v7 on v6

--- a/solution.py
+++ b/solution.py
@@ -20,10 +20,11 @@
 VECTORS = 2
 SLOPE = 0.25 * TIME_STEP
 SPREAD = TIME_STEP * DIFFUSIVITY
-HEIGHTS = VECTORS * 2
-DEPTHS = HEIGHTS + VECTORS * 2
-GRAMS = DEPTHS + 2
+DEPTHS = VECTORS * 2
+RIM = DEPTHS + 2
+GRAMS = RIM
 BLOCKS = GRAMS + 1
+POWERS = ITERS
 
 
 def next_row(tile):
@@ -91,8 +92,16 @@
     return lax.axis_index("grp") * (levels - part), part
 
 
+def pack_rim(sub, surface, bottom, target, base):
+    for c in range(2):
+        for v in range(VECTORS):
+            target[base + v * 2 + c] = surface[v, pl.ds(c, sub, stride=2), :]
+        target[base + DEPTHS + c] = bottom[pl.ds(c, sub, stride=2), :].astype(jnp.float32)
+
+
 def edge_kernel(
-    levels, sub, tracer_hbm, zonal_hbm, edge_hbm, tracer, zonal, edge, sems_in, sems_out
+    levels, sub, tracer_hbm, zonal_hbm, surface_hbm, bottom_hbm, edge_hbm,
+    tracer, zonal, surface, bottom, edge, sems_in, sems_out,
 ):
     outer, _, _ = orientation()
     start, part = share(levels)
@@ -105,10 +114,18 @@
     arrivals = [
         move(tracer_hbm.at[v], tracer.at[v], sems_in.at[v]) for v in range(VECTORS)
     ] + [move(zonal_hbm.at[pl.ds(start, part)], zonal, sems_in.at[VECTORS])]
+    small = [
+        move(surface_hbm, surface, sems_in.at[VECTORS + 1]),
+        move(bottom_hbm, bottom, sems_in.at[VECTORS + 2]),
+    ]
     departures = []
     for v, arrival in enumerate(arrivals):
         number = part if v == VECTORS else levels
         arrival.wait()
+        if v == VECTORS:
+            for copy in small:
+                copy.wait()
+            pack_rim(sub, surface, bottom, edge, v * levels + number)
 
         def body(k, carry, v=v):
             source = zonal if v == VECTORS else tracer.at[v]
@@ -116,14 +133,15 @@
             return carry
 
         lax.fori_loop(0, number, body, 0, unroll=steps(number, 10))
-        rows = pl.ds(v * levels, number)
+        rows = pl.ds(v * levels, number + (RIM if v == VECTORS else 0))
         departures.append(move(edge.at[rows], edge_hbm.at[rows], sems_out.at[v]))
     for departure in departures:
         departure.wait()
 
 
 def first_kernel(
-    levels, sub, edge, tracer, zonal, merid, bottom, cross, mate, raw, mate_raw, flow_in, mate_flow
+    levels, sub, edge, tracer, zonal, merid, surface, bottom,
+    cross, mate, raw, mate_raw, flow_in, mate_flow,
 ):
     del edge
     outer, inner, sign = orientation()
@@ -136,6 +154,7 @@
     along = [side_depths(d) for d in depth]
     cross[VECTORS * levels] = depth[0]
     mate[VECTORS * levels] = depth[1]
+    pack_rim(sub, surface, bottom, mate_flow, levels)
 
     def body(k, carry):
         level = k.astype(jnp.float32)
@@ -177,7 +196,7 @@
 def second_kernel(
     levels, sub, raw, cross, mate, mate_raw, flow_in, mate_flow,
     raw_far, cross_far, mate_far, mate_raw_far, mate_flow_far, flow_other,
-    merid, surface, bottom, tracer, message, flow_far,
+    merid, tracer, message, flow_far, powers,
 ):
     outer, inner, sign = orientation()
     start, part = share(levels)
@@ -189,6 +208,7 @@
         return carry
 
     lax.fori_loop(0, part, unpack, 0, unroll=steps(part, 10))
+    powers_of_heights(levels, part, mate_flow, mate_flow_far, raw_far, powers)
     near = [(raw, cross), (mate_raw, mate)]
     far = [(raw_far, cross_far), (mate_raw_far, mate_far)]
     depth = [cross[last], mate[last]]
@@ -238,26 +258,106 @@
 
     sums = lax.fori_loop(0, levels, body, (zero,) * 7, unroll=steps(levels, 10))
     gain = STERIC_GAIN / levels
-    subs = lax.broadcasted_iota(jnp.int32, zero.shape, 0)
-    packed = zero
-    for i, gram in enumerate(sums[4:]):
-        packed = jnp.where(subs == i, jnp.sum(gram, axis=0, keepdims=True), packed)
-    message[GRAMS] = packed
+    rows = list(sums[4:])
+    residual = []
     for v in range(VECTORS):
+        residual.append([gain * sums[v * 2 + c] + powers[POWERS, v, c] for c in range(2)])
         for c, where in enumerate((outer, inner)):
-            message[v * 2 + where] = gain * sums[v * 2 + c]
-            message[HEIGHTS + v * 2 + c] = surface[v, pl.ds(c, sub, stride=2), :]
+            message[v * 2 + where] = residual[v][c]
+
+    def product(one, two):
+        return one[0] * two[0] + one[1] * two[1]
+
+    heights = [[powers[0, v, c] for c in range(2)] for v in range(VECTORS)]
+    for n, (i, j) in enumerate(((0, 0), (0, 1), (1, 1))):
+        rows[n] = rows[n] + product(heights[i], heights[j])
+    for i in range(VECTORS):
+        for j in range(VECTORS):
+            for m in range(POWERS):
+                rows.append(product([powers[m, i, c] for c in range(2)], residual[j]))
+    message[GRAMS] = pack_rows(rows)
     for c in range(2):
-        message[DEPTHS + c] = bottom[pl.ds(c, sub, stride=2), :].astype(jnp.float32)
+        message[DEPTHS + c] = mate_flow[levels + DEPTHS + c]
+
+
+def pack_rows(tiles):
+    shape = tiles[0].shape
+    sub, lane = (lax.broadcasted_iota(jnp.int32, shape, axis) for axis in (0, 1))
+    half = shape[1] // 2
+    packed = jnp.zeros(shape, jnp.float32)
+    for n, tile in enumerate(tiles):
+        row = jnp.sum(tile, axis=0, keepdims=True)
+        row = row + pltpu.roll(row, half, 1)
+        place = (sub == n % shape[0]) & ((lane < half) == (n < shape[0]))
+        packed = jnp.where(place, row, packed)
+    return packed
+
+
+def unpack_rows(packed, count):
+    lane = lax.broadcasted_iota(jnp.int32, packed.shape, 1)
+    low = lane < packed.shape[1] // 2
+    sums = [
+        jnp.sum(jnp.where(side, packed, 0.0), axis=1, keepdims=True)
+        for side in (low, jnp.logical_not(low))
+    ]
+    size = packed.shape[0]
+    return [sums[n // size][n % size : n % size + 1] for n in range(count)]
+
+
+def powers_of_heights(levels, part, mate_flow, mate_flow_far, raw_far, powers):
+    outer, inner, _ = orientation()
+    cross_base = VECTORS * levels + part
+    line = [
+        (mate_flow_far, levels, inner),
+        (mate_flow_far, levels, outer),
+        (mate_flow, levels, inner),
+        (mate_flow, levels, outer),
+        (raw_far, cross_base, inner),
+        (raw_far, cross_base, outer),
+    ]
+    depth = [ref[base + DEPTHS + where] for ref, base, where in line]
+    faces = [SURFACE_COUPLING * jnp.minimum(a, b) for a, b in zip(depth, depth[1:])]
+    sides = [side_depths(SURFACE_COUPLING * d) for d in depth[1:5]]
+    for v in range(VECTORS):
+        field = [
+            jnp.where(d > 0, ref[base + v * 2 + where], 0.0)
+            for d, (ref, base, where) in zip(depth, line)
+        ]
+
+        def bend(field, first, last):
+            found = []
+            for j in range(first, last):
+                west, centre, east = field[j - 1 : j + 2]
+                north, south = sides[j - 1]
+                found.append(
+                    (faces[j] * (east - centre) - faces[j - 1] * (centre - west))
+                    + (north * (next_row(centre) - centre) - south * (centre - prior_row(centre)))
+                )
+            return found
+
+        lap = bend(field, 1, 5)
+        image = [None] + [h - p for h, p in zip(field[1:5], lap)]
+        again = [p - q for p, q in zip(image[2:4], bend(image, 2, 4))]
+        for c, where in enumerate((3, 2)):
+            powers[0, v, c] = field[where]
+            powers[1, v, c] = image[where]
+            powers[2, v, c] = again[where - 2]
+            powers[POWERS, v, c] = lap[where - 1]
 
 
 def total(tile):
     return jnp.sum(jnp.sum(tile, axis=0, keepdims=True), axis=1, keepdims=True)
 
 
+def combine(one, factor, two):
+    longest = max(len(one), len(two))
+    one, two = (list(c) + [0.0] * (longest - len(c)) for c in (one, two))
+    return [a + factor * b for a, b in zip(one, two)]
+
+
 def third_kernel(
-    levels, sub, count, pair, fetched, fetched_mate, tracer, tracer_out, surface_out, growth,
-    pole, residual, answer, image, height, depth, face_x, face_y, face_z, packed,
+    levels, sub, count, pair, fetched, fetched_mate, surface, tracer, tracer_out, surface_out, growth,
+    pole, residual, answer, image, depth, face_x, face_y, face_z, packed,
 ):
     width = 2 * count
     me = lax.axis_index("lon")
@@ -269,13 +369,11 @@
         packed[owner] = block(GRAMS)
         for c in range(2):
             x = 2 * owner + c
-            floor = block(DEPTHS + c)
-            depth[x] = floor
+            depth[x] = block(DEPTHS + c)
             for v in range(VECTORS):
-                tall = jnp.where(floor > 0, block(HEIGHTS + v * 2 + c), 0.0)
-                height[v, x] = tall
-                pole[v, x + 1] = tall
-                residual[v, x] = block(v * 2 + c)
+                value = block(v * 2 + c)
+                residual[v, x] = value
+                pole[v, x + 1] = value
 
     for slot in range(2):
         place(me ^ slot, lambda row, slot=slot: pair[slot, row])
@@ -315,20 +413,11 @@
     def start(d, carry):
         sums = list(carry)
         for v, _, x in each(d):
-            value = residual[v, x] + spread(pole, face_x, face_y, face_z, v, x)
-            residual[v, x] = value
-            sums[v] = sums[v] + value * value
+            sums[v] = sums[v] + residual[v, x] * residual[v, x]
         return tuple(sums)
 
     norm = [total(t) for t in over(start, none)]
-
-    def aim(d, carry):
-        for v, _, x in each(d):
-            pole[v, x + 1] = residual[v, x]
-        return carry
-
-    over(aim, 0)
-    wrap(pole, width)
+    share, left, aim = ([[v for _ in range(VECTORS)] for v in ([], [1.0], [1.0])])
 
     def apply(d, carry):
         sums = list(carry)
@@ -342,13 +431,14 @@
     for iteration in range(ITERS):
         energy = [total(t) for t in over(apply, none)]
         size = [n / e for n, e in zip(norm, energy)]
-        held = height if iteration == 0 else answer
+        share = [combine(s, z, a) for s, z, a in zip(share, size, aim)]
         if iteration + 1 < ITERS:
 
-            def advance(d, carry, size=size, held=held):
+            def advance(d, carry, size=size, first=iteration == 0):
                 sums = list(carry)
                 for v, _, x in each(d):
-                    answer[v, x] = held[v, x] + size[v] * pole[v, x + 1]
+                    gone = size[v] * pole[v, x + 1]
+                    answer[v, x] = gone if first else answer[v, x] + gone
                     value = residual[v, x] - size[v] * image[v, x]
                     residual[v, x] = value
                     sums[v] = sums[v] + value * value
@@ -356,6 +446,8 @@
 
             fresh = [total(t) for t in over(advance, none)]
             ratio = [f / n for f, n in zip(fresh, norm)]
+            left = [combine(l, -z, [0.0] + a) for l, z, a in zip(left, size, aim)]
+            aim = [combine(l, q, a) for l, q, a in zip(left, ratio, aim)]
 
             def turn(d, carry, ratio=ratio):
                 for v, _, x in each(d):
@@ -369,16 +461,22 @@
     def finish(d, carry):
         grams = list(carry)
         for x in (2 * d, 2 * d + 1):
-            a, b = (held[v, x] + size[v] * pole[v, x + 1] for v in range(VECTORS))
+            a, b = (answer[v, x] + size[v] * pole[v, x + 1] for v in range(VECTORS))
             answer[0, x], answer[1, x] = a, b
             grams = [grams[0] + a * a, grams[1] + a * b, grams[2] + b * b]
         return (*grams, carry[3] + packed[d])
 
-    *grams, share_of = over(finish, (zero,) * 4)
+    *grams, packed_sums = over(finish, (zero,) * 4)
+    sums = unpack_rows(packed_sums, 3 + VECTORS * VECTORS * POWERS)
+
+    def heights_with(i, j):
+        first = 3 + (i * VECTORS + j) * POWERS
+        return sum(c * t for c, t in zip(share[j], sums[first : first + POWERS]))
+
     cells = (levels + 1) * width * sub * LANES
     one, mix, two = (
-        (total(g) + jnp.sum(share_of[i : i + 1], axis=1, keepdims=True)) / cells
-        for i, g in enumerate(grams)
+        (sums[n] + total(grams[n]) + (heights_with(i, j) + heights_with(j, i))) / cells
+        for n, (i, j) in enumerate(((0, 0), (0, 1), (1, 1)))
     )
     scale_one = jnp.sqrt(one + EPSILON)
     cross = mix / scale_one
@@ -395,9 +493,13 @@
     lax.fori_loop(0, levels, scale, 0, unroll=steps(levels, 10))
     for c in range(2):
         x = 2 * me + c
-        unit = answer[0, x] * over_one
+        first, second = (
+            jnp.where(depth[x] > 0, surface[v, pl.ds(c, sub, stride=2), :], 0.0) + answer[v, x]
+            for v in range(VECTORS)
+        )
+        unit = first * over_one
         surface_out[0, pl.ds(c, sub, stride=2), :] = unit
-        surface_out[1, pl.ds(c, sub, stride=2), :] = (answer[1, x] - cross * unit) * over_two
+        surface_out[1, pl.ds(c, sub, stride=2), :] = (second - cross * unit) * over_two
     for i, value in enumerate((scale_one, cross, scale_two)):
         growth[i] = value[0, 0]
 
@@ -462,26 +564,28 @@
     tracer_pert, zonal_flow, merid_flow = map(tiled, (tracer_pert, zonal_flow, merid_flow))
     outward = [(i, (i + 1) % count if i % 2 else (i - 1) % count) for i in range(count)]
     part = (levels + 1) // 2
-    bottom = tiled(bottom_level)
-    edge_rows = VECTORS * levels + part
+    surface, bottom = tiled(surface_pert), tiled(bottom_level)
+    edge_rows = VECTORS * levels + part + RIM
 
     edge = pl.pallas_call(
         functools.partial(edge_kernel, levels, sub),
         out_shape=shaped(edge_rows),
-        in_specs=[hbm] * 2,
+        in_specs=[hbm] * 4,
         out_specs=hbm,
         scratch_shapes=[
             both,
             pltpu.VMEM((part, sub * 2, LANES), f32),
+            pltpu.VMEM((vectors, sub * 2, LANES), f32),
+            pltpu.VMEM((sub * 2, LANES), jnp.int32),
             held(edge_rows),
-            pltpu.SemaphoreType.DMA((VECTORS + 1,)),
+            pltpu.SemaphoreType.DMA((VECTORS + 3,)),
             pltpu.SemaphoreType.DMA((VECTORS + 1,)),
         ],
         compiler_params=pltpu.CompilerParams(vmem_limit_bytes=60 * 2**20),
         name="edge_columns",
-    )(tracer_pert, zonal_flow)
+    )(tracer_pert, zonal_flow, surface, bottom)
     edge_far = lax.ppermute(edge, "lon", outward)
-    flow_other = lax.ppermute(edge_far[VECTORS * levels :], "grp", [(0, 1), (1, 0)])
+    flow_other = lax.ppermute(edge_far[VECTORS * levels : edge_rows - RIM], "grp", [(0, 1), (1, 0)])
     cross, mate, raw, mate_raw, flow_in, mate_flow = pl.pallas_call(
         functools.partial(first_kernel, levels, sub),
         out_shape=(
@@ -490,13 +594,13 @@
             shaped(VECTORS * levels),
             shaped(VECTORS * levels),
             shaped(levels),
-            shaped(levels),
+            shaped(levels + RIM),
         ),
-        in_specs=[pl.BlockSpec(memory_space=pl.ANY)] + [vmem] * 4,
+        in_specs=[pl.BlockSpec(memory_space=pl.ANY)] + [vmem] * 5,
         out_specs=(vmem,) * 6,
         compiler_params=params,
         name="partial_step",
-    )(edge, tracer_pert, zonal_flow, merid_flow, bottom)
+    )(edge, tracer_pert, zonal_flow, merid_flow, surface, bottom)
     cross_far = lax.ppermute(cross, "lon", outward)
     mate_far, mate_raw_far, mate_flow_far = (swap(x, 1) for x in (mate, mate_raw, mate_flow))
     tracer, message = pl.pallas_call(
@@ -505,15 +609,15 @@
             jax.ShapeDtypeStruct((vectors, levels, sub * 2, LANES), f32),
             shaped(BLOCKS),
         ),
-        in_specs=[vmem] * 15,
+        in_specs=[vmem] * 13,
         out_specs=(vmem, vmem),
-        scratch_shapes=[held(levels)],
+        scratch_shapes=[held(levels), held(POWERS + 1, vectors, 2)],
         compiler_params=params,
         name="both_steps",
     )(
         raw, cross, mate, mate_raw, flow_in, mate_flow,
         edge_far, cross_far, mate_far, mate_raw_far, mate_flow_far, flow_other,
-        merid_flow, tiled(surface_pert), bottom,
+        merid_flow,
     )
     tracer_vec, surface_vec, growth = pl.pallas_call(
         functools.partial(third_kernel, levels, sub, count),
@@ -522,11 +626,11 @@
             jax.ShapeDtypeStruct((vectors, sub * 2, LANES), f32),
             jax.ShapeDtypeStruct((3,), f32),
         ),
-        in_specs=[vmem] * 4,
+        in_specs=[vmem] * 5,
         out_specs=(vmem, vmem, pl.BlockSpec(memory_space=pltpu.SMEM)),
         scratch_shapes=[
             held(vectors, width + 2),
-            *[held(vectors, width)] * 4,
+            *[held(vectors, width)] * 3,
             held(width),
             held(width + 1),
             held(width),
@@ -535,7 +639,7 @@
         ],
         compiler_params=pltpu.CompilerParams(vmem_limit_bytes=32 * 2**20),
         name="surface_and_scale",
-    )(*gather(message), tracer)
+    )(*gather(message), surface, tracer)
     return (untiled(tracer_vec, 2), untiled(surface_vec, 2), growth)
 
 

time: 46.7 us -> 45.8 us (0.981)
  waiting for transfers between devices: 15.2 us -> 14.3 us
    ppermute x4, waiting for transfers between devices: 5.47 us -> 4.46 us  [gather(): fetched.append(lax.ppermute(pair, 'lon', moves))]
  transfers between devices with their start and end apart: 12 -> 12, of which waited for: 6 -> 7; matrix products, arithmetic and copies ran while one was open for 0% -> 0% of each run, Pallas kernels for 3% -> 3%
where the time goes in v7:
time: 45.8 us; the launch traced here: 45.6 us
  starting transfers between devices  21.9 us (48%)
  waiting for transfers between devices  14.3 us (31%)
  Pallas kernels  7.54 us (16%)
  local copies, waits for them, and re-layouts  1.08 us (2%)
  between operations  0.75 us (2%)
    ppermute x5, starting transfers between devices, swap(): return lax.ppermute(array, 'lon', [(i, i ^ mask) for i in range(count)])  7.69 us
    ppermute x4, starting transfers between devices, gather(): fetched.append(lax.ppermute(pair, 'lon', moves))  6.59 us
    ppermute x1, starting transfers between devices, on_device(): edge_far = lax.ppermute(edge, 'lon', outward)  5.51 us
    ppermute x4, waiting for transfers between devices, gather(): fetched.append(lax.ppermute(pair, 'lon', moves))  4.46 us
    ppermute x1, waiting for transfers between devices, on_device(): edge_far = lax.ppermute(edge, 'lon', outward)  4.3 us
    ppermute x1, waiting for transfers between devices, on_device(): cross_far = lax.ppermute(cross, 'lon', outward)  3.24 us
    pallas_call x1, Pallas kernels, on_device(): pl.pallas_call(functools.partial(third_kernel, levels, sub, count), out_s...  2.66 us
    ppermute x5, waiting for transfers between devices, swap(): return lax.ppermute(array, 'lon', [(i, i ^ mask) for i in range(count)])  2.3 us
  transfers between devices with their start and end apart: 12, of which 7 were waited for; matrix products, arithmetic and copies ran while one was open for 0% of the time, Pallas kernels for 3%

profile of v7, /device:TPU:0, one launch (start us, length us, event | category | flops | bytes accessed | tf_op | source)
XLA Modules:
  0.0 45.6 jit_solution(3005827025086841543)
XLA Ops:
  0.6 0.0 copy-start
  0.6 0.0 copy-start.2
  0.7 0.0 copy-start.3
  0.7 0.0 copy-start.4
  0.7 0.0 copy-start.5
  0.7 2.0 %edge_columns.1.edge = f32[131,8,128]{2,1,0:T(8,128)} custom-call(f32[2,50,16,128]{3,2,1,0:T(8,128)} %bitcast.41, f32[50,16,128]{2,1,0:T(8,128)} %bitcast.43, f32[2,16,128]{2,1,0:T(8,128)} %bitcast.47, s32[16,128]{1,0:T(8,128)} %bitcast.50), custom_call_target="tpu_custom_call" | custom-call | tf_op jit(solution)/shard_map/edge_columns/pallas_call | solution.py:570
  2.7 5.5 %collective-permute-start = (f32[131,8,128]{2,1,0:T(8,128)}, f32[131,8,128]{2,1,0:T(8,128)S(1)}, u32[]{:S(2)}, u32[]{:S(2)}) collective-permute-start(f32[131,8,128]{2,1,0:T(8,128)} %edge_columns.1.edge), channel_id=1, source_target_pairs={{0,15},{1,2},{2,1},{3,4},{4,3},{5,6},{6,5},{7,8},{8,7},{9,10},{10,... | collective-permute-start | bytes 1609736 | tf_op jit(solution)/shard_map/ppermute | solution.py:587
  8.2 0.0 copy-done
  8.2 0.0 copy-done.2
  8.3 0.0 copy-done.3
  8.3 0.0 copy-done.4
  8.3 0.0 copy-done.5
  8.3 0.0 copy-start.1
  8.3 1.0 %copy-done.1 = f32[131,8,128]{2,1,0:T(8,128)S(1)} copy-done((f32[131,8,128]{2,1,0:T(8,128)S(1)}, f32[131,8,128]{2,1,0:T(8,128)}, u32[]{:S(2)}) %copy-start.1) | copy-done | bytes 536600
  9.3 1.2 %partial_step.1 = (f32[101,8,128]{2,1,0:T(8,128)S(1)}, f32[101,8,128]{2,1,0:T(8,128)S(1)}, f32[100,8,128]{2,1,0:T(8,128)S(1)}, f32[100,8,128]{2,1,0:T(8,128)S(1)...) custom-call(f32[131,8,128]{2,1,0:T(8,128)S(1)} %copy-done.1, f32[2,50,16,128]{3,2,1,0:T(8,128)S(1)} %bitcast.42, ...), custom_call_target="tpu_custom_call" | custom-call | tf_op jit(solution)/shard_map/partial_step/pallas_call | solution.py:589
  10.5 0.1 collective-permute-start.1
  10.6 0.0 collective-permute-start.2
  10.7 0.5 %collective-permute-start.3 = (f32[100,8,128]{2,1,0:T(8,128)S(1)}, f32[100,8,128]{2,1,0:T(8,128)S(1)}, u32[]{:S(2)}, u32[]{:S(2)}) collective-permute-start(f32[100,8,128]{2,1,0:T(8,128)S(1)} %get-tuple-element.17.mate_raw), channel_id=1, source_target_pairs={{0,1},{1,0},{2,3},{3,2},{4,5},{5,4},{6,7},{7,6},{8,9},{9,8},{10,11... | collective-permute-start | bytes 1228808 | tf_op jit(solution)/shard_map/ppermute | solution.py:521
  11.2 0.1 collective-permute-start.4
  11.3 4.3 %collective-permute-done.raw_far = f32[131,8,128]{2,1,0:T(8,128)S(1)} collective-permute-done((f32[131,8,128]{2,1,0:T(8,128)}, f32[131,8,128]{2,1,0:T(8,128)S(1)}, u32[]{:S(2)}, u32[]{:S(2)}) %collective-permute-start) | collective-permute-done | bytes 536608 | tf_op jit(solution)/shard_map/ppermute | solution.py:587
  15.6 2.0 %collective-permute-start.5 = (f32[25,8,128]{2,1,0:T(8,128)S(1)}, f32[25,8,128]{2,1,0:T(8,128)S(1)}, u32[]{:S(2)}, u32[]{:S(2)}) collective-permute-start(f32[25,8,128]{2,1,0:T(8,128)S(1)} %slice.4), channel_id=1, source_target_pairs={{0,16},{16,0},{1,17},{17,1},{2,18},{18,2},{3,19},{19,3},{4,20},{20... | collective-permute-start | bytes 307208 | tf_op jit(solution)/shard_map/ppermute | solution.py:588
  17.6 0.0 collective-permute-done.4.mate_flow_far
  17.6 0.0 collective-permute-done.3.mate_raw_far
  17.6 3.2 %collective-permute-done.1.cross_far = f32[101,8,128]{2,1,0:T(8,128)S(1)} collective-permute-done((f32[101,8,128]{2,1,0:T(8,128)S(1)}, f32[101,8,128]{2,1,0:T(8,128)S(1)}, u32[]{:S(2)}, u32[]{:S(2)}) %collective-permute-start.1) | collective-permute-done | bytes 413728 | tf_op jit(solution)/shard_map/ppermute | solution.py:604
  20.8 0.0 collective-permute-done.2.mate_far
  20.8 0.0 collective-permute-done.5.flow_other
  20.8 1.6 %both_steps.1 = (f32[2,50,16,128]{3,2,1,0:T(8,128)S(1)}, f32[7,8,128]{2,1,0:T(8,128)S(1)}) custom-call(f32[100,8,128]{2,1,0:T(8,128)S(1)} %get-tuple-element.14.raw, f32[101,8,128]{2,1,0:T(8,128)S(1)} %get-tuple-element.15.cross, f32[101,8,128]{2,1,0:T(8,128)S(1)} %get-tuple-element.16.mate, f32[100,8,128]{2,1,0:T(8,128)S(1)} %get-tuple-element.17.mate_raw, ...), custom_call_target="tpu_custom_call" | custom-call | tf_op jit(solution)/shard_map/both_steps/pallas_call | solution.py:606
  22.5 7.0 %collective-permute-start.6 = (f32[7,8,128]{2,1,0:T(8,128)S(1)}, f32[7,8,128]{2,1,0:T(8,128)S(1)}, u32[]{:S(2)}, u32[]{:S(2)}) collective-permute-start(f32[7,8,128]{2,1,0:T(8,128)S(1)} %get-tuple-element.20), channel_id=1, source_target_pairs={{0,1},{1,0},{2,3},{3,2},{4,5},{5,4},{6,7},{7,6},{8,9},{9,8},{10,11... | collective-permute-start | bytes 86024 | tf_op jit(solution)/shard_map/ppermute | solution.py:521
  29.4 0.9 %collective-permute-done.6 = f32[7,8,128]{2,1,0:T(8,128)S(1)} collective-permute-done((f32[7,8,128]{2,1,0:T(8,128)S(1)}, f32[7,8,128]{2,1,0:T(8,128)S(1)}, u32[]{:S(2)}, u32[]{:S(2)}) %collective-permute-start.6) | collective-permute-done | bytes 28704 | tf_op jit(solution)/shard_map/ppermute | solution.py:521
  30.3 5.3 %collective-permute-start.10 = (f32[2,7,8,128]{3,2,1,0:T(8,128)S(1)}, f32[2,7,8,128]{3,2,1,0:T(8,128)S(1)}, u32[]{:S(2)}, u32[]{:S(2)}) collective-permute-start(f32[2,7,8,128]{3,2,1,0:T(8,128)S(1)} %pad_maximum_fusion.1.pair), channel_id=1, source_target_pairs={{0,14},{1,13},{2,12},{3,15},{4,10},{5,9},{6,8},{7,11},{8,6},{9,5},... | collective-permute-start | bytes 172040 | tf_op jit(solution)/shard_map/ppermute | solution.py:540
  35.6 0.0 collective-permute-start.9
  35.6 0.6 %collective-permute-start.8 = (f32[2,7,8,128]{3,2,1,0:T(8,128)S(1)}, f32[2,7,8,128]{3,2,1,0:T(8,128)S(1)}, u32[]{:S(2)}, u32[]{:S(2)}) collective-permute-start(f32[2,7,8,128]{3,2,1,0:T(8,128)S(1)} %pad_maximum_fusion.1.pair), channel_id=1, source_target_pairs={{0,6},{1,5},{2,4},{3,7},{4,2},{5,1},{6,0},{7,3},{8,14},{9,13},{10,... | collective-permute-start | bytes 172040 | tf_op jit(solution)/shard_map/ppermute | solution.py:540
  36.2 0.7 %collective-permute-start.7 = (f32[2,7,8,128]{3,2,1,0:T(8,128)S(1)}, f32[2,7,8,128]{3,2,1,0:T(8,128)S(1)}, u32[]{:S(2)}, u32[]{:S(2)}) collective-permute-start(f32[2,7,8,128]{3,2,1,0:T(8,128)S(1)} %pad_maximum_fusion.1.pair), channel_id=1, source_target_pairs={{1,3},{3,1},{5,7},{7,5},{9,11},{11,9},{13,15},{15,13},{17,19},{19,... | collective-permute-start | bytes 172040 | tf_op jit(solution)/shard_map/ppermute | solution.py:540
  36.9 1.5 %collective-permute-done.10 = f32[2,7,8,128]{3,2,1,0:T(8,128)S(1)} collective-permute-done((f32[2,7,8,128]{3,2,1,0:T(8,128)S(1)}, f32[2,7,8,128]{3,2,1,0:T(8,128)S(1)}, u32[]{:S(2)}, u32[]{:S(2)}) %collective-permute-start.10) | collective-permute-done | bytes 57376 | tf_op jit(solution)/shard_map/ppermute | solution.py:540
  38.4 2.4 %collective-permute-done.9 = f32[2,7,8,128]{3,2,1,0:T(8,128)S(1)} collective-permute-done((f32[2,7,8,128]{3,2,1,0:T(8,128)S(1)}, f32[2,7,8,128]{3,2,1,0:T(8,128)S(1)}, u32[]{:S(2)}, u32[]{:S(2)}) %collective-permute-start.9) | collective-permute-done | bytes 57376 | tf_op jit(solution)/shard_map/ppermute | solution.py:540
  40.8 0.5 %collective-permute-done.8 = f32[2,7,8,128]{3,2,1,0:T(8,128)S(1)} collective-permute-done((f32[2,7,8,128]{3,2,1,0:T(8,128)S(1)}, f32[2,7,8,128]{3,2,1,0:T(8,128)S(1)}, u32[]{:S(2)}, u32[]{:S(2)}) %collective-permute-start.8) | collective-permute-done | bytes 57376 | tf_op jit(solution)/shard_map/ppermute | solution.py:540
  41.3 0.0 collective-permute-done.7
  41.4 0.1 collective-permute-start.11
  41.5 1.4 %collective-permute-done.11.fetched_mate = f32[4,2,7,8,128]{4,3,2,1,0:T(8,128)S(1)} collective-permute-done((f32[4,2,7,8,128]{4,3,2,1,0:T(8,128)S(1)}, f32[4,2,7,8,128]{4,3,2,1,0:T(8,128)S(1)}, u32[]{:S(2)}, u32[]{:S(2)}) %collective-permute-start.11) | collective-permute-done | bytes 229408 | tf_op jit(solution)/shard_map/ppermute | solution.py:521
  42.9 2.7 %surface_and_scale.1 = (f32[2,50,16,128]{3,2,1,0:T(8,128)}, f32[2,16,128]{2,1,0:T(8,128)}, f32[3]{0:T(128)}) custom-call(f32[2,7,8,128]{3,2,1,0:T(8,128)S(1)} %pad_maximum_fusion.1.pair, f32[4,2,7,8,128]{4,3,2,1,0:T(8,128)S(1)} %pad_maximum_fusion.fetched, f32[4,2,7,8,128]{4,3,2,1,0:T(8,128)S(1)} %collective-permute-done.11.fetched_mate, ...), custom_call_target="tpu_custom_call" | custom-call | tf_op jit(solution)/shard_map/surface_and_scale/pallas_call | solution.py:622
  (3 shorter events, 0.0 us)
Async XLA Ops:
  0.6 7.6 %copy-start = (f32[2,50,2,1024]{3,2,1,0:T(2,128)S(1)}, f32[2,50,2,1024]{3,2,1,0:T(2,128)}, u32[]{:S(2)}) copy-start(f32[2,50,2,1024]{3,2,1,0:T(2,128)} %param.5) | copy-start | bytes 2457604
  0.6 7.6 %copy-start.2 = (f32[50,2,1024]{2,1,0:T(2,128)S(1)}, f32[50,2,1024]{2,1,0:T(2,128)}, u32[]{:S(2)}) copy-start(f32[50,2,1024]{2,1,0:T(2,128)} %param.7) | copy-start | bytes 1228804
  0.7 7.6 %copy-start.3 = (f32[50,2,1024]{2,1,0:T(2,128)S(1)}, f32[50,2,1024]{2,1,0:T(2,128)}, u32[]{:S(2)}) copy-start(f32[50,2,1024]{2,1,0:T(2,128)} %param.8) | copy-start | bytes 1228804
  0.7 7.6 %copy-start.4 = (f32[2,2,1024]{2,1,0:T(2,128)S(1)}, f32[2,2,1024]{2,1,0:T(2,128)}, u32[]{:S(2)}) copy-start(f32[2,2,1024]{2,1,0:T(2,128)} %param.6) | copy-start | bytes 49156
  0.7 7.6 %copy-start.5 = (s32[2,1024]{1,0:T(2,128)S(1)}, s32[2,1024]{1,0:T(2,128)}, u32[]{:S(2)}) copy-start(s32[2,1024]{1,0:T(2,128)} %param.9) | copy-start | bytes 24580
  2.7 12.8 %collective-permute-start = (f32[131,8,128]{2,1,0:T(8,128)}, f32[131,8,128]{2,1,0:T(8,128)S(1)}, u32[]{:S(2)}, u32[]{:S(2)}) collective-permute-start(f32[131,8,128]{2,1,0:T(8,128)} %edge_columns.1.edge), channel_id=1, source_target_pairs={{0,15},{1,2},{2,1},{3,4},{4,3},{5,6},{6,5},{7,8},{8,7},{9,10},{10,... | collective-permute-start | bytes 1609736 | tf_op jit(solution)/shard_map/ppermute | solution.py:587
  8.3 1.1 %copy-start.1 = (f32[131,8,128]{2,1,0:T(8,128)S(1)}, f32[131,8,128]{2,1,0:T(8,128)}, u32[]{:S(2)}) copy-start(f32[131,8,128]{2,1,0:T(8,128)} %edge_columns.1.edge) | copy-start | bytes 1609732
  10.5 10.3 %collective-permute-start.1 = (f32[101,8,128]{2,1,0:T(8,128)S(1)}, f32[101,8,128]{2,1,0:T(8,128)S(1)}, u32[]{:S(2)}, u32[]{:S(2)}) collective-permute-start(f32[101,8,128]{2,1,0:T(8,128)S(1)} %get-tuple-element.15.cross), channel_id=1, source_target_pairs={{0,15},{1,2},{2,1},{3,4},{4,3},{5,6},{6,5},{7,8},{8,7},{9,10},{10,... | collective-permute-start | bytes 1241096 | tf_op jit(solution)/shard_map/ppermute | solution.py:604
  10.6 10.2 %collective-permute-start.2 = (f32[101,8,128]{2,1,0:T(8,128)S(1)}, f32[101,8,128]{2,1,0:T(8,128)S(1)}, u32[]{:S(2)}, u32[]{:S(2)}) collective-permute-start(f32[101,8,128]{2,1,0:T(8,128)S(1)} %get-tuple-element.16.mate), channel_id=1, source_target_pairs={{0,1},{1,0},{2,3},{3,2},{4,5},{5,4},{6,7},{7,6},{8,9},{9,8},{10,11... | collective-permute-start | bytes 1241096 | tf_op jit(solution)/shard_map/ppermute | solution.py:521
  10.7 6.9 %collective-permute-start.3 = (f32[100,8,128]{2,1,0:T(8,128)S(1)}, f32[100,8,128]{2,1,0:T(8,128)S(1)}, u32[]{:S(2)}, u32[]{:S(2)}) collective-permute-start(f32[100,8,128]{2,1,0:T(8,128)S(1)} %get-tuple-element.17.mate_raw), channel_id=1, source_target_pairs={{0,1},{1,0},{2,3},{3,2},{4,5},{5,4},{6,7},{7,6},{8,9},{9,8},{10,11... | collective-permute-start | bytes 1228808 | tf_op jit(solution)/shard_map/ppermute | solution.py:521
  11.2 6.4 %collective-permute-start.4 = (f32[56,8,128]{2,1,0:T(8,128)S(1)}, f32[56,8,128]{2,1,0:T(8,128)S(1)}, u32[]{:S(2)}, u32[]{:S(2)}) collective-permute-start(f32[56,8,128]{2,1,0:T(8,128)S(1)} %get-tuple-element.19.mate_flow), channel_id=1, source_target_pairs={{0,1},{1,0},{2,3},{3,2},{4,5},{5,4},{6,7},{7,6},{8,9},{9,8},{10,11... | collective-permute-start | bytes 688136 | tf_op jit(solution)/shard_map/ppermute | solution.py:521
  15.6 5.3 %collective-permute-start.5 = (f32[25,8,128]{2,1,0:T(8,128)S(1)}, f32[25,8,128]{2,1,0:T(8,128)S(1)}, u32[]{:S(2)}, u32[]{:S(2)}) collective-permute-start(f32[25,8,128]{2,1,0:T(8,128)S(1)} %slice.4), channel_id=1, source_target_pairs={{0,16},{16,0},{1,17},{17,1},{2,18},{18,2},{3,19},{19,3},{4,20},{20... | collective-permute-start | bytes 307208 | tf_op jit(solution)/shard_map/ppermute | solution.py:588
  22.5 7.8 %collective-permute-start.6 = (f32[7,8,128]{2,1,0:T(8,128)S(1)}, f32[7,8,128]{2,1,0:T(8,128)S(1)}, u32[]{:S(2)}, u32[]{:S(2)}) collective-permute-start(f32[7,8,128]{2,1,0:T(8,128)S(1)} %get-tuple-element.20), channel_id=1, source_target_pairs={{0,1},{1,0},{2,3},{3,2},{4,5},{5,4},{6,7},{7,6},{8,9},{9,8},{10,11... | collective-permute-start | bytes 86024 | tf_op jit(solution)/shard_map/ppermute | solution.py:521
  30.3 8.1 %collective-permute-start.10 = (f32[2,7,8,128]{3,2,1,0:T(8,128)S(1)}, f32[2,7,8,128]{3,2,1,0:T(8,128)S(1)}, u32[]{:S(2)}, u32[]{:S(2)}) collective-permute-start(f32[2,7,8,128]{3,2,1,0:T(8,128)S(1)} %pad_maximum_fusion.1.pair), channel_id=1, source_target_pairs={{0,14},{1,13},{2,12},{3,15},{4,10},{5,9},{6,8},{7,11},{8,6},{9,5},... | collective-permute-start | bytes 172040 | tf_op jit(solution)/shard_map/ppermute | solution.py:540
  35.6 5.2 %collective-permute-start.9 = (f32[2,7,8,128]{3,2,1,0:T(8,128)S(1)}, f32[2,7,8,128]{3,2,1,0:T(8,128)S(1)}, u32[]{:S(2)}, u32[]{:S(2)}) collective-permute-start(f32[2,7,8,128]{3,2,1,0:T(8,128)S(1)} %pad_maximum_fusion.1.pair), channel_id=1, source_target_pairs={{0,8},{1,11},{2,10},{3,9},{4,12},{5,15},{6,14},{7,13},{8,0},{9,3},... | collective-permute-start | bytes 172040 | tf_op jit(solution)/shard_map/ppermute | solution.py:540
  35.6 5.8 %collective-permute-start.8 = (f32[2,7,8,128]{3,2,1,0:T(8,128)S(1)}, f32[2,7,8,128]{3,2,1,0:T(8,128)S(1)}, u32[]{:S(2)}, u32[]{:S(2)}) collective-permute-start(f32[2,7,8,128]{3,2,1,0:T(8,128)S(1)} %pad_maximum_fusion.1.pair), channel_id=1, source_target_pairs={{0,6},{1,5},{2,4},{3,7},{4,2},{5,1},{6,0},{7,3},{8,14},{9,13},{10,... | collective-permute-start | bytes 172040 | tf_op jit(solution)/shard_map/ppermute | solution.py:540
  36.2 5.1 %collective-permute-start.7 = (f32[2,7,8,128]{3,2,1,0:T(8,128)S(1)}, f32[2,7,8,128]{3,2,1,0:T(8,128)S(1)}, u32[]{:S(2)}, u32[]{:S(2)}) collective-permute-start(f32[2,7,8,128]{3,2,1,0:T(8,128)S(1)} %pad_maximum_fusion.1.pair), channel_id=1, source_target_pairs={{1,3},{3,1},{5,7},{7,5},{9,11},{11,9},{13,15},{15,13},{17,19},{19,... | collective-permute-start | bytes 172040 | tf_op jit(solution)/shard_map/ppermute | solution.py:540
  41.4 1.6 %collective-permute-start.11 = (f32[4,2,7,8,128]{4,3,2,1,0:T(8,128)S(1)}, f32[4,2,7,8,128]{4,3,2,1,0:T(8,128)S(1)}, u32[]{:S(2)}, u32[]{:S(2)}) collective-permute-start(f32[4,2,7,8,128]{4,3,2,1,0:T(8,128)S(1)} %pad_maximum_fusion.fetched), channel_id=1, source_target_pairs={{0,1},{1,0},{2,3},{3,2},{4,5},{5,4},{6,7},{7,6},{8,9},{9,8},{10,11... | collective-permute-start | bytes 688136 | tf_op jit(solution)/shard_map/ppermute | solution.py:521

commit v8 on v7

--- a/solution.py
+++ b/solution.py
@@ -86,9 +86,8 @@
 
 
 def share(levels):
-    size = lax.axis_size("grp")
-    assert size == 2
-    part = (levels + 1) // 2
+    assert lax.axis_size("grp") == 2 and levels % 2 == 0
+    part = levels // 2
     return lax.axis_index("grp") * (levels - part), part
 
 
@@ -152,8 +151,6 @@
     depth = [column(bottom, where).astype(jnp.float32) for where in (outer, inner)]
     between = jnp.minimum(*depth)
     along = [side_depths(d) for d in depth]
-    cross[VECTORS * levels] = depth[0]
-    mate[VECTORS * levels] = depth[1]
     pack_rim(sub, surface, bottom, mate_flow, levels)
 
     def body(k, carry):
@@ -193,75 +190,102 @@
     )
 
 
-def second_kernel(
-    levels, sub, raw, cross, mate, mate_raw, flow_in, mate_flow,
-    raw_far, cross_far, mate_far, mate_raw_far, mate_flow_far, flow_other,
-    merid, tracer, message, flow_far, powers,
+def halo_kernel(
+    levels, sub, own, raw, cross, mate, mate_raw, flow_in, mate_flow,
+    raw_far, mate_far, mate_raw_far, mate_flow_far, merid, *refs,
 ):
     outer, inner, sign = orientation()
     start, part = share(levels)
-    last = VECTORS * levels
-
-    def unpack(i, carry):
-        flow_far[start + i] = raw_far[VECTORS * levels + i]
-        flow_far[levels - part - start + i] = flow_other[i]
-        return carry
-
-    lax.fori_loop(0, part, unpack, 0, unroll=steps(part, 10))
-    powers_of_heights(levels, part, mate_flow, mate_flow_far, raw_far, powers)
-    near = [(raw, cross), (mate_raw, mate)]
-    far = [(raw_far, cross_far), (mate_raw_far, mate_far)]
-    depth = [cross[last], mate[last]]
-    beside = [jnp.minimum(depth[0], cross_far[last]), jnp.minimum(depth[1], mate_far[last])]
+    first = start if own else levels - part - start
+    if own:
+        done, base, weight, sums, powers = refs
+        powers_of_heights(levels, part, mate_flow, mate_flow_far, raw_far, powers)
+        flow_far = raw_far.at[pl.ds(VECTORS * levels, part)]
+    else:
+        flow_far, done, base, weight, sums = refs
+    near, far = (raw, mate_raw), (raw_far, mate_raw_far)
+    rim = levels + DEPTHS
+    depth = [mate_flow[rim + where] for where in (outer, inner)]
+    beside = [
+        jnp.minimum(depth[0], raw_far[VECTORS * levels + part + DEPTHS + inner]),
+        jnp.minimum(depth[1], mate_flow_far[rim + outer]),
+    ]
     between = jnp.minimum(*depth)
     along = [side_depths(d) for d in depth]
     zero = jnp.zeros_like(between)
 
-    def body(k, carry):
+    def body(i, carry):
+        k = first + i
         level = k.astype(jnp.float32)
         flow = [flow_in[k], mate_flow[k]]
-        beyond = [flow_far[k], mate_flow_far[k]]
+        beyond = [flow_far[i], mate_flow_far[k]]
         turn = [merid[k, pl.ds(where, sub, stride=2), :] for where in (outer, inner)]
         middle = face_pair(level, between, -sign * (flow[0] + flow[1]))
         edges = [
             face_pair(level, beside[c], (sign, -sign)[c] * (flow[c] + beyond[c])) for c in range(2)
         ]
         sides = [side_pairs(level, along[c], turn[c]) for c in range(2)]
-        totals, grams = list(carry[:4]), list(carry[4:])
-        done = []
+        weight[i] = edges[0][1]
+        totals, grams = list(carry[:VECTORS]), list(carry[VECTORS:])
+        fresh = []
         for v in range(VECTORS):
-            own, other = [], []
-            for c in range(2):
-                (first, kept), (first_far, kept_far) = near[c], far[c]
-                row = v * levels + k
-                flux = outflow(edges[c], first[row], first_far[row])
-                own.append(kept[row] - flux)
-                other.append(kept_far[row] + flux)
-            crossing = outflow(middle, *own)
-            fresh = []
-            for c, where in enumerate((outer, inner)):
-                gone = crossing if c == 0 else -crossing
-                value = (
-                    own[c]
-                    - outflow(edges[c], own[c], other[c])
-                    - gone
-                    - divergence_y(sides[c], own[c])
-                )
-                tracer[v, k, pl.ds(where, sub, stride=2), :] = value
-                totals[v * 2 + c] = totals[v * 2 + c] + value
+            row = v * levels + k
+            flux = [outflow(edges[c], near[c][row], far[c][row]) for c in range(2)]
+            outside, inside = cross[row] - flux[0], mate[row] - flux[1]
+            other = mate_far[row] + flux[1]
+            crossing = outflow(middle, outside, inside)
+            base[v, i] = (
+                outside
+                - outflow(edges[0], outside, flux[0])
+                - crossing
+                - divergence_y(sides[0], outside)
+            )
+            value = (
+                inside - outflow(edges[1], inside, other) + crossing - divergence_y(sides[1], inside)
+            )
+            done[v, i] = value
+            totals[v] = totals[v] + value
+            fresh.append(value)
+        return (*totals, *add_products(grams, *fresh))
+
+    found = lax.fori_loop(0, part, body, (zero,) * (VECTORS + 3), unroll=steps(part, 10))
+    for row, tile in enumerate(found):
+        sums[row] = tile
+
+
+def add_products(grams, a, b):
+    return [grams[0] + a * a, grams[1] + a * b, grams[2] + b * b]
+
+
+def second_kernel(
+    levels, sub, cross_far, *refs,
+):
+    outer, inner, _ = orientation()
+    start, part = share(levels)
+    parts = refs[:3], refs[3:6]
+    powers, mate_flow, column, message = refs[6:]
+    zero = jnp.zeros(powers.shape[-2:], jnp.float32)
+    carry = (zero,) * (VECTORS + 3)
+    for first, (base, weight, _) in zip((start, levels - part - start), parts):
+
+        def body(i, carry, first=first, base=base, weight=weight):
+            totals, fresh = [], []
+            for v in range(VECTORS):
+                value = base[v, i] - weight[i] * cross_far[v * levels + first + i]
+                column[v, first + i] = value
+                totals.append(carry[v] + value)
                 fresh.append(value)
-            done.append(fresh)
-        for c in range(2):
-            a, b = done[0][c], done[1][c]
-            grams = [grams[0] + a * a, grams[1] + a * b, grams[2] + b * b]
-        return (*totals, *grams)
-
-    sums = lax.fori_loop(0, levels, body, (zero,) * 7, unroll=steps(levels, 10))
+            return (*totals, *add_products(carry[VECTORS:], *fresh))
+
+        carry = lax.fori_loop(0, part, body, carry, unroll=steps(part, 10))
+    inside = [parts[0][2][row] + parts[1][2][row] for row in range(VECTORS + 3)]
     gain = STERIC_GAIN / levels
-    rows = list(sums[4:])
+    rows = [a + b for a, b in zip(carry[VECTORS:], inside[VECTORS:])]
     residual = []
     for v in range(VECTORS):
-        residual.append([gain * sums[v * 2 + c] + powers[POWERS, v, c] for c in range(2)])
+        residual.append(
+            [gain * total_of + powers[POWERS, v, c] for c, total_of in enumerate((carry[v], inside[v]))]
+        )
         for c, where in enumerate((outer, inner)):
             message[v * 2 + where] = residual[v][c]
 
@@ -356,8 +380,8 @@
 
 
 def third_kernel(
-    levels, sub, count, pair, fetched, fetched_mate, surface, tracer, tracer_out, surface_out, growth,
-    pole, residual, answer, image, depth, face_x, face_y, face_z, packed,
+    levels, sub, count, pair, fetched, fetched_mate, surface, column, done, done_other,
+    tracer_hbm, surface_out, growth, tracer, sems, pole, residual, answer, image, depth, face_x, face_y, face_z, packed,
 ):
     width = 2 * count
     me = lax.axis_index("lon")
@@ -417,7 +441,7 @@
         return tuple(sums)
 
     norm = [total(t) for t in over(start, none)]
-    share, left, aim = ([[v for _ in range(VECTORS)] for v in ([], [1.0], [1.0])])
+    taken, left, aim = ([[v for _ in range(VECTORS)] for v in ([], [1.0], [1.0])])
 
     def apply(d, carry):
         sums = list(carry)
@@ -431,7 +455,7 @@
     for iteration in range(ITERS):
         energy = [total(t) for t in over(apply, none)]
         size = [n / e for n, e in zip(norm, energy)]
-        share = [combine(s, z, a) for s, z, a in zip(share, size, aim)]
+        taken = [combine(s, z, a) for s, z, a in zip(taken, size, aim)]
         if iteration + 1 < ITERS:
 
             def advance(d, carry, size=size, first=iteration == 0):
@@ -471,7 +495,7 @@
 
     def heights_with(i, j):
         first = 3 + (i * VECTORS + j) * POWERS
-        return sum(c * t for c, t in zip(share[j], sums[first : first + POWERS]))
+        return sum(c * t for c, t in zip(taken[j], sums[first : first + POWERS]))
 
     cells = (levels + 1) * width * sub * LANES
     one, mix, two = (
@@ -484,13 +508,28 @@
     scale_two = jnp.sqrt(rest + EPSILON)
     over_one, over_two = 1.0 / scale_one, 1.0 / scale_two
 
-    def scale(k, carry):
-        unit = tracer[0, k] * over_one
-        tracer_out[0, k] = unit
-        tracer_out[1, k] = (tracer[1, k] - cross * unit) * over_two
-        return carry
-
-    lax.fori_loop(0, levels, scale, 0, unroll=steps(levels, 10))
+    outer, inner, _ = orientation()
+    begin, part = share(levels)
+    departures = []
+    for half, (first, source) in enumerate(((begin, done), (levels - part - begin, done_other))):
+
+        def scale(i, carry, first=first, source=source):
+            k = first + i
+            for where, one, two in (
+                (outer, column[0, k], column[1, k]),
+                (inner, source[0, i], source[1, i]),
+            ):
+                unit = one * over_one
+                place = pl.ds(where, sub, stride=2)
+                tracer[0, k, place, :] = unit
+                tracer[1, k, place, :] = (two - cross * unit) * over_two
+            return carry
+
+        lax.fori_loop(0, part, scale, 0, unroll=steps(part, 10))
+        rows = pl.ds(first, part)
+        departure = pltpu.make_async_copy(tracer.at[:, rows], tracer_hbm.at[:, rows], sems.at[half])
+        departure.start()
+        departures.append(departure)
     for c in range(2):
         x = 2 * me + c
         first, second = (
@@ -502,6 +541,8 @@
         surface_out[1, pl.ds(c, sub, stride=2), :] = (second - cross * unit) * over_two
     for i, value in enumerate((scale_one, cross, scale_two)):
         growth[i] = value[0, 0]
+    for departure in departures:
+        departure.wait()
 
 
 def tiled(array):
@@ -563,7 +604,7 @@
     both = pltpu.VMEM((vectors, levels, sub * 2, LANES), f32)
     tracer_pert, zonal_flow, merid_flow = map(tiled, (tracer_pert, zonal_flow, merid_flow))
     outward = [(i, (i + 1) % count if i % 2 else (i - 1) % count) for i in range(count)]
-    part = (levels + 1) // 2
+    part = levels // 2
     surface, bottom = tiled(surface_pert), tiled(bottom_level)
     edge_rows = VECTORS * levels + part + RIM
 
@@ -589,8 +630,8 @@
     cross, mate, raw, mate_raw, flow_in, mate_flow = pl.pallas_call(
         functools.partial(first_kernel, levels, sub),
         out_shape=(
-            shaped(VECTORS * levels + 1),
-            shaped(VECTORS * levels + 1),
+            shaped(VECTORS * levels),
+            shaped(VECTORS * levels),
             shaped(VECTORS * levels),
             shaped(VECTORS * levels),
             shaped(levels),
@@ -603,22 +644,38 @@
     )(edge, tracer_pert, zonal_flow, merid_flow, surface, bottom)
     cross_far = lax.ppermute(cross, "lon", outward)
     mate_far, mate_raw_far, mate_flow_far = (swap(x, 1) for x in (mate, mate_raw, mate_flow))
-    tracer, message = pl.pallas_call(
+    arrived = (
+        raw, cross, mate, mate_raw, flow_in, mate_flow,
+        edge_far, mate_far, mate_raw_far, mate_flow_far, merid_flow,
+    )
+    halves = (
+        shaped(vectors, part),
+        shaped(vectors, part),
+        shaped(part),
+        shaped(VECTORS + 3),
+    )
+
+    def halo(own, *operands):
+        shapes = halves + ((shaped(POWERS + 1, vectors, 2),) if own else ())
+        return pl.pallas_call(
+            functools.partial(halo_kernel, levels, sub, own),
+            out_shape=shapes,
+            in_specs=[vmem] * len(operands),
+            out_specs=(vmem,) * len(shapes),
+            compiler_params=params,
+            name="own_levels" if own else "other_levels",
+        )(*operands)
+
+    done, *near_half, powers = halo(True, *arrived)
+    done_other, *far_half = halo(False, *arrived, flow_other)
+    column, message = pl.pallas_call(
         functools.partial(second_kernel, levels, sub),
-        out_shape=(
-            jax.ShapeDtypeStruct((vectors, levels, sub * 2, LANES), f32),
-            shaped(BLOCKS),
-        ),
-        in_specs=[vmem] * 13,
+        out_shape=(shaped(vectors, levels), shaped(BLOCKS)),
+        in_specs=[vmem] * 9,
         out_specs=(vmem, vmem),
-        scratch_shapes=[held(levels), held(POWERS + 1, vectors, 2)],
         compiler_params=params,
-        name="both_steps",
-    )(
-        raw, cross, mate, mate_raw, flow_in, mate_flow,
-        edge_far, cross_far, mate_far, mate_raw_far, mate_flow_far, flow_other,
-        merid_flow,
-    )
+        name="outer_column",
+    )(cross_far, *near_half, *far_half, powers, mate_flow)
     tracer_vec, surface_vec, growth = pl.pallas_call(
         functools.partial(third_kernel, levels, sub, count),
         out_shape=(
@@ -626,9 +683,11 @@
             jax.ShapeDtypeStruct((vectors, sub * 2, LANES), f32),
             jax.ShapeDtypeStruct((3,), f32),
         ),
-        in_specs=[vmem] * 5,
-        out_specs=(vmem, vmem, pl.BlockSpec(memory_space=pltpu.SMEM)),
+        in_specs=[vmem] * 7,
+        out_specs=(hbm, vmem, pl.BlockSpec(memory_space=pltpu.SMEM)),
         scratch_shapes=[
+            both,
+            pltpu.SemaphoreType.DMA((2,)),
             held(vectors, width + 2),
             *[held(vectors, width)] * 3,
             held(width),
@@ -639,7 +698,7 @@
         ],
         compiler_params=pltpu.CompilerParams(vmem_limit_bytes=32 * 2**20),
         name="surface_and_scale",
-    )(*gather(message), surface, tracer)
+    )(*gather(message), surface, column, done, done_other)
     return (untiled(tracer_vec, 2), untiled(surface_vec, 2), growth)
 
 

time: 45.8 us -> 48.7 us (1.063)
  waiting for transfers between devices: 14.3 us -> 15.6 us
  Pallas kernels: 7.54 us -> 8.61 us
  starting transfers between devices: 21.9 us -> 22.4 us
    ppermute x1, waiting for transfers between devices: 3.24 us -> 0.1 us  [on_device(): cross_far = lax.ppermute(cross, 'lon', outward)]
    ppermute x4, waiting for transfers between devices: 4.46 us -> 7.32 us  [gather(): fetched.append(lax.ppermute(pair, 'lon', moves))]
    pallas_call x0 -> x2, Pallas kernels: none -> 1.87 us  [halo(): pl.pallas_call(functools.partial(halo_kernel, levels, sub, own), out_shap...]
    ppermute x1, waiting for transfers between devices: 0.01 us -> 1.71 us  [on_device(): lax.ppermute(edge_far[VECTORS * levels:edge_rows - RIM], 'grp', [(0, 1),...]
    pallas_call x1, Pallas kernels: 1.64 us -> 0.24 us  [on_device(): pl.pallas_call(functools.partial(second_kernel, levels, sub), out_shape=(...]
    ppermute x4, starting transfers between devices: 6.59 us -> 7.44 us  [gather(): fetched.append(lax.ppermute(pair, 'lon', moves))]
    pallas_call x1, Pallas kernels: 2.66 us -> 3.25 us  [on_device(): pl.pallas_call(functools.partial(third_kernel, levels, sub, count), out_s...]
    ppermute x5, starting transfers between devices: 7.69 us -> 7.16 us  [swap(): return lax.ppermute(array, 'lon', [(i, i ^ mask) for i in range(count)])]
  transfers between devices with their start and end apart: 12 -> 12, of which waited for: 7 -> 7; matrix products, arithmetic and copies ran while one was open for 0% -> 0% of each run, Pallas kernels for 3% -> 6%
where the time goes in v8:
time: 48.7 us; the launch traced here: 48.5 us
  starting transfers between devices  22.4 us (46%)
  waiting for transfers between devices  15.6 us (32%)
  Pallas kernels  8.61 us (18%)
  local copies, waits for them, and re-layouts  1.08 us (2%)
  between operations  0.77 us (2%)
    ppermute x4, starting transfers between devices, gather(): fetched.append(lax.ppermute(pair, 'lon', moves))  7.44 us
    ppermute x4, waiting for transfers between devices, gather(): fetched.append(lax.ppermute(pair, 'lon', moves))  7.32 us
    ppermute x5, starting transfers between devices, swap(): return lax.ppermute(array, 'lon', [(i, i ^ mask) for i in range(count)])  7.16 us
    ppermute x1, starting transfers between devices, on_device(): edge_far = lax.ppermute(edge, 'lon', outward)  5.51 us
    ppermute x1, waiting for transfers between devices, on_device(): edge_far = lax.ppermute(edge, 'lon', outward)  4.16 us
    pallas_call x1, Pallas kernels, on_device(): pl.pallas_call(functools.partial(third_kernel, levels, sub, count), out_s...  3.25 us
    ppermute x5, waiting for transfers between devices, swap(): return lax.ppermute(array, 'lon', [(i, i ^ mask) for i in range(count)])  2.34 us
    pallas_call x1, Pallas kernels, on_device(): pl.pallas_call(functools.partial(edge_kernel, levels, sub), out_shape=sha...  2.05 us
  transfers between devices with their start and end apart: 12, of which 7 were waited for; matrix products, arithmetic and copies ran while one was open for 0% of the time, Pallas kernels for 6%

profile of v8, /device:TPU:0, one launch (start us, length us, event | category | flops | bytes accessed | tf_op | source)
XLA Modules:
  0.0 48.5 jit_solution(6425216167482730372)
XLA Ops:
  0.6 0.0 copy-start
  0.6 0.0 copy-start.1
  0.7 0.0 copy-start.3
  0.7 0.0 copy-start.4
  0.7 0.0 copy-start.5
  0.7 2.0 %edge_columns.1.edge = f32[131,8,128]{2,1,0:T(8,128)} custom-call(f32[2,50,16,128]{3,2,1,0:T(8,128)} %bitcast.44, f32[50,16,128]{2,1,0:T(8,128)} %bitcast.46, f32[2,16,128]{2,1,0:T(8,128)} %bitcast.48, s32[16,128]{1,0:T(8,128)} %bitcast.51), custom_call_target="tpu_custom_call" | custom-call | tf_op jit(solution)/shard_map/edge_columns/pallas_call | solution.py:611
  2.7 5.5 %collective-permute-start.1 = (f32[131,8,128]{2,1,0:T(8,128)}, f32[131,8,128]{2,1,0:T(8,128)S(1)}, u32[]{:S(2)}, u32[]{:S(2)}) collective-permute-start(f32[131,8,128]{2,1,0:T(8,128)} %edge_columns.1.edge), channel_id=1, source_target_pairs={{0,15},{1,2},{2,1},{3,4},{4,3},{5,6},{6,5},{7,8},{8,7},{9,10},{10,... | collective-permute-start | bytes 1609736 | tf_op jit(solution)/shard_map/ppermute | solution.py:628
  8.2 0.0 copy-done
  8.2 0.0 copy-done.1
  8.3 0.0 copy-done.3
  8.3 0.0 copy-done.4
  8.3 0.0 copy-done.5
  8.3 0.0 copy-start.2
  8.3 1.0 %copy-done.2 = f32[131,8,128]{2,1,0:T(8,128)S(1)} copy-done((f32[131,8,128]{2,1,0:T(8,128)S(1)}, f32[131,8,128]{2,1,0:T(8,128)}, u32[]{:S(2)}) %copy-start.2) | copy-done | bytes 536600
  9.3 1.2 %partial_step.1 = (f32[100,8,128]{2,1,0:T(8,128)S(1)}, f32[100,8,128]{2,1,0:T(8,128)S(1)}, f32[100,8,128]{2,1,0:T(8,128)S(1)}, f32[100,8,128]{2,1,0:T(8,128)S(1)...) custom-call(f32[131,8,128]{2,1,0:T(8,128)S(1)} %copy-done.2, f32[2,50,16,128]{3,2,1,0:T(8,128)S(1)} %bitcast.45, ...), custom_call_target="tpu_custom_call" | custom-call | tf_op jit(solution)/shard_map/partial_step/pallas_call | solution.py:630
  10.5 0.1 collective-permute-start.2
  10.6 0.5 %collective-permute-start.3 = (f32[100,8,128]{2,1,0:T(8,128)S(1)}, f32[100,8,128]{2,1,0:T(8,128)S(1)}, u32[]{:S(2)}, u32[]{:S(2)}) collective-permute-start(f32[100,8,128]{2,1,0:T(8,128)S(1)} %get-tuple-element.26.mate_raw), channel_id=1, source_target_pairs={{0,1},{1,0},{2,3},{3,2},{4,5},{5,4},{6,7},{7,6},{8,9},{9,8},{10,11... | collective-permute-start | bytes 1228808 | tf_op jit(solution)/shard_map/ppermute | solution.py:562
  11.1 0.3 collective-permute-start
  11.4 0.0 collective-permute-start.4
  11.4 4.2 %collective-permute-done.1.raw_far = f32[131,8,128]{2,1,0:T(8,128)S(1)} collective-permute-done((f32[131,8,128]{2,1,0:T(8,128)}, f32[131,8,128]{2,1,0:T(8,128)S(1)}, u32[]{:S(2)}, u32[]{:S(2)}) %collective-permute-start.1) | collective-permute-done | bytes 536608 | tf_op jit(solution)/shard_map/ppermute | solution.py:628
  15.6 2.0 %collective-permute-start.5 = (f32[25,8,128]{2,1,0:T(8,128)S(1)}, f32[25,8,128]{2,1,0:T(8,128)S(1)}, u32[]{:S(2)}, u32[]{:S(2)}) collective-permute-start(f32[25,8,128]{2,1,0:T(8,128)S(1)} %slice.4), channel_id=1, source_target_pairs={{0,16},{16,0},{1,17},{17,1},{2,18},{18,2},{3,19},{19,3},{4,20},{20... | collective-permute-start | bytes 307208 | tf_op jit(solution)/shard_map/ppermute | solution.py:629
  17.6 0.0 collective-permute-done.4.mate_flow_far
  17.6 0.0 collective-permute-done.2.mate_far
  17.6 0.0 collective-permute-done.3.mate_raw_far
  17.6 1.0 %own_levels.1 = (f32[2,25,8,128]{3,2,1,0:T(8,128)S(1)}, f32[2,25,8,128]{3,2,1,0:T(8,128)S(1)}, f32[25,8,128]{2,1,0:T(8,128)S(1)}, f32[5,8,128]{2,1,0:T(8,128)S(1)}, f32[4,2,2,8,128]{4,3,2,1,0:T(8,128)S(1)}) custom-call(f32[100,8,128]{2,1,0:T(8,128)S(1)} %get-tuple-element.24.raw, f32[100,8,128]{2,1,0:T(8,128)S(1)} %get-tuple-element.23.cross, ...), custom_call_target="tpu_custom_call" | custom-call | tf_op jit(solution)/shard_map/own_levels/pallas_call | solution.py:660
  18.6 1.7 %collective-permute-done.5.refs_0_ = f32[25,8,128]{2,1,0:T(8,128)S(1)} collective-permute-done((f32[25,8,128]{2,1,0:T(8,128)S(1)}, f32[25,8,128]{2,1,0:T(8,128)S(1)}, u32[]{:S(2)}, u32[]{:S(2)}) %collective-permute-start.5) | collective-permute-done | bytes 102432 | tf_op jit(solution)/shard_map/ppermute | solution.py:629
  20.3 0.9 %other_levels.1 = (f32[2,25,8,128]{3,2,1,0:T(8,128)S(1)}, f32[2,25,8,128]{3,2,1,0:T(8,128)S(1)}, f32[25,8,128]{2,1,0:T(8,128)S(1)}, f32[5,8,128]{2,1,0:T(8,128)S(1)}) custom-call(f32[100,8,128]{2,1,0:T(8,128)S(1)} %get-tuple-element.24.raw, f32[100,8,128]{2,1,0:T(8,128)S(1)} %get-tuple-element.23.cross, f32[100,8,128]{2,1,0:T(8,128)S(1)} %get-tuple-element.25.mate, ...), custom_call_target="tpu_custom_call" | custom-call | tf_op jit(solution)/shard_map/other_levels/pallas_call | solution.py:660
  21.2 0.1 collective-permute-done.cross_far
  21.3 0.2 outer_column.1
  21.5 6.5 %collective-permute-start.6 = (f32[7,8,128]{2,1,0:T(8,128)S(1)}, f32[7,8,128]{2,1,0:T(8,128)S(1)}, u32[]{:S(2)}, u32[]{:S(2)}) collective-permute-start(f32[7,8,128]{2,1,0:T(8,128)S(1)} %get-tuple-element.36), channel_id=1, source_target_pairs={{0,1},{1,0},{2,3},{3,2},{4,5},{5,4},{6,7},{7,6},{8,9},{9,8},{10,11... | collective-permute-start | bytes 86024 | tf_op jit(solution)/shard_map/ppermute | solution.py:562
  28.0 0.9 %collective-permute-done.6 = f32[7,8,128]{2,1,0:T(8,128)S(1)} collective-permute-done((f32[7,8,128]{2,1,0:T(8,128)S(1)}, f32[7,8,128]{2,1,0:T(8,128)S(1)}, u32[]{:S(2)}, u32[]{:S(2)}) %collective-permute-start.6) | collective-permute-done | bytes 28704 | tf_op jit(solution)/shard_map/ppermute | solution.py:562
  28.9 0.7 %collective-permute-start.7 = (f32[2,7,8,128]{3,2,1,0:T(8,128)S(1)}, f32[2,7,8,128]{3,2,1,0:T(8,128)S(1)}, u32[]{:S(2)}, u32[]{:S(2)}) collective-permute-start(f32[2,7,8,128]{3,2,1,0:T(8,128)S(1)} %pad_maximum_fusion.1.pair), channel_id=1, source_target_pairs={{1,3},{3,1},{5,7},{7,5},{9,11},{11,9},{13,15},{15,13},{17,19},{19,... | collective-permute-start | bytes 172040 | tf_op jit(solution)/shard_map/ppermute | solution.py:581
  29.6 4.2 %collective-permute-start.8 = (f32[2,7,8,128]{3,2,1,0:T(8,128)S(1)}, f32[2,7,8,128]{3,2,1,0:T(8,128)S(1)}, u32[]{:S(2)}, u32[]{:S(2)}) collective-permute-start(f32[2,7,8,128]{3,2,1,0:T(8,128)S(1)} %pad_maximum_fusion.1.pair), channel_id=1, source_target_pairs={{0,6},{1,5},{2,4},{3,7},{4,2},{5,1},{6,0},{7,3},{8,14},{9,13},{10,... | collective-permute-start | bytes 172040 | tf_op jit(solution)/shard_map/ppermute | solution.py:581
  33.8 2.6 %collective-permute-start.9 = (f32[2,7,8,128]{3,2,1,0:T(8,128)S(1)}, f32[2,7,8,128]{3,2,1,0:T(8,128)S(1)}, u32[]{:S(2)}, u32[]{:S(2)}) collective-permute-start(f32[2,7,8,128]{3,2,1,0:T(8,128)S(1)} %pad_maximum_fusion.1.pair), channel_id=1, source_target_pairs={{0,8},{1,11},{2,10},{3,9},{4,12},{5,15},{6,14},{7,13},{8,0},{9,3},... | collective-permute-start | bytes 172040 | tf_op jit(solution)/shard_map/ppermute | solution.py:581
  36.4 0.0 collective-permute-start.10
  36.4 0.0 collective-permute-done.7
  36.4 0.0 collective-permute-done.8
  36.4 4.7 %collective-permute-done.9 = f32[2,7,8,128]{3,2,1,0:T(8,128)S(1)} collective-permute-done((f32[2,7,8,128]{3,2,1,0:T(8,128)S(1)}, f32[2,7,8,128]{3,2,1,0:T(8,128)S(1)}, u32[]{:S(2)}, u32[]{:S(2)}) %collective-permute-start.9) | collective-permute-done | bytes 57376 | tf_op jit(solution)/shard_map/ppermute | solution.py:581
  41.0 2.6 %collective-permute-done.10 = f32[2,7,8,128]{3,2,1,0:T(8,128)S(1)} collective-permute-done((f32[2,7,8,128]{3,2,1,0:T(8,128)S(1)}, f32[2,7,8,128]{3,2,1,0:T(8,128)S(1)}, u32[]{:S(2)}, u32[]{:S(2)}) %collective-permute-start.10) | collective-permute-done | bytes 57376 | tf_op jit(solution)/shard_map/ppermute | solution.py:581
  43.7 0.1 collective-permute-start.11
  43.8 1.5 %collective-permute-done.11.fetched_mate = f32[4,2,7,8,128]{4,3,2,1,0:T(8,128)S(1)} collective-permute-done((f32[4,2,7,8,128]{4,3,2,1,0:T(8,128)S(1)}, f32[4,2,7,8,128]{4,3,2,1,0:T(8,128)S(1)}, u32[]{:S(2)}, u32[]{:S(2)}) %collective-permute-start.11) | collective-permute-done | bytes 229408 | tf_op jit(solution)/shard_map/ppermute | solution.py:562
  45.3 3.3 %surface_and_scale.1 = (f32[2,50,16,128]{3,2,1,0:T(8,128)}, f32[2,16,128]{2,1,0:T(8,128)}, f32[3]{0:T(128)}) custom-call(f32[2,7,8,128]{3,2,1,0:T(8,128)S(1)} %pad_maximum_fusion.1.pair, f32[4,2,7,8,128]{4,3,2,1,0:T(8,128)S(1)} %pad_maximum_fusion.fetched, f32[4,2,7,8,128]{4,3,2,1,0:T(8,128)S(1)} %collective-permute-done.11.fetched_mate, ...), custom_call_target="tpu_custom_call" | custom-call | tf_op jit(solution)/shard_map/surface_and_scale/pallas_call | solution.py:679
  (3 shorter events, 0.0 us)
Async XLA Ops:
  0.6 7.6 %copy-start = (f32[50,2,1024]{2,1,0:T(2,128)S(1)}, f32[50,2,1024]{2,1,0:T(2,128)}, u32[]{:S(2)}) copy-start(f32[50,2,1024]{2,1,0:T(2,128)} %param.8) | copy-start | bytes 1228804
  0.6 7.6 %copy-start.1 = (f32[2,50,2,1024]{3,2,1,0:T(2,128)S(1)}, f32[2,50,2,1024]{3,2,1,0:T(2,128)}, u32[]{:S(2)}) copy-start(f32[2,50,2,1024]{3,2,1,0:T(2,128)} %param.5) | copy-start | bytes 2457604
  0.7 7.6 %copy-start.3 = (f32[50,2,1024]{2,1,0:T(2,128)S(1)}, f32[50,2,1024]{2,1,0:T(2,128)}, u32[]{:S(2)}) copy-start(f32[50,2,1024]{2,1,0:T(2,128)} %param.7) | copy-start | bytes 1228804
  0.7 7.6 %copy-start.4 = (f32[2,2,1024]{2,1,0:T(2,128)S(1)}, f32[2,2,1024]{2,1,0:T(2,128)}, u32[]{:S(2)}) copy-start(f32[2,2,1024]{2,1,0:T(2,128)} %param.6) | copy-start | bytes 49156
  0.7 7.6 %copy-start.5 = (s32[2,1024]{1,0:T(2,128)S(1)}, s32[2,1024]{1,0:T(2,128)}, u32[]{:S(2)}) copy-start(s32[2,1024]{1,0:T(2,128)} %param.9) | copy-start | bytes 24580
  2.7 12.8 %collective-permute-start.1 = (f32[131,8,128]{2,1,0:T(8,128)}, f32[131,8,128]{2,1,0:T(8,128)S(1)}, u32[]{:S(2)}, u32[]{:S(2)}) collective-permute-start(f32[131,8,128]{2,1,0:T(8,128)} %edge_columns.1.edge), channel_id=1, source_target_pairs={{0,15},{1,2},{2,1},{3,4},{4,3},{5,6},{6,5},{7,8},{8,7},{9,10},{10,... | collective-permute-start | bytes 1609736 | tf_op jit(solution)/shard_map/ppermute | solution.py:628
  8.3 1.1 %copy-start.2 = (f32[131,8,128]{2,1,0:T(8,128)S(1)}, f32[131,8,128]{2,1,0:T(8,128)}, u32[]{:S(2)}) copy-start(f32[131,8,128]{2,1,0:T(8,128)} %edge_columns.1.edge) | copy-start | bytes 1609732
  10.5 7.0 %collective-permute-start.2 = (f32[100,8,128]{2,1,0:T(8,128)S(1)}, f32[100,8,128]{2,1,0:T(8,128)S(1)}, u32[]{:S(2)}, u32[]{:S(2)}) collective-permute-start(f32[100,8,128]{2,1,0:T(8,128)S(1)} %get-tuple-element.25.mate), channel_id=1, source_target_pairs={{0,1},{1,0},{2,3},{3,2},{4,5},{5,4},{6,7},{7,6},{8,9},{9,8},{10,11... | collective-permute-start | bytes 1228808 | tf_op jit(solution)/shard_map/ppermute | solution.py:562
  10.6 7.0 %collective-permute-start.3 = (f32[100,8,128]{2,1,0:T(8,128)S(1)}, f32[100,8,128]{2,1,0:T(8,128)S(1)}, u32[]{:S(2)}, u32[]{:S(2)}) collective-permute-start(f32[100,8,128]{2,1,0:T(8,128)S(1)} %get-tuple-element.26.mate_raw), channel_id=1, source_target_pairs={{0,1},{1,0},{2,3},{3,2},{4,5},{5,4},{6,7},{7,6},{8,9},{9,8},{10,11... | collective-permute-start | bytes 1228808 | tf_op jit(solution)/shard_map/ppermute | solution.py:562
  11.1 10.2 %collective-permute-start = (f32[100,8,128]{2,1,0:T(8,128)S(1)}, f32[100,8,128]{2,1,0:T(8,128)S(1)}, u32[]{:S(2)}, u32[]{:S(2)}) collective-permute-start(f32[100,8,128]{2,1,0:T(8,128)S(1)} %get-tuple-element.23.cross), channel_id=1, source_target_pairs={{0,15},{1,2},{2,1},{3,4},{4,3},{5,6},{6,5},{7,8},{8,7},{9,10},{10,... | collective-permute-start | bytes 1228808 | tf_op jit(solution)/shard_map/ppermute | solution.py:645
  11.4 6.2 %collective-permute-start.4 = (f32[56,8,128]{2,1,0:T(8,128)S(1)}, f32[56,8,128]{2,1,0:T(8,128)S(1)}, u32[]{:S(2)}, u32[]{:S(2)}) collective-permute-start(f32[56,8,128]{2,1,0:T(8,128)S(1)} %get-tuple-element.28.mate_flow.refs_7_), channel_id=1, source_target_pairs={{0,1},{1,0},{2,3},{3,2},{4,5},{5,4},{6,7},{7,6},{8,9},{9,8},{10,11... | collective-permute-start | bytes 688136 | tf_op jit(solution)/shard_map/ppermute | solution.py:562
  15.6 4.7 %collective-permute-start.5 = (f32[25,8,128]{2,1,0:T(8,128)S(1)}, f32[25,8,128]{2,1,0:T(8,128)S(1)}, u32[]{:S(2)}, u32[]{:S(2)}) collective-permute-start(f32[25,8,128]{2,1,0:T(8,128)S(1)} %slice.4), channel_id=1, source_target_pairs={{0,16},{16,0},{1,17},{17,1},{2,18},{18,2},{3,19},{19,3},{4,20},{20... | collective-permute-start | bytes 307208 | tf_op jit(solution)/shard_map/ppermute | solution.py:629
  21.5 7.4 %collective-permute-start.6 = (f32[7,8,128]{2,1,0:T(8,128)S(1)}, f32[7,8,128]{2,1,0:T(8,128)S(1)}, u32[]{:S(2)}, u32[]{:S(2)}) collective-permute-start(f32[7,8,128]{2,1,0:T(8,128)S(1)} %get-tuple-element.36), channel_id=1, source_target_pairs={{0,1},{1,0},{2,3},{3,2},{4,5},{5,4},{6,7},{7,6},{8,9},{9,8},{10,11... | collective-permute-start | bytes 86024 | tf_op jit(solution)/shard_map/ppermute | solution.py:562
  28.9 7.5 %collective-permute-start.7 = (f32[2,7,8,128]{3,2,1,0:T(8,128)S(1)}, f32[2,7,8,128]{3,2,1,0:T(8,128)S(1)}, u32[]{:S(2)}, u32[]{:S(2)}) collective-permute-start(f32[2,7,8,128]{3,2,1,0:T(8,128)S(1)} %pad_maximum_fusion.1.pair), channel_id=1, source_target_pairs={{1,3},{3,1},{5,7},{7,5},{9,11},{11,9},{13,15},{15,13},{17,19},{19,... | collective-permute-start | bytes 172040 | tf_op jit(solution)/shard_map/ppermute | solution.py:581
  29.6 6.8 %collective-permute-start.8 = (f32[2,7,8,128]{3,2,1,0:T(8,128)S(1)}, f32[2,7,8,128]{3,2,1,0:T(8,128)S(1)}, u32[]{:S(2)}, u32[]{:S(2)}) collective-permute-start(f32[2,7,8,128]{3,2,1,0:T(8,128)S(1)} %pad_maximum_fusion.1.pair), channel_id=1, source_target_pairs={{0,6},{1,5},{2,4},{3,7},{4,2},{5,1},{6,0},{7,3},{8,14},{9,13},{10,... | collective-permute-start | bytes 172040 | tf_op jit(solution)/shard_map/ppermute | solution.py:581
  33.8 7.3 %collective-permute-start.9 = (f32[2,7,8,128]{3,2,1,0:T(8,128)S(1)}, f32[2,7,8,128]{3,2,1,0:T(8,128)S(1)}, u32[]{:S(2)}, u32[]{:S(2)}) collective-permute-start(f32[2,7,8,128]{3,2,1,0:T(8,128)S(1)} %pad_maximum_fusion.1.pair), channel_id=1, source_target_pairs={{0,8},{1,11},{2,10},{3,9},{4,12},{5,15},{6,14},{7,13},{8,0},{9,3},... | collective-permute-start | bytes 172040 | tf_op jit(solution)/shard_map/ppermute | solution.py:581
  36.4 7.3 %collective-permute-start.10 = (f32[2,7,8,128]{3,2,1,0:T(8,128)S(1)}, f32[2,7,8,128]{3,2,1,0:T(8,128)S(1)}, u32[]{:S(2)}, u32[]{:S(2)}) collective-permute-start(f32[2,7,8,128]{3,2,1,0:T(8,128)S(1)} %pad_maximum_fusion.1.pair), channel_id=1, source_target_pairs={{0,14},{1,13},{2,12},{3,15},{4,10},{5,9},{6,8},{7,11},{8,6},{9,5},... | collective-permute-start | bytes 172040 | tf_op jit(solution)/shard_map/ppermute | solution.py:581
  43.7 1.6 %collective-permute-start.11 = (f32[4,2,7,8,128]{4,3,2,1,0:T(8,128)S(1)}, f32[4,2,7,8,128]{4,3,2,1,0:T(8,128)S(1)}, u32[]{:S(2)}, u32[]{:S(2)}) collective-permute-start(f32[4,2,7,8,128]{4,3,2,1,0:T(8,128)S(1)} %pad_maximum_fusion.fetched), channel_id=1, source_target_pairs={{0,1},{1,0},{2,3},{3,2},{4,5},{5,4},{6,7},{7,6},{8,9},{9,8},{10,11... | collective-permute-start | bytes 688136 | tf_op jit(solution)/shard_map/ppermute | solution.py:562

commit v9 on v8

--- a/solution.py
+++ b/solution.py
@@ -569,7 +569,7 @@
         lists[core].append(mask)
         loads[core] += mask % 2 + mask // 2
     longest = max(map(len, lists))
-    return list(zip(*([0] * (longest - len(one)) + one[::-1] for one in lists)))
+    return list(zip(*(one + [0] * (longest - len(one)) for one in lists)))
 
 
 def gather(block):

time: 48.7 us -> 45.9 us (0.943)
  waiting for transfers between devices: 15.6 us -> 12.7 us
    ppermute x4, waiting for transfers between devices: 7.32 us -> 4.47 us  [gather(): fetched.append(lax.ppermute(pair, 'lon', moves))]
  transfers between devices with their start and end apart: 12 -> 12, of which waited for: 7 -> 8; matrix products, arithmetic and copies ran while one was open for 0% -> 0% of each run, Pallas kernels for 6% -> 7%
where the time goes in v9:
time: 45.9 us; the launch traced here: 45.7 us
  starting transfers between devices  22.4 us (49%)
  waiting for transfers between devices  12.7 us (28%)
  Pallas kernels  8.62 us (19%)
  local copies, waits for them, and re-layouts  1.08 us (2%)
  between operations  0.76 us (2%)
    ppermute x4, starting transfers between devices, gather(): fetched.append(lax.ppermute(pair, 'lon', moves))  7.44 us
    ppermute x5, starting transfers between devices, swap(): return lax.ppermute(array, 'lon', [(i, i ^ mask) for i in range(count)])  7.21 us
    ppermute x1, starting transfers between devices, on_device(): edge_far = lax.ppermute(edge, 'lon', outward)  5.51 us
    ppermute x4, waiting for transfers between devices, gather(): fetched.append(lax.ppermute(pair, 'lon', moves))  4.47 us
    ppermute x1, waiting for transfers between devices, on_device(): edge_far = lax.ppermute(edge, 'lon', outward)  4.16 us
    pallas_call x1, Pallas kernels, on_device(): pl.pallas_call(functools.partial(third_kernel, levels, sub, count), out_s...  3.26 us
    ppermute x5, waiting for transfers between devices, swap(): return lax.ppermute(array, 'lon', [(i, i ^ mask) for i in range(count)])  2.3 us
    pallas_call x1, Pallas kernels, on_device(): pl.pallas_call(functools.partial(edge_kernel, levels, sub), out_shape=sha...  2.05 us
  transfers between devices with their start and end apart: 12, of which 8 were waited for; matrix products, arithmetic and copies ran while one was open for 0% of the time, Pallas kernels for 7%

profile of v9, /device:TPU:0, one launch (start us, length us, event | category | flops | bytes accessed | tf_op | source)
XLA Modules:
  0.0 45.7 jit_solution(7789173711794556468)
XLA Ops:
  0.6 0.0 copy-start
  0.6 0.0 copy-start.1
  0.7 0.0 copy-start.3
  0.7 0.0 copy-start.4
  0.7 0.0 copy-start.5
  0.7 2.0 %edge_columns.1.edge = f32[131,8,128]{2,1,0:T(8,128)} custom-call(f32[2,50,16,128]{3,2,1,0:T(8,128)} %bitcast.44, f32[50,16,128]{2,1,0:T(8,128)} %bitcast.46, f32[2,16,128]{2,1,0:T(8,128)} %bitcast.48, s32[16,128]{1,0:T(8,128)} %bitcast.51), custom_call_target="tpu_custom_call" | custom-call | tf_op jit(solution)/shard_map/edge_columns/pallas_call | solution.py:611
  2.7 5.5 %collective-permute-start.1 = (f32[131,8,128]{2,1,0:T(8,128)}, f32[131,8,128]{2,1,0:T(8,128)S(1)}, u32[]{:S(2)}, u32[]{:S(2)}) collective-permute-start(f32[131,8,128]{2,1,0:T(8,128)} %edge_columns.1.edge), channel_id=1, source_target_pairs={{0,15},{1,2},{2,1},{3,4},{4,3},{5,6},{6,5},{7,8},{8,7},{9,10},{10,... | collective-permute-start | bytes 1609736 | tf_op jit(solution)/shard_map/ppermute | solution.py:628
  8.2 0.0 copy-done
  8.2 0.0 copy-done.1
  8.3 0.0 copy-done.3
  8.3 0.0 copy-done.4
  8.3 0.0 copy-done.5
  8.3 0.0 copy-start.2
  8.3 1.0 %copy-done.2 = f32[131,8,128]{2,1,0:T(8,128)S(1)} copy-done((f32[131,8,128]{2,1,0:T(8,128)S(1)}, f32[131,8,128]{2,1,0:T(8,128)}, u32[]{:S(2)}) %copy-start.2) | copy-done | bytes 536600
  9.3 1.2 %partial_step.1 = (f32[100,8,128]{2,1,0:T(8,128)S(1)}, f32[100,8,128]{2,1,0:T(8,128)S(1)}, f32[100,8,128]{2,1,0:T(8,128)S(1)}, f32[100,8,128]{2,1,0:T(8,128)S(1)...) custom-call(f32[131,8,128]{2,1,0:T(8,128)S(1)} %copy-done.2, f32[2,50,16,128]{3,2,1,0:T(8,128)S(1)} %bitcast.45, ...), custom_call_target="tpu_custom_call" | custom-call | tf_op jit(solution)/shard_map/partial_step/pallas_call | solution.py:630
  10.5 0.1 collective-permute-start.2
  10.6 0.5 %collective-permute-start.3 = (f32[100,8,128]{2,1,0:T(8,128)S(1)}, f32[100,8,128]{2,1,0:T(8,128)S(1)}, u32[]{:S(2)}, u32[]{:S(2)}) collective-permute-start(f32[100,8,128]{2,1,0:T(8,128)S(1)} %get-tuple-element.26.mate_raw), channel_id=1, source_target_pairs={{0,1},{1,0},{2,3},{3,2},{4,5},{5,4},{6,7},{7,6},{8,9},{9,8},{10,11... | collective-permute-start | bytes 1228808 | tf_op jit(solution)/shard_map/ppermute | solution.py:562
  11.1 0.3 collective-permute-start
  11.4 0.0 collective-permute-start.4
  11.4 4.2 %collective-permute-done.1.raw_far = f32[131,8,128]{2,1,0:T(8,128)S(1)} collective-permute-done((f32[131,8,128]{2,1,0:T(8,128)}, f32[131,8,128]{2,1,0:T(8,128)S(1)}, u32[]{:S(2)}, u32[]{:S(2)}) %collective-permute-start.1) | collective-permute-done | bytes 536608 | tf_op jit(solution)/shard_map/ppermute | solution.py:628
  15.6 2.0 %collective-permute-start.5 = (f32[25,8,128]{2,1,0:T(8,128)S(1)}, f32[25,8,128]{2,1,0:T(8,128)S(1)}, u32[]{:S(2)}, u32[]{:S(2)}) collective-permute-start(f32[25,8,128]{2,1,0:T(8,128)S(1)} %slice.4), channel_id=1, source_target_pairs={{0,16},{16,0},{1,17},{17,1},{2,18},{18,2},{3,19},{19,3},{4,20},{20... | collective-permute-start | bytes 307208 | tf_op jit(solution)/shard_map/ppermute | solution.py:629
  17.6 0.0 collective-permute-done.4.mate_flow_far
  17.6 0.0 collective-permute-done.2.mate_far
  17.6 0.0 collective-permute-done.3.mate_raw_far
  17.6 1.0 %own_levels.1 = (f32[2,25,8,128]{3,2,1,0:T(8,128)S(1)}, f32[2,25,8,128]{3,2,1,0:T(8,128)S(1)}, f32[25,8,128]{2,1,0:T(8,128)S(1)}, f32[5,8,128]{2,1,0:T(8,128)S(1)}, f32[4,2,2,8,128]{4,3,2,1,0:T(8,128)S(1)}) custom-call(f32[100,8,128]{2,1,0:T(8,128)S(1)} %get-tuple-element.24.raw, f32[100,8,128]{2,1,0:T(8,128)S(1)} %get-tuple-element.23.cross, ...), custom_call_target="tpu_custom_call" | custom-call | tf_op jit(solution)/shard_map/own_levels/pallas_call | solution.py:660
  18.6 1.7 %collective-permute-done.5.refs_0_ = f32[25,8,128]{2,1,0:T(8,128)S(1)} collective-permute-done((f32[25,8,128]{2,1,0:T(8,128)S(1)}, f32[25,8,128]{2,1,0:T(8,128)S(1)}, u32[]{:S(2)}, u32[]{:S(2)}) %collective-permute-start.5) | collective-permute-done | bytes 102432 | tf_op jit(solution)/shard_map/ppermute | solution.py:629
  20.3 0.9 %other_levels.1 = (f32[2,25,8,128]{3,2,1,0:T(8,128)S(1)}, f32[2,25,8,128]{3,2,1,0:T(8,128)S(1)}, f32[25,8,128]{2,1,0:T(8,128)S(1)}, f32[5,8,128]{2,1,0:T(8,128)S(1)}) custom-call(f32[100,8,128]{2,1,0:T(8,128)S(1)} %get-tuple-element.24.raw, f32[100,8,128]{2,1,0:T(8,128)S(1)} %get-tuple-element.23.cross, f32[100,8,128]{2,1,0:T(8,128)S(1)} %get-tuple-element.25.mate, ...), custom_call_target="tpu_custom_call" | custom-call | tf_op jit(solution)/shard_map/other_levels/pallas_call | solution.py:660
  21.2 0.1 collective-permute-done.cross_far
  21.3 0.2 outer_column.1
  21.5 6.5 %collective-permute-start.6 = (f32[7,8,128]{2,1,0:T(8,128)S(1)}, f32[7,8,128]{2,1,0:T(8,128)S(1)}, u32[]{:S(2)}, u32[]{:S(2)}) collective-permute-start(f32[7,8,128]{2,1,0:T(8,128)S(1)} %get-tuple-element.36), channel_id=1, source_target_pairs={{0,1},{1,0},{2,3},{3,2},{4,5},{5,4},{6,7},{7,6},{8,9},{9,8},{10,11... | collective-permute-start | bytes 86024 | tf_op jit(solution)/shard_map/ppermute | solution.py:562
  28.0 0.9 %collective-permute-done.6 = f32[7,8,128]{2,1,0:T(8,128)S(1)} collective-permute-done((f32[7,8,128]{2,1,0:T(8,128)S(1)}, f32[7,8,128]{2,1,0:T(8,128)S(1)}, u32[]{:S(2)}, u32[]{:S(2)}) %collective-permute-start.6) | collective-permute-done | bytes 28704 | tf_op jit(solution)/shard_map/ppermute | solution.py:562
  28.9 6.2 %collective-permute-start.7 = (f32[2,7,8,128]{3,2,1,0:T(8,128)S(1)}, f32[2,7,8,128]{3,2,1,0:T(8,128)S(1)}, u32[]{:S(2)}, u32[]{:S(2)}) collective-permute-start(f32[2,7,8,128]{3,2,1,0:T(8,128)S(1)} %pad_maximum_fusion.1.pair), channel_id=1, source_target_pairs={{0,14},{1,13},{2,12},{3,15},{4,10},{5,9},{6,8},{7,11},{8,6},{9,5},... | collective-permute-start | bytes 172040 | tf_op jit(solution)/shard_map/ppermute | solution.py:581
  35.1 0.0 collective-permute-start.8
  35.1 0.6 %collective-permute-start.9 = (f32[2,7,8,128]{3,2,1,0:T(8,128)S(1)}, f32[2,7,8,128]{3,2,1,0:T(8,128)S(1)}, u32[]{:S(2)}, u32[]{:S(2)}) collective-permute-start(f32[2,7,8,128]{3,2,1,0:T(8,128)S(1)} %pad_maximum_fusion.1.pair), channel_id=1, source_target_pairs={{0,6},{1,5},{2,4},{3,7},{4,2},{5,1},{6,0},{7,3},{8,14},{9,13},{10,... | collective-permute-start | bytes 172040 | tf_op jit(solution)/shard_map/ppermute | solution.py:581
  35.7 0.7 %collective-permute-start.10 = (f32[2,7,8,128]{3,2,1,0:T(8,128)S(1)}, f32[2,7,8,128]{3,2,1,0:T(8,128)S(1)}, u32[]{:S(2)}, u32[]{:S(2)}) collective-permute-start(f32[2,7,8,128]{3,2,1,0:T(8,128)S(1)} %pad_maximum_fusion.1.pair), channel_id=1, source_target_pairs={{1,3},{3,1},{5,7},{7,5},{9,11},{11,9},{13,15},{15,13},{17,19},{19,... | collective-permute-start | bytes 172040 | tf_op jit(solution)/shard_map/ppermute | solution.py:581
  36.4 1.5 %collective-permute-done.7 = f32[2,7,8,128]{3,2,1,0:T(8,128)S(1)} collective-permute-done((f32[2,7,8,128]{3,2,1,0:T(8,128)S(1)}, f32[2,7,8,128]{3,2,1,0:T(8,128)S(1)}, u32[]{:S(2)}, u32[]{:S(2)}) %collective-permute-start.7) | collective-permute-done | bytes 57376 | tf_op jit(solution)/shard_map/ppermute | solution.py:581
  37.9 2.4 %collective-permute-done.8 = f32[2,7,8,128]{3,2,1,0:T(8,128)S(1)} collective-permute-done((f32[2,7,8,128]{3,2,1,0:T(8,128)S(1)}, f32[2,7,8,128]{3,2,1,0:T(8,128)S(1)}, u32[]{:S(2)}, u32[]{:S(2)}) %collective-permute-start.8) | collective-permute-done | bytes 57376 | tf_op jit(solution)/shard_map/ppermute | solution.py:581
  40.3 0.5 %collective-permute-done.9 = f32[2,7,8,128]{3,2,1,0:T(8,128)S(1)} collective-permute-done((f32[2,7,8,128]{3,2,1,0:T(8,128)S(1)}, f32[2,7,8,128]{3,2,1,0:T(8,128)S(1)}, u32[]{:S(2)}, u32[]{:S(2)}) %collective-permute-start.9) | collective-permute-done | bytes 57376 | tf_op jit(solution)/shard_map/ppermute | solution.py:581
  40.8 0.0 collective-permute-done.10
  40.9 0.1 collective-permute-start.11
  41.0 1.4 %collective-permute-done.11.fetched_mate = f32[4,2,7,8,128]{4,3,2,1,0:T(8,128)S(1)} collective-permute-done((f32[4,2,7,8,128]{4,3,2,1,0:T(8,128)S(1)}, f32[4,2,7,8,128]{4,3,2,1,0:T(8,128)S(1)}, u32[]{:S(2)}, u32[]{:S(2)}) %collective-permute-start.11) | collective-permute-done | bytes 229408 | tf_op jit(solution)/shard_map/ppermute | solution.py:562
  42.4 3.3 %surface_and_scale.1 = (f32[2,50,16,128]{3,2,1,0:T(8,128)}, f32[2,16,128]{2,1,0:T(8,128)}, f32[3]{0:T(128)}) custom-call(f32[2,7,8,128]{3,2,1,0:T(8,128)S(1)} %pad_maximum_fusion.1.pair, f32[4,2,7,8,128]{4,3,2,1,0:T(8,128)S(1)} %pad_maximum_fusion.fetched, f32[4,2,7,8,128]{4,3,2,1,0:T(8,128)S(1)} %collective-permute-done.11.fetched_mate, ...), custom_call_target="tpu_custom_call" | custom-call | tf_op jit(solution)/shard_map/surface_and_scale/pallas_call | solution.py:679
  (3 shorter events, 0.0 us)
Async XLA Ops:
  0.6 7.6 %copy-start = (f32[50,2,1024]{2,1,0:T(2,128)S(1)}, f32[50,2,1024]{2,1,0:T(2,128)}, u32[]{:S(2)}) copy-start(f32[50,2,1024]{2,1,0:T(2,128)} %param.8) | copy-start | bytes 1228804
  0.6 7.6 %copy-start.1 = (f32[2,50,2,1024]{3,2,1,0:T(2,128)S(1)}, f32[2,50,2,1024]{3,2,1,0:T(2,128)}, u32[]{:S(2)}) copy-start(f32[2,50,2,1024]{3,2,1,0:T(2,128)} %param.5) | copy-start | bytes 2457604
  0.7 7.6 %copy-start.3 = (f32[50,2,1024]{2,1,0:T(2,128)S(1)}, f32[50,2,1024]{2,1,0:T(2,128)}, u32[]{:S(2)}) copy-start(f32[50,2,1024]{2,1,0:T(2,128)} %param.7) | copy-start | bytes 1228804
  0.7 7.6 %copy-start.4 = (f32[2,2,1024]{2,1,0:T(2,128)S(1)}, f32[2,2,1024]{2,1,0:T(2,128)}, u32[]{:S(2)}) copy-start(f32[2,2,1024]{2,1,0:T(2,128)} %param.6) | copy-start | bytes 49156
  0.7 7.6 %copy-start.5 = (s32[2,1024]{1,0:T(2,128)S(1)}, s32[2,1024]{1,0:T(2,128)}, u32[]{:S(2)}) copy-start(s32[2,1024]{1,0:T(2,128)} %param.9) | copy-start | bytes 24580
  2.7 12.8 %collective-permute-start.1 = (f32[131,8,128]{2,1,0:T(8,128)}, f32[131,8,128]{2,1,0:T(8,128)S(1)}, u32[]{:S(2)}, u32[]{:S(2)}) collective-permute-start(f32[131,8,128]{2,1,0:T(8,128)} %edge_columns.1.edge), channel_id=1, source_target_pairs={{0,15},{1,2},{2,1},{3,4},{4,3},{5,6},{6,5},{7,8},{8,7},{9,10},{10,... | collective-permute-start | bytes 1609736 | tf_op jit(solution)/shard_map/ppermute | solution.py:628
  8.3 1.1 %copy-start.2 = (f32[131,8,128]{2,1,0:T(8,128)S(1)}, f32[131,8,128]{2,1,0:T(8,128)}, u32[]{:S(2)}) copy-start(f32[131,8,128]{2,1,0:T(8,128)} %edge_columns.1.edge) | copy-start | bytes 1609732
  10.5 7.0 %collective-permute-start.2 = (f32[100,8,128]{2,1,0:T(8,128)S(1)}, f32[100,8,128]{2,1,0:T(8,128)S(1)}, u32[]{:S(2)}, u32[]{:S(2)}) collective-permute-start(f32[100,8,128]{2,1,0:T(8,128)S(1)} %get-tuple-element.25.mate), channel_id=1, source_target_pairs={{0,1},{1,0},{2,3},{3,2},{4,5},{5,4},{6,7},{7,6},{8,9},{9,8},{10,11... | collective-permute-start | bytes 1228808 | tf_op jit(solution)/shard_map/ppermute | solution.py:562
  10.6 7.0 %collective-permute-start.3 = (f32[100,8,128]{2,1,0:T(8,128)S(1)}, f32[100,8,128]{2,1,0:T(8,128)S(1)}, u32[]{:S(2)}, u32[]{:S(2)}) collective-permute-start(f32[100,8,128]{2,1,0:T(8,128)S(1)} %get-tuple-element.26.mate_raw), channel_id=1, source_target_pairs={{0,1},{1,0},{2,3},{3,2},{4,5},{5,4},{6,7},{7,6},{8,9},{9,8},{10,11... | collective-permute-start | bytes 1228808 | tf_op jit(solution)/shard_map/ppermute | solution.py:562
  11.1 10.2 %collective-permute-start = (f32[100,8,128]{2,1,0:T(8,128)S(1)}, f32[100,8,128]{2,1,0:T(8,128)S(1)}, u32[]{:S(2)}, u32[]{:S(2)}) collective-permute-start(f32[100,8,128]{2,1,0:T(8,128)S(1)} %get-tuple-element.23.cross), channel_id=1, source_target_pairs={{0,15},{1,2},{2,1},{3,4},{4,3},{5,6},{6,5},{7,8},{8,7},{9,10},{10,... | collective-permute-start | bytes 1228808 | tf_op jit(solution)/shard_map/ppermute | solution.py:645
  11.4 6.2 %collective-permute-start.4 = (f32[56,8,128]{2,1,0:T(8,128)S(1)}, f32[56,8,128]{2,1,0:T(8,128)S(1)}, u32[]{:S(2)}, u32[]{:S(2)}) collective-permute-start(f32[56,8,128]{2,1,0:T(8,128)S(1)} %get-tuple-element.28.mate_flow.refs_7_), channel_id=1, source_target_pairs={{0,1},{1,0},{2,3},{3,2},{4,5},{5,4},{6,7},{7,6},{8,9},{9,8},{10,11... | collective-permute-start | bytes 688136 | tf_op jit(solution)/shard_map/ppermute | solution.py:562
  15.6 4.7 %collective-permute-start.5 = (f32[25,8,128]{2,1,0:T(8,128)S(1)}, f32[25,8,128]{2,1,0:T(8,128)S(1)}, u32[]{:S(2)}, u32[]{:S(2)}) collective-permute-start(f32[25,8,128]{2,1,0:T(8,128)S(1)} %slice.4), channel_id=1, source_target_pairs={{0,16},{16,0},{1,17},{17,1},{2,18},{18,2},{3,19},{19,3},{4,20},{20... | collective-permute-start | bytes 307208 | tf_op jit(solution)/shard_map/ppermute | solution.py:629
  21.5 7.4 %collective-permute-start.6 = (f32[7,8,128]{2,1,0:T(8,128)S(1)}, f32[7,8,128]{2,1,0:T(8,128)S(1)}, u32[]{:S(2)}, u32[]{:S(2)}) collective-permute-start(f32[7,8,128]{2,1,0:T(8,128)S(1)} %get-tuple-element.36), channel_id=1, source_target_pairs={{0,1},{1,0},{2,3},{3,2},{4,5},{5,4},{6,7},{7,6},{8,9},{9,8},{10,11... | collective-permute-start | bytes 86024 | tf_op jit(solution)/shard_map/ppermute | solution.py:562
  28.9 9.0 %collective-permute-start.7 = (f32[2,7,8,128]{3,2,1,0:T(8,128)S(1)}, f32[2,7,8,128]{3,2,1,0:T(8,128)S(1)}, u32[]{:S(2)}, u32[]{:S(2)}) collective-permute-start(f32[2,7,8,128]{3,2,1,0:T(8,128)S(1)} %pad_maximum_fusion.1.pair), channel_id=1, source_target_pairs={{0,14},{1,13},{2,12},{3,15},{4,10},{5,9},{6,8},{7,11},{8,6},{9,5},... | collective-permute-start | bytes 172040 | tf_op jit(solution)/shard_map/ppermute | solution.py:581
  35.1 5.2 %collective-permute-start.8 = (f32[2,7,8,128]{3,2,1,0:T(8,128)S(1)}, f32[2,7,8,128]{3,2,1,0:T(8,128)S(1)}, u32[]{:S(2)}, u32[]{:S(2)}) collective-permute-start(f32[2,7,8,128]{3,2,1,0:T(8,128)S(1)} %pad_maximum_fusion.1.pair), channel_id=1, source_target_pairs={{0,8},{1,11},{2,10},{3,9},{4,12},{5,15},{6,14},{7,13},{8,0},{9,3},... | collective-permute-start | bytes 172040 | tf_op jit(solution)/shard_map/ppermute | solution.py:581
  35.1 5.8 %collective-permute-start.9 = (f32[2,7,8,128]{3,2,1,0:T(8,128)S(1)}, f32[2,7,8,128]{3,2,1,0:T(8,128)S(1)}, u32[]{:S(2)}, u32[]{:S(2)}) collective-permute-start(f32[2,7,8,128]{3,2,1,0:T(8,128)S(1)} %pad_maximum_fusion.1.pair), channel_id=1, source_target_pairs={{0,6},{1,5},{2,4},{3,7},{4,2},{5,1},{6,0},{7,3},{8,14},{9,13},{10,... | collective-permute-start | bytes 172040 | tf_op jit(solution)/shard_map/ppermute | solution.py:581
  35.7 5.1 %collective-permute-start.10 = (f32[2,7,8,128]{3,2,1,0:T(8,128)S(1)}, f32[2,7,8,128]{3,2,1,0:T(8,128)S(1)}, u32[]{:S(2)}, u32[]{:S(2)}) collective-permute-start(f32[2,7,8,128]{3,2,1,0:T(8,128)S(1)} %pad_maximum_fusion.1.pair), channel_id=1, source_target_pairs={{1,3},{3,1},{5,7},{7,5},{9,11},{11,9},{13,15},{15,13},{17,19},{19,... | collective-permute-start | bytes 172040 | tf_op jit(solution)/shard_map/ppermute | solution.py:581
  40.9 1.6 %collective-permute-start.11 = (f32[4,2,7,8,128]{4,3,2,1,0:T(8,128)S(1)}, f32[4,2,7,8,128]{4,3,2,1,0:T(8,128)S(1)}, u32[]{:S(2)}, u32[]{:S(2)}) collective-permute-start(f32[4,2,7,8,128]{4,3,2,1,0:T(8,128)S(1)} %pad_maximum_fusion.fetched), channel_id=1, source_target_pairs={{0,1},{1,0},{2,3},{3,2},{4,5},{5,4},{6,7},{7,6},{8,9},{9,8},{10,11... | collective-permute-start | bytes 688136 | tf_op jit(solution)/shard_map/ppermute | solution.py:562

commit v10 on v9

--- a/solution.py
+++ b/solution.py
@@ -99,8 +99,8 @@
 
 
 def edge_kernel(
-    levels, sub, tracer_hbm, zonal_hbm, surface_hbm, bottom_hbm, edge_hbm,
-    tracer, zonal, surface, bottom, edge, sems_in, sems_out,
+    levels, sub, tracer_hbm, zonal_hbm, surface_hbm, bottom_hbm, edge_hbm, flow_hbm,
+    tracer, zonal, surface, bottom, edge, flow, sems_in, sems_out,
 ):
     outer, _, _ = orientation()
     start, part = share(levels)
@@ -110,29 +110,31 @@
         copy.start()
         return copy
 
-    arrivals = [
-        move(tracer_hbm.at[v], tracer.at[v], sems_in.at[v]) for v in range(VECTORS)
-    ] + [move(zonal_hbm.at[pl.ds(start, part)], zonal, sems_in.at[VECTORS])]
-    small = [
-        move(surface_hbm, surface, sems_in.at[VECTORS + 1]),
-        move(bottom_hbm, bottom, sems_in.at[VECTORS + 2]),
+    first = [
+        move(zonal_hbm.at[pl.ds(start, part)], zonal, sems_in.at[0]),
+        move(surface_hbm, surface, sems_in.at[1]),
+        move(bottom_hbm, bottom, sems_in.at[2]),
     ]
-    departures = []
+    arrivals = [move(tracer_hbm.at[v], tracer.at[v], sems_in.at[3 + v]) for v in range(VECTORS)]
+    for copy in first:
+        copy.wait()
+
+    def take(k, carry):
+        flow[k] = zonal[k, pl.ds(outer, sub, stride=2), :]
+        return carry
+
+    lax.fori_loop(0, part, take, 0, unroll=steps(part, 10))
+    departures = [move(flow, flow_hbm, sems_out.at[VECTORS])]
+    pack_rim(sub, surface, bottom, edge, VECTORS * levels)
     for v, arrival in enumerate(arrivals):
-        number = part if v == VECTORS else levels
         arrival.wait()
-        if v == VECTORS:
-            for copy in small:
-                copy.wait()
-            pack_rim(sub, surface, bottom, edge, v * levels + number)
 
         def body(k, carry, v=v):
-            source = zonal if v == VECTORS else tracer.at[v]
-            edge[v * levels + k] = source[k, pl.ds(outer, sub, stride=2), :]
+            edge[v * levels + k] = tracer[v, k, pl.ds(outer, sub, stride=2), :]
             return carry
 
-        lax.fori_loop(0, number, body, 0, unroll=steps(number, 10))
-        rows = pl.ds(v * levels, number + (RIM if v == VECTORS else 0))
+        lax.fori_loop(0, levels, body, 0, unroll=steps(levels, 10))
+        rows = pl.ds(v * levels, levels + (RIM if v == VECTORS - 1 else 0))
         departures.append(move(edge.at[rows], edge_hbm.at[rows], sems_out.at[v]))
     for departure in departures:
         departure.wait()
@@ -191,41 +193,42 @@
 
 
 def halo_kernel(
-    levels, sub, own, raw, cross, mate, mate_raw, flow_in, mate_flow,
-    raw_far, mate_far, mate_raw_far, mate_flow_far, merid, *refs,
+    levels, sub, raw, cross, mate, mate_raw, flow_in, mate_flow,
+    raw_far, mate_far, mate_raw_far, mate_flow_far, flow_half, flow_other, merid,
+    done, base, weight, sums, powers, flow_far,
 ):
     outer, inner, sign = orientation()
     start, part = share(levels)
-    first = start if own else levels - part - start
-    if own:
-        done, base, weight, sums, powers = refs
-        powers_of_heights(levels, part, mate_flow, mate_flow_far, raw_far, powers)
-        flow_far = raw_far.at[pl.ds(VECTORS * levels, part)]
-    else:
-        flow_far, done, base, weight, sums = refs
+
+    def unpack(i, carry):
+        flow_far[start + i] = flow_half[i]
+        flow_far[levels - part - start + i] = flow_other[i]
+        return carry
+
+    lax.fori_loop(0, part, unpack, 0, unroll=steps(part, 10))
+    powers_of_heights(levels, mate_flow, mate_flow_far, raw_far, powers)
     near, far = (raw, mate_raw), (raw_far, mate_raw_far)
     rim = levels + DEPTHS
     depth = [mate_flow[rim + where] for where in (outer, inner)]
     beside = [
-        jnp.minimum(depth[0], raw_far[VECTORS * levels + part + DEPTHS + inner]),
+        jnp.minimum(depth[0], raw_far[VECTORS * levels + DEPTHS + inner]),
         jnp.minimum(depth[1], mate_flow_far[rim + outer]),
     ]
     between = jnp.minimum(*depth)
     along = [side_depths(d) for d in depth]
     zero = jnp.zeros_like(between)
 
-    def body(i, carry):
-        k = first + i
+    def body(k, carry):
         level = k.astype(jnp.float32)
         flow = [flow_in[k], mate_flow[k]]
-        beyond = [flow_far[i], mate_flow_far[k]]
+        beyond = [flow_far[k], mate_flow_far[k]]
         turn = [merid[k, pl.ds(where, sub, stride=2), :] for where in (outer, inner)]
         middle = face_pair(level, between, -sign * (flow[0] + flow[1]))
         edges = [
             face_pair(level, beside[c], (sign, -sign)[c] * (flow[c] + beyond[c])) for c in range(2)
         ]
         sides = [side_pairs(level, along[c], turn[c]) for c in range(2)]
-        weight[i] = edges[0][1]
+        weight[k] = edges[0][1]
         totals, grams = list(carry[:VECTORS]), list(carry[VECTORS:])
         fresh = []
         for v in range(VECTORS):
@@ -234,7 +237,7 @@
             outside, inside = cross[row] - flux[0], mate[row] - flux[1]
             other = mate_far[row] + flux[1]
             crossing = outflow(middle, outside, inside)
-            base[v, i] = (
+            base[v, k] = (
                 outside
                 - outflow(edges[0], outside, flux[0])
                 - crossing
@@ -243,44 +246,48 @@
             value = (
                 inside - outflow(edges[1], inside, other) + crossing - divergence_y(sides[1], inside)
             )
-            done[v, i] = value
+            done[v, k] = value
             totals[v] = totals[v] + value
             fresh.append(value)
         return (*totals, *add_products(grams, *fresh))
 
-    found = lax.fori_loop(0, part, body, (zero,) * (VECTORS + 3), unroll=steps(part, 10))
+    found = lax.fori_loop(0, levels, body, (zero,) * (VECTORS + 3), unroll=steps(levels, 10))
     for row, tile in enumerate(found):
         sums[row] = tile
 
 
+def interleave_kernel(levels, sub, column, done, tracer):
+    outer, inner, _ = orientation()
+
+    def body(k, carry):
+        for v in range(VECTORS):
+            tracer[v, k, pl.ds(outer, sub, stride=2), :] = column[v, k]
+            tracer[v, k, pl.ds(inner, sub, stride=2), :] = done[v, k]
+        return carry
+
+    lax.fori_loop(0, levels, body, 0, unroll=steps(levels, 10))
+
+
 def add_products(grams, a, b):
     return [grams[0] + a * a, grams[1] + a * b, grams[2] + b * b]
 
 
-def second_kernel(
-    levels, sub, cross_far, *refs,
-):
+def second_kernel(levels, cross_far, base, weight, inside, powers, mate_flow, column, message):
     outer, inner, _ = orientation()
-    start, part = share(levels)
-    parts = refs[:3], refs[3:6]
-    powers, mate_flow, column, message = refs[6:]
     zero = jnp.zeros(powers.shape[-2:], jnp.float32)
-    carry = (zero,) * (VECTORS + 3)
-    for first, (base, weight, _) in zip((start, levels - part - start), parts):
-
-        def body(i, carry, first=first, base=base, weight=weight):
-            totals, fresh = [], []
-            for v in range(VECTORS):
-                value = base[v, i] - weight[i] * cross_far[v * levels + first + i]
-                column[v, first + i] = value
-                totals.append(carry[v] + value)
-                fresh.append(value)
-            return (*totals, *add_products(carry[VECTORS:], *fresh))
-
-        carry = lax.fori_loop(0, part, body, carry, unroll=steps(part, 10))
-    inside = [parts[0][2][row] + parts[1][2][row] for row in range(VECTORS + 3)]
+
+    def body(k, carry):
+        totals, fresh = [], []
+        for v in range(VECTORS):
+            value = base[v, k] - weight[k] * cross_far[v * levels + k]
+            column[v, k] = value
+            totals.append(carry[v] + value)
+            fresh.append(value)
+        return (*totals, *add_products(carry[VECTORS:], *fresh))
+
+    carry = lax.fori_loop(0, levels, body, (zero,) * (VECTORS + 3), unroll=steps(levels, 10))
     gain = STERIC_GAIN / levels
-    rows = [a + b for a, b in zip(carry[VECTORS:], inside[VECTORS:])]
+    rows = [a + inside[VECTORS + n] for n, a in enumerate(carry[VECTORS:])]
     residual = []
     for v in range(VECTORS):
         residual.append(
@@ -328,16 +335,15 @@
     return [sums[n // size][n % size : n % size + 1] for n in range(count)]
 
 
-def powers_of_heights(levels, part, mate_flow, mate_flow_far, raw_far, powers):
+def powers_of_heights(levels, mate_flow, mate_flow_far, raw_far, powers):
     outer, inner, _ = orientation()
-    cross_base = VECTORS * levels + part
     line = [
         (mate_flow_far, levels, inner),
         (mate_flow_far, levels, outer),
         (mate_flow, levels, inner),
         (mate_flow, levels, outer),
-        (raw_far, cross_base, inner),
-        (raw_far, cross_base, outer),
+        (raw_far, VECTORS * levels, inner),
+        (raw_far, VECTORS * levels, outer),
     ]
     depth = [ref[base + DEPTHS + where] for ref, base, where in line]
     faces = [SURFACE_COUPLING * jnp.minimum(a, b) for a, b in zip(depth, depth[1:])]
@@ -380,8 +386,8 @@
 
 
 def third_kernel(
-    levels, sub, count, pair, fetched, fetched_mate, surface, column, done, done_other,
-    tracer_hbm, surface_out, growth, tracer, sems, pole, residual, answer, image, depth, face_x, face_y, face_z, packed,
+    levels, sub, count, pair, fetched, fetched_mate, surface, tracer,
+    tracer_hbm, surface_out, growth, scaled, sems, pole, residual, answer, image, depth, face_x, face_y, face_z, packed,
 ):
     width = 2 * count
     me = lax.axis_index("lon")
@@ -508,26 +514,19 @@
     scale_two = jnp.sqrt(rest + EPSILON)
     over_one, over_two = 1.0 / scale_one, 1.0 / scale_two
 
-    outer, inner, _ = orientation()
-    begin, part = share(levels)
+    chunk = steps(levels, 10)
     departures = []
-    for half, (first, source) in enumerate(((begin, done), (levels - part - begin, done_other))):
-
-        def scale(i, carry, first=first, source=source):
-            k = first + i
-            for where, one, two in (
-                (outer, column[0, k], column[1, k]),
-                (inner, source[0, i], source[1, i]),
-            ):
-                unit = one * over_one
-                place = pl.ds(where, sub, stride=2)
-                tracer[0, k, place, :] = unit
-                tracer[1, k, place, :] = (two - cross * unit) * over_two
-            return carry
-
-        lax.fori_loop(0, part, scale, 0, unroll=steps(part, 10))
-        rows = pl.ds(first, part)
-        departure = pltpu.make_async_copy(tracer.at[:, rows], tracer_hbm.at[:, rows], sems.at[half])
+
+    def scale(k, carry):
+        unit = tracer[0, k] * over_one
+        scaled[0, k] = unit
+        scaled[1, k] = (tracer[1, k] - cross * unit) * over_two
+        return carry
+
+    for n in range(levels // chunk):
+        lax.fori_loop(n * chunk, (n + 1) * chunk, scale, 0, unroll=chunk)
+        rows = pl.ds(n * chunk, chunk)
+        departure = pltpu.make_async_copy(scaled.at[:, rows], tracer_hbm.at[:, rows], sems.at[n])
         departure.start()
         departures.append(departure)
     for c in range(2):
@@ -606,27 +605,29 @@
     outward = [(i, (i + 1) % count if i % 2 else (i - 1) % count) for i in range(count)]
     part = levels // 2
     surface, bottom = tiled(surface_pert), tiled(bottom_level)
-    edge_rows = VECTORS * levels + part + RIM
-
-    edge = pl.pallas_call(
+
+    packed = shaped(VECTORS * levels + RIM), shaped(part)
+    edge, flow_edge = pl.pallas_call(
         functools.partial(edge_kernel, levels, sub),
-        out_shape=shaped(edge_rows),
+        out_shape=packed,
         in_specs=[hbm] * 4,
-        out_specs=hbm,
+        out_specs=(hbm, hbm),
         scratch_shapes=[
             both,
             pltpu.VMEM((part, sub * 2, LANES), f32),
             pltpu.VMEM((vectors, sub * 2, LANES), f32),
             pltpu.VMEM((sub * 2, LANES), jnp.int32),
-            held(edge_rows),
+            held(VECTORS * levels + RIM),
+            held(part),
             pltpu.SemaphoreType.DMA((VECTORS + 3,)),
             pltpu.SemaphoreType.DMA((VECTORS + 1,)),
         ],
         compiler_params=pltpu.CompilerParams(vmem_limit_bytes=60 * 2**20),
         name="edge_columns",
     )(tracer_pert, zonal_flow, surface, bottom)
+    flow_half = lax.ppermute(flow_edge, "lon", outward)
     edge_far = lax.ppermute(edge, "lon", outward)
-    flow_other = lax.ppermute(edge_far[VECTORS * levels : edge_rows - RIM], "grp", [(0, 1), (1, 0)])
+    flow_other = lax.ppermute(flow_half, "grp", [(0, 1), (1, 0)])
     cross, mate, raw, mate_raw, flow_in, mate_flow = pl.pallas_call(
         functools.partial(first_kernel, levels, sub),
         out_shape=(
@@ -644,38 +645,40 @@
     )(edge, tracer_pert, zonal_flow, merid_flow, surface, bottom)
     cross_far = lax.ppermute(cross, "lon", outward)
     mate_far, mate_raw_far, mate_flow_far = (swap(x, 1) for x in (mate, mate_raw, mate_flow))
-    arrived = (
+    done, *rest = pl.pallas_call(
+        functools.partial(halo_kernel, levels, sub),
+        out_shape=(
+            shaped(vectors, levels),
+            shaped(vectors, levels),
+            shaped(levels),
+            shaped(VECTORS + 3),
+            shaped(POWERS + 1, vectors, 2),
+        ),
+        in_specs=[vmem] * 13,
+        out_specs=(vmem,) * 5,
+        scratch_shapes=[held(levels)],
+        compiler_params=params,
+        name="both_steps",
+    )(
         raw, cross, mate, mate_raw, flow_in, mate_flow,
-        edge_far, mate_far, mate_raw_far, mate_flow_far, merid_flow,
+        edge_far, mate_far, mate_raw_far, mate_flow_far, flow_half, flow_other, merid_flow,
     )
-    halves = (
-        shaped(vectors, part),
-        shaped(vectors, part),
-        shaped(part),
-        shaped(VECTORS + 3),
-    )
-
-    def halo(own, *operands):
-        shapes = halves + ((shaped(POWERS + 1, vectors, 2),) if own else ())
-        return pl.pallas_call(
-            functools.partial(halo_kernel, levels, sub, own),
-            out_shape=shapes,
-            in_specs=[vmem] * len(operands),
-            out_specs=(vmem,) * len(shapes),
-            compiler_params=params,
-            name="own_levels" if own else "other_levels",
-        )(*operands)
-
-    done, *near_half, powers = halo(True, *arrived)
-    done_other, *far_half = halo(False, *arrived, flow_other)
     column, message = pl.pallas_call(
-        functools.partial(second_kernel, levels, sub),
+        functools.partial(second_kernel, levels),
         out_shape=(shaped(vectors, levels), shaped(BLOCKS)),
-        in_specs=[vmem] * 9,
+        in_specs=[vmem] * 6,
         out_specs=(vmem, vmem),
         compiler_params=params,
         name="outer_column",
-    )(cross_far, *near_half, *far_half, powers, mate_flow)
+    )(cross_far, *rest, mate_flow)
+    tracer = pl.pallas_call(
+        functools.partial(interleave_kernel, levels, sub),
+        out_shape=jax.ShapeDtypeStruct((vectors, levels, sub * 2, LANES), f32),
+        in_specs=[vmem] * 2,
+        out_specs=vmem,
+        compiler_params=params,
+        name="interleave",
+    )(column, done)
     tracer_vec, surface_vec, growth = pl.pallas_call(
         functools.partial(third_kernel, levels, sub, count),
         out_shape=(
@@ -683,11 +686,11 @@
             jax.ShapeDtypeStruct((vectors, sub * 2, LANES), f32),
             jax.ShapeDtypeStruct((3,), f32),
         ),
-        in_specs=[vmem] * 7,
+        in_specs=[vmem] * 5,
         out_specs=(hbm, vmem, pl.BlockSpec(memory_space=pltpu.SMEM)),
         scratch_shapes=[
             both,
-            pltpu.SemaphoreType.DMA((2,)),
+            pltpu.SemaphoreType.DMA((levels // steps(levels, 10),)),
             held(vectors, width + 2),
             *[held(vectors, width)] * 3,
             held(width),
@@ -698,7 +701,7 @@
         ],
         compiler_params=pltpu.CompilerParams(vmem_limit_bytes=32 * 2**20),
         name="surface_and_scale",
-    )(*gather(message), surface, column, done, done_other)
+    )(*gather(message), surface, tracer)
     return (untiled(tracer_vec, 2), untiled(surface_vec, 2), growth)
 
 

time: 45.9 us -> 44.5 us (0.969)
  waiting for transfers between devices: 12.7 us -> 10.9 us
  local copies, waits for them, and re-layouts: 1.08 us -> 2.03 us
    ppermute x1, starting transfers between devices: 5.51 us -> 0.08 us  [on_device(): edge_far = lax.ppermute(edge, 'lon', outward)]
    ppermute x1 -> x2, starting transfers between devices: 2 us -> 7 us  [the longest x1 5.51 us: on_device(): flow_half = lax.ppermute(flow_edge, 'lon', outward)]
    ppermute x1, waiting for transfers between devices: 4.16 us -> 0.01 us  [on_device(): edge_far = lax.ppermute(edge, 'lon', outward)]
    ppermute x1, starting transfers between devices: 0.29 us -> 4.36 us  [on_device(): cross_far = lax.ppermute(cross, 'lon', outward)]
    ppermute x5, starting transfers between devices: 7.21 us -> 4.86 us  [swap(): return lax.ppermute(array, 'lon', [(i, i ^ mask) for i in range(count)])]
    ppermute x4, starting transfers between devices: 7.44 us -> 5.94 us  [gather(): fetched.append(lax.ppermute(pair, 'lon', moves))]
    ppermute x1 -> x2, waiting for transfers between devices: 1.71 us -> 3.17 us  [the longest x1 3.17 us: on_device(): flow_other = lax.ppermute(flow_half, 'grp', [(0, 1), (1, 0)])]
    ppermute x5, waiting for transfers between devices: 2.3 us -> 3.59 us  [swap(): return lax.ppermute(array, 'lon', [(i, i ^ mask) for i in range(count)])]
  transfers between devices with their start and end apart: 12 -> 13, of which waited for: 8 -> 7; matrix products, arithmetic and copies ran while one was open for 0% -> 0% of each run, Pallas kernels for 7% -> 6%
where the time goes in v10:
time: 44.5 us; the launch traced here: 44.3 us
  starting transfers between devices  22.2 us (50%)
  waiting for transfers between devices  10.9 us (24%)
  Pallas kernels  8.3 us (19%)
  local copies, waits for them, and re-layouts  2.03 us (5%)
  between operations  0.76 us (2%)
    ppermute x4, starting transfers between devices, gather(): fetched.append(lax.ppermute(pair, 'lon', moves))  5.94 us
    ppermute x1, starting transfers between devices, on_device(): flow_half = lax.ppermute(flow_edge, 'lon', outward)  5.51 us
    ppermute x5, starting transfers between devices, swap(): return lax.ppermute(array, 'lon', [(i, i ^ mask) for i in range(count)])  4.86 us
    ppermute x1, starting transfers between devices, on_device(): cross_far = lax.ppermute(cross, 'lon', outward)  4.36 us
    ppermute x4, waiting for transfers between devices, gather(): fetched.append(lax.ppermute(pair, 'lon', moves))  4.17 us
    ppermute x5, waiting for transfers between devices, swap(): return lax.ppermute(array, 'lon', [(i, i ^ mask) for i in range(count)])  3.59 us
    ppermute x1, waiting for transfers between devices, on_device(): flow_other = lax.ppermute(flow_half, 'grp', [(0, 1), (1, 0)])  3.17 us
    pallas_call x1, Pallas kernels, on_device(): pl.pallas_call(functools.partial(third_kernel, levels, sub, count), out_s...  3.13 us
  transfers between devices with their start and end apart: 13, of which 7 were waited for; matrix products, arithmetic and copies ran while one was open for 0% of the time, Pallas kernels for 6%

profile of v10, /device:TPU:0, one launch (start us, length us, event | category | flops | bytes accessed | tf_op | source)
XLA Modules:
  0.0 44.3 jit_solution(3700893389759051778)
XLA Ops:
  0.6 0.0 copy-start
  0.6 0.0 copy-start.1
  0.7 0.0 copy-start.5
  0.7 0.0 copy-start.6
  0.7 2.1 %edge_columns.1 = (f32[106,8,128]{2,1,0:T(8,128)}, f32[25,8,128]{2,1,0:T(8,128)}) custom-call(f32[2,50,16,128]{3,2,1,0:T(8,128)} %bitcast.41, f32[50,16,128]{2,1,0:T(8,128)} %bitcast.43, f32[2,16,128]{2,1,0:T(8,128)} %bitcast.47, s32[16,128]{1,0:T(8,128)} %bitcast.50), custom_call_target="tpu_custom_call" | custom-call | tf_op jit(solution)/shard_map/edge_columns/pallas_call | solution.py:610
  2.8 5.5 %collective-permute-start.5 = (f32[25,8,128]{2,1,0:T(8,128)}, f32[25,8,128]{2,1,0:T(8,128)S(1)}, u32[]{:S(2)}, u32[]{:S(2)}) collective-permute-start(f32[25,8,128]{2,1,0:T(8,128)} %get-tuple-element.28), channel_id=1, source_target_pairs={{0,15},{1,2},{2,1},{3,4},{4,3},{5,6},{6,5},{7,8},{8,7},{9,10},{10,... | collective-permute-start | bytes 307208 | tf_op jit(solution)/shard_map/ppermute | solution.py:628
  8.3 0.1 collective-permute-start.1
  8.4 0.0 copy-done
  8.4 0.0 copy-done.1
  8.4 0.0 copy-done.5
  8.4 0.0 copy-done.6
  8.4 0.0 copy-start.2
  8.4 1.0 %copy-done.2 = f32[50,2,1024]{2,1,0:T(2,128)S(1)} copy-done((f32[50,2,1024]{2,1,0:T(2,128)S(1)}, f32[50,2,1024]{2,1,0:T(2,128)}, u32[]{:S(2)}) %copy-start.2) | copy-done | bytes 409624
  9.4 0.0 copy-start.4
  9.4 1.0 %copy-done.4 = f32[106,8,128]{2,1,0:T(8,128)S(1)} copy-done((f32[106,8,128]{2,1,0:T(8,128)S(1)}, f32[106,8,128]{2,1,0:T(8,128)}, u32[]{:S(2)}) %copy-start.4) | copy-done | bytes 434200
  10.4 0.0 copy-start.3
  10.4 1.2 %partial_step.1 = (f32[100,8,128]{2,1,0:T(8,128)S(1)}, f32[100,8,128]{2,1,0:T(8,128)S(1)}, f32[100,8,128]{2,1,0:T(8,128)S(1)}, f32[100,8,128]{2,1,0:T(8,128)S(1)...) custom-call(f32[106,8,128]{2,1,0:T(8,128)S(1)} %copy-done.4, f32[2,50,16,128]{3,2,1,0:T(8,128)S(1)} %bitcast.42, ...), custom_call_target="tpu_custom_call" | custom-call | tf_op jit(solution)/shard_map/partial_step/pallas_call | solution.py:631
  11.6 0.1 collective-permute-start.2
  11.7 0.5 %collective-permute-start.3 = (f32[100,8,128]{2,1,0:T(8,128)S(1)}, f32[100,8,128]{2,1,0:T(8,128)S(1)}, u32[]{:S(2)}, u32[]{:S(2)}) collective-permute-start(f32[100,8,128]{2,1,0:T(8,128)S(1)} %get-tuple-element.25.mate_raw), channel_id=1, source_target_pairs={{0,1},{1,0},{2,3},{3,2},{4,5},{5,4},{6,7},{7,6},{8,9},{9,8},{10,11... | collective-permute-start | bytes 1228808 | tf_op jit(solution)/shard_map/ppermute | solution.py:561
  12.2 4.4 %collective-permute-start = (f32[100,8,128]{2,1,0:T(8,128)S(1)}, f32[100,8,128]{2,1,0:T(8,128)S(1)}, u32[]{:S(2)}, u32[]{:S(2)}) collective-permute-start(f32[100,8,128]{2,1,0:T(8,128)S(1)} %get-tuple-element.22.cross), channel_id=1, source_target_pairs={{0,15},{1,2},{2,1},{3,4},{4,3},{5,6},{6,5},{7,8},{8,7},{9,10},{10,... | collective-permute-start | bytes 1228808 | tf_op jit(solution)/shard_map/ppermute | solution.py:646
  16.6 0.0 collective-permute-done.5.flow_half
  16.6 1.5 %collective-permute-start.6 = (f32[25,8,128]{2,1,0:T(8,128)S(1)}, f32[25,8,128]{2,1,0:T(8,128)S(1)}, u32[]{:S(2)}, u32[]{:S(2)}) collective-permute-start(f32[25,8,128]{2,1,0:T(8,128)S(1)} %collective-permute-done.5.flow_half), channel_id=1, source_target_pairs={{0,16},{16,0},{1,17},{17,1},{2,18},{18,2},{3,19},{19,3},{4,20},{20... | collective-permute-start | bytes 307208 | tf_op jit(solution)/shard_map/ppermute | solution.py:630
  18.1 3.2 %collective-permute-done.6.flow_other = f32[25,8,128]{2,1,0:T(8,128)S(1)} collective-permute-done((f32[25,8,128]{2,1,0:T(8,128)S(1)}, f32[25,8,128]{2,1,0:T(8,128)S(1)}, u32[]{:S(2)}, u32[]{:S(2)}) %collective-permute-start.6) | collective-permute-done | bytes 102432 | tf_op jit(solution)/shard_map/ppermute | solution.py:630
  21.2 0.0 collective-permute-start.4
  21.2 1.5 %collective-permute-done.4.mate_flow_far = f32[56,8,128]{2,1,0:T(8,128)S(1)} collective-permute-done((f32[56,8,128]{2,1,0:T(8,128)S(1)}, f32[56,8,128]{2,1,0:T(8,128)S(1)}, u32[]{:S(2)}, u32[]{:S(2)}) %collective-permute-start.4) | collective-permute-done | bytes 229408 | tf_op jit(solution)/shard_map/ppermute | solution.py:561
  22.7 0.0 collective-permute-done.2.mate_far
  22.7 0.0 collective-permute-done.3.mate_raw_far
  22.7 0.0 collective-permute-done.1.raw_far
  22.7 0.0 copy-done.3
  22.8 1.5 %both_steps.1 = (f32[2,50,8,128]{3,2,1,0:T(8,128)S(1)}, f32[2,50,8,128]{3,2,1,0:T(8,128)S(1)}, f32[50,8,128]{2,1,0:T(8,128)S(1)}, f32[5,8,128]{2,1,0:T(8,128)S(1)}, f32[4,2,2,8,128]{4,3,2,1,0:T(8,128)S(1)}) custom-call(f32[100,8,128]{2,1,0:T(8,128)S(1)} %get-tuple-element.23.raw, f32[100,8,128]{2,1,0:T(8,128)S(1)} %get-tuple-element.22.cross, ...), custom_call_target="tpu_custom_call" | custom-call | tf_op jit(solution)/shard_map/both_steps/pallas_call | solution.py:648
  24.3 0.0 collective-permute-done.cross_far
  24.3 0.2 outer_column.1
  24.5 4.1 %collective-permute-start.7 = (f32[7,8,128]{2,1,0:T(8,128)S(1)}, f32[7,8,128]{2,1,0:T(8,128)S(1)}, u32[]{:S(2)}, u32[]{:S(2)}) collective-permute-start(f32[7,8,128]{2,1,0:T(8,128)S(1)} %get-tuple-element.33), channel_id=1, source_target_pairs={{0,1},{1,0},{2,3},{3,2},{4,5},{5,4},{6,7},{7,6},{8,9},{9,8},{10,11... | collective-permute-start | bytes 86024 | tf_op jit(solution)/shard_map/ppermute | solution.py:561
  28.6 0.9 %collective-permute-done.7 = f32[7,8,128]{2,1,0:T(8,128)S(1)} collective-permute-done((f32[7,8,128]{2,1,0:T(8,128)S(1)}, f32[7,8,128]{2,1,0:T(8,128)S(1)}, u32[]{:S(2)}, u32[]{:S(2)}) %collective-permute-start.7) | collective-permute-done | bytes 28704 | tf_op jit(solution)/shard_map/ppermute | solution.py:561
  29.5 4.4 %collective-permute-start.8 = (f32[2,7,8,128]{3,2,1,0:T(8,128)S(1)}, f32[2,7,8,128]{3,2,1,0:T(8,128)S(1)}, u32[]{:S(2)}, u32[]{:S(2)}) collective-permute-start(f32[2,7,8,128]{3,2,1,0:T(8,128)S(1)} %pad_maximum_fusion.1.pair), channel_id=1, source_target_pairs={{0,14},{1,13},{2,12},{3,15},{4,10},{5,9},{6,8},{7,11},{8,6},{9,5},... | collective-permute-start | bytes 172040 | tf_op jit(solution)/shard_map/ppermute | solution.py:580
  33.8 0.0 collective-permute-start.9
  33.8 0.9 %collective-permute-start.10 = (f32[2,7,8,128]{3,2,1,0:T(8,128)S(1)}, f32[2,7,8,128]{3,2,1,0:T(8,128)S(1)}, u32[]{:S(2)}, u32[]{:S(2)}) collective-permute-start(f32[2,7,8,128]{3,2,1,0:T(8,128)S(1)} %pad_maximum_fusion.1.pair), channel_id=1, source_target_pairs={{0,6},{1,5},{2,4},{3,7},{4,2},{5,1},{6,0},{7,3},{8,14},{9,13},{10,... | collective-permute-start | bytes 172040 | tf_op jit(solution)/shard_map/ppermute | solution.py:580
  34.8 0.7 %collective-permute-start.11 = (f32[2,7,8,128]{3,2,1,0:T(8,128)S(1)}, f32[2,7,8,128]{3,2,1,0:T(8,128)S(1)}, u32[]{:S(2)}, u32[]{:S(2)}) collective-permute-start(f32[2,7,8,128]{3,2,1,0:T(8,128)S(1)} %pad_maximum_fusion.1.pair), channel_id=1, source_target_pairs={{1,3},{3,1},{5,7},{7,5},{9,11},{11,9},{13,15},{15,13},{17,19},{19,... | collective-permute-start | bytes 172040 | tf_op jit(solution)/shard_map/ppermute | solution.py:580
  35.4 1.4 %collective-permute-done.8 = f32[2,7,8,128]{3,2,1,0:T(8,128)S(1)} collective-permute-done((f32[2,7,8,128]{3,2,1,0:T(8,128)S(1)}, f32[2,7,8,128]{3,2,1,0:T(8,128)S(1)}, u32[]{:S(2)}, u32[]{:S(2)}) %collective-permute-start.8) | collective-permute-done | bytes 57376 | tf_op jit(solution)/shard_map/ppermute | solution.py:580
  36.8 2.2 %collective-permute-done.9 = f32[2,7,8,128]{3,2,1,0:T(8,128)S(1)} collective-permute-done((f32[2,7,8,128]{3,2,1,0:T(8,128)S(1)}, f32[2,7,8,128]{3,2,1,0:T(8,128)S(1)}, u32[]{:S(2)}, u32[]{:S(2)}) %collective-permute-start.9) | collective-permute-done | bytes 57376 | tf_op jit(solution)/shard_map/ppermute | solution.py:580
  39.1 0.5 %collective-permute-done.10 = f32[2,7,8,128]{3,2,1,0:T(8,128)S(1)} collective-permute-done((f32[2,7,8,128]{3,2,1,0:T(8,128)S(1)}, f32[2,7,8,128]{3,2,1,0:T(8,128)S(1)}, u32[]{:S(2)}, u32[]{:S(2)}) %collective-permute-start.10) | collective-permute-done | bytes 57376 | tf_op jit(solution)/shard_map/ppermute | solution.py:580
  39.6 0.0 collective-permute-done.11
  39.6 0.2 collective-permute-start.12
  39.8 0.1 interleave.1.tracer
  39.9 1.2 %collective-permute-done.12.fetched_mate = f32[4,2,7,8,128]{4,3,2,1,0:T(8,128)S(1)} collective-permute-done((f32[4,2,7,8,128]{4,3,2,1,0:T(8,128)S(1)}, f32[4,2,7,8,128]{4,3,2,1,0:T(8,128)S(1)}, u32[]{:S(2)}, u32[]{:S(2)}) %collective-permute-start.12) | collective-permute-done | bytes 229408 | tf_op jit(solution)/shard_map/ppermute | solution.py:561
  41.2 3.1 %surface_and_scale.1 = (f32[2,50,16,128]{3,2,1,0:T(8,128)}, f32[2,16,128]{2,1,0:T(8,128)}, f32[3]{0:T(128)}) custom-call(f32[2,7,8,128]{3,2,1,0:T(8,128)S(1)} %pad_maximum_fusion.1.pair, f32[4,2,7,8,128]{4,3,2,1,0:T(8,128)S(1)} %pad_maximum_fusion.fetched, f32[4,2,7,8,128]{4,3,2,1,0:T(8,128)S(1)} %collective-permute-done.12.fetched_mate, ...), custom_call_target="tpu_custom_call" | custom-call | tf_op jit(solution)/shard_map/surface_and_scale/pallas_call | solution.py:682
  (2 shorter events, 0.0 us)
Async XLA Ops:
  0.6 7.8 %copy-start = (f32[2,50,2,1024]{3,2,1,0:T(2,128)S(1)}, f32[2,50,2,1024]{3,2,1,0:T(2,128)}, u32[]{:S(2)}) copy-start(f32[2,50,2,1024]{3,2,1,0:T(2,128)} %param.5) | copy-start | bytes 2457604
  0.6 7.8 %copy-start.1 = (f32[50,2,1024]{2,1,0:T(2,128)S(1)}, f32[50,2,1024]{2,1,0:T(2,128)}, u32[]{:S(2)}) copy-start(f32[50,2,1024]{2,1,0:T(2,128)} %param.7) | copy-start | bytes 1228804
  0.7 7.8 %copy-start.5 = (f32[2,2,1024]{2,1,0:T(2,128)S(1)}, f32[2,2,1024]{2,1,0:T(2,128)}, u32[]{:S(2)}) copy-start(f32[2,2,1024]{2,1,0:T(2,128)} %param.6) | copy-start | bytes 49156
  0.7 7.8 %copy-start.6 = (s32[2,1024]{1,0:T(2,128)S(1)}, s32[2,1024]{1,0:T(2,128)}, u32[]{:S(2)}) copy-start(s32[2,1024]{1,0:T(2,128)} %param.9) | copy-start | bytes 24580
  2.8 13.8 %collective-permute-start.5 = (f32[25,8,128]{2,1,0:T(8,128)}, f32[25,8,128]{2,1,0:T(8,128)S(1)}, u32[]{:S(2)}, u32[]{:S(2)}) collective-permute-start(f32[25,8,128]{2,1,0:T(8,128)} %get-tuple-element.28), channel_id=1, source_target_pairs={{0,15},{1,2},{2,1},{3,4},{4,3},{5,6},{6,5},{7,8},{8,7},{9,10},{10,... | collective-permute-start | bytes 307208 | tf_op jit(solution)/shard_map/ppermute | solution.py:628
  8.3 14.4 %collective-permute-start.1 = (f32[106,8,128]{2,1,0:T(8,128)}, f32[106,8,128]{2,1,0:T(8,128)S(1)}, u32[]{:S(2)}, u32[]{:S(2)}) collective-permute-start(f32[106,8,128]{2,1,0:T(8,128)} %get-tuple-element.21.edge), channel_id=1, source_target_pairs={{0,15},{1,2},{2,1},{3,4},{4,3},{5,6},{6,5},{7,8},{8,7},{9,10},{10,... | collective-permute-start | bytes 1302536 | tf_op jit(solution)/shard_map/ppermute | solution.py:629
  8.4 1.0 %copy-start.2 = (f32[50,2,1024]{2,1,0:T(2,128)S(1)}, f32[50,2,1024]{2,1,0:T(2,128)}, u32[]{:S(2)}) copy-start(f32[50,2,1024]{2,1,0:T(2,128)} %param.8) | copy-start | bytes 1228804
  9.4 1.0 %copy-start.4 = (f32[106,8,128]{2,1,0:T(8,128)S(1)}, f32[106,8,128]{2,1,0:T(8,128)}, u32[]{:S(2)}) copy-start(f32[106,8,128]{2,1,0:T(8,128)} %get-tuple-element.21.edge) | copy-start | bytes 1302532
  10.4 12.3 %copy-start.3 = (f32[50,2,1024]{2,1,0:T(2,128)S(1)}, f32[50,2,1024]{2,1,0:T(2,128)}, u32[]{:S(2)}) copy-start(f32[50,2,1024]{2,1,0:T(2,128)} %param.8) | copy-start | bytes 1228804
  11.6 11.1 %collective-permute-start.2 = (f32[100,8,128]{2,1,0:T(8,128)S(1)}, f32[100,8,128]{2,1,0:T(8,128)S(1)}, u32[]{:S(2)}, u32[]{:S(2)}) collective-permute-start(f32[100,8,128]{2,1,0:T(8,128)S(1)} %get-tuple-element.24.mate), channel_id=1, source_target_pairs={{0,1},{1,0},{2,3},{3,2},{4,5},{5,4},{6,7},{7,6},{8,9},{9,8},{10,11... | collective-permute-start | bytes 1228808 | tf_op jit(solution)/shard_map/ppermute | solution.py:561
  11.7 11.0 %collective-permute-start.3 = (f32[100,8,128]{2,1,0:T(8,128)S(1)}, f32[100,8,128]{2,1,0:T(8,128)S(1)}, u32[]{:S(2)}, u32[]{:S(2)}) collective-permute-start(f32[100,8,128]{2,1,0:T(8,128)S(1)} %get-tuple-element.25.mate_raw), channel_id=1, source_target_pairs={{0,1},{1,0},{2,3},{3,2},{4,5},{5,4},{6,7},{7,6},{8,9},{9,8},{10,11... | collective-permute-start | bytes 1228808 | tf_op jit(solution)/shard_map/ppermute | solution.py:561
  12.2 12.1 %collective-permute-start = (f32[100,8,128]{2,1,0:T(8,128)S(1)}, f32[100,8,128]{2,1,0:T(8,128)S(1)}, u32[]{:S(2)}, u32[]{:S(2)}) collective-permute-start(f32[100,8,128]{2,1,0:T(8,128)S(1)} %get-tuple-element.22.cross), channel_id=1, source_target_pairs={{0,15},{1,2},{2,1},{3,4},{4,3},{5,6},{6,5},{7,8},{8,7},{9,10},{10,... | collective-permute-start | bytes 1228808 | tf_op jit(solution)/shard_map/ppermute | solution.py:646
  16.6 4.7 %collective-permute-start.6 = (f32[25,8,128]{2,1,0:T(8,128)S(1)}, f32[25,8,128]{2,1,0:T(8,128)S(1)}, u32[]{:S(2)}, u32[]{:S(2)}) collective-permute-start(f32[25,8,128]{2,1,0:T(8,128)S(1)} %collective-permute-done.5.flow_half), channel_id=1, source_target_pairs={{0,16},{16,0},{1,17},{17,1},{2,18},{18,2},{3,19},{19,3},{4,20},{20... | collective-permute-start | bytes 307208 | tf_op jit(solution)/shard_map/ppermute | solution.py:630
  21.2 1.5 %collective-permute-start.4 = (f32[56,8,128]{2,1,0:T(8,128)S(1)}, f32[56,8,128]{2,1,0:T(8,128)S(1)}, u32[]{:S(2)}, u32[]{:S(2)}) collective-permute-start(f32[56,8,128]{2,1,0:T(8,128)S(1)} %get-tuple-element.27.mate_flow), channel_id=1, source_target_pairs={{0,1},{1,0},{2,3},{3,2},{4,5},{5,4},{6,7},{7,6},{8,9},{9,8},{10,11... | collective-permute-start | bytes 688136 | tf_op jit(solution)/shard_map/ppermute | solution.py:561
  24.5 5.0 %collective-permute-start.7 = (f32[7,8,128]{2,1,0:T(8,128)S(1)}, f32[7,8,128]{2,1,0:T(8,128)S(1)}, u32[]{:S(2)}, u32[]{:S(2)}) collective-permute-start(f32[7,8,128]{2,1,0:T(8,128)S(1)} %get-tuple-element.33), channel_id=1, source_target_pairs={{0,1},{1,0},{2,3},{3,2},{4,5},{5,4},{6,7},{7,6},{8,9},{9,8},{10,11... | collective-permute-start | bytes 86024 | tf_op jit(solution)/shard_map/ppermute | solution.py:561
  29.5 7.3 %collective-permute-start.8 = (f32[2,7,8,128]{3,2,1,0:T(8,128)S(1)}, f32[2,7,8,128]{3,2,1,0:T(8,128)S(1)}, u32[]{:S(2)}, u32[]{:S(2)}) collective-permute-start(f32[2,7,8,128]{3,2,1,0:T(8,128)S(1)} %pad_maximum_fusion.1.pair), channel_id=1, source_target_pairs={{0,14},{1,13},{2,12},{3,15},{4,10},{5,9},{6,8},{7,11},{8,6},{9,5},... | collective-permute-start | bytes 172040 | tf_op jit(solution)/shard_map/ppermute | solution.py:580
  33.8 5.2 %collective-permute-start.9 = (f32[2,7,8,128]{3,2,1,0:T(8,128)S(1)}, f32[2,7,8,128]{3,2,1,0:T(8,128)S(1)}, u32[]{:S(2)}, u32[]{:S(2)}) collective-permute-start(f32[2,7,8,128]{3,2,1,0:T(8,128)S(1)} %pad_maximum_fusion.1.pair), channel_id=1, source_target_pairs={{0,8},{1,11},{2,10},{3,9},{4,12},{5,15},{6,14},{7,13},{8,0},{9,3},... | collective-permute-start | bytes 172040 | tf_op jit(solution)/shard_map/ppermute | solution.py:580
  33.8 5.8 %collective-permute-start.10 = (f32[2,7,8,128]{3,2,1,0:T(8,128)S(1)}, f32[2,7,8,128]{3,2,1,0:T(8,128)S(1)}, u32[]{:S(2)}, u32[]{:S(2)}) collective-permute-start(f32[2,7,8,128]{3,2,1,0:T(8,128)S(1)} %pad_maximum_fusion.1.pair), channel_id=1, source_target_pairs={{0,6},{1,5},{2,4},{3,7},{4,2},{5,1},{6,0},{7,3},{8,14},{9,13},{10,... | collective-permute-start | bytes 172040 | tf_op jit(solution)/shard_map/ppermute | solution.py:580
  34.8 4.8 %collective-permute-start.11 = (f32[2,7,8,128]{3,2,1,0:T(8,128)S(1)}, f32[2,7,8,128]{3,2,1,0:T(8,128)S(1)}, u32[]{:S(2)}, u32[]{:S(2)}) collective-permute-start(f32[2,7,8,128]{3,2,1,0:T(8,128)S(1)} %pad_maximum_fusion.1.pair), channel_id=1, source_target_pairs={{1,3},{3,1},{5,7},{7,5},{9,11},{11,9},{13,15},{15,13},{17,19},{19,... | collective-permute-start | bytes 172040 | tf_op jit(solution)/shard_map/ppermute | solution.py:580
  39.6 1.6 %collective-permute-start.12 = (f32[4,2,7,8,128]{4,3,2,1,0:T(8,128)S(1)}, f32[4,2,7,8,128]{4,3,2,1,0:T(8,128)S(1)}, u32[]{:S(2)}, u32[]{:S(2)}) collective-permute-start(f32[4,2,7,8,128]{4,3,2,1,0:T(8,128)S(1)} %pad_maximum_fusion.fetched), channel_id=1, source_target_pairs={{0,1},{1,0},{2,3},{3,2},{4,5},{5,4},{6,7},{7,6},{8,9},{9,8},{10,11... | collective-permute-start | bytes 688136 | tf_op jit(solution)/shard_map/ppermute | solution.py:561

commit v11 on v10

--- a/solution.py
+++ b/solution.py
@@ -98,34 +98,36 @@
         target[base + DEPTHS + c] = bottom[pl.ds(c, sub, stride=2), :].astype(jnp.float32)
 
 
-def edge_kernel(
-    levels, sub, tracer_hbm, zonal_hbm, surface_hbm, bottom_hbm, edge_hbm, flow_hbm,
-    tracer, zonal, surface, bottom, edge, flow, sems_in, sems_out,
-):
+def move(source, target, sem):
+    copy = pltpu.make_async_copy(source, target, sem)
+    copy.start()
+    return copy
+
+
+def flow_kernel(levels, sub, zonal_hbm, flow, zonal, sem):
     outer, _, _ = orientation()
     start, part = share(levels)
-
-    def move(source, target, sem):
-        copy = pltpu.make_async_copy(source, target, sem)
-        copy.start()
-        return copy
-
-    first = [
-        move(zonal_hbm.at[pl.ds(start, part)], zonal, sems_in.at[0]),
-        move(surface_hbm, surface, sems_in.at[1]),
-        move(bottom_hbm, bottom, sems_in.at[2]),
-    ]
-    arrivals = [move(tracer_hbm.at[v], tracer.at[v], sems_in.at[3 + v]) for v in range(VECTORS)]
-    for copy in first:
-        copy.wait()
-
-    def take(k, carry):
+    move(zonal_hbm.at[pl.ds(start, part)], zonal, sem).wait()
+
+    def body(k, carry):
         flow[k] = zonal[k, pl.ds(outer, sub, stride=2), :]
         return carry
 
-    lax.fori_loop(0, part, take, 0, unroll=steps(part, 10))
-    departures = [move(flow, flow_hbm, sems_out.at[VECTORS])]
+    lax.fori_loop(0, part, body, 0, unroll=part)
+
+
+def edge_kernel(
+    levels, sub, flow, tracer_hbm, surface_hbm, bottom_hbm, edge_hbm,
+    tracer, surface, bottom, edge, sems_in, sems_out,
+):
+    del flow
+    outer, _, _ = orientation()
+    small = [move(surface_hbm, surface, sems_in.at[0]), move(bottom_hbm, bottom, sems_in.at[1])]
+    arrivals = [move(tracer_hbm.at[v], tracer.at[v], sems_in.at[2 + v]) for v in range(VECTORS)]
+    for copy in small:
+        copy.wait()
     pack_rim(sub, surface, bottom, edge, VECTORS * levels)
+    departures = []
     for v, arrival in enumerate(arrivals):
         arrival.wait()
 
@@ -387,7 +389,7 @@
 
 def third_kernel(
     levels, sub, count, pair, fetched, fetched_mate, surface, tracer,
-    tracer_hbm, surface_out, growth, scaled, sems, pole, residual, answer, image, depth, face_x, face_y, face_z, packed,
+    scaled, surface_out, growth, pole, residual, answer, image, depth, face_x, face_y, face_z, packed,
 ):
     width = 2 * count
     me = lax.axis_index("lon")
@@ -514,21 +516,13 @@
     scale_two = jnp.sqrt(rest + EPSILON)
     over_one, over_two = 1.0 / scale_one, 1.0 / scale_two
 
-    chunk = steps(levels, 10)
-    departures = []
-
     def scale(k, carry):
         unit = tracer[0, k] * over_one
         scaled[0, k] = unit
         scaled[1, k] = (tracer[1, k] - cross * unit) * over_two
         return carry
 
-    for n in range(levels // chunk):
-        lax.fori_loop(n * chunk, (n + 1) * chunk, scale, 0, unroll=chunk)
-        rows = pl.ds(n * chunk, chunk)
-        departure = pltpu.make_async_copy(scaled.at[:, rows], tracer_hbm.at[:, rows], sems.at[n])
-        departure.start()
-        departures.append(departure)
+    lax.fori_loop(0, levels, scale, 0, unroll=steps(levels, 10))
     for c in range(2):
         x = 2 * me + c
         first, second = (
@@ -540,8 +534,6 @@
         surface_out[1, pl.ds(c, sub, stride=2), :] = (second - cross * unit) * over_two
     for i, value in enumerate((scale_one, cross, scale_two)):
         growth[i] = value[0, 0]
-    for departure in departures:
-        departure.wait()
 
 
 def tiled(array):
@@ -606,28 +598,35 @@
     part = levels // 2
     surface, bottom = tiled(surface_pert), tiled(bottom_level)
 
-    packed = shaped(VECTORS * levels + RIM), shaped(part)
-    edge, flow_edge = pl.pallas_call(
+    first_params = pltpu.CompilerParams(vmem_limit_bytes=60 * 2**20)
+    flow_edge = pl.pallas_call(
+        functools.partial(flow_kernel, levels, sub),
+        out_shape=shaped(part),
+        in_specs=[hbm],
+        out_specs=vmem,
+        scratch_shapes=[pltpu.VMEM((part, sub * 2, LANES), f32), pltpu.SemaphoreType.DMA],
+        compiler_params=first_params,
+        name="flow_column",
+    )(zonal_flow)
+    flow_half = lax.ppermute(flow_edge, "lon", outward)
+    flow_other = lax.ppermute(flow_half, "grp", [(0, 1), (1, 0)])
+    edge = pl.pallas_call(
         functools.partial(edge_kernel, levels, sub),
-        out_shape=packed,
-        in_specs=[hbm] * 4,
-        out_specs=(hbm, hbm),
+        out_shape=shaped(VECTORS * levels + RIM),
+        in_specs=[pl.BlockSpec(memory_space=pl.ANY)] + [hbm] * 3,
+        out_specs=hbm,
         scratch_shapes=[
             both,
-            pltpu.VMEM((part, sub * 2, LANES), f32),
             pltpu.VMEM((vectors, sub * 2, LANES), f32),
             pltpu.VMEM((sub * 2, LANES), jnp.int32),
             held(VECTORS * levels + RIM),
-            held(part),
-            pltpu.SemaphoreType.DMA((VECTORS + 3,)),
-            pltpu.SemaphoreType.DMA((VECTORS + 1,)),
+            pltpu.SemaphoreType.DMA((VECTORS + 2,)),
+            pltpu.SemaphoreType.DMA((VECTORS,)),
         ],
-        compiler_params=pltpu.CompilerParams(vmem_limit_bytes=60 * 2**20),
+        compiler_params=first_params,
         name="edge_columns",
-    )(tracer_pert, zonal_flow, surface, bottom)
-    flow_half = lax.ppermute(flow_edge, "lon", outward)
+    )(flow_edge, tracer_pert, surface, bottom)
     edge_far = lax.ppermute(edge, "lon", outward)
-    flow_other = lax.ppermute(flow_half, "grp", [(0, 1), (1, 0)])
     cross, mate, raw, mate_raw, flow_in, mate_flow = pl.pallas_call(
         functools.partial(first_kernel, levels, sub),
         out_shape=(
@@ -687,10 +686,8 @@
             jax.ShapeDtypeStruct((3,), f32),
         ),
         in_specs=[vmem] * 5,
-        out_specs=(hbm, vmem, pl.BlockSpec(memory_space=pltpu.SMEM)),
+        out_specs=(vmem, vmem, pl.BlockSpec(memory_space=pltpu.SMEM)),
         scratch_shapes=[
-            both,
-            pltpu.SemaphoreType.DMA((levels // steps(levels, 10),)),
             held(vectors, width + 2),
             *[held(vectors, width)] * 3,
             held(width),

time: 44.5 us -> 44.8 us (level)
  Pallas kernels: 8.3 us -> 9.31 us
  local copies, waits for them, and re-layouts: 2.03 us -> 1.03 us
    pallas_call x1 -> x2, Pallas kernels: 2.14 us -> 3.62 us  [the longest x1 1.97 us: on_device(): pl.pallas_call(functools.partial(edge_kernel, levels, sub), out_shape=sha...]
    unnamed x14 -> x12, local copies, waits for them, and re-layouts: 2.03 us -> 1.03 us
    pallas_call x1, Pallas kernels: 3.13 us -> 2.68 us  [on_device(): pl.pallas_call(functools.partial(third_kernel, levels, sub, count), out_s...]
  transfers between devices with their start and end apart: 13 -> 13, of which waited for: 7 -> 8; matrix products, arithmetic and copies ran while one was open for 0% -> 0% of each run, Pallas kernels for 6% -> 11%
where the time goes in v11:
time: 44.8 us; the launch traced here: 44.6 us
  starting transfers between devices  22.3 us (50%)
  waiting for transfers between devices  11.1 us (25%)
  Pallas kernels  9.31 us (21%)
  local copies, waits for them, and re-layouts  1.03 us (2%)
  between operations  0.75 us (2%)
    ppermute x4, starting transfers between devices, gather(): fetched.append(lax.ppermute(pair, 'lon', moves))  5.94 us
    ppermute x1, starting transfers between devices, on_device(): flow_half = lax.ppermute(flow_edge, 'lon', outward)  5.51 us
    ppermute x5, starting transfers between devices, swap(): return lax.ppermute(array, 'lon', [(i, i ^ mask) for i in range(count)])  4.86 us
    ppermute x1, starting transfers between devices, on_device(): cross_far = lax.ppermute(cross, 'lon', outward)  4.37 us
    ppermute x4, waiting for transfers between devices, gather(): fetched.append(lax.ppermute(pair, 'lon', moves))  4.22 us
    ppermute x5, waiting for transfers between devices, swap(): return lax.ppermute(array, 'lon', [(i, i ^ mask) for i in range(count)])  3.66 us
    ppermute x1, waiting for transfers between devices, on_device(): flow_other = lax.ppermute(flow_half, 'grp', [(0, 1), (1, 0)])  3.17 us
    pallas_call x1, Pallas kernels, on_device(): pl.pallas_call(functools.partial(third_kernel, levels, sub, count), out_s...  2.68 us
  transfers between devices with their start and end apart: 13, of which 8 were waited for; matrix products, arithmetic and copies ran while one was open for 0% of the time, Pallas kernels for 11%

profile of v11, /device:TPU:0, one launch (start us, length us, event | category | flops | bytes accessed | tf_op | source)
XLA Modules:
  0.0 44.6 jit_solution(2911057933098060614)
XLA Ops:
  0.6 0.0 copy-start.3
  0.6 1.6 %flow_column.1.flow = f32[25,8,128]{2,1,0:T(8,128)} custom-call(f32[50,16,128]{2,1,0:T(8,128)} %bitcast.43), custom_call_target="tpu_custom_call" | custom-call | tf_op jit(solution)/shard_map/flow_column/pallas_call | solution.py:602
  2.3 0.0 copy-start
  2.3 5.5 %collective-permute-start.5 = (f32[25,8,128]{2,1,0:T(8,128)}, f32[25,8,128]{2,1,0:T(8,128)S(1)}, u32[]{:S(2)}, u32[]{:S(2)}) collective-permute-start(f32[25,8,128]{2,1,0:T(8,128)} %flow_column.1.flow), channel_id=1, source_target_pairs={{0,15},{1,2},{2,1},{3,4},{4,3},{5,6},{6,5},{7,8},{8,7},{9,10},{10,... | collective-permute-start | bytes 307208 | tf_op jit(solution)/shard_map/ppermute | solution.py:611
  7.8 0.0 copy-start.2
  7.8 0.0 copy-start.4
  7.8 0.0 copy-start.5
  7.8 2.0 %edge_columns.1.edge = f32[106,8,128]{2,1,0:T(8,128)} custom-call(f32[25,8,128]{2,1,0:T(8,128)} %flow_column.1.flow, f32[2,50,16,128]{3,2,1,0:T(8,128)} %bitcast.41, f32[2,16,128]{2,1,0:T(8,128)} %bitcast.47, s32[16,128]{1,0:T(8,128)} %bitcast.50), custom_call_target="tpu_custom_call" | custom-call | tf_op jit(solution)/shard_map/edge_columns/pallas_call | solution.py:613
  9.8 0.1 collective-permute-start.1
  9.9 0.0 copy-done.3
  9.9 0.0 copy-done
  9.9 0.0 copy-done.2
  9.9 0.0 copy-done.4
  9.9 0.0 copy-done.5
  10.0 0.0 copy-start.1
  10.0 1.0 %copy-done.1 = f32[106,8,128]{2,1,0:T(8,128)S(1)} copy-done((f32[106,8,128]{2,1,0:T(8,128)S(1)}, f32[106,8,128]{2,1,0:T(8,128)}, u32[]{:S(2)}) %copy-start.1) | copy-done | bytes 434200
  11.0 1.2 %partial_step.1 = (f32[100,8,128]{2,1,0:T(8,128)S(1)}, f32[100,8,128]{2,1,0:T(8,128)S(1)}, f32[100,8,128]{2,1,0:T(8,128)S(1)}, f32[100,8,128]{2,1,0:T(8,128)S(1)...) custom-call(f32[106,8,128]{2,1,0:T(8,128)S(1)} %copy-done.1, f32[2,50,16,128]{3,2,1,0:T(8,128)S(1)} %bitcast.42, ...), custom_call_target="tpu_custom_call" | custom-call | tf_op jit(solution)/shard_map/partial_step/pallas_call | solution.py:630
  12.2 0.1 collective-permute-start.2
  12.3 0.5 %collective-permute-start.3 = (f32[100,8,128]{2,1,0:T(8,128)S(1)}, f32[100,8,128]{2,1,0:T(8,128)S(1)}, u32[]{:S(2)}, u32[]{:S(2)}) collective-permute-start(f32[100,8,128]{2,1,0:T(8,128)S(1)} %get-tuple-element.22.mate_raw), channel_id=1, source_target_pairs={{0,1},{1,0},{2,3},{3,2},{4,5},{5,4},{6,7},{7,6},{8,9},{9,8},{10,11... | collective-permute-start | bytes 1228808 | tf_op jit(solution)/shard_map/ppermute | solution.py:553
  12.8 4.4 %collective-permute-start = (f32[100,8,128]{2,1,0:T(8,128)S(1)}, f32[100,8,128]{2,1,0:T(8,128)S(1)}, u32[]{:S(2)}, u32[]{:S(2)}) collective-permute-start(f32[100,8,128]{2,1,0:T(8,128)S(1)} %get-tuple-element.19.cross), channel_id=1, source_target_pairs={{0,15},{1,2},{2,1},{3,4},{4,3},{5,6},{6,5},{7,8},{8,7},{9,10},{10,... | collective-permute-start | bytes 1228808 | tf_op jit(solution)/shard_map/ppermute | solution.py:645
  17.1 0.0 collective-permute-done.5.flow_half
  17.1 1.5 %collective-permute-start.6 = (f32[25,8,128]{2,1,0:T(8,128)S(1)}, f32[25,8,128]{2,1,0:T(8,128)S(1)}, u32[]{:S(2)}, u32[]{:S(2)}) collective-permute-start(f32[25,8,128]{2,1,0:T(8,128)S(1)} %collective-permute-done.5.flow_half), channel_id=1, source_target_pairs={{0,16},{16,0},{1,17},{17,1},{2,18},{18,2},{3,19},{19,3},{4,20},{20... | collective-permute-start | bytes 307208 | tf_op jit(solution)/shard_map/ppermute | solution.py:612
  18.6 3.2 %collective-permute-done.6.flow_other = f32[25,8,128]{2,1,0:T(8,128)S(1)} collective-permute-done((f32[25,8,128]{2,1,0:T(8,128)S(1)}, f32[25,8,128]{2,1,0:T(8,128)S(1)}, u32[]{:S(2)}, u32[]{:S(2)}) %collective-permute-start.6) | collective-permute-done | bytes 102432 | tf_op jit(solution)/shard_map/ppermute | solution.py:612
  21.8 0.0 collective-permute-start.4
  21.8 1.5 %collective-permute-done.4.mate_flow_far = f32[56,8,128]{2,1,0:T(8,128)S(1)} collective-permute-done((f32[56,8,128]{2,1,0:T(8,128)S(1)}, f32[56,8,128]{2,1,0:T(8,128)S(1)}, u32[]{:S(2)}, u32[]{:S(2)}) %collective-permute-start.4) | collective-permute-done | bytes 229408 | tf_op jit(solution)/shard_map/ppermute | solution.py:553
  23.3 0.0 collective-permute-done.2.mate_far
  23.3 0.0 collective-permute-done.3.mate_raw_far
  23.3 0.0 collective-permute-done.1.raw_far
  23.3 1.5 %both_steps.1 = (f32[2,50,8,128]{3,2,1,0:T(8,128)S(1)}, f32[2,50,8,128]{3,2,1,0:T(8,128)S(1)}, f32[50,8,128]{2,1,0:T(8,128)S(1)}, f32[5,8,128]{2,1,0:T(8,128)S(1)}, f32[4,2,2,8,128]{4,3,2,1,0:T(8,128)S(1)}) custom-call(f32[100,8,128]{2,1,0:T(8,128)S(1)} %get-tuple-element.20.raw, f32[100,8,128]{2,1,0:T(8,128)S(1)} %get-tuple-element.19.cross, ...), custom_call_target="tpu_custom_call" | custom-call | tf_op jit(solution)/shard_map/both_steps/pallas_call | solution.py:647
  24.8 0.1 collective-permute-done.cross_far
  24.9 0.2 outer_column.1
  25.1 4.2 %collective-permute-start.7 = (f32[7,8,128]{2,1,0:T(8,128)S(1)}, f32[7,8,128]{2,1,0:T(8,128)S(1)}, u32[]{:S(2)}, u32[]{:S(2)}) collective-permute-start(f32[7,8,128]{2,1,0:T(8,128)S(1)} %get-tuple-element.29), channel_id=1, source_target_pairs={{0,1},{1,0},{2,3},{3,2},{4,5},{5,4},{6,7},{7,6},{8,9},{9,8},{10,11... | collective-permute-start | bytes 86024 | tf_op jit(solution)/shard_map/ppermute | solution.py:553
  29.3 0.9 %collective-permute-done.7 = f32[7,8,128]{2,1,0:T(8,128)S(1)} collective-permute-done((f32[7,8,128]{2,1,0:T(8,128)S(1)}, f32[7,8,128]{2,1,0:T(8,128)S(1)}, u32[]{:S(2)}, u32[]{:S(2)}) %collective-permute-start.7) | collective-permute-done | bytes 28704 | tf_op jit(solution)/shard_map/ppermute | solution.py:553
  30.2 4.2 %collective-permute-start.8 = (f32[2,7,8,128]{3,2,1,0:T(8,128)S(1)}, f32[2,7,8,128]{3,2,1,0:T(8,128)S(1)}, u32[]{:S(2)}, u32[]{:S(2)}) collective-permute-start(f32[2,7,8,128]{3,2,1,0:T(8,128)S(1)} %pad_maximum_fusion.1.pair), channel_id=1, source_target_pairs={{0,14},{1,13},{2,12},{3,15},{4,10},{5,9},{6,8},{7,11},{8,6},{9,5},... | collective-permute-start | bytes 172040 | tf_op jit(solution)/shard_map/ppermute | solution.py:572
  34.4 0.0 collective-permute-start.9
  34.4 1.1 %collective-permute-start.10 = (f32[2,7,8,128]{3,2,1,0:T(8,128)S(1)}, f32[2,7,8,128]{3,2,1,0:T(8,128)S(1)}, u32[]{:S(2)}, u32[]{:S(2)}) collective-permute-start(f32[2,7,8,128]{3,2,1,0:T(8,128)S(1)} %pad_maximum_fusion.1.pair), channel_id=1, source_target_pairs={{0,6},{1,5},{2,4},{3,7},{4,2},{5,1},{6,0},{7,3},{8,14},{9,13},{10,... | collective-permute-start | bytes 172040 | tf_op jit(solution)/shard_map/ppermute | solution.py:572
  35.4 0.7 %collective-permute-start.11 = (f32[2,7,8,128]{3,2,1,0:T(8,128)S(1)}, f32[2,7,8,128]{3,2,1,0:T(8,128)S(1)}, u32[]{:S(2)}, u32[]{:S(2)}) collective-permute-start(f32[2,7,8,128]{3,2,1,0:T(8,128)S(1)} %pad_maximum_fusion.1.pair), channel_id=1, source_target_pairs={{1,3},{3,1},{5,7},{7,5},{9,11},{11,9},{13,15},{15,13},{17,19},{19,... | collective-permute-start | bytes 172040 | tf_op jit(solution)/shard_map/ppermute | solution.py:572
  36.1 1.1 %collective-permute-done.8 = f32[2,7,8,128]{3,2,1,0:T(8,128)S(1)} collective-permute-done((f32[2,7,8,128]{3,2,1,0:T(8,128)S(1)}, f32[2,7,8,128]{3,2,1,0:T(8,128)S(1)}, u32[]{:S(2)}, u32[]{:S(2)}) %collective-permute-start.8) | collective-permute-done | bytes 57376 | tf_op jit(solution)/shard_map/ppermute | solution.py:572
  37.2 2.2 %collective-permute-done.9 = f32[2,7,8,128]{3,2,1,0:T(8,128)S(1)} collective-permute-done((f32[2,7,8,128]{3,2,1,0:T(8,128)S(1)}, f32[2,7,8,128]{3,2,1,0:T(8,128)S(1)}, u32[]{:S(2)}, u32[]{:S(2)}) %collective-permute-start.9) | collective-permute-done | bytes 57376 | tf_op jit(solution)/shard_map/ppermute | solution.py:572
  39.4 0.9 %collective-permute-done.10 = f32[2,7,8,128]{3,2,1,0:T(8,128)S(1)} collective-permute-done((f32[2,7,8,128]{3,2,1,0:T(8,128)S(1)}, f32[2,7,8,128]{3,2,1,0:T(8,128)S(1)}, u32[]{:S(2)}, u32[]{:S(2)}) %collective-permute-start.10) | collective-permute-done | bytes 57376 | tf_op jit(solution)/shard_map/ppermute | solution.py:572
  40.3 0.0 collective-permute-done.11
  40.3 0.1 collective-permute-start.12
  40.5 0.1 interleave.1.tracer
  40.6 1.3 %collective-permute-done.12.fetched_mate = f32[4,2,7,8,128]{4,3,2,1,0:T(8,128)S(1)} collective-permute-done((f32[4,2,7,8,128]{4,3,2,1,0:T(8,128)S(1)}, f32[4,2,7,8,128]{4,3,2,1,0:T(8,128)S(1)}, u32[]{:S(2)}, u32[]{:S(2)}) %collective-permute-start.12) | collective-permute-done | bytes 229408 | tf_op jit(solution)/shard_map/ppermute | solution.py:553
  41.9 2.7 %surface_and_scale.1 = (f32[2,50,16,128]{3,2,1,0:T(8,128)}, f32[2,16,128]{2,1,0:T(8,128)}, f32[3]{0:T(128)}) custom-call(f32[2,7,8,128]{3,2,1,0:T(8,128)S(1)} %pad_maximum_fusion.1.pair, f32[4,2,7,8,128]{4,3,2,1,0:T(8,128)S(1)} %pad_maximum_fusion.fetched, f32[4,2,7,8,128]{4,3,2,1,0:T(8,128)S(1)} %collective-permute-done.12.fetched_mate, ...), custom_call_target="tpu_custom_call" | custom-call | tf_op jit(solution)/shard_map/surface_and_scale/pallas_call | solution.py:681
  (2 shorter events, 0.0 us)
Async XLA Ops:
  0.6 9.3 %copy-start.3 = (f32[50,2,1024]{2,1,0:T(2,128)S(1)}, f32[50,2,1024]{2,1,0:T(2,128)}, u32[]{:S(2)}) copy-start(f32[50,2,1024]{2,1,0:T(2,128)} %param.8) | copy-start | bytes 1228804
  2.3 7.6 %copy-start = (f32[2,50,2,1024]{3,2,1,0:T(2,128)S(1)}, f32[2,50,2,1024]{3,2,1,0:T(2,128)}, u32[]{:S(2)}) copy-start(f32[2,50,2,1024]{3,2,1,0:T(2,128)} %param.5) | copy-start | bytes 2457604
  2.3 14.8 %collective-permute-start.5 = (f32[25,8,128]{2,1,0:T(8,128)}, f32[25,8,128]{2,1,0:T(8,128)S(1)}, u32[]{:S(2)}, u32[]{:S(2)}) collective-permute-start(f32[25,8,128]{2,1,0:T(8,128)} %flow_column.1.flow), channel_id=1, source_target_pairs={{0,15},{1,2},{2,1},{3,4},{4,3},{5,6},{6,5},{7,8},{8,7},{9,10},{10,... | collective-permute-start | bytes 307208 | tf_op jit(solution)/shard_map/ppermute | solution.py:611
  7.8 2.1 %copy-start.2 = (f32[50,2,1024]{2,1,0:T(2,128)S(1)}, f32[50,2,1024]{2,1,0:T(2,128)}, u32[]{:S(2)}) copy-start(f32[50,2,1024]{2,1,0:T(2,128)} %param.7) | copy-start | bytes 1228804
  7.8 2.1 %copy-start.4 = (f32[2,2,1024]{2,1,0:T(2,128)S(1)}, f32[2,2,1024]{2,1,0:T(2,128)}, u32[]{:S(2)}) copy-start(f32[2,2,1024]{2,1,0:T(2,128)} %param.6) | copy-start | bytes 49156
  7.8 2.1 %copy-start.5 = (s32[2,1024]{1,0:T(2,128)S(1)}, s32[2,1024]{1,0:T(2,128)}, u32[]{:S(2)}) copy-start(s32[2,1024]{1,0:T(2,128)} %param.9) | copy-start | bytes 24580
  9.8 13.5 %collective-permute-start.1 = (f32[106,8,128]{2,1,0:T(8,128)}, f32[106,8,128]{2,1,0:T(8,128)S(1)}, u32[]{:S(2)}, u32[]{:S(2)}) collective-permute-start(f32[106,8,128]{2,1,0:T(8,128)} %edge_columns.1.edge), channel_id=1, source_target_pairs={{0,15},{1,2},{2,1},{3,4},{4,3},{5,6},{6,5},{7,8},{8,7},{9,10},{10,... | collective-permute-start | bytes 1302536 | tf_op jit(solution)/shard_map/ppermute | solution.py:629
  10.0 1.0 %copy-start.1 = (f32[106,8,128]{2,1,0:T(8,128)S(1)}, f32[106,8,128]{2,1,0:T(8,128)}, u32[]{:S(2)}) copy-start(f32[106,8,128]{2,1,0:T(8,128)} %edge_columns.1.edge) | copy-start | bytes 1302532
  12.2 11.1 %collective-permute-start.2 = (f32[100,8,128]{2,1,0:T(8,128)S(1)}, f32[100,8,128]{2,1,0:T(8,128)S(1)}, u32[]{:S(2)}, u32[]{:S(2)}) collective-permute-start(f32[100,8,128]{2,1,0:T(8,128)S(1)} %get-tuple-element.21.mate), channel_id=1, source_target_pairs={{0,1},{1,0},{2,3},{3,2},{4,5},{5,4},{6,7},{7,6},{8,9},{9,8},{10,11... | collective-permute-start | bytes 1228808 | tf_op jit(solution)/shard_map/ppermute | solution.py:553
  12.3 11.0 %collective-permute-start.3 = (f32[100,8,128]{2,1,0:T(8,128)S(1)}, f32[100,8,128]{2,1,0:T(8,128)S(1)}, u32[]{:S(2)}, u32[]{:S(2)}) collective-permute-start(f32[100,8,128]{2,1,0:T(8,128)S(1)} %get-tuple-element.22.mate_raw), channel_id=1, source_target_pairs={{0,1},{1,0},{2,3},{3,2},{4,5},{5,4},{6,7},{7,6},{8,9},{9,8},{10,11... | collective-permute-start | bytes 1228808 | tf_op jit(solution)/shard_map/ppermute | solution.py:553
  12.8 12.1 %collective-permute-start = (f32[100,8,128]{2,1,0:T(8,128)S(1)}, f32[100,8,128]{2,1,0:T(8,128)S(1)}, u32[]{:S(2)}, u32[]{:S(2)}) collective-permute-start(f32[100,8,128]{2,1,0:T(8,128)S(1)} %get-tuple-element.19.cross), channel_id=1, source_target_pairs={{0,15},{1,2},{2,1},{3,4},{4,3},{5,6},{6,5},{7,8},{8,7},{9,10},{10,... | collective-permute-start | bytes 1228808 | tf_op jit(solution)/shard_map/ppermute | solution.py:645
  17.1 4.7 %collective-permute-start.6 = (f32[25,8,128]{2,1,0:T(8,128)S(1)}, f32[25,8,128]{2,1,0:T(8,128)S(1)}, u32[]{:S(2)}, u32[]{:S(2)}) collective-permute-start(f32[25,8,128]{2,1,0:T(8,128)S(1)} %collective-permute-done.5.flow_half), channel_id=1, source_target_pairs={{0,16},{16,0},{1,17},{17,1},{2,18},{18,2},{3,19},{19,3},{4,20},{20... | collective-permute-start | bytes 307208 | tf_op jit(solution)/shard_map/ppermute | solution.py:612
  21.8 1.5 %collective-permute-start.4 = (f32[56,8,128]{2,1,0:T(8,128)S(1)}, f32[56,8,128]{2,1,0:T(8,128)S(1)}, u32[]{:S(2)}, u32[]{:S(2)}) collective-permute-start(f32[56,8,128]{2,1,0:T(8,128)S(1)} %get-tuple-element.24.mate_flow), channel_id=1, source_target_pairs={{0,1},{1,0},{2,3},{3,2},{4,5},{5,4},{6,7},{7,6},{8,9},{9,8},{10,11... | collective-permute-start | bytes 688136 | tf_op jit(solution)/shard_map/ppermute | solution.py:553
  25.1 5.0 %collective-permute-start.7 = (f32[7,8,128]{2,1,0:T(8,128)S(1)}, f32[7,8,128]{2,1,0:T(8,128)S(1)}, u32[]{:S(2)}, u32[]{:S(2)}) collective-permute-start(f32[7,8,128]{2,1,0:T(8,128)S(1)} %get-tuple-element.29), channel_id=1, source_target_pairs={{0,1},{1,0},{2,3},{3,2},{4,5},{5,4},{6,7},{7,6},{8,9},{9,8},{10,11... | collective-permute-start | bytes 86024 | tf_op jit(solution)/shard_map/ppermute | solution.py:553
  30.2 7.1 %collective-permute-start.8 = (f32[2,7,8,128]{3,2,1,0:T(8,128)S(1)}, f32[2,7,8,128]{3,2,1,0:T(8,128)S(1)}, u32[]{:S(2)}, u32[]{:S(2)}) collective-permute-start(f32[2,7,8,128]{3,2,1,0:T(8,128)S(1)} %pad_maximum_fusion.1.pair), channel_id=1, source_target_pairs={{0,14},{1,13},{2,12},{3,15},{4,10},{5,9},{6,8},{7,11},{8,6},{9,5},... | collective-permute-start | bytes 172040 | tf_op jit(solution)/shard_map/ppermute | solution.py:572
  34.4 5.1 %collective-permute-start.9 = (f32[2,7,8,128]{3,2,1,0:T(8,128)S(1)}, f32[2,7,8,128]{3,2,1,0:T(8,128)S(1)}, u32[]{:S(2)}, u32[]{:S(2)}) collective-permute-start(f32[2,7,8,128]{3,2,1,0:T(8,128)S(1)} %pad_maximum_fusion.1.pair), channel_id=1, source_target_pairs={{0,8},{1,11},{2,10},{3,9},{4,12},{5,15},{6,14},{7,13},{8,0},{9,3},... | collective-permute-start | bytes 172040 | tf_op jit(solution)/shard_map/ppermute | solution.py:572
  34.4 6.0 %collective-permute-start.10 = (f32[2,7,8,128]{3,2,1,0:T(8,128)S(1)}, f32[2,7,8,128]{3,2,1,0:T(8,128)S(1)}, u32[]{:S(2)}, u32[]{:S(2)}) collective-permute-start(f32[2,7,8,128]{3,2,1,0:T(8,128)S(1)} %pad_maximum_fusion.1.pair), channel_id=1, source_target_pairs={{0,6},{1,5},{2,4},{3,7},{4,2},{5,1},{6,0},{7,3},{8,14},{9,13},{10,... | collective-permute-start | bytes 172040 | tf_op jit(solution)/shard_map/ppermute | solution.py:572
  35.4 4.9 %collective-permute-start.11 = (f32[2,7,8,128]{3,2,1,0:T(8,128)S(1)}, f32[2,7,8,128]{3,2,1,0:T(8,128)S(1)}, u32[]{:S(2)}, u32[]{:S(2)}) collective-permute-start(f32[2,7,8,128]{3,2,1,0:T(8,128)S(1)} %pad_maximum_fusion.1.pair), channel_id=1, source_target_pairs={{1,3},{3,1},{5,7},{7,5},{9,11},{11,9},{13,15},{15,13},{17,19},{19,... | collective-permute-start | bytes 172040 | tf_op jit(solution)/shard_map/ppermute | solution.py:572
  40.3 1.6 %collective-permute-start.12 = (f32[4,2,7,8,128]{4,3,2,1,0:T(8,128)S(1)}, f32[4,2,7,8,128]{4,3,2,1,0:T(8,128)S(1)}, u32[]{:S(2)}, u32[]{:S(2)}) collective-permute-start(f32[4,2,7,8,128]{4,3,2,1,0:T(8,128)S(1)} %pad_maximum_fusion.fetched), channel_id=1, source_target_pairs={{0,1},{1,0},{2,3},{3,2},{4,5},{5,4},{6,7},{7,6},{8,9},{9,8},{10,11... | collective-permute-start | bytes 688136 | tf_op jit(solution)/shard_map/ppermute | solution.py:553

commit v12 on v10

--- a/solution.py
+++ b/solution.py
@@ -387,7 +387,7 @@
 
 def third_kernel(
     levels, sub, count, pair, fetched, fetched_mate, surface, tracer,
-    tracer_hbm, surface_out, growth, scaled, sems, pole, residual, answer, image, depth, face_x, face_y, face_z, packed,
+    scaled, surface_out, growth, pole, residual, answer, image, depth, face_x, face_y, face_z, packed,
 ):
     width = 2 * count
     me = lax.axis_index("lon")
@@ -514,21 +514,13 @@
     scale_two = jnp.sqrt(rest + EPSILON)
     over_one, over_two = 1.0 / scale_one, 1.0 / scale_two
 
-    chunk = steps(levels, 10)
-    departures = []
-
     def scale(k, carry):
         unit = tracer[0, k] * over_one
         scaled[0, k] = unit
         scaled[1, k] = (tracer[1, k] - cross * unit) * over_two
         return carry
 
-    for n in range(levels // chunk):
-        lax.fori_loop(n * chunk, (n + 1) * chunk, scale, 0, unroll=chunk)
-        rows = pl.ds(n * chunk, chunk)
-        departure = pltpu.make_async_copy(scaled.at[:, rows], tracer_hbm.at[:, rows], sems.at[n])
-        departure.start()
-        departures.append(departure)
+    lax.fori_loop(0, levels, scale, 0, unroll=steps(levels, 10))
     for c in range(2):
         x = 2 * me + c
         first, second = (
@@ -540,8 +532,6 @@
         surface_out[1, pl.ds(c, sub, stride=2), :] = (second - cross * unit) * over_two
     for i, value in enumerate((scale_one, cross, scale_two)):
         growth[i] = value[0, 0]
-    for departure in departures:
-        departure.wait()
 
 
 def tiled(array):
@@ -687,10 +677,8 @@
             jax.ShapeDtypeStruct((3,), f32),
         ),
         in_specs=[vmem] * 5,
-        out_specs=(hbm, vmem, pl.BlockSpec(memory_space=pltpu.SMEM)),
+        out_specs=(vmem, vmem, pl.BlockSpec(memory_space=pltpu.SMEM)),
         scratch_shapes=[
-            both,
-            pltpu.SemaphoreType.DMA((levels // steps(levels, 10),)),
             held(vectors, width + 2),
             *[held(vectors, width)] * 3,
             held(width),

time: 44.5 us -> 44.1 us (level)
  Pallas kernels: 8.3 us -> 7.85 us
    pallas_call x1, Pallas kernels: 3.13 us -> 2.68 us  [on_device(): pl.pallas_call(functools.partial(third_kernel, levels, sub, count), out_s...]
where the time goes in v12:
time: 44.1 us; the launch traced here: 43.9 us
  starting transfers between devices  22.2 us (50%)
  waiting for transfers between devices  10.9 us (25%)
  Pallas kernels  7.85 us (18%)
  local copies, waits for them, and re-layouts  2.03 us (5%)
  between operations  0.76 us (2%)
    ppermute x4, starting transfers between devices, gather(): fetched.append(lax.ppermute(pair, 'lon', moves))  5.94 us
    ppermute x1, starting transfers between devices, on_device(): flow_half = lax.ppermute(flow_edge, 'lon', outward)  5.51 us
    ppermute x5, starting transfers between devices, swap(): return lax.ppermute(array, 'lon', [(i, i ^ mask) for i in range(count)])  4.86 us
    ppermute x1, starting transfers between devices, on_device(): cross_far = lax.ppermute(cross, 'lon', outward)  4.36 us
    ppermute x4, waiting for transfers between devices, gather(): fetched.append(lax.ppermute(pair, 'lon', moves))  4.17 us
    ppermute x5, waiting for transfers between devices, swap(): return lax.ppermute(array, 'lon', [(i, i ^ mask) for i in range(count)])  3.59 us
    ppermute x1, waiting for transfers between devices, on_device(): flow_other = lax.ppermute(flow_half, 'grp', [(0, 1), (1, 0)])  3.17 us
    pallas_call x1, Pallas kernels, on_device(): pl.pallas_call(functools.partial(third_kernel, levels, sub, count), out_s...  2.68 us
  transfers between devices with their start and end apart: 13, of which 7 were waited for; matrix products, arithmetic and copies ran while one was open for 0% of the time, Pallas kernels for 6%

profile of v12, /device:TPU:0, one launch (start us, length us, event | category | flops | bytes accessed | tf_op | source)
XLA Modules:
  0.0 43.9 jit_solution(12642987999324603868)
XLA Ops:
  0.6 0.0 copy-start
  0.6 0.0 copy-start.1
  0.7 0.0 copy-start.5
  0.7 0.0 copy-start.6
  0.7 2.1 %edge_columns.1 = (f32[106,8,128]{2,1,0:T(8,128)}, f32[25,8,128]{2,1,0:T(8,128)}) custom-call(f32[2,50,16,128]{3,2,1,0:T(8,128)} %bitcast.41, f32[50,16,128]{2,1,0:T(8,128)} %bitcast.43, f32[2,16,128]{2,1,0:T(8,128)} %bitcast.47, s32[16,128]{1,0:T(8,128)} %bitcast.50), custom_call_target="tpu_custom_call" | custom-call | tf_op jit(solution)/shard_map/edge_columns/pallas_call | solution.py:600
  2.8 5.5 %collective-permute-start.5 = (f32[25,8,128]{2,1,0:T(8,128)}, f32[25,8,128]{2,1,0:T(8,128)S(1)}, u32[]{:S(2)}, u32[]{:S(2)}) collective-permute-start(f32[25,8,128]{2,1,0:T(8,128)} %get-tuple-element.28), channel_id=1, source_target_pairs={{0,15},{1,2},{2,1},{3,4},{4,3},{5,6},{6,5},{7,8},{8,7},{9,10},{10,... | collective-permute-start | bytes 307208 | tf_op jit(solution)/shard_map/ppermute | solution.py:618
  8.3 0.1 collective-permute-start.1
  8.4 0.0 copy-done
  8.4 0.0 copy-done.1
  8.4 0.0 copy-done.5
  8.4 0.0 copy-done.6
  8.4 0.0 copy-start.2
  8.4 1.0 %copy-done.2 = f32[50,2,1024]{2,1,0:T(2,128)S(1)} copy-done((f32[50,2,1024]{2,1,0:T(2,128)S(1)}, f32[50,2,1024]{2,1,0:T(2,128)}, u32[]{:S(2)}) %copy-start.2) | copy-done | bytes 409624
  9.4 0.0 copy-start.4
  9.4 1.0 %copy-done.4 = f32[106,8,128]{2,1,0:T(8,128)S(1)} copy-done((f32[106,8,128]{2,1,0:T(8,128)S(1)}, f32[106,8,128]{2,1,0:T(8,128)}, u32[]{:S(2)}) %copy-start.4) | copy-done | bytes 434200
  10.4 0.0 copy-start.3
  10.4 1.2 %partial_step.1 = (f32[100,8,128]{2,1,0:T(8,128)S(1)}, f32[100,8,128]{2,1,0:T(8,128)S(1)}, f32[100,8,128]{2,1,0:T(8,128)S(1)}, f32[100,8,128]{2,1,0:T(8,128)S(1)...) custom-call(f32[106,8,128]{2,1,0:T(8,128)S(1)} %copy-done.4, f32[2,50,16,128]{3,2,1,0:T(8,128)S(1)} %bitcast.42, ...), custom_call_target="tpu_custom_call" | custom-call | tf_op jit(solution)/shard_map/partial_step/pallas_call | solution.py:621
  11.6 0.1 collective-permute-start.2
  11.7 0.5 %collective-permute-start.3 = (f32[100,8,128]{2,1,0:T(8,128)S(1)}, f32[100,8,128]{2,1,0:T(8,128)S(1)}, u32[]{:S(2)}, u32[]{:S(2)}) collective-permute-start(f32[100,8,128]{2,1,0:T(8,128)S(1)} %get-tuple-element.25.mate_raw), channel_id=1, source_target_pairs={{0,1},{1,0},{2,3},{3,2},{4,5},{5,4},{6,7},{7,6},{8,9},{9,8},{10,11... | collective-permute-start | bytes 1228808 | tf_op jit(solution)/shard_map/ppermute | solution.py:551
  12.2 4.4 %collective-permute-start = (f32[100,8,128]{2,1,0:T(8,128)S(1)}, f32[100,8,128]{2,1,0:T(8,128)S(1)}, u32[]{:S(2)}, u32[]{:S(2)}) collective-permute-start(f32[100,8,128]{2,1,0:T(8,128)S(1)} %get-tuple-element.22.cross), channel_id=1, source_target_pairs={{0,15},{1,2},{2,1},{3,4},{4,3},{5,6},{6,5},{7,8},{8,7},{9,10},{10,... | collective-permute-start | bytes 1228808 | tf_op jit(solution)/shard_map/ppermute | solution.py:636
  16.6 0.0 collective-permute-done.5.flow_half
  16.6 1.5 %collective-permute-start.6 = (f32[25,8,128]{2,1,0:T(8,128)S(1)}, f32[25,8,128]{2,1,0:T(8,128)S(1)}, u32[]{:S(2)}, u32[]{:S(2)}) collective-permute-start(f32[25,8,128]{2,1,0:T(8,128)S(1)} %collective-permute-done.5.flow_half), channel_id=1, source_target_pairs={{0,16},{16,0},{1,17},{17,1},{2,18},{18,2},{3,19},{19,3},{4,20},{20... | collective-permute-start | bytes 307208 | tf_op jit(solution)/shard_map/ppermute | solution.py:620
  18.1 3.2 %collective-permute-done.6.flow_other = f32[25,8,128]{2,1,0:T(8,128)S(1)} collective-permute-done((f32[25,8,128]{2,1,0:T(8,128)S(1)}, f32[25,8,128]{2,1,0:T(8,128)S(1)}, u32[]{:S(2)}, u32[]{:S(2)}) %collective-permute-start.6) | collective-permute-done | bytes 102432 | tf_op jit(solution)/shard_map/ppermute | solution.py:620
  21.2 0.0 collective-permute-start.4
  21.2 1.5 %collective-permute-done.4.mate_flow_far = f32[56,8,128]{2,1,0:T(8,128)S(1)} collective-permute-done((f32[56,8,128]{2,1,0:T(8,128)S(1)}, f32[56,8,128]{2,1,0:T(8,128)S(1)}, u32[]{:S(2)}, u32[]{:S(2)}) %collective-permute-start.4) | collective-permute-done | bytes 229408 | tf_op jit(solution)/shard_map/ppermute | solution.py:551
  22.7 0.0 collective-permute-done.2.mate_far
  22.7 0.0 collective-permute-done.3.mate_raw_far
  22.7 0.0 collective-permute-done.1.raw_far
  22.7 0.0 copy-done.3
  22.8 1.5 %both_steps.1 = (f32[2,50,8,128]{3,2,1,0:T(8,128)S(1)}, f32[2,50,8,128]{3,2,1,0:T(8,128)S(1)}, f32[50,8,128]{2,1,0:T(8,128)S(1)}, f32[5,8,128]{2,1,0:T(8,128)S(1)}, f32[4,2,2,8,128]{4,3,2,1,0:T(8,128)S(1)}) custom-call(f32[100,8,128]{2,1,0:T(8,128)S(1)} %get-tuple-element.23.raw, f32[100,8,128]{2,1,0:T(8,128)S(1)} %get-tuple-element.22.cross, ...), custom_call_target="tpu_custom_call" | custom-call | tf_op jit(solution)/shard_map/both_steps/pallas_call | solution.py:638
  24.3 0.0 collective-permute-done.cross_far
  24.3 0.2 outer_column.1
  24.5 4.1 %collective-permute-start.7 = (f32[7,8,128]{2,1,0:T(8,128)S(1)}, f32[7,8,128]{2,1,0:T(8,128)S(1)}, u32[]{:S(2)}, u32[]{:S(2)}) collective-permute-start(f32[7,8,128]{2,1,0:T(8,128)S(1)} %get-tuple-element.33), channel_id=1, source_target_pairs={{0,1},{1,0},{2,3},{3,2},{4,5},{5,4},{6,7},{7,6},{8,9},{9,8},{10,11... | collective-permute-start | bytes 86024 | tf_op jit(solution)/shard_map/ppermute | solution.py:551
  28.6 0.9 %collective-permute-done.7 = f32[7,8,128]{2,1,0:T(8,128)S(1)} collective-permute-done((f32[7,8,128]{2,1,0:T(8,128)S(1)}, f32[7,8,128]{2,1,0:T(8,128)S(1)}, u32[]{:S(2)}, u32[]{:S(2)}) %collective-permute-start.7) | collective-permute-done | bytes 28704 | tf_op jit(solution)/shard_map/ppermute | solution.py:551
  29.5 4.4 %collective-permute-start.8 = (f32[2,7,8,128]{3,2,1,0:T(8,128)S(1)}, f32[2,7,8,128]{3,2,1,0:T(8,128)S(1)}, u32[]{:S(2)}, u32[]{:S(2)}) collective-permute-start(f32[2,7,8,128]{3,2,1,0:T(8,128)S(1)} %pad_maximum_fusion.1.pair), channel_id=1, source_target_pairs={{0,14},{1,13},{2,12},{3,15},{4,10},{5,9},{6,8},{7,11},{8,6},{9,5},... | collective-permute-start | bytes 172040 | tf_op jit(solution)/shard_map/ppermute | solution.py:570
  33.8 0.0 collective-permute-start.9
  33.8 0.9 %collective-permute-start.10 = (f32[2,7,8,128]{3,2,1,0:T(8,128)S(1)}, f32[2,7,8,128]{3,2,1,0:T(8,128)S(1)}, u32[]{:S(2)}, u32[]{:S(2)}) collective-permute-start(f32[2,7,8,128]{3,2,1,0:T(8,128)S(1)} %pad_maximum_fusion.1.pair), channel_id=1, source_target_pairs={{0,6},{1,5},{2,4},{3,7},{4,2},{5,1},{6,0},{7,3},{8,14},{9,13},{10,... | collective-permute-start | bytes 172040 | tf_op jit(solution)/shard_map/ppermute | solution.py:570
  34.8 0.7 %collective-permute-start.11 = (f32[2,7,8,128]{3,2,1,0:T(8,128)S(1)}, f32[2,7,8,128]{3,2,1,0:T(8,128)S(1)}, u32[]{:S(2)}, u32[]{:S(2)}) collective-permute-start(f32[2,7,8,128]{3,2,1,0:T(8,128)S(1)} %pad_maximum_fusion.1.pair), channel_id=1, source_target_pairs={{1,3},{3,1},{5,7},{7,5},{9,11},{11,9},{13,15},{15,13},{17,19},{19,... | collective-permute-start | bytes 172040 | tf_op jit(solution)/shard_map/ppermute | solution.py:570
  35.4 1.4 %collective-permute-done.8 = f32[2,7,8,128]{3,2,1,0:T(8,128)S(1)} collective-permute-done((f32[2,7,8,128]{3,2,1,0:T(8,128)S(1)}, f32[2,7,8,128]{3,2,1,0:T(8,128)S(1)}, u32[]{:S(2)}, u32[]{:S(2)}) %collective-permute-start.8) | collective-permute-done | bytes 57376 | tf_op jit(solution)/shard_map/ppermute | solution.py:570
  36.8 2.2 %collective-permute-done.9 = f32[2,7,8,128]{3,2,1,0:T(8,128)S(1)} collective-permute-done((f32[2,7,8,128]{3,2,1,0:T(8,128)S(1)}, f32[2,7,8,128]{3,2,1,0:T(8,128)S(1)}, u32[]{:S(2)}, u32[]{:S(2)}) %collective-permute-start.9) | collective-permute-done | bytes 57376 | tf_op jit(solution)/shard_map/ppermute | solution.py:570
  39.1 0.5 %collective-permute-done.10 = f32[2,7,8,128]{3,2,1,0:T(8,128)S(1)} collective-permute-done((f32[2,7,8,128]{3,2,1,0:T(8,128)S(1)}, f32[2,7,8,128]{3,2,1,0:T(8,128)S(1)}, u32[]{:S(2)}, u32[]{:S(2)}) %collective-permute-start.10) | collective-permute-done | bytes 57376 | tf_op jit(solution)/shard_map/ppermute | solution.py:570
  39.6 0.0 collective-permute-done.11
  39.6 0.2 collective-permute-start.12
  39.8 0.1 interleave.1.tracer
  39.9 1.2 %collective-permute-done.12.fetched_mate = f32[4,2,7,8,128]{4,3,2,1,0:T(8,128)S(1)} collective-permute-done((f32[4,2,7,8,128]{4,3,2,1,0:T(8,128)S(1)}, f32[4,2,7,8,128]{4,3,2,1,0:T(8,128)S(1)}, u32[]{:S(2)}, u32[]{:S(2)}) %collective-permute-start.12) | collective-permute-done | bytes 229408 | tf_op jit(solution)/shard_map/ppermute | solution.py:551
  41.2 2.7 %surface_and_scale.1 = (f32[2,50,16,128]{3,2,1,0:T(8,128)}, f32[2,16,128]{2,1,0:T(8,128)}, f32[3]{0:T(128)}) custom-call(f32[2,7,8,128]{3,2,1,0:T(8,128)S(1)} %pad_maximum_fusion.1.pair, f32[4,2,7,8,128]{4,3,2,1,0:T(8,128)S(1)} %pad_maximum_fusion.fetched, f32[4,2,7,8,128]{4,3,2,1,0:T(8,128)S(1)} %collective-permute-done.12.fetched_mate, ...), custom_call_target="tpu_custom_call" | custom-call | tf_op jit(solution)/shard_map/surface_and_scale/pallas_call | solution.py:672
  (2 shorter events, 0.0 us)
Async XLA Ops:
  0.6 7.8 %copy-start = (f32[2,50,2,1024]{3,2,1,0:T(2,128)S(1)}, f32[2,50,2,1024]{3,2,1,0:T(2,128)}, u32[]{:S(2)}) copy-start(f32[2,50,2,1024]{3,2,1,0:T(2,128)} %param.5) | copy-start | bytes 2457604
  0.6 7.8 %copy-start.1 = (f32[50,2,1024]{2,1,0:T(2,128)S(1)}, f32[50,2,1024]{2,1,0:T(2,128)}, u32[]{:S(2)}) copy-start(f32[50,2,1024]{2,1,0:T(2,128)} %param.7) | copy-start | bytes 1228804
  0.7 7.8 %copy-start.5 = (f32[2,2,1024]{2,1,0:T(2,128)S(1)}, f32[2,2,1024]{2,1,0:T(2,128)}, u32[]{:S(2)}) copy-start(f32[2,2,1024]{2,1,0:T(2,128)} %param.6) | copy-start | bytes 49156
  0.7 7.8 %copy-start.6 = (s32[2,1024]{1,0:T(2,128)S(1)}, s32[2,1024]{1,0:T(2,128)}, u32[]{:S(2)}) copy-start(s32[2,1024]{1,0:T(2,128)} %param.9) | copy-start | bytes 24580
  2.8 13.8 %collective-permute-start.5 = (f32[25,8,128]{2,1,0:T(8,128)}, f32[25,8,128]{2,1,0:T(8,128)S(1)}, u32[]{:S(2)}, u32[]{:S(2)}) collective-permute-start(f32[25,8,128]{2,1,0:T(8,128)} %get-tuple-element.28), channel_id=1, source_target_pairs={{0,15},{1,2},{2,1},{3,4},{4,3},{5,6},{6,5},{7,8},{8,7},{9,10},{10,... | collective-permute-start | bytes 307208 | tf_op jit(solution)/shard_map/ppermute | solution.py:618
  8.3 14.4 %collective-permute-start.1 = (f32[106,8,128]{2,1,0:T(8,128)}, f32[106,8,128]{2,1,0:T(8,128)S(1)}, u32[]{:S(2)}, u32[]{:S(2)}) collective-permute-start(f32[106,8,128]{2,1,0:T(8,128)} %get-tuple-element.21.edge), channel_id=1, source_target_pairs={{0,15},{1,2},{2,1},{3,4},{4,3},{5,6},{6,5},{7,8},{8,7},{9,10},{10,... | collective-permute-start | bytes 1302536 | tf_op jit(solution)/shard_map/ppermute | solution.py:619
  8.4 1.0 %copy-start.2 = (f32[50,2,1024]{2,1,0:T(2,128)S(1)}, f32[50,2,1024]{2,1,0:T(2,128)}, u32[]{:S(2)}) copy-start(f32[50,2,1024]{2,1,0:T(2,128)} %param.8) | copy-start | bytes 1228804
  9.4 1.0 %copy-start.4 = (f32[106,8,128]{2,1,0:T(8,128)S(1)}, f32[106,8,128]{2,1,0:T(8,128)}, u32[]{:S(2)}) copy-start(f32[106,8,128]{2,1,0:T(8,128)} %get-tuple-element.21.edge) | copy-start | bytes 1302532
  10.4 12.3 %copy-start.3 = (f32[50,2,1024]{2,1,0:T(2,128)S(1)}, f32[50,2,1024]{2,1,0:T(2,128)}, u32[]{:S(2)}) copy-start(f32[50,2,1024]{2,1,0:T(2,128)} %param.8) | copy-start | bytes 1228804
  11.6 11.1 %collective-permute-start.2 = (f32[100,8,128]{2,1,0:T(8,128)S(1)}, f32[100,8,128]{2,1,0:T(8,128)S(1)}, u32[]{:S(2)}, u32[]{:S(2)}) collective-permute-start(f32[100,8,128]{2,1,0:T(8,128)S(1)} %get-tuple-element.24.mate), channel_id=1, source_target_pairs={{0,1},{1,0},{2,3},{3,2},{4,5},{5,4},{6,7},{7,6},{8,9},{9,8},{10,11... | collective-permute-start | bytes 1228808 | tf_op jit(solution)/shard_map/ppermute | solution.py:551
  11.7 11.0 %collective-permute-start.3 = (f32[100,8,128]{2,1,0:T(8,128)S(1)}, f32[100,8,128]{2,1,0:T(8,128)S(1)}, u32[]{:S(2)}, u32[]{:S(2)}) collective-permute-start(f32[100,8,128]{2,1,0:T(8,128)S(1)} %get-tuple-element.25.mate_raw), channel_id=1, source_target_pairs={{0,1},{1,0},{2,3},{3,2},{4,5},{5,4},{6,7},{7,6},{8,9},{9,8},{10,11... | collective-permute-start | bytes 1228808 | tf_op jit(solution)/shard_map/ppermute | solution.py:551
  12.2 12.1 %collective-permute-start = (f32[100,8,128]{2,1,0:T(8,128)S(1)}, f32[100,8,128]{2,1,0:T(8,128)S(1)}, u32[]{:S(2)}, u32[]{:S(2)}) collective-permute-start(f32[100,8,128]{2,1,0:T(8,128)S(1)} %get-tuple-element.22.cross), channel_id=1, source_target_pairs={{0,15},{1,2},{2,1},{3,4},{4,3},{5,6},{6,5},{7,8},{8,7},{9,10},{10,... | collective-permute-start | bytes 1228808 | tf_op jit(solution)/shard_map/ppermute | solution.py:636
  16.6 4.7 %collective-permute-start.6 = (f32[25,8,128]{2,1,0:T(8,128)S(1)}, f32[25,8,128]{2,1,0:T(8,128)S(1)}, u32[]{:S(2)}, u32[]{:S(2)}) collective-permute-start(f32[25,8,128]{2,1,0:T(8,128)S(1)} %collective-permute-done.5.flow_half), channel_id=1, source_target_pairs={{0,16},{16,0},{1,17},{17,1},{2,18},{18,2},{3,19},{19,3},{4,20},{20... | collective-permute-start | bytes 307208 | tf_op jit(solution)/shard_map/ppermute | solution.py:620
  21.2 1.5 %collective-permute-start.4 = (f32[56,8,128]{2,1,0:T(8,128)S(1)}, f32[56,8,128]{2,1,0:T(8,128)S(1)}, u32[]{:S(2)}, u32[]{:S(2)}) collective-permute-start(f32[56,8,128]{2,1,0:T(8,128)S(1)} %get-tuple-element.27.mate_flow), channel_id=1, source_target_pairs={{0,1},{1,0},{2,3},{3,2},{4,5},{5,4},{6,7},{7,6},{8,9},{9,8},{10,11... | collective-permute-start | bytes 688136 | tf_op jit(solution)/shard_map/ppermute | solution.py:551
  24.5 5.0 %collective-permute-start.7 = (f32[7,8,128]{2,1,0:T(8,128)S(1)}, f32[7,8,128]{2,1,0:T(8,128)S(1)}, u32[]{:S(2)}, u32[]{:S(2)}) collective-permute-start(f32[7,8,128]{2,1,0:T(8,128)S(1)} %get-tuple-element.33), channel_id=1, source_target_pairs={{0,1},{1,0},{2,3},{3,2},{4,5},{5,4},{6,7},{7,6},{8,9},{9,8},{10,11... | collective-permute-start | bytes 86024 | tf_op jit(solution)/shard_map/ppermute | solution.py:551
  29.5 7.3 %collective-permute-start.8 = (f32[2,7,8,128]{3,2,1,0:T(8,128)S(1)}, f32[2,7,8,128]{3,2,1,0:T(8,128)S(1)}, u32[]{:S(2)}, u32[]{:S(2)}) collective-permute-start(f32[2,7,8,128]{3,2,1,0:T(8,128)S(1)} %pad_maximum_fusion.1.pair), channel_id=1, source_target_pairs={{0,14},{1,13},{2,12},{3,15},{4,10},{5,9},{6,8},{7,11},{8,6},{9,5},... | collective-permute-start | bytes 172040 | tf_op jit(solution)/shard_map/ppermute | solution.py:570
  33.8 5.2 %collective-permute-start.9 = (f32[2,7,8,128]{3,2,1,0:T(8,128)S(1)}, f32[2,7,8,128]{3,2,1,0:T(8,128)S(1)}, u32[]{:S(2)}, u32[]{:S(2)}) collective-permute-start(f32[2,7,8,128]{3,2,1,0:T(8,128)S(1)} %pad_maximum_fusion.1.pair), channel_id=1, source_target_pairs={{0,8},{1,11},{2,10},{3,9},{4,12},{5,15},{6,14},{7,13},{8,0},{9,3},... | collective-permute-start | bytes 172040 | tf_op jit(solution)/shard_map/ppermute | solution.py:570
  33.8 5.8 %collective-permute-start.10 = (f32[2,7,8,128]{3,2,1,0:T(8,128)S(1)}, f32[2,7,8,128]{3,2,1,0:T(8,128)S(1)}, u32[]{:S(2)}, u32[]{:S(2)}) collective-permute-start(f32[2,7,8,128]{3,2,1,0:T(8,128)S(1)} %pad_maximum_fusion.1.pair), channel_id=1, source_target_pairs={{0,6},{1,5},{2,4},{3,7},{4,2},{5,1},{6,0},{7,3},{8,14},{9,13},{10,... | collective-permute-start | bytes 172040 | tf_op jit(solution)/shard_map/ppermute | solution.py:570
  34.8 4.8 %collective-permute-start.11 = (f32[2,7,8,128]{3,2,1,0:T(8,128)S(1)}, f32[2,7,8,128]{3,2,1,0:T(8,128)S(1)}, u32[]{:S(2)}, u32[]{:S(2)}) collective-permute-start(f32[2,7,8,128]{3,2,1,0:T(8,128)S(1)} %pad_maximum_fusion.1.pair), channel_id=1, source_target_pairs={{1,3},{3,1},{5,7},{7,5},{9,11},{11,9},{13,15},{15,13},{17,19},{19,... | collective-permute-start | bytes 172040 | tf_op jit(solution)/shard_map/ppermute | solution.py:570
  39.6 1.6 %collective-permute-start.12 = (f32[4,2,7,8,128]{4,3,2,1,0:T(8,128)S(1)}, f32[4,2,7,8,128]{4,3,2,1,0:T(8,128)S(1)}, u32[]{:S(2)}, u32[]{:S(2)}) collective-permute-start(f32[4,2,7,8,128]{4,3,2,1,0:T(8,128)S(1)} %pad_maximum_fusion.fetched), channel_id=1, source_target_pairs={{0,1},{1,0},{2,3},{3,2},{4,5},{5,4},{6,7},{7,6},{8,9},{9,8},{10,11... | collective-permute-start | bytes 688136 | tf_op jit(solution)/shard_map/ppermute | solution.py:551

commit v13 on v12

--- a/solution.py
+++ b/solution.py
@@ -285,7 +285,7 @@
             fresh.append(value)
         return (*totals, *add_products(carry[VECTORS:], *fresh))
 
-    carry = lax.fori_loop(0, levels, body, (zero,) * (VECTORS + 3), unroll=steps(levels, 10))
+    carry = lax.fori_loop(0, levels, body, (zero,) * (VECTORS + 3), unroll=steps(levels, 50))
     gain = STERIC_GAIN / levels
     rows = [a + inside[VECTORS + n] for n, a in enumerate(carry[VECTORS:])]
     residual = []
@@ -385,41 +385,40 @@
     return [a + factor * b for a, b in zip(one, two)]
 
 
-def third_kernel(
-    levels, sub, count, pair, fetched, fetched_mate, surface, tracer,
-    scaled, surface_out, growth, pole, residual, answer, image, depth, face_x, face_y, face_z, packed,
-):
+def third_kernel(levels, sub, count, *refs):
+    masks_of = chip_masks(count)
+    blocks = 1 + 2 * len(masks_of)
+    (surface, tracer, scaled, surface_out, growth) = refs[blocks : blocks + 5]
+    (pole, residual, answer, image, depth, face_x, face_y, face_z, packed) = refs[blocks + 5 :]
     width = 2 * count
     me = lax.axis_index("lon")
     core = lax.rem(me, 2)
     zero = jnp.zeros((sub, LANES), jnp.float32)
     none = (zero,) * VECTORS
 
-    def place(owner, block):
-        packed[owner] = block(GRAMS)
-        for c in range(2):
-            x = 2 * owner + c
-            depth[x] = block(DEPTHS + c)
-            for v in range(VECTORS):
-                value = block(v * 2 + c)
-                residual[v, x] = value
-                pole[v, x + 1] = value
-
-    for slot in range(2):
-        place(me ^ slot, lambda row, slot=slot: pair[slot, row])
-    for ref, flip in ((fetched, 0), (fetched_mate, 1)):
-        for j, masks in enumerate(chip_masks(count)):
-            mask = jnp.where((core ^ flip) == 0, *masks)
-            for slot in range(2):
-                owner = me ^ flip ^ slot ^ (2 * mask)
-
-                def put(owner=owner, ref=ref, j=j, slot=slot):
-                    place(owner, lambda row: ref[j, slot, row])
-
-                if all(masks):
-                    put()
-                else:
-                    pl.when(mask > 0)(put)
+    def place(first, block):
+        packed[first // 2] = block[2 * RIM]
+        for slot in range(2):
+            for c in range(2):
+                x = 2 * (first ^ slot) + c
+                depth[x] = block[RIM * slot + DEPTHS + c]
+                for v in range(VECTORS):
+                    value = block[RIM * slot + v * 2 + c]
+                    residual[v, x] = value
+                    pole[v, x + 1] = value
+
+    place(me, refs[0])
+    for n, block in enumerate(refs[1:blocks]):
+        flip, masks = n // len(masks_of), masks_of[n % len(masks_of)]
+        mask = jnp.where((core ^ flip) == 0, *masks)
+
+        def put(first=me ^ flip ^ (2 * mask), block=block):
+            place(first, block)
+
+        if all(masks):
+            put()
+        else:
+            pl.when(mask > 0)(put)
 
     def over(body, init):
         return lax.fori_loop(0, count, body, init, unroll=steps(count, 16))
@@ -494,9 +493,10 @@
             a, b = (answer[v, x] + size[v] * pole[v, x + 1] for v in range(VECTORS))
             answer[0, x], answer[1, x] = a, b
             grams = [grams[0] + a * a, grams[1] + a * b, grams[2] + b * b]
-        return (*grams, carry[3] + packed[d])
-
-    *grams, packed_sums = over(finish, (zero,) * 4)
+        return (*grams, carry[3])
+
+    *grams, _ = over(finish, (zero,) * 4)
+    packed_sums = sum((packed[n] for n in range(1, count // 2)), packed[0])
     sums = unpack_rows(packed_sums, 3 + VECTORS * VECTORS * POWERS)
 
     def heights_with(i, j):
@@ -520,7 +520,7 @@
         scaled[1, k] = (tracer[1, k] - cross * unit) * over_two
         return carry
 
-    lax.fori_loop(0, levels, scale, 0, unroll=steps(levels, 10))
+    lax.fori_loop(0, levels, scale, 0, unroll=steps(levels, 50))
     for c in range(2):
         x = 2 * me + c
         first, second = (
@@ -563,13 +563,13 @@
 
 def gather(block):
     count = lax.axis_size("lon")
-    pair = jnp.stack([block, swap(block, 1)])
+    beside = swap(block, 1)
+    pair = jnp.concatenate([block[:RIM], beside[:RIM], block[RIM:] + beside[RIM:]])
     fetched = []
     for masks in chip_masks(count):
         moves = [(i, i ^ (2 * masks[i % 2])) for i in range(count) if masks[i % 2]]
         fetched.append(lax.ppermute(pair, "lon", moves))
-    fetched = jnp.stack(fetched)
-    return pair, fetched, swap(fetched, 1)
+    return pair, *fetched, *(swap(one, 1) for one in fetched)
 
 
 def on_device(tracer_pert, surface_pert, zonal_flow, merid_flow, bottom_level):
@@ -669,6 +669,7 @@
         compiler_params=params,
         name="interleave",
     )(column, done)
+    blocks = gather(message)
     tracer_vec, surface_vec, growth = pl.pallas_call(
         functools.partial(third_kernel, levels, sub, count),
         out_shape=(
@@ -676,7 +677,7 @@
             jax.ShapeDtypeStruct((vectors, sub * 2, LANES), f32),
             jax.ShapeDtypeStruct((3,), f32),
         ),
-        in_specs=[vmem] * 5,
+        in_specs=[vmem] * (len(blocks) + 2),
         out_specs=(vmem, vmem, pl.BlockSpec(memory_space=pltpu.SMEM)),
         scratch_shapes=[
             held(vectors, width + 2),
@@ -685,11 +686,11 @@
             held(width + 1),
             held(width),
             held(width),
-            held(count),
+            held(count // 2),
         ],
         compiler_params=pltpu.CompilerParams(vmem_limit_bytes=32 * 2**20),
         name="surface_and_scale",
-    )(*gather(message), surface, tracer)
+    )(*blocks, surface, tracer)
     return (untiled(tracer_vec, 2), untiled(surface_vec, 2), growth)
 
 

time: 44.1 us -> 43.6 us (0.989)
  waiting for transfers between devices: 10.9 us -> 10.1 us
  starting transfers between devices: 22.2 us -> 22.7 us
    ppermute x5 -> x8, waiting for transfers between devices: 3.59 us -> 3.12 us  [swap(): return lax.ppermute(array, 'lon', [(i, i ^ mask) for i in range(count)])]
    ppermute x5 -> x8, starting transfers between devices: 4.86 us -> 5.21 us  [swap(): return lax.ppermute(array, 'lon', [(i, i ^ mask) for i in range(count)])]
  transfers between devices with their start and end apart: 13 -> 16, of which waited for: 7 -> 9; matrix products, arithmetic and copies ran while one was open for 0% -> 0% of each run, Pallas kernels for 6% -> 7%
where the time goes in v13:
time: 43.6 us; the launch traced here: 43.3 us
  starting transfers between devices  22.7 us (52%)
  waiting for transfers between devices  10.1 us (23%)
  Pallas kernels  7.72 us (18%)
  local copies, waits for them, and re-layouts  2.03 us (5%)
  between operations  0.78 us (2%)
    ppermute x4, starting transfers between devices, gather(): fetched.append(lax.ppermute(pair, 'lon', moves))  6 us
    ppermute x1, starting transfers between devices, on_device(): flow_half = lax.ppermute(flow_edge, 'lon', outward)  5.51 us
    ppermute x8, starting transfers between devices, swap(): return lax.ppermute(array, 'lon', [(i, i ^ mask) for i in range(count)])  5.21 us
    ppermute x1, starting transfers between devices, on_device(): cross_far = lax.ppermute(cross, 'lon', outward)  4.36 us
    ppermute x4, waiting for transfers between devices, gather(): fetched.append(lax.ppermute(pair, 'lon', moves))  3.84 us
    ppermute x1, waiting for transfers between devices, on_device(): flow_other = lax.ppermute(flow_half, 'grp', [(0, 1), (1, 0)])  3.17 us
    ppermute x8, waiting for transfers between devices, swap(): return lax.ppermute(array, 'lon', [(i, i ^ mask) for i in range(count)])  3.12 us
    pallas_call x1, Pallas kernels, on_device(): pl.pallas_call(functools.partial(third_kernel, levels, sub, count), out_s...  2.54 us
  transfers between devices with their start and end apart: 16, of which 9 were waited for; matrix products, arithmetic and copies ran while one was open for 0% of the time, Pallas kernels for 7%

profile of v13, /device:TPU:0, one launch (start us, length us, event | category | flops | bytes accessed | tf_op | source)
XLA Modules:
  0.0 43.3 jit_solution(5788570171717804769)
XLA Ops:
  0.6 0.0 copy-start
  0.6 0.0 copy-start.1
  0.7 0.0 copy-start.5
  0.7 0.0 copy-start.6
  0.7 2.1 %edge_columns.1 = (f32[106,8,128]{2,1,0:T(8,128)}, f32[25,8,128]{2,1,0:T(8,128)}) custom-call(f32[2,50,16,128]{3,2,1,0:T(8,128)} %bitcast.35, f32[50,16,128]{2,1,0:T(8,128)} %bitcast.37, f32[2,16,128]{2,1,0:T(8,128)} %bitcast.41, s32[16,128]{1,0:T(8,128)} %bitcast.44), custom_call_target="tpu_custom_call" | custom-call | tf_op jit(solution)/shard_map/edge_columns/pallas_call | solution.py:600
  2.8 5.5 %collective-permute-start.5 = (f32[25,8,128]{2,1,0:T(8,128)}, f32[25,8,128]{2,1,0:T(8,128)S(1)}, u32[]{:S(2)}, u32[]{:S(2)}) collective-permute-start(f32[25,8,128]{2,1,0:T(8,128)} %get-tuple-element.28), channel_id=1, source_target_pairs={{0,15},{1,2},{2,1},{3,4},{4,3},{5,6},{6,5},{7,8},{8,7},{9,10},{10,... | collective-permute-start | bytes 307208 | tf_op jit(solution)/shard_map/ppermute | solution.py:618
  8.3 0.1 collective-permute-start.1
  8.4 0.0 copy-done
  8.4 0.0 copy-done.5
  8.4 0.0 copy-start.2
  8.4 1.0 %copy-done.2 = f32[50,2,1024]{2,1,0:T(2,128)S(1)} copy-done((f32[50,2,1024]{2,1,0:T(2,128)S(1)}, f32[50,2,1024]{2,1,0:T(2,128)}, u32[]{:S(2)}) %copy-start.2) | copy-done | bytes 409624
  9.4 1.0 %copy-done.4 = f32[106,8,128]{2,1,0:T(8,128)S(1)} copy-done((f32[106,8,128]{2,1,0:T(8,128)S(1)}, f32[106,8,128]{2,1,0:T(8,128)}, u32[]{:S(2)}) %copy-start.4) | copy-done | bytes 434200
  10.4 1.2 %partial_step.1 = (f32[100,8,128]{2,1,0:T(8,128)S(1)}, f32[100,8,128]{2,1,0:T(8,128)S(1)}, f32[100,8,128]{2,1,0:T(8,128)S(1)}, f32[100,8,128]{2,1,0:T(8,128)S(1)...) custom-call(f32[106,8,128]{2,1,0:T(8,128)S(1)} %copy-done.4, f32[2,50,16,128]{3,2,1,0:T(8,128)S(1)} %bitcast.36, ...), custom_call_target="tpu_custom_call" | custom-call | tf_op jit(solution)/shard_map/partial_step/pallas_call | solution.py:621
  11.6 0.1 collective-permute-start.2
  11.7 0.5 %collective-permute-start.3 = (f32[100,8,128]{2,1,0:T(8,128)S(1)}, f32[100,8,128]{2,1,0:T(8,128)S(1)}, u32[]{:S(2)}, u32[]{:S(2)}) collective-permute-start(f32[100,8,128]{2,1,0:T(8,128)S(1)} %get-tuple-element.25.mate_raw), channel_id=1, source_target_pairs={{0,1},{1,0},{2,3},{3,2},{4,5},{5,4},{6,7},{7,6},{8,9},{9,8},{10,11... | collective-permute-start | bytes 1228808 | tf_op jit(solution)/shard_map/ppermute | solution.py:551
  12.2 4.4 %collective-permute-start = (f32[100,8,128]{2,1,0:T(8,128)S(1)}, f32[100,8,128]{2,1,0:T(8,128)S(1)}, u32[]{:S(2)}, u32[]{:S(2)}) collective-permute-start(f32[100,8,128]{2,1,0:T(8,128)S(1)} %get-tuple-element.22.cross), channel_id=1, source_target_pairs={{0,15},{1,2},{2,1},{3,4},{4,3},{5,6},{6,5},{7,8},{8,7},{9,10},{10,... | collective-permute-start | bytes 1228808 | tf_op jit(solution)/shard_map/ppermute | solution.py:636
  16.6 0.0 collective-permute-done.5.flow_half
  16.6 1.5 %collective-permute-start.6 = (f32[25,8,128]{2,1,0:T(8,128)S(1)}, f32[25,8,128]{2,1,0:T(8,128)S(1)}, u32[]{:S(2)}, u32[]{:S(2)}) collective-permute-start(f32[25,8,128]{2,1,0:T(8,128)S(1)} %collective-permute-done.5.flow_half), channel_id=1, source_target_pairs={{0,16},{16,0},{1,17},{17,1},{2,18},{18,2},{3,19},{19,3},{4,20},{20... | collective-permute-start | bytes 307208 | tf_op jit(solution)/shard_map/ppermute | solution.py:620
  18.1 3.2 %collective-permute-done.6.flow_other = f32[25,8,128]{2,1,0:T(8,128)S(1)} collective-permute-done((f32[25,8,128]{2,1,0:T(8,128)S(1)}, f32[25,8,128]{2,1,0:T(8,128)S(1)}, u32[]{:S(2)}, u32[]{:S(2)}) %collective-permute-start.6) | collective-permute-done | bytes 102432 | tf_op jit(solution)/shard_map/ppermute | solution.py:620
  21.2 0.0 collective-permute-start.4
  21.2 1.5 %collective-permute-done.4.mate_flow_far = f32[56,8,128]{2,1,0:T(8,128)S(1)} collective-permute-done((f32[56,8,128]{2,1,0:T(8,128)S(1)}, f32[56,8,128]{2,1,0:T(8,128)S(1)}, u32[]{:S(2)}, u32[]{:S(2)}) %collective-permute-start.4) | collective-permute-done | bytes 229408 | tf_op jit(solution)/shard_map/ppermute | solution.py:551
  22.7 0.0 collective-permute-done.2.mate_far
  22.7 0.0 collective-permute-done.3.mate_raw_far
  22.7 0.0 collective-permute-done.1.raw_far
  22.7 0.0 copy-done.3
  22.8 1.5 %both_steps.1 = (f32[2,50,8,128]{3,2,1,0:T(8,128)S(1)}, f32[2,50,8,128]{3,2,1,0:T(8,128)S(1)}, f32[50,8,128]{2,1,0:T(8,128)S(1)}, f32[5,8,128]{2,1,0:T(8,128)S(1)}, f32[4,2,2,8,128]{4,3,2,1,0:T(8,128)S(1)}) custom-call(f32[100,8,128]{2,1,0:T(8,128)S(1)} %get-tuple-element.23.raw, f32[100,8,128]{2,1,0:T(8,128)S(1)} %get-tuple-element.22.cross, ...), custom_call_target="tpu_custom_call" | custom-call | tf_op jit(solution)/shard_map/both_steps/pallas_call | solution.py:638
  24.3 0.0 collective-permute-done.cross_far
  24.3 0.2 outer_column.1
  24.5 4.1 %collective-permute-start.7 = (f32[7,8,128]{2,1,0:T(8,128)S(1)}, f32[7,8,128]{2,1,0:T(8,128)S(1)}, u32[]{:S(2)}, u32[]{:S(2)}) collective-permute-start(f32[7,8,128]{2,1,0:T(8,128)S(1)} %get-tuple-element.33), channel_id=1, source_target_pairs={{0,1},{1,0},{2,3},{3,2},{4,5},{5,4},{6,7},{7,6},{8,9},{9,8},{10,11... | collective-permute-start | bytes 86024 | tf_op jit(solution)/shard_map/ppermute | solution.py:551
  28.6 0.9 %collective-permute-done.7 = f32[7,8,128]{2,1,0:T(8,128)S(1)} collective-permute-done((f32[7,8,128]{2,1,0:T(8,128)S(1)}, f32[7,8,128]{2,1,0:T(8,128)S(1)}, u32[]{:S(2)}, u32[]{:S(2)}) %collective-permute-start.7) | collective-permute-done | bytes 28704 | tf_op jit(solution)/shard_map/ppermute | solution.py:551
  29.5 4.4 %collective-permute-start.8 = (f32[13,8,128]{2,1,0:T(8,128)S(1)}, f32[13,8,128]{2,1,0:T(8,128)S(1)}, u32[]{:S(2)}, u32[]{:S(2)}) collective-permute-start(f32[13,8,128]{2,1,0:T(8,128)S(1)} %pad_maximum_fusion.refs_0_), channel_id=1, source_target_pairs={{0,14},{1,13},{2,12},{3,15},{4,10},{5,9},{6,8},{7,11},{8,6},{9,5},... | collective-permute-start | bytes 159752 | tf_op jit(solution)/shard_map/ppermute | solution.py:571
  33.9 0.0 collective-permute-start.9
  33.9 0.9 %collective-permute-start.10 = (f32[13,8,128]{2,1,0:T(8,128)S(1)}, f32[13,8,128]{2,1,0:T(8,128)S(1)}, u32[]{:S(2)}, u32[]{:S(2)}) collective-permute-start(f32[13,8,128]{2,1,0:T(8,128)S(1)} %pad_maximum_fusion.refs_0_), channel_id=1, source_target_pairs={{0,6},{1,5},{2,4},{3,7},{4,2},{5,1},{6,0},{7,3},{8,14},{9,13},{10,... | collective-permute-start | bytes 159752 | tf_op jit(solution)/shard_map/ppermute | solution.py:571
  34.9 0.7 %collective-permute-start.11 = (f32[13,8,128]{2,1,0:T(8,128)S(1)}, f32[13,8,128]{2,1,0:T(8,128)S(1)}, u32[]{:S(2)}, u32[]{:S(2)}) collective-permute-start(f32[13,8,128]{2,1,0:T(8,128)S(1)} %pad_maximum_fusion.refs_0_), channel_id=1, source_target_pairs={{1,3},{3,1},{5,7},{7,5},{9,11},{11,9},{13,15},{15,13},{17,19},{19,... | collective-permute-start | bytes 159752 | tf_op jit(solution)/shard_map/ppermute | solution.py:571
  35.5 1.3 %collective-permute-done.8.refs_1_ = f32[13,8,128]{2,1,0:T(8,128)S(1)} collective-permute-done((f32[13,8,128]{2,1,0:T(8,128)S(1)}, f32[13,8,128]{2,1,0:T(8,128)S(1)}, u32[]{:S(2)}, u32[]{:S(2)}) %collective-permute-start.8) | collective-permute-done | bytes 53280 | tf_op jit(solution)/shard_map/ppermute | solution.py:571
  36.8 0.0 collective-permute-start.12
  36.8 2.2 %collective-permute-done.9.refs_2_ = f32[13,8,128]{2,1,0:T(8,128)S(1)} collective-permute-done((f32[13,8,128]{2,1,0:T(8,128)S(1)}, f32[13,8,128]{2,1,0:T(8,128)S(1)}, u32[]{:S(2)}, u32[]{:S(2)}) %collective-permute-start.9) | collective-permute-done | bytes 53280 | tf_op jit(solution)/shard_map/ppermute | solution.py:571
  39.0 0.0 collective-permute-start.13
  39.0 0.3 collective-permute-done.10.refs_3_
  39.4 0.2 collective-permute-start.14
  39.5 0.0 collective-permute-done.11.refs_4_
  39.5 0.3 collective-permute-start.15
  39.9 0.1 interleave.1.refs_10_
  40.0 0.0 collective-permute-done.12.refs_5_
  40.0 0.3 collective-permute-done.13.refs_6_
  40.3 0.3 collective-permute-done.14.refs_7_
  40.6 0.2 collective-permute-done.15.refs_8_
  40.8 2.5 %surface_and_scale.1 = (f32[2,50,16,128]{3,2,1,0:T(8,128)}, f32[2,16,128]{2,1,0:T(8,128)}, f32[3]{0:T(128)}) custom-call(f32[13,8,128]{2,1,0:T(8,128)S(1)} %pad_maximum_fusion.refs_0_, f32[13,8,128]{2,1,0:T(8,128)S(1)} %collective-permute-done.8.refs_1_, f32[13,8,128]{2,1,0:T(8,128)S(1)} %collective-permute-done.9.refs_2_, ...), custom_call_target="tpu_custom_call" | custom-call | tf_op jit(solution)/shard_map/surface_and_scale/pallas_call | solution.py:673
  (8 shorter events, 0.0 us)
Async XLA Ops:
  0.6 7.8 %copy-start = (f32[2,50,2,1024]{3,2,1,0:T(2,128)S(1)}, f32[2,50,2,1024]{3,2,1,0:T(2,128)}, u32[]{:S(2)}) copy-start(f32[2,50,2,1024]{3,2,1,0:T(2,128)} %param.5) | copy-start | bytes 2457604
  0.6 7.8 %copy-start.1 = (f32[50,2,1024]{2,1,0:T(2,128)S(1)}, f32[50,2,1024]{2,1,0:T(2,128)}, u32[]{:S(2)}) copy-start(f32[50,2,1024]{2,1,0:T(2,128)} %param.7) | copy-start | bytes 1228804
  0.7 7.8 %copy-start.5 = (f32[2,2,1024]{2,1,0:T(2,128)S(1)}, f32[2,2,1024]{2,1,0:T(2,128)}, u32[]{:S(2)}) copy-start(f32[2,2,1024]{2,1,0:T(2,128)} %param.6) | copy-start | bytes 49156
  0.7 7.8 %copy-start.6 = (s32[2,1024]{1,0:T(2,128)S(1)}, s32[2,1024]{1,0:T(2,128)}, u32[]{:S(2)}) copy-start(s32[2,1024]{1,0:T(2,128)} %param.9) | copy-start | bytes 24580
  2.8 13.8 %collective-permute-start.5 = (f32[25,8,128]{2,1,0:T(8,128)}, f32[25,8,128]{2,1,0:T(8,128)S(1)}, u32[]{:S(2)}, u32[]{:S(2)}) collective-permute-start(f32[25,8,128]{2,1,0:T(8,128)} %get-tuple-element.28), channel_id=1, source_target_pairs={{0,15},{1,2},{2,1},{3,4},{4,3},{5,6},{6,5},{7,8},{8,7},{9,10},{10,... | collective-permute-start | bytes 307208 | tf_op jit(solution)/shard_map/ppermute | solution.py:618
  8.3 14.4 %collective-permute-start.1 = (f32[106,8,128]{2,1,0:T(8,128)}, f32[106,8,128]{2,1,0:T(8,128)S(1)}, u32[]{:S(2)}, u32[]{:S(2)}) collective-permute-start(f32[106,8,128]{2,1,0:T(8,128)} %get-tuple-element.21.edge), channel_id=1, source_target_pairs={{0,15},{1,2},{2,1},{3,4},{4,3},{5,6},{6,5},{7,8},{8,7},{9,10},{10,... | collective-permute-start | bytes 1302536 | tf_op jit(solution)/shard_map/ppermute | solution.py:619
  8.4 1.0 %copy-start.2 = (f32[50,2,1024]{2,1,0:T(2,128)S(1)}, f32[50,2,1024]{2,1,0:T(2,128)}, u32[]{:S(2)}) copy-start(f32[50,2,1024]{2,1,0:T(2,128)} %param.8) | copy-start | bytes 1228804
  9.4 1.0 %copy-start.4 = (f32[106,8,128]{2,1,0:T(8,128)S(1)}, f32[106,8,128]{2,1,0:T(8,128)}, u32[]{:S(2)}) copy-start(f32[106,8,128]{2,1,0:T(8,128)} %get-tuple-element.21.edge) | copy-start | bytes 1302532
  10.4 12.3 %copy-start.3 = (f32[50,2,1024]{2,1,0:T(2,128)S(1)}, f32[50,2,1024]{2,1,0:T(2,128)}, u32[]{:S(2)}) copy-start(f32[50,2,1024]{2,1,0:T(2,128)} %param.8) | copy-start | bytes 1228804
  11.6 11.1 %collective-permute-start.2 = (f32[100,8,128]{2,1,0:T(8,128)S(1)}, f32[100,8,128]{2,1,0:T(8,128)S(1)}, u32[]{:S(2)}, u32[]{:S(2)}) collective-permute-start(f32[100,8,128]{2,1,0:T(8,128)S(1)} %get-tuple-element.24.mate), channel_id=1, source_target_pairs={{0,1},{1,0},{2,3},{3,2},{4,5},{5,4},{6,7},{7,6},{8,9},{9,8},{10,11... | collective-permute-start | bytes 1228808 | tf_op jit(solution)/shard_map/ppermute | solution.py:551
  11.7 11.0 %collective-permute-start.3 = (f32[100,8,128]{2,1,0:T(8,128)S(1)}, f32[100,8,128]{2,1,0:T(8,128)S(1)}, u32[]{:S(2)}, u32[]{:S(2)}) collective-permute-start(f32[100,8,128]{2,1,0:T(8,128)S(1)} %get-tuple-element.25.mate_raw), channel_id=1, source_target_pairs={{0,1},{1,0},{2,3},{3,2},{4,5},{5,4},{6,7},{7,6},{8,9},{9,8},{10,11... | collective-permute-start | bytes 1228808 | tf_op jit(solution)/shard_map/ppermute | solution.py:551
  12.2 12.1 %collective-permute-start = (f32[100,8,128]{2,1,0:T(8,128)S(1)}, f32[100,8,128]{2,1,0:T(8,128)S(1)}, u32[]{:S(2)}, u32[]{:S(2)}) collective-permute-start(f32[100,8,128]{2,1,0:T(8,128)S(1)} %get-tuple-element.22.cross), channel_id=1, source_target_pairs={{0,15},{1,2},{2,1},{3,4},{4,3},{5,6},{6,5},{7,8},{8,7},{9,10},{10,... | collective-permute-start | bytes 1228808 | tf_op jit(solution)/shard_map/ppermute | solution.py:636
  16.6 4.7 %collective-permute-start.6 = (f32[25,8,128]{2,1,0:T(8,128)S(1)}, f32[25,8,128]{2,1,0:T(8,128)S(1)}, u32[]{:S(2)}, u32[]{:S(2)}) collective-permute-start(f32[25,8,128]{2,1,0:T(8,128)S(1)} %collective-permute-done.5.flow_half), channel_id=1, source_target_pairs={{0,16},{16,0},{1,17},{17,1},{2,18},{18,2},{3,19},{19,3},{4,20},{20... | collective-permute-start | bytes 307208 | tf_op jit(solution)/shard_map/ppermute | solution.py:620
  21.2 1.5 %collective-permute-start.4 = (f32[56,8,128]{2,1,0:T(8,128)S(1)}, f32[56,8,128]{2,1,0:T(8,128)S(1)}, u32[]{:S(2)}, u32[]{:S(2)}) collective-permute-start(f32[56,8,128]{2,1,0:T(8,128)S(1)} %get-tuple-element.27.mate_flow), channel_id=1, source_target_pairs={{0,1},{1,0},{2,3},{3,2},{4,5},{5,4},{6,7},{7,6},{8,9},{9,8},{10,11... | collective-permute-start | bytes 688136 | tf_op jit(solution)/shard_map/ppermute | solution.py:551
  24.5 5.0 %collective-permute-start.7 = (f32[7,8,128]{2,1,0:T(8,128)S(1)}, f32[7,8,128]{2,1,0:T(8,128)S(1)}, u32[]{:S(2)}, u32[]{:S(2)}) collective-permute-start(f32[7,8,128]{2,1,0:T(8,128)S(1)} %get-tuple-element.33), channel_id=1, source_target_pairs={{0,1},{1,0},{2,3},{3,2},{4,5},{5,4},{6,7},{7,6},{8,9},{9,8},{10,11... | collective-permute-start | bytes 86024 | tf_op jit(solution)/shard_map/ppermute | solution.py:551
  29.5 7.3 %collective-permute-start.8 = (f32[13,8,128]{2,1,0:T(8,128)S(1)}, f32[13,8,128]{2,1,0:T(8,128)S(1)}, u32[]{:S(2)}, u32[]{:S(2)}) collective-permute-start(f32[13,8,128]{2,1,0:T(8,128)S(1)} %pad_maximum_fusion.refs_0_), channel_id=1, source_target_pairs={{0,14},{1,13},{2,12},{3,15},{4,10},{5,9},{6,8},{7,11},{8,6},{9,5},... | collective-permute-start | bytes 159752 | tf_op jit(solution)/shard_map/ppermute | solution.py:571
  33.9 5.1 %collective-permute-start.9 = (f32[13,8,128]{2,1,0:T(8,128)S(1)}, f32[13,8,128]{2,1,0:T(8,128)S(1)}, u32[]{:S(2)}, u32[]{:S(2)}) collective-permute-start(f32[13,8,128]{2,1,0:T(8,128)S(1)} %pad_maximum_fusion.refs_0_), channel_id=1, source_target_pairs={{0,8},{1,11},{2,10},{3,9},{4,12},{5,15},{6,14},{7,13},{8,0},{9,3},... | collective-permute-start | bytes 159752 | tf_op jit(solution)/shard_map/ppermute | solution.py:571
  33.9 5.4 %collective-permute-start.10 = (f32[13,8,128]{2,1,0:T(8,128)S(1)}, f32[13,8,128]{2,1,0:T(8,128)S(1)}, u32[]{:S(2)}, u32[]{:S(2)}) collective-permute-start(f32[13,8,128]{2,1,0:T(8,128)S(1)} %pad_maximum_fusion.refs_0_), channel_id=1, source_target_pairs={{0,6},{1,5},{2,4},{3,7},{4,2},{5,1},{6,0},{7,3},{8,14},{9,13},{10,... | collective-permute-start | bytes 159752 | tf_op jit(solution)/shard_map/ppermute | solution.py:571
  34.9 4.7 %collective-permute-start.11 = (f32[13,8,128]{2,1,0:T(8,128)S(1)}, f32[13,8,128]{2,1,0:T(8,128)S(1)}, u32[]{:S(2)}, u32[]{:S(2)}) collective-permute-start(f32[13,8,128]{2,1,0:T(8,128)S(1)} %pad_maximum_fusion.refs_0_), channel_id=1, source_target_pairs={{1,3},{3,1},{5,7},{7,5},{9,11},{11,9},{13,15},{15,13},{17,19},{19,... | collective-permute-start | bytes 159752 | tf_op jit(solution)/shard_map/ppermute | solution.py:571
  36.8 3.2 %collective-permute-start.12 = (f32[13,8,128]{2,1,0:T(8,128)S(1)}, f32[13,8,128]{2,1,0:T(8,128)S(1)}, u32[]{:S(2)}, u32[]{:S(2)}) collective-permute-start(f32[13,8,128]{2,1,0:T(8,128)S(1)} %collective-permute-done.8.refs_1_), channel_id=1, source_target_pairs={{0,1},{1,0},{2,3},{3,2},{4,5},{5,4},{6,7},{7,6},{8,9},{9,8},{10,11... | collective-permute-start | bytes 159752 | tf_op jit(solution)/shard_map/ppermute | solution.py:551
  39.0 1.2 %collective-permute-start.13 = (f32[13,8,128]{2,1,0:T(8,128)S(1)}, f32[13,8,128]{2,1,0:T(8,128)S(1)}, u32[]{:S(2)}, u32[]{:S(2)}) collective-permute-start(f32[13,8,128]{2,1,0:T(8,128)S(1)} %collective-permute-done.9.refs_2_), channel_id=1, source_target_pairs={{0,1},{1,0},{2,3},{3,2},{4,5},{5,4},{6,7},{7,6},{8,9},{9,8},{10,11... | collective-permute-start | bytes 159752 | tf_op jit(solution)/shard_map/ppermute | solution.py:551
  39.4 1.2 %collective-permute-start.14 = (f32[13,8,128]{2,1,0:T(8,128)S(1)}, f32[13,8,128]{2,1,0:T(8,128)S(1)}, u32[]{:S(2)}, u32[]{:S(2)}) collective-permute-start(f32[13,8,128]{2,1,0:T(8,128)S(1)} %collective-permute-done.10.refs_3_), channel_id=1, source_target_pairs={{0,1},{1,0},{2,3},{3,2},{4,5},{5,4},{6,7},{7,6},{8,9},{9,8},{10,11... | collective-permute-start | bytes 159752 | tf_op jit(solution)/shard_map/ppermute | solution.py:551
  39.5 1.2 %collective-permute-start.15 = (f32[13,8,128]{2,1,0:T(8,128)S(1)}, f32[13,8,128]{2,1,0:T(8,128)S(1)}, u32[]{:S(2)}, u32[]{:S(2)}) collective-permute-start(f32[13,8,128]{2,1,0:T(8,128)S(1)} %collective-permute-done.11.refs_4_), channel_id=1, source_target_pairs={{0,1},{1,0},{2,3},{3,2},{4,5},{5,4},{6,7},{7,6},{8,9},{9,8},{10,11... | collective-permute-start | bytes 159752 | tf_op jit(solution)/shard_map/ppermute | solution.py:551

commit v14 on v13

--- a/solution.py
+++ b/solution.py
@@ -99,45 +99,39 @@
 
 
 def edge_kernel(
-    levels, sub, tracer_hbm, zonal_hbm, surface_hbm, bottom_hbm, edge_hbm, flow_hbm,
-    tracer, zonal, surface, bottom, edge, flow, sems_in, sems_out,
+    levels, sub, tracer_hbm, zonal_hbm, surface_hbm, bottom_hbm, edge, flow,
+    tracer, zonal, surface, bottom, sems,
 ):
     outer, _, _ = orientation()
     start, part = share(levels)
-
-    def move(source, target, sem):
-        copy = pltpu.make_async_copy(source, target, sem)
+    pairs = [
+        (zonal_hbm.at[pl.ds(start, part)], zonal),
+        (surface_hbm, surface),
+        (bottom_hbm, bottom),
+        *((tracer_hbm.at[v], tracer.at[v]) for v in range(VECTORS)),
+    ]
+    copies = [
+        pltpu.make_async_copy(source, target, sems.at[i]) for i, (source, target) in enumerate(pairs)
+    ]
+    for copy in copies:
         copy.start()
-        return copy
-
-    first = [
-        move(zonal_hbm.at[pl.ds(start, part)], zonal, sems_in.at[0]),
-        move(surface_hbm, surface, sems_in.at[1]),
-        move(bottom_hbm, bottom, sems_in.at[2]),
-    ]
-    arrivals = [move(tracer_hbm.at[v], tracer.at[v], sems_in.at[3 + v]) for v in range(VECTORS)]
-    for copy in first:
+    for copy in copies[:3]:
         copy.wait()
 
     def take(k, carry):
         flow[k] = zonal[k, pl.ds(outer, sub, stride=2), :]
         return carry
 
-    lax.fori_loop(0, part, take, 0, unroll=steps(part, 10))
-    departures = [move(flow, flow_hbm, sems_out.at[VECTORS])]
+    lax.fori_loop(0, part, take, 0, unroll=steps(part, 25))
     pack_rim(sub, surface, bottom, edge, VECTORS * levels)
-    for v, arrival in enumerate(arrivals):
-        arrival.wait()
+    for v in range(VECTORS):
+        copies[3 + v].wait()
 
         def body(k, carry, v=v):
             edge[v * levels + k] = tracer[v, k, pl.ds(outer, sub, stride=2), :]
             return carry
 
-        lax.fori_loop(0, levels, body, 0, unroll=steps(levels, 10))
-        rows = pl.ds(v * levels, levels + (RIM if v == VECTORS - 1 else 0))
-        departures.append(move(edge.at[rows], edge_hbm.at[rows], sems_out.at[v]))
-    for departure in departures:
-        departure.wait()
+        lax.fori_loop(0, levels, body, 0, unroll=steps(levels, 25))
 
 
 def first_kernel(
@@ -596,25 +590,25 @@
     part = levels // 2
     surface, bottom = tiled(surface_pert), tiled(bottom_level)
 
-    packed = shaped(VECTORS * levels + RIM), shaped(part)
+    pinned = [
+        pltpu.with_memory_space_constraint(array, pltpu.HBM)
+        for array in (tracer_pert, zonal_flow, surface, bottom)
+    ]
     edge, flow_edge = pl.pallas_call(
         functools.partial(edge_kernel, levels, sub),
-        out_shape=packed,
+        out_shape=(shaped(VECTORS * levels + RIM), shaped(part)),
         in_specs=[hbm] * 4,
-        out_specs=(hbm, hbm),
+        out_specs=(vmem, vmem),
         scratch_shapes=[
             both,
             pltpu.VMEM((part, sub * 2, LANES), f32),
             pltpu.VMEM((vectors, sub * 2, LANES), f32),
             pltpu.VMEM((sub * 2, LANES), jnp.int32),
-            held(VECTORS * levels + RIM),
-            held(part),
             pltpu.SemaphoreType.DMA((VECTORS + 3,)),
-            pltpu.SemaphoreType.DMA((VECTORS + 1,)),
         ],
-        compiler_params=pltpu.CompilerParams(vmem_limit_bytes=60 * 2**20),
+        compiler_params=pltpu.CompilerParams(vmem_limit_bytes=16 * 2**20),
         name="edge_columns",
-    )(tracer_pert, zonal_flow, surface, bottom)
+    )(*pinned)
     flow_half = lax.ppermute(flow_edge, "lon", outward)
     edge_far = lax.ppermute(edge, "lon", outward)
     flow_other = lax.ppermute(flow_half, "grp", [(0, 1), (1, 0)])

time: 43.6 us -> 42.6 us (0.977)
  local copies, waits for them, and re-layouts: 2.03 us -> 1.02 us
  Pallas kernels: 7.72 us -> 7.02 us
  starting transfers between devices: 22.7 us -> 23.4 us
    unnamed x14 -> x12, local copies, waits for them, and re-layouts: 2.03 us -> 1.02 us
    ppermute x8, starting transfers between devices: 5.21 us -> 5.99 us  [swap(): return lax.ppermute(array, 'lon', [(i, i ^ mask) for i in range(count)])]
    pallas_call x1, Pallas kernels: 2.14 us -> 1.42 us  [on_device(): pl.pallas_call(functools.partial(edge_kernel, levels, sub), out_shape=(sh...]
where the time goes in v14:
time: 42.6 us; the launch traced here: 42.4 us
  starting transfers between devices  23.4 us (55%)
  waiting for transfers between devices  10.1 us (24%)
  Pallas kernels  7.02 us (16%)
  local copies, waits for them, and re-layouts  1.02 us (2%)
  between operations  0.78 us (2%)
    ppermute x4, starting transfers between devices, gather(): fetched.append(lax.ppermute(pair, 'lon', moves))  6 us
    ppermute x8, starting transfers between devices, swap(): return lax.ppermute(array, 'lon', [(i, i ^ mask) for i in range(count)])  5.99 us
    ppermute x1, starting transfers between devices, on_device(): flow_half = lax.ppermute(flow_edge, 'lon', outward)  5.51 us
    ppermute x1, starting transfers between devices, on_device(): cross_far = lax.ppermute(cross, 'lon', outward)  4.36 us
    ppermute x4, waiting for transfers between devices, gather(): fetched.append(lax.ppermute(pair, 'lon', moves))  3.84 us
    ppermute x1, waiting for transfers between devices, on_device(): flow_other = lax.ppermute(flow_half, 'grp', [(0, 1), (1, 0)])  3.17 us
    ppermute x8, waiting for transfers between devices, swap(): return lax.ppermute(array, 'lon', [(i, i ^ mask) for i in range(count)])  3.12 us
    pallas_call x1, Pallas kernels, on_device(): pl.pallas_call(functools.partial(third_kernel, levels, sub, count), out_s...  2.54 us
  transfers between devices with their start and end apart: 16, of which 9 were waited for; matrix products, arithmetic and copies ran while one was open for 0% of the time, Pallas kernels for 7%

profile of v14, /device:TPU:0, one launch (start us, length us, event | category | flops | bytes accessed | tf_op | source)
XLA Modules:
  0.0 42.4 jit_solution(8688480087392460118)
XLA Ops:
  0.6 0.0 copy-start
  0.6 0.0 copy-start.1
  0.7 0.0 copy-start.4
  0.7 0.0 copy-start.5
  0.7 1.4 %edge_columns.1 = (f32[106,8,128]{2,1,0:T(8,128)S(1)}, f32[25,8,128]{2,1,0:T(8,128)S(1)}) custom-call(f32[2,50,16,128]{3,2,1,0:T(8,128)} %bitcast.35, f32[50,16,128]{2,1,0:T(8,128)} %bitcast.37, f32[2,16,128]{2,1,0:T(8,128)} %bitcast.41, s32[16,128]{1,0:T(8,128)} %bitcast.44), custom_call_target="tpu_custom_call" | custom-call | tf_op jit(solution)/shard_map/edge_columns/pallas_call | solution.py:597
  2.1 5.5 %collective-permute-start.5 = (f32[25,8,128]{2,1,0:T(8,128)S(1)}, f32[25,8,128]{2,1,0:T(8,128)S(1)}, u32[]{:S(2)}, u32[]{:S(2)}) collective-permute-start(f32[25,8,128]{2,1,0:T(8,128)S(1)} %get-tuple-element.28), channel_id=1, source_target_pairs={{0,15},{1,2},{2,1},{3,4},{4,3},{5,6},{6,5},{7,8},{8,7},{9,10},{10,... | collective-permute-start | bytes 307208 | tf_op jit(solution)/shard_map/ppermute | solution.py:612
  7.6 0.1 collective-permute-start.1
  7.7 0.0 copy-done
  7.7 0.0 copy-done.1
  7.7 0.0 copy-done.4
  7.7 0.0 copy-done.5
  7.7 0.0 copy-start.2
  7.7 1.0 %copy-done.2 = f32[50,2,1024]{2,1,0:T(2,128)S(1)} copy-done((f32[50,2,1024]{2,1,0:T(2,128)S(1)}, f32[50,2,1024]{2,1,0:T(2,128)}, u32[]{:S(2)}) %copy-start.2) | copy-done | bytes 409624
  8.7 1.2 %partial_step.1 = (f32[100,8,128]{2,1,0:T(8,128)S(1)}, f32[100,8,128]{2,1,0:T(8,128)S(1)}, f32[100,8,128]{2,1,0:T(8,128)S(1)}, f32[100,8,128]{2,1,0:T(8,128)S(1)...) custom-call(f32[106,8,128]{2,1,0:T(8,128)S(1)} %get-tuple-element.21.edge, f32[2,50,16,128]{3,2,1,0:T(8,128)S(1)} %bitcast.36, ...), custom_call_target="tpu_custom_call" | custom-call | tf_op jit(solution)/shard_map/partial_step/pallas_call | solution.py:615
  9.9 0.1 collective-permute-start.2
  10.0 0.5 %collective-permute-start.3 = (f32[100,8,128]{2,1,0:T(8,128)S(1)}, f32[100,8,128]{2,1,0:T(8,128)S(1)}, u32[]{:S(2)}, u32[]{:S(2)}) collective-permute-start(f32[100,8,128]{2,1,0:T(8,128)S(1)} %get-tuple-element.25.mate_raw), channel_id=1, source_target_pairs={{0,1},{1,0},{2,3},{3,2},{4,5},{5,4},{6,7},{7,6},{8,9},{9,8},{10,11... | collective-permute-start | bytes 1228808 | tf_op jit(solution)/shard_map/ppermute | solution.py:545
  10.5 4.4 %collective-permute-start = (f32[100,8,128]{2,1,0:T(8,128)S(1)}, f32[100,8,128]{2,1,0:T(8,128)S(1)}, u32[]{:S(2)}, u32[]{:S(2)}) collective-permute-start(f32[100,8,128]{2,1,0:T(8,128)S(1)} %get-tuple-element.22.cross), channel_id=1, source_target_pairs={{0,15},{1,2},{2,1},{3,4},{4,3},{5,6},{6,5},{7,8},{8,7},{9,10},{10,... | collective-permute-start | bytes 1228808 | tf_op jit(solution)/shard_map/ppermute | solution.py:630
  14.8 0.0 collective-permute-done.5.flow_half
  14.9 1.5 %collective-permute-start.6 = (f32[25,8,128]{2,1,0:T(8,128)S(1)}, f32[25,8,128]{2,1,0:T(8,128)S(1)}, u32[]{:S(2)}, u32[]{:S(2)}) collective-permute-start(f32[25,8,128]{2,1,0:T(8,128)S(1)} %collective-permute-done.5.flow_half), channel_id=1, source_target_pairs={{0,16},{16,0},{1,17},{17,1},{2,18},{18,2},{3,19},{19,3},{4,20},{20... | collective-permute-start | bytes 307208 | tf_op jit(solution)/shard_map/ppermute | solution.py:614
  16.3 3.2 %collective-permute-done.6.flow_other = f32[25,8,128]{2,1,0:T(8,128)S(1)} collective-permute-done((f32[25,8,128]{2,1,0:T(8,128)S(1)}, f32[25,8,128]{2,1,0:T(8,128)S(1)}, u32[]{:S(2)}, u32[]{:S(2)}) %collective-permute-start.6) | collective-permute-done | bytes 102432 | tf_op jit(solution)/shard_map/ppermute | solution.py:614
  19.5 0.0 collective-permute-start.4
  19.5 1.5 %collective-permute-done.4.mate_flow_far = f32[56,8,128]{2,1,0:T(8,128)S(1)} collective-permute-done((f32[56,8,128]{2,1,0:T(8,128)S(1)}, f32[56,8,128]{2,1,0:T(8,128)S(1)}, u32[]{:S(2)}, u32[]{:S(2)}) %collective-permute-start.4) | collective-permute-done | bytes 229408 | tf_op jit(solution)/shard_map/ppermute | solution.py:545
  21.0 0.0 collective-permute-done.2.mate_far
  21.0 0.0 collective-permute-done.3.mate_raw_far
  21.0 0.0 collective-permute-done.1.raw_far
  21.0 1.5 %both_steps.1 = (f32[2,50,8,128]{3,2,1,0:T(8,128)S(1)}, f32[2,50,8,128]{3,2,1,0:T(8,128)S(1)}, f32[50,8,128]{2,1,0:T(8,128)S(1)}, f32[5,8,128]{2,1,0:T(8,128)S(1)}, f32[4,2,2,8,128]{4,3,2,1,0:T(8,128)S(1)}) custom-call(f32[100,8,128]{2,1,0:T(8,128)S(1)} %get-tuple-element.23.raw, f32[100,8,128]{2,1,0:T(8,128)S(1)} %get-tuple-element.22.cross, ...), custom_call_target="tpu_custom_call" | custom-call | tf_op jit(solution)/shard_map/both_steps/pallas_call | solution.py:632
  22.6 0.0 collective-permute-done.cross_far
  22.6 0.2 outer_column.1
  22.8 4.9 %collective-permute-start.7 = (f32[7,8,128]{2,1,0:T(8,128)S(1)}, f32[7,8,128]{2,1,0:T(8,128)S(1)}, u32[]{:S(2)}, u32[]{:S(2)}) collective-permute-start(f32[7,8,128]{2,1,0:T(8,128)S(1)} %get-tuple-element.33), channel_id=1, source_target_pairs={{0,1},{1,0},{2,3},{3,2},{4,5},{5,4},{6,7},{7,6},{8,9},{9,8},{10,11... | collective-permute-start | bytes 86024 | tf_op jit(solution)/shard_map/ppermute | solution.py:545
  27.7 0.9 %collective-permute-done.7 = f32[7,8,128]{2,1,0:T(8,128)S(1)} collective-permute-done((f32[7,8,128]{2,1,0:T(8,128)S(1)}, f32[7,8,128]{2,1,0:T(8,128)S(1)}, u32[]{:S(2)}, u32[]{:S(2)}) %collective-permute-start.7) | collective-permute-done | bytes 28704 | tf_op jit(solution)/shard_map/ppermute | solution.py:545
  28.6 4.4 %collective-permute-start.8 = (f32[13,8,128]{2,1,0:T(8,128)S(1)}, f32[13,8,128]{2,1,0:T(8,128)S(1)}, u32[]{:S(2)}, u32[]{:S(2)}) collective-permute-start(f32[13,8,128]{2,1,0:T(8,128)S(1)} %pad_maximum_fusion.refs_0_), channel_id=1, source_target_pairs={{0,14},{1,13},{2,12},{3,15},{4,10},{5,9},{6,8},{7,11},{8,6},{9,5},... | collective-permute-start | bytes 159752 | tf_op jit(solution)/shard_map/ppermute | solution.py:565
  33.0 0.0 collective-permute-start.9
  33.0 0.9 %collective-permute-start.10 = (f32[13,8,128]{2,1,0:T(8,128)S(1)}, f32[13,8,128]{2,1,0:T(8,128)S(1)}, u32[]{:S(2)}, u32[]{:S(2)}) collective-permute-start(f32[13,8,128]{2,1,0:T(8,128)S(1)} %pad_maximum_fusion.refs_0_), channel_id=1, source_target_pairs={{0,6},{1,5},{2,4},{3,7},{4,2},{5,1},{6,0},{7,3},{8,14},{9,13},{10,... | collective-permute-start | bytes 159752 | tf_op jit(solution)/shard_map/ppermute | solution.py:565
  33.9 0.7 %collective-permute-start.11 = (f32[13,8,128]{2,1,0:T(8,128)S(1)}, f32[13,8,128]{2,1,0:T(8,128)S(1)}, u32[]{:S(2)}, u32[]{:S(2)}) collective-permute-start(f32[13,8,128]{2,1,0:T(8,128)S(1)} %pad_maximum_fusion.refs_0_), channel_id=1, source_target_pairs={{1,3},{3,1},{5,7},{7,5},{9,11},{11,9},{13,15},{15,13},{17,19},{19,... | collective-permute-start | bytes 159752 | tf_op jit(solution)/shard_map/ppermute | solution.py:565
  34.6 1.3 %collective-permute-done.8.refs_1_ = f32[13,8,128]{2,1,0:T(8,128)S(1)} collective-permute-done((f32[13,8,128]{2,1,0:T(8,128)S(1)}, f32[13,8,128]{2,1,0:T(8,128)S(1)}, u32[]{:S(2)}, u32[]{:S(2)}) %collective-permute-start.8) | collective-permute-done | bytes 53280 | tf_op jit(solution)/shard_map/ppermute | solution.py:565
  35.9 0.0 collective-permute-start.12
  35.9 2.2 %collective-permute-done.9.refs_2_ = f32[13,8,128]{2,1,0:T(8,128)S(1)} collective-permute-done((f32[13,8,128]{2,1,0:T(8,128)S(1)}, f32[13,8,128]{2,1,0:T(8,128)S(1)}, u32[]{:S(2)}, u32[]{:S(2)}) %collective-permute-start.9) | collective-permute-done | bytes 53280 | tf_op jit(solution)/shard_map/ppermute | solution.py:565
  38.1 0.0 collective-permute-start.13
  38.1 0.3 collective-permute-done.10.refs_3_
  38.4 0.2 collective-permute-start.14
  38.6 0.0 collective-permute-done.11.refs_4_
  38.6 0.3 collective-permute-start.15
  39.0 0.1 interleave.1.refs_10_
  39.1 0.0 collective-permute-done.12.refs_5_
  39.1 0.3 collective-permute-done.13.refs_6_
  39.3 0.3 collective-permute-done.14.refs_7_
  39.7 0.2 collective-permute-done.15.refs_8_
  39.9 2.5 %surface_and_scale.1 = (f32[2,50,16,128]{3,2,1,0:T(8,128)}, f32[2,16,128]{2,1,0:T(8,128)}, f32[3]{0:T(128)}) custom-call(f32[13,8,128]{2,1,0:T(8,128)S(1)} %pad_maximum_fusion.refs_0_, f32[13,8,128]{2,1,0:T(8,128)S(1)} %collective-permute-done.8.refs_1_, f32[13,8,128]{2,1,0:T(8,128)S(1)} %collective-permute-done.9.refs_2_, ...), custom_call_target="tpu_custom_call" | custom-call | tf_op jit(solution)/shard_map/surface_and_scale/pallas_call | solution.py:667
  (6 shorter events, 0.0 us)
Async XLA Ops:
  0.6 7.1 %copy-start = (f32[2,50,2,1024]{3,2,1,0:T(2,128)S(1)}, f32[2,50,2,1024]{3,2,1,0:T(2,128)}, u32[]{:S(2)}) copy-start(f32[2,50,2,1024]{3,2,1,0:T(2,128)} %param.5) | copy-start | bytes 2457604
  0.6 7.0 %copy-start.1 = (f32[50,2,1024]{2,1,0:T(2,128)S(1)}, f32[50,2,1024]{2,1,0:T(2,128)}, u32[]{:S(2)}) copy-start(f32[50,2,1024]{2,1,0:T(2,128)} %param.7) | copy-start | bytes 1228804
  0.7 7.0 %copy-start.4 = (f32[2,2,1024]{2,1,0:T(2,128)S(1)}, f32[2,2,1024]{2,1,0:T(2,128)}, u32[]{:S(2)}) copy-start(f32[2,2,1024]{2,1,0:T(2,128)} %param.6) | copy-start | bytes 49156
  0.7 7.0 %copy-start.5 = (s32[2,1024]{1,0:T(2,128)S(1)}, s32[2,1024]{1,0:T(2,128)}, u32[]{:S(2)}) copy-start(s32[2,1024]{1,0:T(2,128)} %param.9) | copy-start | bytes 24580
  2.1 12.8 %collective-permute-start.5 = (f32[25,8,128]{2,1,0:T(8,128)S(1)}, f32[25,8,128]{2,1,0:T(8,128)S(1)}, u32[]{:S(2)}, u32[]{:S(2)}) collective-permute-start(f32[25,8,128]{2,1,0:T(8,128)S(1)} %get-tuple-element.28), channel_id=1, source_target_pairs={{0,15},{1,2},{2,1},{3,4},{4,3},{5,6},{6,5},{7,8},{8,7},{9,10},{10,... | collective-permute-start | bytes 307208 | tf_op jit(solution)/shard_map/ppermute | solution.py:612
  7.6 13.4 %collective-permute-start.1 = (f32[106,8,128]{2,1,0:T(8,128)S(1)}, f32[106,8,128]{2,1,0:T(8,128)S(1)}, u32[]{:S(2)}, u32[]{:S(2)}) collective-permute-start(f32[106,8,128]{2,1,0:T(8,128)S(1)} %get-tuple-element.21.edge), channel_id=1, source_target_pairs={{0,15},{1,2},{2,1},{3,4},{4,3},{5,6},{6,5},{7,8},{8,7},{9,10},{10,... | collective-permute-start | bytes 1302536 | tf_op jit(solution)/shard_map/ppermute | solution.py:613
  7.7 1.0 %copy-start.2 = (f32[50,2,1024]{2,1,0:T(2,128)S(1)}, f32[50,2,1024]{2,1,0:T(2,128)}, u32[]{:S(2)}) copy-start(f32[50,2,1024]{2,1,0:T(2,128)} %param.8) | copy-start | bytes 1228804
  8.7 12.3 %copy-start.3 = (f32[50,2,1024]{2,1,0:T(2,128)S(1)}, f32[50,2,1024]{2,1,0:T(2,128)}, u32[]{:S(2)}) copy-start(f32[50,2,1024]{2,1,0:T(2,128)} %param.8) | copy-start | bytes 1228804
  9.9 11.1 %collective-permute-start.2 = (f32[100,8,128]{2,1,0:T(8,128)S(1)}, f32[100,8,128]{2,1,0:T(8,128)S(1)}, u32[]{:S(2)}, u32[]{:S(2)}) collective-permute-start(f32[100,8,128]{2,1,0:T(8,128)S(1)} %get-tuple-element.24.mate), channel_id=1, source_target_pairs={{0,1},{1,0},{2,3},{3,2},{4,5},{5,4},{6,7},{7,6},{8,9},{9,8},{10,11... | collective-permute-start | bytes 1228808 | tf_op jit(solution)/shard_map/ppermute | solution.py:545
  10.0 11.0 %collective-permute-start.3 = (f32[100,8,128]{2,1,0:T(8,128)S(1)}, f32[100,8,128]{2,1,0:T(8,128)S(1)}, u32[]{:S(2)}, u32[]{:S(2)}) collective-permute-start(f32[100,8,128]{2,1,0:T(8,128)S(1)} %get-tuple-element.25.mate_raw), channel_id=1, source_target_pairs={{0,1},{1,0},{2,3},{3,2},{4,5},{5,4},{6,7},{7,6},{8,9},{9,8},{10,11... | collective-permute-start | bytes 1228808 | tf_op jit(solution)/shard_map/ppermute | solution.py:545
  10.5 12.1 %collective-permute-start = (f32[100,8,128]{2,1,0:T(8,128)S(1)}, f32[100,8,128]{2,1,0:T(8,128)S(1)}, u32[]{:S(2)}, u32[]{:S(2)}) collective-permute-start(f32[100,8,128]{2,1,0:T(8,128)S(1)} %get-tuple-element.22.cross), channel_id=1, source_target_pairs={{0,15},{1,2},{2,1},{3,4},{4,3},{5,6},{6,5},{7,8},{8,7},{9,10},{10,... | collective-permute-start | bytes 1228808 | tf_op jit(solution)/shard_map/ppermute | solution.py:630
  14.9 4.7 %collective-permute-start.6 = (f32[25,8,128]{2,1,0:T(8,128)S(1)}, f32[25,8,128]{2,1,0:T(8,128)S(1)}, u32[]{:S(2)}, u32[]{:S(2)}) collective-permute-start(f32[25,8,128]{2,1,0:T(8,128)S(1)} %collective-permute-done.5.flow_half), channel_id=1, source_target_pairs={{0,16},{16,0},{1,17},{17,1},{2,18},{18,2},{3,19},{19,3},{4,20},{20... | collective-permute-start | bytes 307208 | tf_op jit(solution)/shard_map/ppermute | solution.py:614
  19.5 1.5 %collective-permute-start.4 = (f32[56,8,128]{2,1,0:T(8,128)S(1)}, f32[56,8,128]{2,1,0:T(8,128)S(1)}, u32[]{:S(2)}, u32[]{:S(2)}) collective-permute-start(f32[56,8,128]{2,1,0:T(8,128)S(1)} %get-tuple-element.27.mate_flow), channel_id=1, source_target_pairs={{0,1},{1,0},{2,3},{3,2},{4,5},{5,4},{6,7},{7,6},{8,9},{9,8},{10,11... | collective-permute-start | bytes 688136 | tf_op jit(solution)/shard_map/ppermute | solution.py:545
  22.8 5.8 %collective-permute-start.7 = (f32[7,8,128]{2,1,0:T(8,128)S(1)}, f32[7,8,128]{2,1,0:T(8,128)S(1)}, u32[]{:S(2)}, u32[]{:S(2)}) collective-permute-start(f32[7,8,128]{2,1,0:T(8,128)S(1)} %get-tuple-element.33), channel_id=1, source_target_pairs={{0,1},{1,0},{2,3},{3,2},{4,5},{5,4},{6,7},{7,6},{8,9},{9,8},{10,11... | collective-permute-start | bytes 86024 | tf_op jit(solution)/shard_map/ppermute | solution.py:545
  28.6 7.3 %collective-permute-start.8 = (f32[13,8,128]{2,1,0:T(8,128)S(1)}, f32[13,8,128]{2,1,0:T(8,128)S(1)}, u32[]{:S(2)}, u32[]{:S(2)}) collective-permute-start(f32[13,8,128]{2,1,0:T(8,128)S(1)} %pad_maximum_fusion.refs_0_), channel_id=1, source_target_pairs={{0,14},{1,13},{2,12},{3,15},{4,10},{5,9},{6,8},{7,11},{8,6},{9,5},... | collective-permute-start | bytes 159752 | tf_op jit(solution)/shard_map/ppermute | solution.py:565
  33.0 5.1 %collective-permute-start.9 = (f32[13,8,128]{2,1,0:T(8,128)S(1)}, f32[13,8,128]{2,1,0:T(8,128)S(1)}, u32[]{:S(2)}, u32[]{:S(2)}) collective-permute-start(f32[13,8,128]{2,1,0:T(8,128)S(1)} %pad_maximum_fusion.refs_0_), channel_id=1, source_target_pairs={{0,8},{1,11},{2,10},{3,9},{4,12},{5,15},{6,14},{7,13},{8,0},{9,3},... | collective-permute-start | bytes 159752 | tf_op jit(solution)/shard_map/ppermute | solution.py:565
  33.0 5.4 %collective-permute-start.10 = (f32[13,8,128]{2,1,0:T(8,128)S(1)}, f32[13,8,128]{2,1,0:T(8,128)S(1)}, u32[]{:S(2)}, u32[]{:S(2)}) collective-permute-start(f32[13,8,128]{2,1,0:T(8,128)S(1)} %pad_maximum_fusion.refs_0_), channel_id=1, source_target_pairs={{0,6},{1,5},{2,4},{3,7},{4,2},{5,1},{6,0},{7,3},{8,14},{9,13},{10,... | collective-permute-start | bytes 159752 | tf_op jit(solution)/shard_map/ppermute | solution.py:565
  33.9 4.7 %collective-permute-start.11 = (f32[13,8,128]{2,1,0:T(8,128)S(1)}, f32[13,8,128]{2,1,0:T(8,128)S(1)}, u32[]{:S(2)}, u32[]{:S(2)}) collective-permute-start(f32[13,8,128]{2,1,0:T(8,128)S(1)} %pad_maximum_fusion.refs_0_), channel_id=1, source_target_pairs={{1,3},{3,1},{5,7},{7,5},{9,11},{11,9},{13,15},{15,13},{17,19},{19,... | collective-permute-start | bytes 159752 | tf_op jit(solution)/shard_map/ppermute | solution.py:565
  35.9 3.2 %collective-permute-start.12 = (f32[13,8,128]{2,1,0:T(8,128)S(1)}, f32[13,8,128]{2,1,0:T(8,128)S(1)}, u32[]{:S(2)}, u32[]{:S(2)}) collective-permute-start(f32[13,8,128]{2,1,0:T(8,128)S(1)} %collective-permute-done.8.refs_1_), channel_id=1, source_target_pairs={{0,1},{1,0},{2,3},{3,2},{4,5},{5,4},{6,7},{7,6},{8,9},{9,8},{10,11... | collective-permute-start | bytes 159752 | tf_op jit(solution)/shard_map/ppermute | solution.py:545
  38.1 1.2 %collective-permute-start.13 = (f32[13,8,128]{2,1,0:T(8,128)S(1)}, f32[13,8,128]{2,1,0:T(8,128)S(1)}, u32[]{:S(2)}, u32[]{:S(2)}) collective-permute-start(f32[13,8,128]{2,1,0:T(8,128)S(1)} %collective-permute-done.9.refs_2_), channel_id=1, source_target_pairs={{0,1},{1,0},{2,3},{3,2},{4,5},{5,4},{6,7},{7,6},{8,9},{9,8},{10,11... | collective-permute-start | bytes 159752 | tf_op jit(solution)/shard_map/ppermute | solution.py:545
  38.4 1.2 %collective-permute-start.14 = (f32[13,8,128]{2,1,0:T(8,128)S(1)}, f32[13,8,128]{2,1,0:T(8,128)S(1)}, u32[]{:S(2)}, u32[]{:S(2)}) collective-permute-start(f32[13,8,128]{2,1,0:T(8,128)S(1)} %collective-permute-done.10.refs_3_), channel_id=1, source_target_pairs={{0,1},{1,0},{2,3},{3,2},{4,5},{5,4},{6,7},{7,6},{8,9},{9,8},{10,11... | collective-permute-start | bytes 159752 | tf_op jit(solution)/shard_map/ppermute | solution.py:545
  38.6 1.2 %collective-permute-start.15 = (f32[13,8,128]{2,1,0:T(8,128)S(1)}, f32[13,8,128]{2,1,0:T(8,128)S(1)}, u32[]{:S(2)}, u32[]{:S(2)}) collective-permute-start(f32[13,8,128]{2,1,0:T(8,128)S(1)} %collective-permute-done.11.refs_4_), channel_id=1, source_target_pairs={{0,1},{1,0},{2,3},{3,2},{4,5},{5,4},{6,7},{7,6},{8,9},{9,8},{10,11... | collective-permute-start | bytes 159752 | tf_op jit(solution)/shard_map/ppermute | solution.py:545

commit v15 on v14

--- a/solution.py
+++ b/solution.py
@@ -135,10 +135,25 @@
 
 
 def first_kernel(
-    levels, sub, edge, tracer, zonal, merid, surface, bottom,
+    levels, sub, edge, tracer_hbm, zonal_hbm, merid_hbm, surface_hbm, bottom_hbm,
     cross, mate, raw, mate_raw, flow_in, mate_flow,
+    tracer, zonal, merid, surface, bottom, sems,
 ):
     del edge
+    pairs = (
+        (surface_hbm, surface),
+        (bottom_hbm, bottom),
+        (zonal_hbm, zonal),
+        (merid_hbm, merid),
+        (tracer_hbm, tracer),
+    )
+    copies = [
+        pltpu.make_async_copy(source, target, sems.at[i]) for i, (source, target) in enumerate(pairs)
+    ]
+    for copy in copies:
+        copy.start()
+    for copy in copies:
+        copy.wait()
     outer, inner, sign = orientation()
 
     def column(ref, where, *lead):
@@ -622,11 +637,22 @@
             shaped(levels),
             shaped(levels + RIM),
         ),
-        in_specs=[pl.BlockSpec(memory_space=pl.ANY)] + [vmem] * 5,
+        in_specs=[pl.BlockSpec(memory_space=pl.ANY)] + [hbm] * 5,
         out_specs=(vmem,) * 6,
+        scratch_shapes=[
+            both,
+            pltpu.VMEM((levels, sub * 2, LANES), f32),
+            pltpu.VMEM((levels, sub * 2, LANES), f32),
+            pltpu.VMEM((vectors, sub * 2, LANES), f32),
+            pltpu.VMEM((sub * 2, LANES), jnp.int32),
+            pltpu.SemaphoreType.DMA((5,)),
+        ],
         compiler_params=params,
         name="partial_step",
-    )(edge, tracer_pert, zonal_flow, merid_flow, surface, bottom)
+    )(
+        edge, pinned[0], pinned[1], pltpu.with_memory_space_constraint(merid_flow, pltpu.HBM),
+        pinned[2], pinned[3],
+    )
     cross_far = lax.ppermute(cross, "lon", outward)
     mate_far, mate_raw_far, mate_flow_far = (swap(x, 1) for x in (mate, mate_raw, mate_flow))
     done, *rest = pl.pallas_call(

time: 42.6 us -> 42.5 us (level)
  Pallas kernels: 7.02 us -> 8.46 us
  local copies, waits for them, and re-layouts: 1.02 us -> 0.01 us
  starting transfers between devices: 23.4 us -> 22.9 us
    pallas_call x1, Pallas kernels: 1.2 us -> 2.72 us  [on_device(): pl.pallas_call(functools.partial(first_kernel, levels, sub), out_shape=(s...]
    unnamed x12 -> x4, local copies, waits for them, and re-layouts: 1.02 us -> 0.01 us
    ppermute x8, starting transfers between devices: 5.99 us -> 5.5 us  [swap(): return lax.ppermute(array, 'lon', [(i, i ^ mask) for i in range(count)])]
  transfers between devices with their start and end apart: 16 -> 16, of which waited for: 9 -> 9; matrix products, arithmetic and copies ran while one was open for 0% -> 0% of each run, Pallas kernels for 7% -> 10%
where the time goes in v15:
time: 42.5 us; the launch traced here: 42.3 us
  starting transfers between devices  22.9 us (54%)
  waiting for transfers between devices  10.1 us (24%)
  Pallas kernels  8.46 us (20%)
  between operations  0.73 us (2%)
    ppermute x4, starting transfers between devices, gather(): fetched.append(lax.ppermute(pair, 'lon', moves))  6 us
    ppermute x1, starting transfers between devices, on_device(): flow_half = lax.ppermute(flow_edge, 'lon', outward)  5.51 us
    ppermute x8, starting transfers between devices, swap(): return lax.ppermute(array, 'lon', [(i, i ^ mask) for i in range(count)])  5.5 us
    ppermute x1, starting transfers between devices, on_device(): cross_far = lax.ppermute(cross, 'lon', outward)  4.36 us
    ppermute x4, waiting for transfers between devices, gather(): fetched.append(lax.ppermute(pair, 'lon', moves))  3.84 us
    ppermute x1, waiting for transfers between devices, on_device(): flow_other = lax.ppermute(flow_half, 'grp', [(0, 1), (1, 0)])  3.17 us
    ppermute x8, waiting for transfers between devices, swap(): return lax.ppermute(array, 'lon', [(i, i ^ mask) for i in range(count)])  3.12 us
    pallas_call x1, Pallas kernels, on_device(): pl.pallas_call(functools.partial(first_kernel, levels, sub), out_shape=(s...  2.72 us
  transfers between devices with their start and end apart: 16, of which 9 were waited for; matrix products, arithmetic and copies ran while one was open for 0% of the time, Pallas kernels for 10%

profile of v15, /device:TPU:0, one launch (start us, length us, event | category | flops | bytes accessed | tf_op | source)
XLA Modules:
  0.0 42.3 jit_solution(2497344444441353665)
XLA Ops:
  0.6 1.3 %edge_columns.1 = (f32[106,8,128]{2,1,0:T(8,128)S(1)}, f32[25,8,128]{2,1,0:T(8,128)S(1)}) custom-call(f32[2,50,16,128]{3,2,1,0:T(8,128)} %bitcast.40, f32[50,16,128]{2,1,0:T(8,128)} %bitcast.42, f32[2,16,128]{2,1,0:T(8,128)} %bitcast.37, s32[16,128]{1,0:T(8,128)} %bitcast.44), custom_call_target="tpu_custom_call" | custom-call | tf_op jit(solution)/shard_map/edge_columns/pallas_call | solution.py:612
  2.0 5.5 %collective-permute-start.5 = (f32[25,8,128]{2,1,0:T(8,128)S(1)}, f32[25,8,128]{2,1,0:T(8,128)S(1)}, u32[]{:S(2)}, u32[]{:S(2)}) collective-permute-start(f32[25,8,128]{2,1,0:T(8,128)S(1)} %get-tuple-element.28), channel_id=1, source_target_pairs={{0,15},{1,2},{2,1},{3,4},{4,3},{5,6},{6,5},{7,8},{8,7},{9,10},{10,... | collective-permute-start | bytes 307208 | tf_op jit(solution)/shard_map/ppermute | solution.py:627
  7.5 0.1 collective-permute-start.1
  7.6 0.0 copy-start
  7.6 2.7 %partial_step.1 = (f32[100,8,128]{2,1,0:T(8,128)S(1)}, f32[100,8,128]{2,1,0:T(8,128)S(1)}, f32[100,8,128]{2,1,0:T(8,128)S(1)}, f32[100,8,128]{2,1,0:T(8,128)S(1)...) custom-call(f32[106,8,128]{2,1,0:T(8,128)S(1)} %get-tuple-element.21.edge, f32[2,50,16,128]{3,2,1,0:T(8,128)} %bitcast.41, ...), custom_call_target="tpu_custom_call" | custom-call | tf_op jit(solution)/shard_map/partial_step/pallas_call | solution.py:630
  10.3 0.1 collective-permute-start.2
  10.4 0.5 %collective-permute-start.3 = (f32[100,8,128]{2,1,0:T(8,128)S(1)}, f32[100,8,128]{2,1,0:T(8,128)S(1)}, u32[]{:S(2)}, u32[]{:S(2)}) collective-permute-start(f32[100,8,128]{2,1,0:T(8,128)S(1)} %get-tuple-element.25.mate_raw), channel_id=1, source_target_pairs={{0,1},{1,0},{2,3},{3,2},{4,5},{5,4},{6,7},{7,6},{8,9},{9,8},{10,11... | collective-permute-start | bytes 1228808 | tf_op jit(solution)/shard_map/ppermute | solution.py:560
  10.9 4.4 %collective-permute-start = (f32[100,8,128]{2,1,0:T(8,128)S(1)}, f32[100,8,128]{2,1,0:T(8,128)S(1)}, u32[]{:S(2)}, u32[]{:S(2)}) collective-permute-start(f32[100,8,128]{2,1,0:T(8,128)S(1)} %get-tuple-element.22.cross), channel_id=1, source_target_pairs={{0,15},{1,2},{2,1},{3,4},{4,3},{5,6},{6,5},{7,8},{8,7},{9,10},{10,... | collective-permute-start | bytes 1228808 | tf_op jit(solution)/shard_map/ppermute | solution.py:656
  15.2 0.0 collective-permute-done.5.flow_half
  15.2 1.5 %collective-permute-start.6 = (f32[25,8,128]{2,1,0:T(8,128)S(1)}, f32[25,8,128]{2,1,0:T(8,128)S(1)}, u32[]{:S(2)}, u32[]{:S(2)}) collective-permute-start(f32[25,8,128]{2,1,0:T(8,128)S(1)} %collective-permute-done.5.flow_half), channel_id=1, source_target_pairs={{0,16},{16,0},{1,17},{17,1},{2,18},{18,2},{3,19},{19,3},{4,20},{20... | collective-permute-start | bytes 307208 | tf_op jit(solution)/shard_map/ppermute | solution.py:629
  16.7 3.2 %collective-permute-done.6.flow_other = f32[25,8,128]{2,1,0:T(8,128)S(1)} collective-permute-done((f32[25,8,128]{2,1,0:T(8,128)S(1)}, f32[25,8,128]{2,1,0:T(8,128)S(1)}, u32[]{:S(2)}, u32[]{:S(2)}) %collective-permute-start.6) | collective-permute-done | bytes 102432 | tf_op jit(solution)/shard_map/ppermute | solution.py:629
  19.9 0.0 collective-permute-start.4
  19.9 1.5 %collective-permute-done.4.mate_flow_far = f32[56,8,128]{2,1,0:T(8,128)S(1)} collective-permute-done((f32[56,8,128]{2,1,0:T(8,128)S(1)}, f32[56,8,128]{2,1,0:T(8,128)S(1)}, u32[]{:S(2)}, u32[]{:S(2)}) %collective-permute-start.4) | collective-permute-done | bytes 229408 | tf_op jit(solution)/shard_map/ppermute | solution.py:560
  21.4 0.0 collective-permute-done.2.mate_far
  21.4 0.0 collective-permute-done.3.mate_raw_far
  21.4 0.0 collective-permute-done.1.raw_far
  21.4 0.0 copy-done
  21.4 1.5 %both_steps.1 = (f32[2,50,8,128]{3,2,1,0:T(8,128)S(1)}, f32[2,50,8,128]{3,2,1,0:T(8,128)S(1)}, f32[50,8,128]{2,1,0:T(8,128)S(1)}, f32[5,8,128]{2,1,0:T(8,128)S(1)}, f32[4,2,2,8,128]{4,3,2,1,0:T(8,128)S(1)}) custom-call(f32[100,8,128]{2,1,0:T(8,128)S(1)} %get-tuple-element.23.raw, f32[100,8,128]{2,1,0:T(8,128)S(1)} %get-tuple-element.22.cross, ...), custom_call_target="tpu_custom_call" | custom-call | tf_op jit(solution)/shard_map/both_steps/pallas_call | solution.py:658
  22.9 0.0 collective-permute-done.cross_far
  22.9 0.2 outer_column.1
  23.2 4.4 %collective-permute-start.7 = (f32[7,8,128]{2,1,0:T(8,128)S(1)}, f32[7,8,128]{2,1,0:T(8,128)S(1)}, u32[]{:S(2)}, u32[]{:S(2)}) collective-permute-start(f32[7,8,128]{2,1,0:T(8,128)S(1)} %get-tuple-element.33), channel_id=1, source_target_pairs={{0,1},{1,0},{2,3},{3,2},{4,5},{5,4},{6,7},{7,6},{8,9},{9,8},{10,11... | collective-permute-start | bytes 86024 | tf_op jit(solution)/shard_map/ppermute | solution.py:560
  27.6 0.9 %collective-permute-done.7 = f32[7,8,128]{2,1,0:T(8,128)S(1)} collective-permute-done((f32[7,8,128]{2,1,0:T(8,128)S(1)}, f32[7,8,128]{2,1,0:T(8,128)S(1)}, u32[]{:S(2)}, u32[]{:S(2)}) %collective-permute-start.7) | collective-permute-done | bytes 28704 | tf_op jit(solution)/shard_map/ppermute | solution.py:560
  28.5 4.4 %collective-permute-start.8 = (f32[13,8,128]{2,1,0:T(8,128)S(1)}, f32[13,8,128]{2,1,0:T(8,128)S(1)}, u32[]{:S(2)}, u32[]{:S(2)}) collective-permute-start(f32[13,8,128]{2,1,0:T(8,128)S(1)} %pad_maximum_fusion.refs_0_), channel_id=1, source_target_pairs={{0,14},{1,13},{2,12},{3,15},{4,10},{5,9},{6,8},{7,11},{8,6},{9,5},... | collective-permute-start | bytes 159752 | tf_op jit(solution)/shard_map/ppermute | solution.py:580
  32.9 0.0 collective-permute-start.9
  32.9 0.9 %collective-permute-start.10 = (f32[13,8,128]{2,1,0:T(8,128)S(1)}, f32[13,8,128]{2,1,0:T(8,128)S(1)}, u32[]{:S(2)}, u32[]{:S(2)}) collective-permute-start(f32[13,8,128]{2,1,0:T(8,128)S(1)} %pad_maximum_fusion.refs_0_), channel_id=1, source_target_pairs={{0,6},{1,5},{2,4},{3,7},{4,2},{5,1},{6,0},{7,3},{8,14},{9,13},{10,... | collective-permute-start | bytes 159752 | tf_op jit(solution)/shard_map/ppermute | solution.py:580
  33.8 0.7 %collective-permute-start.11 = (f32[13,8,128]{2,1,0:T(8,128)S(1)}, f32[13,8,128]{2,1,0:T(8,128)S(1)}, u32[]{:S(2)}, u32[]{:S(2)}) collective-permute-start(f32[13,8,128]{2,1,0:T(8,128)S(1)} %pad_maximum_fusion.refs_0_), channel_id=1, source_target_pairs={{1,3},{3,1},{5,7},{7,5},{9,11},{11,9},{13,15},{15,13},{17,19},{19,... | collective-permute-start | bytes 159752 | tf_op jit(solution)/shard_map/ppermute | solution.py:580
  34.5 1.3 %collective-permute-done.8.refs_1_ = f32[13,8,128]{2,1,0:T(8,128)S(1)} collective-permute-done((f32[13,8,128]{2,1,0:T(8,128)S(1)}, f32[13,8,128]{2,1,0:T(8,128)S(1)}, u32[]{:S(2)}, u32[]{:S(2)}) %collective-permute-start.8) | collective-permute-done | bytes 53280 | tf_op jit(solution)/shard_map/ppermute | solution.py:580
  35.8 0.0 collective-permute-start.12
  35.8 2.2 %collective-permute-done.9.refs_2_ = f32[13,8,128]{2,1,0:T(8,128)S(1)} collective-permute-done((f32[13,8,128]{2,1,0:T(8,128)S(1)}, f32[13,8,128]{2,1,0:T(8,128)S(1)}, u32[]{:S(2)}, u32[]{:S(2)}) %collective-permute-start.9) | collective-permute-done | bytes 53280 | tf_op jit(solution)/shard_map/ppermute | solution.py:580
  38.0 0.0 collective-permute-start.13
  38.0 0.3 collective-permute-done.10.refs_3_
  38.3 0.2 collective-permute-start.14
  38.5 0.0 collective-permute-done.11.refs_4_
  38.5 0.3 collective-permute-start.15
  38.8 0.0 copy-start.1
  38.8 0.1 interleave.1.refs_10_
  39.0 0.0 collective-permute-done.12.refs_5_
  39.0 0.3 collective-permute-done.13.refs_6_
  39.2 0.3 collective-permute-done.14.refs_7_
  39.6 0.2 collective-permute-done.15.refs_8_
  39.7 0.0 copy-done.1
  39.8 2.5 %surface_and_scale.1 = (f32[2,50,16,128]{3,2,1,0:T(8,128)}, f32[2,16,128]{2,1,0:T(8,128)}, f32[3]{0:T(128)}) custom-call(f32[13,8,128]{2,1,0:T(8,128)S(1)} %pad_maximum_fusion.refs_0_, f32[13,8,128]{2,1,0:T(8,128)S(1)} %collective-permute-done.8.refs_1_, f32[13,8,128]{2,1,0:T(8,128)S(1)} %collective-permute-done.9.refs_2_, ...), custom_call_target="tpu_custom_call" | custom-call | tf_op jit(solution)/shard_map/surface_and_scale/pallas_call | solution.py:693
  (4 shorter events, 0.0 us)
Async XLA Ops:
  2.0 13.3 %collective-permute-start.5 = (f32[25,8,128]{2,1,0:T(8,128)S(1)}, f32[25,8,128]{2,1,0:T(8,128)S(1)}, u32[]{:S(2)}, u32[]{:S(2)}) collective-permute-start(f32[25,8,128]{2,1,0:T(8,128)S(1)} %get-tuple-element.28), channel_id=1, source_target_pairs={{0,15},{1,2},{2,1},{3,4},{4,3},{5,6},{6,5},{7,8},{8,7},{9,10},{10,... | collective-permute-start | bytes 307208 | tf_op jit(solution)/shard_map/ppermute | solution.py:627
  7.5 13.9 %collective-permute-start.1 = (f32[106,8,128]{2,1,0:T(8,128)S(1)}, f32[106,8,128]{2,1,0:T(8,128)S(1)}, u32[]{:S(2)}, u32[]{:S(2)}) collective-permute-start(f32[106,8,128]{2,1,0:T(8,128)S(1)} %get-tuple-element.21.edge), channel_id=1, source_target_pairs={{0,15},{1,2},{2,1},{3,4},{4,3},{5,6},{6,5},{7,8},{8,7},{9,10},{10,... | collective-permute-start | bytes 1302536 | tf_op jit(solution)/shard_map/ppermute | solution.py:628
  7.6 13.8 %copy-start = (f32[50,2,1024]{2,1,0:T(2,128)S(1)}, f32[50,2,1024]{2,1,0:T(2,128)}, u32[]{:S(2)}) copy-start(f32[50,2,1024]{2,1,0:T(2,128)} %param.8) | copy-start | bytes 1228804
  10.3 11.1 %collective-permute-start.2 = (f32[100,8,128]{2,1,0:T(8,128)S(1)}, f32[100,8,128]{2,1,0:T(8,128)S(1)}, u32[]{:S(2)}, u32[]{:S(2)}) collective-permute-start(f32[100,8,128]{2,1,0:T(8,128)S(1)} %get-tuple-element.24.mate), channel_id=1, source_target_pairs={{0,1},{1,0},{2,3},{3,2},{4,5},{5,4},{6,7},{7,6},{8,9},{9,8},{10,11... | collective-permute-start | bytes 1228808 | tf_op jit(solution)/shard_map/ppermute | solution.py:560
  10.4 11.0 %collective-permute-start.3 = (f32[100,8,128]{2,1,0:T(8,128)S(1)}, f32[100,8,128]{2,1,0:T(8,128)S(1)}, u32[]{:S(2)}, u32[]{:S(2)}) collective-permute-start(f32[100,8,128]{2,1,0:T(8,128)S(1)} %get-tuple-element.25.mate_raw), channel_id=1, source_target_pairs={{0,1},{1,0},{2,3},{3,2},{4,5},{5,4},{6,7},{7,6},{8,9},{9,8},{10,11... | collective-permute-start | bytes 1228808 | tf_op jit(solution)/shard_map/ppermute | solution.py:560
  10.9 12.1 %collective-permute-start = (f32[100,8,128]{2,1,0:T(8,128)S(1)}, f32[100,8,128]{2,1,0:T(8,128)S(1)}, u32[]{:S(2)}, u32[]{:S(2)}) collective-permute-start(f32[100,8,128]{2,1,0:T(8,128)S(1)} %get-tuple-element.22.cross), channel_id=1, source_target_pairs={{0,15},{1,2},{2,1},{3,4},{4,3},{5,6},{6,5},{7,8},{8,7},{9,10},{10,... | collective-permute-start | bytes 1228808 | tf_op jit(solution)/shard_map/ppermute | solution.py:656
  15.2 4.7 %collective-permute-start.6 = (f32[25,8,128]{2,1,0:T(8,128)S(1)}, f32[25,8,128]{2,1,0:T(8,128)S(1)}, u32[]{:S(2)}, u32[]{:S(2)}) collective-permute-start(f32[25,8,128]{2,1,0:T(8,128)S(1)} %collective-permute-done.5.flow_half), channel_id=1, source_target_pairs={{0,16},{16,0},{1,17},{17,1},{2,18},{18,2},{3,19},{19,3},{4,20},{20... | collective-permute-start | bytes 307208 | tf_op jit(solution)/shard_map/ppermute | solution.py:629
  19.9 1.5 %collective-permute-start.4 = (f32[56,8,128]{2,1,0:T(8,128)S(1)}, f32[56,8,128]{2,1,0:T(8,128)S(1)}, u32[]{:S(2)}, u32[]{:S(2)}) collective-permute-start(f32[56,8,128]{2,1,0:T(8,128)S(1)} %get-tuple-element.27.mate_flow), channel_id=1, source_target_pairs={{0,1},{1,0},{2,3},{3,2},{4,5},{5,4},{6,7},{7,6},{8,9},{9,8},{10,11... | collective-permute-start | bytes 688136 | tf_op jit(solution)/shard_map/ppermute | solution.py:560
  23.2 5.3 %collective-permute-start.7 = (f32[7,8,128]{2,1,0:T(8,128)S(1)}, f32[7,8,128]{2,1,0:T(8,128)S(1)}, u32[]{:S(2)}, u32[]{:S(2)}) collective-permute-start(f32[7,8,128]{2,1,0:T(8,128)S(1)} %get-tuple-element.33), channel_id=1, source_target_pairs={{0,1},{1,0},{2,3},{3,2},{4,5},{5,4},{6,7},{7,6},{8,9},{9,8},{10,11... | collective-permute-start | bytes 86024 | tf_op jit(solution)/shard_map/ppermute | solution.py:560
  28.5 7.3 %collective-permute-start.8 = (f32[13,8,128]{2,1,0:T(8,128)S(1)}, f32[13,8,128]{2,1,0:T(8,128)S(1)}, u32[]{:S(2)}, u32[]{:S(2)}) collective-permute-start(f32[13,8,128]{2,1,0:T(8,128)S(1)} %pad_maximum_fusion.refs_0_), channel_id=1, source_target_pairs={{0,14},{1,13},{2,12},{3,15},{4,10},{5,9},{6,8},{7,11},{8,6},{9,5},... | collective-permute-start | bytes 159752 | tf_op jit(solution)/shard_map/ppermute | solution.py:580
  32.9 5.1 %collective-permute-start.9 = (f32[13,8,128]{2,1,0:T(8,128)S(1)}, f32[13,8,128]{2,1,0:T(8,128)S(1)}, u32[]{:S(2)}, u32[]{:S(2)}) collective-permute-start(f32[13,8,128]{2,1,0:T(8,128)S(1)} %pad_maximum_fusion.refs_0_), channel_id=1, source_target_pairs={{0,8},{1,11},{2,10},{3,9},{4,12},{5,15},{6,14},{7,13},{8,0},{9,3},... | collective-permute-start | bytes 159752 | tf_op jit(solution)/shard_map/ppermute | solution.py:580
  32.9 5.4 %collective-permute-start.10 = (f32[13,8,128]{2,1,0:T(8,128)S(1)}, f32[13,8,128]{2,1,0:T(8,128)S(1)}, u32[]{:S(2)}, u32[]{:S(2)}) collective-permute-start(f32[13,8,128]{2,1,0:T(8,128)S(1)} %pad_maximum_fusion.refs_0_), channel_id=1, source_target_pairs={{0,6},{1,5},{2,4},{3,7},{4,2},{5,1},{6,0},{7,3},{8,14},{9,13},{10,... | collective-permute-start | bytes 159752 | tf_op jit(solution)/shard_map/ppermute | solution.py:580
  33.8 4.7 %collective-permute-start.11 = (f32[13,8,128]{2,1,0:T(8,128)S(1)}, f32[13,8,128]{2,1,0:T(8,128)S(1)}, u32[]{:S(2)}, u32[]{:S(2)}) collective-permute-start(f32[13,8,128]{2,1,0:T(8,128)S(1)} %pad_maximum_fusion.refs_0_), channel_id=1, source_target_pairs={{1,3},{3,1},{5,7},{7,5},{9,11},{11,9},{13,15},{15,13},{17,19},{19,... | collective-permute-start | bytes 159752 | tf_op jit(solution)/shard_map/ppermute | solution.py:580
  35.8 3.2 %collective-permute-start.12 = (f32[13,8,128]{2,1,0:T(8,128)S(1)}, f32[13,8,128]{2,1,0:T(8,128)S(1)}, u32[]{:S(2)}, u32[]{:S(2)}) collective-permute-start(f32[13,8,128]{2,1,0:T(8,128)S(1)} %collective-permute-done.8.refs_1_), channel_id=1, source_target_pairs={{0,1},{1,0},{2,3},{3,2},{4,5},{5,4},{6,7},{7,6},{8,9},{9,8},{10,11... | collective-permute-start | bytes 159752 | tf_op jit(solution)/shard_map/ppermute | solution.py:560
  38.0 1.2 %collective-permute-start.13 = (f32[13,8,128]{2,1,0:T(8,128)S(1)}, f32[13,8,128]{2,1,0:T(8,128)S(1)}, u32[]{:S(2)}, u32[]{:S(2)}) collective-permute-start(f32[13,8,128]{2,1,0:T(8,128)S(1)} %collective-permute-done.9.refs_2_), channel_id=1, source_target_pairs={{0,1},{1,0},{2,3},{3,2},{4,5},{5,4},{6,7},{7,6},{8,9},{9,8},{10,11... | collective-permute-start | bytes 159752 | tf_op jit(solution)/shard_map/ppermute | solution.py:560
  38.3 1.2 %collective-permute-start.14 = (f32[13,8,128]{2,1,0:T(8,128)S(1)}, f32[13,8,128]{2,1,0:T(8,128)S(1)}, u32[]{:S(2)}, u32[]{:S(2)}) collective-permute-start(f32[13,8,128]{2,1,0:T(8,128)S(1)} %collective-permute-done.10.refs_3_), channel_id=1, source_target_pairs={{0,1},{1,0},{2,3},{3,2},{4,5},{5,4},{6,7},{7,6},{8,9},{9,8},{10,11... | collective-permute-start | bytes 159752 | tf_op jit(solution)/shard_map/ppermute | solution.py:560
  38.5 1.2 %collective-permute-start.15 = (f32[13,8,128]{2,1,0:T(8,128)S(1)}, f32[13,8,128]{2,1,0:T(8,128)S(1)}, u32[]{:S(2)}, u32[]{:S(2)}) collective-permute-start(f32[13,8,128]{2,1,0:T(8,128)S(1)} %collective-permute-done.11.refs_4_), channel_id=1, source_target_pairs={{0,1},{1,0},{2,3},{3,2},{4,5},{5,4},{6,7},{7,6},{8,9},{9,8},{10,11... | collective-permute-start | bytes 159752 | tf_op jit(solution)/shard_map/ppermute | solution.py:560
  38.8 0.9 %copy-start.1 = (f32[2,2,1024]{2,1,0:T(2,128)S(1)}, f32[2,2,1024]{2,1,0:T(2,128)}, u32[]{:S(2)}) copy-start(f32[2,2,1024]{2,1,0:T(2,128)} %param.6) | copy-start | bytes 49156

commit v16 on v14

--- a/solution.py
+++ b/solution.py
@@ -123,7 +123,11 @@
         return carry
 
     lax.fori_loop(0, part, take, 0, unroll=steps(part, 25))
-    pack_rim(sub, surface, bottom, edge, VECTORS * levels)
+    shared = jnp.where(lax.axis_index("grp") == 0, outer, 1 - outer)
+    flow[part] = bottom[pl.ds(shared, sub, stride=2), :].astype(jnp.float32)
+    for c in range(2):
+        for v in range(VECTORS):
+            edge[VECTORS * levels + v * 2 + c] = surface[v, pl.ds(c, sub, stride=2), :]
     for v in range(VECTORS):
         copies[3 + v].wait()
 
@@ -200,12 +204,15 @@
         return carry
 
     lax.fori_loop(0, part, unpack, 0, unroll=steps(part, 10))
-    powers_of_heights(levels, mate_flow, mate_flow_far, raw_far, powers)
+    first = lax.axis_index("grp") == 0
+    fetched, told = flow_half[part], flow_other[part]
+    depth_far = [jnp.where(first, fetched, told), jnp.where(first, told, fetched)]
+    powers_of_heights(levels, mate_flow, mate_flow_far, raw_far, depth_far, powers)
     near, far = (raw, mate_raw), (raw_far, mate_raw_far)
     rim = levels + DEPTHS
     depth = [mate_flow[rim + where] for where in (outer, inner)]
     beside = [
-        jnp.minimum(depth[0], raw_far[VECTORS * levels + DEPTHS + inner]),
+        jnp.minimum(depth[0], depth_far[0]),
         jnp.minimum(depth[1], mate_flow_far[rim + outer]),
     ]
     between = jnp.minimum(*depth)
@@ -329,7 +336,7 @@
     return [sums[n // size][n % size : n % size + 1] for n in range(count)]
 
 
-def powers_of_heights(levels, mate_flow, mate_flow_far, raw_far, powers):
+def powers_of_heights(levels, mate_flow, mate_flow_far, raw_far, beyond, powers):
     outer, inner, _ = orientation()
     line = [
         (mate_flow_far, levels, inner),
@@ -339,7 +346,7 @@
         (raw_far, VECTORS * levels, inner),
         (raw_far, VECTORS * levels, outer),
     ]
-    depth = [ref[base + DEPTHS + where] for ref, base, where in line]
+    depth = [ref[base + DEPTHS + where] for ref, base, where in line[:4]] + beyond
     faces = [SURFACE_COUPLING * jnp.minimum(a, b) for a, b in zip(depth, depth[1:])]
     sides = [side_depths(SURFACE_COUPLING * d) for d in depth[1:5]]
     for v in range(VECTORS):
@@ -596,7 +603,7 @@
     ]
     edge, flow_edge = pl.pallas_call(
         functools.partial(edge_kernel, levels, sub),
-        out_shape=(shaped(VECTORS * levels + RIM), shaped(part)),
+        out_shape=(shaped(VECTORS * levels + DEPTHS), shaped(part + 1)),
         in_specs=[hbm] * 4,
         out_specs=(vmem, vmem),
         scratch_shapes=[

time: 42.6 us -> 42.5 us (level)
  no operation moved by 1% of the time
where the time goes in v16:
time: 42.5 us; the launch traced here: 42.3 us
  starting transfers between devices  23.3 us (55%)
  waiting for transfers between devices  10.2 us (24%)
  Pallas kernels  7.03 us (17%)
  local copies, waits for them, and re-layouts  1.02 us (2%)
  between operations  0.78 us (2%)
    ppermute x4, starting transfers between devices, gather(): fetched.append(lax.ppermute(pair, 'lon', moves))  6 us
    ppermute x8, starting transfers between devices, swap(): return lax.ppermute(array, 'lon', [(i, i ^ mask) for i in range(count)])  5.81 us
    ppermute x1, starting transfers between devices, on_device(): flow_half = lax.ppermute(flow_edge, 'lon', outward)  5.51 us
    ppermute x1, starting transfers between devices, on_device(): cross_far = lax.ppermute(cross, 'lon', outward)  4.36 us
    ppermute x4, waiting for transfers between devices, gather(): fetched.append(lax.ppermute(pair, 'lon', moves))  3.86 us
    ppermute x1, waiting for transfers between devices, on_device(): flow_other = lax.ppermute(flow_half, 'grp', [(0, 1), (1, 0)])  3.21 us
    ppermute x8, waiting for transfers between devices, swap(): return lax.ppermute(array, 'lon', [(i, i ^ mask) for i in range(count)])  3.14 us
    pallas_call x1, Pallas kernels, on_device(): pl.pallas_call(functools.partial(third_kernel, levels, sub, count), out_s...  2.54 us
  transfers between devices with their start and end apart: 16, of which 9 were waited for; matrix products, arithmetic and copies ran while one was open for 0% of the time, Pallas kernels for 7%

profile of v16, /device:TPU:0, one launch (start us, length us, event | category | flops | bytes accessed | tf_op | source)
XLA Modules:
  0.0 42.3 jit_solution(15246521140872625969)
XLA Ops:
  0.6 0.0 copy-start
  0.6 0.0 copy-start.1
  0.7 0.0 copy-start.4
  0.7 0.0 copy-start.5
  0.7 1.4 %edge_columns.1 = (f32[104,8,128]{2,1,0:T(8,128)S(1)}, f32[26,8,128]{2,1,0:T(8,128)S(1)}) custom-call(f32[2,50,16,128]{3,2,1,0:T(8,128)} %bitcast.35, f32[50,16,128]{2,1,0:T(8,128)} %bitcast.37, f32[2,16,128]{2,1,0:T(8,128)} %bitcast.41, s32[16,128]{1,0:T(8,128)} %bitcast.44), custom_call_target="tpu_custom_call" | custom-call | tf_op jit(solution)/shard_map/edge_columns/pallas_call | solution.py:604
  2.1 5.5 %collective-permute-start.5 = (f32[26,8,128]{2,1,0:T(8,128)S(1)}, f32[26,8,128]{2,1,0:T(8,128)S(1)}, u32[]{:S(2)}, u32[]{:S(2)}) collective-permute-start(f32[26,8,128]{2,1,0:T(8,128)S(1)} %get-tuple-element.28), channel_id=1, source_target_pairs={{0,15},{1,2},{2,1},{3,4},{4,3},{5,6},{6,5},{7,8},{8,7},{9,10},{10,... | collective-permute-start | bytes 319496 | tf_op jit(solution)/shard_map/ppermute | solution.py:619
  7.6 0.1 collective-permute-start.1
  7.7 0.0 copy-done
  7.7 0.0 copy-done.1
  7.7 0.0 copy-done.4
  7.7 0.0 copy-done.5
  7.7 0.0 copy-start.2
  7.7 1.0 %copy-done.2 = f32[50,2,1024]{2,1,0:T(2,128)S(1)} copy-done((f32[50,2,1024]{2,1,0:T(2,128)S(1)}, f32[50,2,1024]{2,1,0:T(2,128)}, u32[]{:S(2)}) %copy-start.2) | copy-done | bytes 409624
  8.7 1.2 %partial_step.1 = (f32[100,8,128]{2,1,0:T(8,128)S(1)}, f32[100,8,128]{2,1,0:T(8,128)S(1)}, f32[100,8,128]{2,1,0:T(8,128)S(1)}, f32[100,8,128]{2,1,0:T(8,128)S(1)...) custom-call(f32[104,8,128]{2,1,0:T(8,128)S(1)} %get-tuple-element.21.edge, f32[2,50,16,128]{3,2,1,0:T(8,128)S(1)} %bitcast.36, ...), custom_call_target="tpu_custom_call" | custom-call | tf_op jit(solution)/shard_map/partial_step/pallas_call | solution.py:622
  9.9 0.1 collective-permute-start.2
  10.0 0.5 %collective-permute-start.3 = (f32[100,8,128]{2,1,0:T(8,128)S(1)}, f32[100,8,128]{2,1,0:T(8,128)S(1)}, u32[]{:S(2)}, u32[]{:S(2)}) collective-permute-start(f32[100,8,128]{2,1,0:T(8,128)S(1)} %get-tuple-element.25.mate_raw), channel_id=1, source_target_pairs={{0,1},{1,0},{2,3},{3,2},{4,5},{5,4},{6,7},{7,6},{8,9},{9,8},{10,11... | collective-permute-start | bytes 1228808 | tf_op jit(solution)/shard_map/ppermute | solution.py:552
  10.5 4.4 %collective-permute-start = (f32[100,8,128]{2,1,0:T(8,128)S(1)}, f32[100,8,128]{2,1,0:T(8,128)S(1)}, u32[]{:S(2)}, u32[]{:S(2)}) collective-permute-start(f32[100,8,128]{2,1,0:T(8,128)S(1)} %get-tuple-element.22.cross), channel_id=1, source_target_pairs={{0,15},{1,2},{2,1},{3,4},{4,3},{5,6},{6,5},{7,8},{8,7},{9,10},{10,... | collective-permute-start | bytes 1228808 | tf_op jit(solution)/shard_map/ppermute | solution.py:637
  14.9 0.0 collective-permute-done.5.flow_half
  14.9 1.5 %collective-permute-start.6 = (f32[26,8,128]{2,1,0:T(8,128)S(1)}, f32[26,8,128]{2,1,0:T(8,128)S(1)}, u32[]{:S(2)}, u32[]{:S(2)}) collective-permute-start(f32[26,8,128]{2,1,0:T(8,128)S(1)} %collective-permute-done.5.flow_half), channel_id=1, source_target_pairs={{0,16},{16,0},{1,17},{17,1},{2,18},{18,2},{3,19},{19,3},{4,20},{20... | collective-permute-start | bytes 319496 | tf_op jit(solution)/shard_map/ppermute | solution.py:621
  16.4 3.2 %collective-permute-done.6.flow_other = f32[26,8,128]{2,1,0:T(8,128)S(1)} collective-permute-done((f32[26,8,128]{2,1,0:T(8,128)S(1)}, f32[26,8,128]{2,1,0:T(8,128)S(1)}, u32[]{:S(2)}, u32[]{:S(2)}) %collective-permute-start.6) | collective-permute-done | bytes 106528 | tf_op jit(solution)/shard_map/ppermute | solution.py:621
  19.6 0.0 collective-permute-start.4
  19.6 1.5 %collective-permute-done.4.mate_flow_far = f32[56,8,128]{2,1,0:T(8,128)S(1)} collective-permute-done((f32[56,8,128]{2,1,0:T(8,128)S(1)}, f32[56,8,128]{2,1,0:T(8,128)S(1)}, u32[]{:S(2)}, u32[]{:S(2)}) %collective-permute-start.4) | collective-permute-done | bytes 229408 | tf_op jit(solution)/shard_map/ppermute | solution.py:552
  21.1 0.0 collective-permute-done.2.mate_far
  21.1 0.0 collective-permute-done.3.mate_raw_far
  21.1 0.0 collective-permute-done.1.raw_far
  21.1 1.5 %both_steps.1 = (f32[2,50,8,128]{3,2,1,0:T(8,128)S(1)}, f32[2,50,8,128]{3,2,1,0:T(8,128)S(1)}, f32[50,8,128]{2,1,0:T(8,128)S(1)}, f32[5,8,128]{2,1,0:T(8,128)S(1)}, f32[4,2,2,8,128]{4,3,2,1,0:T(8,128)S(1)}) custom-call(f32[100,8,128]{2,1,0:T(8,128)S(1)} %get-tuple-element.23.raw, f32[100,8,128]{2,1,0:T(8,128)S(1)} %get-tuple-element.22.cross, ...), custom_call_target="tpu_custom_call" | custom-call | tf_op jit(solution)/shard_map/both_steps/pallas_call | solution.py:639
  22.6 0.0 collective-permute-done.cross_far
  22.6 0.2 outer_column.1
  22.9 4.7 %collective-permute-start.7 = (f32[7,8,128]{2,1,0:T(8,128)S(1)}, f32[7,8,128]{2,1,0:T(8,128)S(1)}, u32[]{:S(2)}, u32[]{:S(2)}) collective-permute-start(f32[7,8,128]{2,1,0:T(8,128)S(1)} %get-tuple-element.33), channel_id=1, source_target_pairs={{0,1},{1,0},{2,3},{3,2},{4,5},{5,4},{6,7},{7,6},{8,9},{9,8},{10,11... | collective-permute-start | bytes 86024 | tf_op jit(solution)/shard_map/ppermute | solution.py:552
  27.6 0.9 %collective-permute-done.7 = f32[7,8,128]{2,1,0:T(8,128)S(1)} collective-permute-done((f32[7,8,128]{2,1,0:T(8,128)S(1)}, f32[7,8,128]{2,1,0:T(8,128)S(1)}, u32[]{:S(2)}, u32[]{:S(2)}) %collective-permute-start.7) | collective-permute-done | bytes 28704 | tf_op jit(solution)/shard_map/ppermute | solution.py:552
  28.5 4.5 %collective-permute-start.8 = (f32[13,8,128]{2,1,0:T(8,128)S(1)}, f32[13,8,128]{2,1,0:T(8,128)S(1)}, u32[]{:S(2)}, u32[]{:S(2)}) collective-permute-start(f32[13,8,128]{2,1,0:T(8,128)S(1)} %pad_maximum_fusion.refs_0_), channel_id=1, source_target_pairs={{0,14},{1,13},{2,12},{3,15},{4,10},{5,9},{6,8},{7,11},{8,6},{9,5},... | collective-permute-start | bytes 159752 | tf_op jit(solution)/shard_map/ppermute | solution.py:572
  32.9 0.0 collective-permute-start.9
  32.9 0.9 %collective-permute-start.10 = (f32[13,8,128]{2,1,0:T(8,128)S(1)}, f32[13,8,128]{2,1,0:T(8,128)S(1)}, u32[]{:S(2)}, u32[]{:S(2)}) collective-permute-start(f32[13,8,128]{2,1,0:T(8,128)S(1)} %pad_maximum_fusion.refs_0_), channel_id=1, source_target_pairs={{0,6},{1,5},{2,4},{3,7},{4,2},{5,1},{6,0},{7,3},{8,14},{9,13},{10,... | collective-permute-start | bytes 159752 | tf_op jit(solution)/shard_map/ppermute | solution.py:572
  33.8 0.7 %collective-permute-start.11 = (f32[13,8,128]{2,1,0:T(8,128)S(1)}, f32[13,8,128]{2,1,0:T(8,128)S(1)}, u32[]{:S(2)}, u32[]{:S(2)}) collective-permute-start(f32[13,8,128]{2,1,0:T(8,128)S(1)} %pad_maximum_fusion.refs_0_), channel_id=1, source_target_pairs={{1,3},{3,1},{5,7},{7,5},{9,11},{11,9},{13,15},{15,13},{17,19},{19,... | collective-permute-start | bytes 159752 | tf_op jit(solution)/shard_map/ppermute | solution.py:572
  34.5 1.3 %collective-permute-done.8.refs_1_ = f32[13,8,128]{2,1,0:T(8,128)S(1)} collective-permute-done((f32[13,8,128]{2,1,0:T(8,128)S(1)}, f32[13,8,128]{2,1,0:T(8,128)S(1)}, u32[]{:S(2)}, u32[]{:S(2)}) %collective-permute-start.8) | collective-permute-done | bytes 53280 | tf_op jit(solution)/shard_map/ppermute | solution.py:572
  35.7 0.0 collective-permute-start.12
  35.7 2.3 %collective-permute-done.9.refs_2_ = f32[13,8,128]{2,1,0:T(8,128)S(1)} collective-permute-done((f32[13,8,128]{2,1,0:T(8,128)S(1)}, f32[13,8,128]{2,1,0:T(8,128)S(1)}, u32[]{:S(2)}, u32[]{:S(2)}) %collective-permute-start.9) | collective-permute-done | bytes 53280 | tf_op jit(solution)/shard_map/ppermute | solution.py:572
  38.0 0.0 collective-permute-start.13
  38.0 0.3 collective-permute-done.10.refs_3_
  38.3 0.2 collective-permute-start.14
  38.5 0.0 collective-permute-done.11.refs_4_
  38.5 0.3 collective-permute-start.15
  38.9 0.1 interleave.1.refs_10_
  39.0 0.0 collective-permute-done.12.refs_5_
  39.0 0.3 collective-permute-done.13.refs_6_
  39.3 0.3 collective-permute-done.14.refs_7_
  39.6 0.2 collective-permute-done.15.refs_8_
  39.8 2.5 %surface_and_scale.1 = (f32[2,50,16,128]{3,2,1,0:T(8,128)}, f32[2,16,128]{2,1,0:T(8,128)}, f32[3]{0:T(128)}) custom-call(f32[13,8,128]{2,1,0:T(8,128)S(1)} %pad_maximum_fusion.refs_0_, f32[13,8,128]{2,1,0:T(8,128)S(1)} %collective-permute-done.8.refs_1_, f32[13,8,128]{2,1,0:T(8,128)S(1)} %collective-permute-done.9.refs_2_, ...), custom_call_target="tpu_custom_call" | custom-call | tf_op jit(solution)/shard_map/surface_and_scale/pallas_call | solution.py:674
  (6 shorter events, 0.0 us)
Async XLA Ops:
  0.6 7.1 %copy-start = (f32[2,50,2,1024]{3,2,1,0:T(2,128)S(1)}, f32[2,50,2,1024]{3,2,1,0:T(2,128)}, u32[]{:S(2)}) copy-start(f32[2,50,2,1024]{3,2,1,0:T(2,128)} %param.5) | copy-start | bytes 2457604
  0.6 7.0 %copy-start.1 = (f32[50,2,1024]{2,1,0:T(2,128)S(1)}, f32[50,2,1024]{2,1,0:T(2,128)}, u32[]{:S(2)}) copy-start(f32[50,2,1024]{2,1,0:T(2,128)} %param.7) | copy-start | bytes 1228804
  0.7 7.0 %copy-start.4 = (f32[2,2,1024]{2,1,0:T(2,128)S(1)}, f32[2,2,1024]{2,1,0:T(2,128)}, u32[]{:S(2)}) copy-start(f32[2,2,1024]{2,1,0:T(2,128)} %param.6) | copy-start | bytes 49156
  0.7 7.0 %copy-start.5 = (s32[2,1024]{1,0:T(2,128)S(1)}, s32[2,1024]{1,0:T(2,128)}, u32[]{:S(2)}) copy-start(s32[2,1024]{1,0:T(2,128)} %param.9) | copy-start | bytes 24580
  2.1 12.8 %collective-permute-start.5 = (f32[26,8,128]{2,1,0:T(8,128)S(1)}, f32[26,8,128]{2,1,0:T(8,128)S(1)}, u32[]{:S(2)}, u32[]{:S(2)}) collective-permute-start(f32[26,8,128]{2,1,0:T(8,128)S(1)} %get-tuple-element.28), channel_id=1, source_target_pairs={{0,15},{1,2},{2,1},{3,4},{4,3},{5,6},{6,5},{7,8},{8,7},{9,10},{10,... | collective-permute-start | bytes 319496 | tf_op jit(solution)/shard_map/ppermute | solution.py:619
  7.6 13.5 %collective-permute-start.1 = (f32[104,8,128]{2,1,0:T(8,128)S(1)}, f32[104,8,128]{2,1,0:T(8,128)S(1)}, u32[]{:S(2)}, u32[]{:S(2)}) collective-permute-start(f32[104,8,128]{2,1,0:T(8,128)S(1)} %get-tuple-element.21.edge), channel_id=1, source_target_pairs={{0,15},{1,2},{2,1},{3,4},{4,3},{5,6},{6,5},{7,8},{8,7},{9,10},{10,... | collective-permute-start | bytes 1277960 | tf_op jit(solution)/shard_map/ppermute | solution.py:620
  7.7 1.0 %copy-start.2 = (f32[50,2,1024]{2,1,0:T(2,128)S(1)}, f32[50,2,1024]{2,1,0:T(2,128)}, u32[]{:S(2)}) copy-start(f32[50,2,1024]{2,1,0:T(2,128)} %param.8) | copy-start | bytes 1228804
  8.7 12.4 %copy-start.3 = (f32[50,2,1024]{2,1,0:T(2,128)S(1)}, f32[50,2,1024]{2,1,0:T(2,128)}, u32[]{:S(2)}) copy-start(f32[50,2,1024]{2,1,0:T(2,128)} %param.8) | copy-start | bytes 1228804
  9.9 11.1 %collective-permute-start.2 = (f32[100,8,128]{2,1,0:T(8,128)S(1)}, f32[100,8,128]{2,1,0:T(8,128)S(1)}, u32[]{:S(2)}, u32[]{:S(2)}) collective-permute-start(f32[100,8,128]{2,1,0:T(8,128)S(1)} %get-tuple-element.24.mate), channel_id=1, source_target_pairs={{0,1},{1,0},{2,3},{3,2},{4,5},{5,4},{6,7},{7,6},{8,9},{9,8},{10,11... | collective-permute-start | bytes 1228808 | tf_op jit(solution)/shard_map/ppermute | solution.py:552
  10.0 11.1 %collective-permute-start.3 = (f32[100,8,128]{2,1,0:T(8,128)S(1)}, f32[100,8,128]{2,1,0:T(8,128)S(1)}, u32[]{:S(2)}, u32[]{:S(2)}) collective-permute-start(f32[100,8,128]{2,1,0:T(8,128)S(1)} %get-tuple-element.25.mate_raw), channel_id=1, source_target_pairs={{0,1},{1,0},{2,3},{3,2},{4,5},{5,4},{6,7},{7,6},{8,9},{9,8},{10,11... | collective-permute-start | bytes 1228808 | tf_op jit(solution)/shard_map/ppermute | solution.py:552
  10.5 12.1 %collective-permute-start = (f32[100,8,128]{2,1,0:T(8,128)S(1)}, f32[100,8,128]{2,1,0:T(8,128)S(1)}, u32[]{:S(2)}, u32[]{:S(2)}) collective-permute-start(f32[100,8,128]{2,1,0:T(8,128)S(1)} %get-tuple-element.22.cross), channel_id=1, source_target_pairs={{0,15},{1,2},{2,1},{3,4},{4,3},{5,6},{6,5},{7,8},{8,7},{9,10},{10,... | collective-permute-start | bytes 1228808 | tf_op jit(solution)/shard_map/ppermute | solution.py:637
  14.9 4.7 %collective-permute-start.6 = (f32[26,8,128]{2,1,0:T(8,128)S(1)}, f32[26,8,128]{2,1,0:T(8,128)S(1)}, u32[]{:S(2)}, u32[]{:S(2)}) collective-permute-start(f32[26,8,128]{2,1,0:T(8,128)S(1)} %collective-permute-done.5.flow_half), channel_id=1, source_target_pairs={{0,16},{16,0},{1,17},{17,1},{2,18},{18,2},{3,19},{19,3},{4,20},{20... | collective-permute-start | bytes 319496 | tf_op jit(solution)/shard_map/ppermute | solution.py:621
  19.6 1.5 %collective-permute-start.4 = (f32[56,8,128]{2,1,0:T(8,128)S(1)}, f32[56,8,128]{2,1,0:T(8,128)S(1)}, u32[]{:S(2)}, u32[]{:S(2)}) collective-permute-start(f32[56,8,128]{2,1,0:T(8,128)S(1)} %get-tuple-element.27.mate_flow), channel_id=1, source_target_pairs={{0,1},{1,0},{2,3},{3,2},{4,5},{5,4},{6,7},{7,6},{8,9},{9,8},{10,11... | collective-permute-start | bytes 688136 | tf_op jit(solution)/shard_map/ppermute | solution.py:552
  22.9 5.6 %collective-permute-start.7 = (f32[7,8,128]{2,1,0:T(8,128)S(1)}, f32[7,8,128]{2,1,0:T(8,128)S(1)}, u32[]{:S(2)}, u32[]{:S(2)}) collective-permute-start(f32[7,8,128]{2,1,0:T(8,128)S(1)} %get-tuple-element.33), channel_id=1, source_target_pairs={{0,1},{1,0},{2,3},{3,2},{4,5},{5,4},{6,7},{7,6},{8,9},{9,8},{10,11... | collective-permute-start | bytes 86024 | tf_op jit(solution)/shard_map/ppermute | solution.py:552
  28.5 7.3 %collective-permute-start.8 = (f32[13,8,128]{2,1,0:T(8,128)S(1)}, f32[13,8,128]{2,1,0:T(8,128)S(1)}, u32[]{:S(2)}, u32[]{:S(2)}) collective-permute-start(f32[13,8,128]{2,1,0:T(8,128)S(1)} %pad_maximum_fusion.refs_0_), channel_id=1, source_target_pairs={{0,14},{1,13},{2,12},{3,15},{4,10},{5,9},{6,8},{7,11},{8,6},{9,5},... | collective-permute-start | bytes 159752 | tf_op jit(solution)/shard_map/ppermute | solution.py:572
  32.9 5.1 %collective-permute-start.9 = (f32[13,8,128]{2,1,0:T(8,128)S(1)}, f32[13,8,128]{2,1,0:T(8,128)S(1)}, u32[]{:S(2)}, u32[]{:S(2)}) collective-permute-start(f32[13,8,128]{2,1,0:T(8,128)S(1)} %pad_maximum_fusion.refs_0_), channel_id=1, source_target_pairs={{0,8},{1,11},{2,10},{3,9},{4,12},{5,15},{6,14},{7,13},{8,0},{9,3},... | collective-permute-start | bytes 159752 | tf_op jit(solution)/shard_map/ppermute | solution.py:572
  32.9 5.4 %collective-permute-start.10 = (f32[13,8,128]{2,1,0:T(8,128)S(1)}, f32[13,8,128]{2,1,0:T(8,128)S(1)}, u32[]{:S(2)}, u32[]{:S(2)}) collective-permute-start(f32[13,8,128]{2,1,0:T(8,128)S(1)} %pad_maximum_fusion.refs_0_), channel_id=1, source_target_pairs={{0,6},{1,5},{2,4},{3,7},{4,2},{5,1},{6,0},{7,3},{8,14},{9,13},{10,... | collective-permute-start | bytes 159752 | tf_op jit(solution)/shard_map/ppermute | solution.py:572
  33.8 4.7 %collective-permute-start.11 = (f32[13,8,128]{2,1,0:T(8,128)S(1)}, f32[13,8,128]{2,1,0:T(8,128)S(1)}, u32[]{:S(2)}, u32[]{:S(2)}) collective-permute-start(f32[13,8,128]{2,1,0:T(8,128)S(1)} %pad_maximum_fusion.refs_0_), channel_id=1, source_target_pairs={{1,3},{3,1},{5,7},{7,5},{9,11},{11,9},{13,15},{15,13},{17,19},{19,... | collective-permute-start | bytes 159752 | tf_op jit(solution)/shard_map/ppermute | solution.py:572
  35.7 3.2 %collective-permute-start.12 = (f32[13,8,128]{2,1,0:T(8,128)S(1)}, f32[13,8,128]{2,1,0:T(8,128)S(1)}, u32[]{:S(2)}, u32[]{:S(2)}) collective-permute-start(f32[13,8,128]{2,1,0:T(8,128)S(1)} %collective-permute-done.8.refs_1_), channel_id=1, source_target_pairs={{0,1},{1,0},{2,3},{3,2},{4,5},{5,4},{6,7},{7,6},{8,9},{9,8},{10,11... | collective-permute-start | bytes 159752 | tf_op jit(solution)/shard_map/ppermute | solution.py:552
  38.0 1.2 %collective-permute-start.13 = (f32[13,8,128]{2,1,0:T(8,128)S(1)}, f32[13,8,128]{2,1,0:T(8,128)S(1)}, u32[]{:S(2)}, u32[]{:S(2)}) collective-permute-start(f32[13,8,128]{2,1,0:T(8,128)S(1)} %collective-permute-done.9.refs_2_), channel_id=1, source_target_pairs={{0,1},{1,0},{2,3},{3,2},{4,5},{5,4},{6,7},{7,6},{8,9},{9,8},{10,11... | collective-permute-start | bytes 159752 | tf_op jit(solution)/shard_map/ppermute | solution.py:552
  38.3 1.2 %collective-permute-start.14 = (f32[13,8,128]{2,1,0:T(8,128)S(1)}, f32[13,8,128]{2,1,0:T(8,128)S(1)}, u32[]{:S(2)}, u32[]{:S(2)}) collective-permute-start(f32[13,8,128]{2,1,0:T(8,128)S(1)} %collective-permute-done.10.refs_3_), channel_id=1, source_target_pairs={{0,1},{1,0},{2,3},{3,2},{4,5},{5,4},{6,7},{7,6},{8,9},{9,8},{10,11... | collective-permute-start | bytes 159752 | tf_op jit(solution)/shard_map/ppermute | solution.py:552
  38.5 1.2 %collective-permute-start.15 = (f32[13,8,128]{2,1,0:T(8,128)S(1)}, f32[13,8,128]{2,1,0:T(8,128)S(1)}, u32[]{:S(2)}, u32[]{:S(2)}) collective-permute-start(f32[13,8,128]{2,1,0:T(8,128)S(1)} %collective-permute-done.11.refs_4_), channel_id=1, source_target_pairs={{0,1},{1,0},{2,3},{3,2},{4,5},{5,4},{6,7},{7,6},{8,9},{9,8},{10,11... | collective-permute-start | bytes 159752 | tf_op jit(solution)/shard_map/ppermute | solution.py:552
